TPU v7x, 32 devices: a whole 2x2x4 slice. The times are simulated.
32 devices in a mesh: groups: 2 (over y), chan: 4 (over z), pipe: 2 (over x), space: 2 (over core).
Axes of the slice: x: 2, y: 2, z: 4, core: 2. Of those that a mesh axis runs over, the one named last changes fastest.
Arguments:
- activations: bfloat16 [2, 4, 8, 8, 16, 256], P('pipe', 'groups', None, 'space', 'chan'), parts along dimension 1, may hold values from -6 to 6
- cotangent: bfloat16 [4, 8, 8, 16, 256], P('groups', None, 'space', 'chan'), parts along dimension 0, may hold values from -1.5 to 1.5
- space_weight: bfloat16 [2, 3, 3, 256, 256], P('pipe'), may hold values from -0.125 to 0.125
- time_weight: bfloat16 [2, 3, 256, 256], P('pipe'), may hold values from -0.21875 to 0.21875
Outputs:
- input_grads: bfloat16 [2, 4, 8, 8, 16, 256], P('pipe', 'groups', None, 'space', 'chan'), parts along dimension 1
- space_grads: float32 [2, 6, 3, 256, 256], P('pipe', 'groups', None, None, 'chan'), parts along dimension 1
- time_grads: float32 [2, 6, 256, 256], P('pipe', 'groups', None, 'chan'), parts along dimension 1
There are 2 independent parts, one for each index of `groups`. A program takes and returns all parts, laid end to end along the dimension named above; an argument that names none is the same for every part. Nothing has to cross between parts.
All inputs are finite; a program needn't handle non-finite values.
Results may differ from a plain program's by a relative error of at most 0.0048.
Values may be sent and summed in bfloat16 or wider, within the bound.
No kernel may reach another device: no remote copies, remote signals or barrier semaphores. Data moves between devices by JAX's collectives and lax.ppermute only.
A program may use at most 64 MiB of HBM per device.

v0:
```python
import jax
import jax.numpy as jnp
from jax import lax
from jax.sharding import PartitionSpec as P


def passed_along(array, axis, by):
    size = lax.axis_size(axis)
    pairs = [(i, i + by) for i in range(size) if 0 <= i + by < size]
    return lax.ppermute(array, axis, pairs)


def extended(cells, sides, width):
    for axis, dim in sides:
        count = lax.axis_size(axis)
        ends = count - 1
        head = lax.slice_in_dim(cells, 0, width, axis=dim)
        tail = lax.slice_in_dim(cells, cells.shape[dim] - width, cells.shape[dim], axis=dim)
        cells = jnp.concatenate(
            [
                lax.ppermute(tail, axis, [(i, (i + 1) % count) for i in range(ends)]),
                cells,
                lax.ppermute(head, axis, [((i + 1) % count, i) for i in range(ends)]),
            ],
            axis=dim,
        )
    return cells


def silu_slope(hidden):
    sigmoid_val = jax.nn.sigmoid(hidden)
    return sigmoid_val * (1.0 + hidden * (1.0 - sigmoid_val))


def tap_columns(padded, row_count, col_count):
    channels = padded.shape[-1]
    return jnp.concatenate(
        [
            padded[:, row_tap : row_tap + row_count, col_tap : col_tap + col_count, :].reshape(
                -1, channels
            )
            for row_tap in range(3)
            for col_tap in range(3)
        ],
        axis=1,
    )


def back_columns(grad_pad, row_count, col_count):
    channels = grad_pad.shape[-1]
    return jnp.concatenate(
        [
            grad_pad[
                :, 2 - row_tap : 2 - row_tap + row_count, 2 - col_tap : 2 - col_tap + col_count, :
            ].reshape(-1, channels)
            for row_tap in range(3)
            for col_tap in range(3)
        ],
        axis=1,
    )


def temporal_grad(upstream, time_kernel):
    frames = upstream.shape[0]
    channels = upstream.shape[-1]
    later = jnp.pad(upstream, ((0, 2), (0, 0), (0, 0), (0, 0)))
    act_grad = None
    for time_tap in range(3):
        lagged = later[time_tap : time_tap + frames].reshape(-1, channels)
        term = lax.dot_general(
            lagged,
            time_kernel[time_tap],
            (((1,), (1,)), ((), ())),
            preferred_element_type=jnp.float32,
        )
        act_grad = term if act_grad is None else act_grad + term
    return act_grad


def lagged_products(active, upstream):
    frames = active.shape[0]
    channels = active.shape[-1]
    earlier = jnp.pad(active, ((2, 0), (0, 0), (0, 0), (0, 0)))
    flat_up = upstream.reshape(-1, channels)
    return jnp.stack(
        [
            lax.dot_general(
                earlier[2 - time_tap : 2 - time_tap + frames].reshape(-1, channels),
                flat_up,
                (((0,), (0,)), ((), ())),
                preferred_element_type=jnp.float32,
            )
            for time_tap in range(3)
        ]
    )


def per_device(activations, cotangent, space_weight, time_weight):
    clip_count = activations.shape[1]
    frames, rows_dev, cols_dev, channels = activations.shape[2:]
    pixels = frames * rows_dev * cols_dev
    pipe_depth = lax.axis_size("pipe")
    section_index = lax.axis_index("pipe")
    kernel_flat = space_weight[0].reshape(9 * channels, channels)
    back_kernel = jnp.transpose(space_weight[0].reshape(9, channels, channels), (0, 2, 1)).reshape(
        9 * channels, channels
    )
    time_kernel = time_weight[0]
    inputs_all = activations[0]

    def section_tick(tick_index, carried):
        outgoing, grads_out, space_total, time_total = carried
        received = passed_along(outgoing, "pipe", -1)
        clip_index = tick_index - (pipe_depth - 1 - section_index)
        active_tick = (clip_index >= 0) & (clip_index < clip_count)
        clamped = jnp.clip(clip_index, 0, clip_count - 1)
        inputs = lax.dynamic_index_in_dim(inputs_all, clamped, 0, keepdims=False)
        supplied = lax.dynamic_index_in_dim(cotangent, clamped, 0, keepdims=False)
        upstream = jnp.where(section_index == pipe_depth - 1, supplied, received)
        rimmed = extended(inputs, (("chan", 2), ("space", 1)), 1)
        columns = tap_columns(rimmed, rows_dev, cols_dev)
        hidden = jnp.dot(columns, kernel_flat, preferred_element_type=jnp.float32)
        act_grad = temporal_grad(upstream, time_kernel)
        hidden_grad = (act_grad * silu_slope(hidden)).astype(jnp.bfloat16)
        grad_pad = extended(
            hidden_grad.reshape(frames, rows_dev, cols_dev, channels),
            (("chan", 2), ("space", 1)),
            1,
        )
        active = jax.nn.silu(hidden).astype(jnp.bfloat16)
        time_tick = lagged_products(active.reshape(frames, rows_dev, cols_dev, channels), upstream)
        conv_grad = jnp.dot(
            back_columns(grad_pad, rows_dev, cols_dev),
            back_kernel,
            preferred_element_type=jnp.float32,
        )
        space_tick = lax.dot_general(
            columns, hidden_grad, (((0,), (0,)), ((), ())), preferred_element_type=jnp.float32
        )
        outgoing = (
            (upstream.reshape(pixels, channels).astype(jnp.float32) + conv_grad)
            .astype(jnp.bfloat16)
            .reshape(frames, rows_dev, cols_dev, channels)
        )
        grads_out = jnp.where(
            active_tick, lax.dynamic_update_index_in_dim(grads_out, outgoing, clamped, 0), grads_out
        )
        space_total = space_total + jnp.where(active_tick, space_tick, 0.0)
        time_total = time_total + jnp.where(active_tick, time_tick, 0.0)
        return (outgoing, grads_out, space_total, time_total)

    initial = (
        jnp.zeros_like(inputs_all[0]),
        jnp.zeros_like(inputs_all),
        jnp.zeros((9 * channels, channels), jnp.float32),
        jnp.zeros((3, channels, channels), jnp.float32),
    )
    final_state = lax.fori_loop(0, clip_count + pipe_depth - 1, section_tick, initial)
    share_width = channels // lax.axis_size("chan")
    totals_all = lax.psum((final_state[2], final_state[3]), ("chan", "space"))
    first_col = lax.axis_index("chan") * share_width
    space_part = lax.dynamic_slice_in_dim(totals_all[0], first_col, share_width, 1)
    time_part = lax.dynamic_slice_in_dim(totals_all[1], first_col, share_width, 2)
    return (
        final_state[1][None],
        space_part.reshape(3, 3, channels, share_width)[None],
        time_part[None],
    )


def solution(mesh):
    return jax.shard_map(
        per_device,
        mesh=mesh,
        in_specs=(
            P("pipe", "groups", None, "space", "chan", None),
            P("groups", None, "space", "chan", None),
            P("pipe", None, None, None, None),
            P("pipe", None, None, None),
        ),
        out_specs=(
            P("pipe", "groups", None, "space", "chan", None),
            P("pipe", "groups", None, None, "chan"),
            P("pipe", "groups", None, "chan"),
        ),
        check_vma=False,
    )
```

profile of v0, /device:TPU:0, one launch (start us, length us, event | category | flops | bytes accessed | tf_op | source)
XLA Modules:
  0.0 306.2 jit_solution(13093225324965239914)
XLA Ops:
  7.2 2.4 copy.26
  10.4 203.3 %while.22 = (s32[]{:T(128)}, bf16[8,4,4,256]{3,2,1,0:T(4,128)(2,1)S(1)}, bf16[2,8,4,4,256]{4,3,2,1,0:T(4,128)(2,1)}, f32[2304,256]{1,0:T(8,128)S(1)}, f32[3,256,...) while((s32[]{:T(128)}, ...), condition=%wide.region_1.2_spmd.clone, body=%wide.region_0.1_spmd.clone.sunk | while | flops 559874048 | bytes 33260356 | solution.py:158
  12.7 5.6 %collective-permute-start.2 = (bf16[8,4,1,256]{3,2,1,0:T(2,128)(2,1)S(1)}, bf16[8,4,1,256]{3,2,1,0:T(2,128)(2,1)S(1)}, u32[]{:S(2)}, u32[]{:S(2)}) collective-permute-start(bf16[8,4,1,256]{3,2,1,0:T(2,128)(2,1)S(1)} %get-tuple-element.532), channel_id=1, source_target_pairs={{0,4},{4,8},{8,12},{1,5},{5,9},{9,13},{2,6},{6,10},{10,14},{3,7},{... | collective-permute-start | bytes 49160 | tf_op jit(solution)/shard_map/while/body/eval_jaxpr/ppermute | solution.py:21
  21.6 3.0 collective-permute-start.4
  27.6 1.6 multiply_convert_fusion.2
  37.2 4.5 %collective-permute-start.6 = (bf16[8,4,1,256]{3,2,1,0:T(2,128)(2,1)S(1)}, bf16[8,4,1,256]{3,2,1,0:T(2,128)(2,1)S(1)}, u32[]{:S(2)}, u32[]{:S(2)}) collective-permute-start(bf16[8,4,1,256]{3,2,1,0:T(2,128)(2,1)S(1)} %get-tuple-element.547), channel_id=1, source_target_pairs={{0,4},{4,8},{8,12},{1,5},{5,9},{9,13},{2,6},{6,10},{10,14},{3,7},{... | collective-permute-start | bytes 49160 | tf_op jit(solution)/shard_map/while/body/eval_jaxpr/ppermute | solution.py:21
  44.5 2.6 collective-permute-start.7
  50.7 1.5 reshape.324
  52.2 1.8 maximum_maximum_fusion.3
  54.7 1.5 reshape.320
  56.2 1.5 reshape.321
  59.2 1.8 fusion.88
  61.0 1.5 reshape.325
  62.5 1.5 reshape.326
  73.1 1.8 add_convert_fusion.2
  76.6 1.5 select_dynamic-update-slice_fusion.2
  80.4 4.5 %collective-permute-start.2 = (bf16[8,4,1,256]{3,2,1,0:T(2,128)(2,1)S(1)}, bf16[8,4,1,256]{3,2,1,0:T(2,128)(2,1)S(1)}, u32[]{:S(2)}, u32[]{:S(2)}) collective-permute-start(bf16[8,4,1,256]{3,2,1,0:T(2,128)(2,1)S(1)} %get-tuple-element.532), channel_id=1, source_target_pairs={{0,4},{4,8},{8,12},{1,5},{5,9},{9,13},{2,6},{6,10},{10,14},{3,7},{... | collective-permute-start | bytes 49160 | tf_op jit(solution)/shard_map/while/body/eval_jaxpr/ppermute | solution.py:21
  88.3 3.2 %collective-permute-start.4 = (bf16[8,1,6,256]{3,2,1,0:T(8,128)(2,1)S(1)}, bf16[8,1,6,256]{3,2,1,0:T(8,128)(2,1)S(1)}, u32[]{:S(2)}, u32[]{:S(2)}) collective-permute-start(bf16[8,1,6,256]{3,2,1,0:T(8,128)(2,1)S(1)} %get-tuple-element.534), channel_id=1, source_target_pairs={{0,1},{2,3},{4,5},{6,7},{8,9},{10,11},{12,13},{14,15},{16,17},{18,... | collective-permute-start | bytes 73736 | tf_op jit(solution)/shard_map/while/body/eval_jaxpr/ppermute | solution.py:21
  94.5 1.6 multiply_convert_fusion.2
  104.1 4.5 %collective-permute-start.6 = (bf16[8,4,1,256]{3,2,1,0:T(2,128)(2,1)S(1)}, bf16[8,4,1,256]{3,2,1,0:T(2,128)(2,1)S(1)}, u32[]{:S(2)}, u32[]{:S(2)}) collective-permute-start(bf16[8,4,1,256]{3,2,1,0:T(2,128)(2,1)S(1)} %get-tuple-element.547), channel_id=1, source_target_pairs={{0,4},{4,8},{8,12},{1,5},{5,9},{9,13},{2,6},{6,10},{10,14},{3,7},{... | collective-permute-start | bytes 49160 | tf_op jit(solution)/shard_map/while/body/eval_jaxpr/ppermute | solution.py:21
  109.7 2.2 fusion.90
  112.6 2.3 collective-permute-start.7
  118.5 1.5 reshape.324
  120.0 1.8 maximum_maximum_fusion.3
  122.6 1.5 reshape.320
  124.0 1.5 reshape.321
  127.0 1.8 fusion.88
  128.8 1.5 reshape.325
  130.3 1.5 reshape.326
  140.9 1.8 add_convert_fusion.2
  144.4 1.5 select_dynamic-update-slice_fusion.2
  148.2 4.5 %collective-permute-start.2 = (bf16[8,4,1,256]{3,2,1,0:T(2,128)(2,1)S(1)}, bf16[8,4,1,256]{3,2,1,0:T(2,128)(2,1)S(1)}, u32[]{:S(2)}, u32[]{:S(2)}) collective-permute-start(bf16[8,4,1,256]{3,2,1,0:T(2,128)(2,1)S(1)} %get-tuple-element.532), channel_id=1, source_target_pairs={{0,4},{4,8},{8,12},{1,5},{5,9},{9,13},{2,6},{6,10},{10,14},{3,7},{... | collective-permute-start | bytes 49160 | tf_op jit(solution)/shard_map/while/body/eval_jaxpr/ppermute | solution.py:21
  156.1 3.2 %collective-permute-start.4 = (bf16[8,1,6,256]{3,2,1,0:T(8,128)(2,1)S(1)}, bf16[8,1,6,256]{3,2,1,0:T(8,128)(2,1)S(1)}, u32[]{:S(2)}, u32[]{:S(2)}) collective-permute-start(bf16[8,1,6,256]{3,2,1,0:T(8,128)(2,1)S(1)} %get-tuple-element.534), channel_id=1, source_target_pairs={{0,1},{2,3},{4,5},{6,7},{8,9},{10,11},{12,13},{14,15},{16,17},{18,... | collective-permute-start | bytes 73736 | tf_op jit(solution)/shard_map/while/body/eval_jaxpr/ppermute | solution.py:21
  162.3 1.6 multiply_convert_fusion.2
  171.9 4.5 %collective-permute-start.6 = (bf16[8,4,1,256]{3,2,1,0:T(2,128)(2,1)S(1)}, bf16[8,4,1,256]{3,2,1,0:T(2,128)(2,1)S(1)}, u32[]{:S(2)}, u32[]{:S(2)}) collective-permute-start(bf16[8,4,1,256]{3,2,1,0:T(2,128)(2,1)S(1)} %get-tuple-element.547), channel_id=1, source_target_pairs={{0,4},{4,8},{8,12},{1,5},{5,9},{9,13},{2,6},{6,10},{10,14},{3,7},{... | collective-permute-start | bytes 49160 | tf_op jit(solution)/shard_map/while/body/eval_jaxpr/ppermute | solution.py:21
  177.5 2.2 fusion.90
  180.4 2.3 collective-permute-start.7
  186.3 1.5 reshape.324
  187.8 1.8 maximum_maximum_fusion.3
  190.3 1.5 reshape.320
  191.8 1.5 reshape.321
  194.8 1.8 fusion.88
  196.6 1.5 reshape.325
  198.1 1.5 reshape.326
  208.7 1.8 add_convert_fusion.2
  212.2 1.5 select_dynamic-update-slice_fusion.2
  215.2 80.3 %all-reduce.5.cloned.1.call-done = (f32[2304,256]{1,0:T(8,128)}, f32[3,256,256]{2,1,0:T(8,128)}) async-done(((f32[2304,256]{1,0:T(8,128)}, f32[3,256,256]{2,1,0:T(8,128)}), (f32[2304,256]{1,0:T(8,128)}, f32[3,256,256]{2,1,0:T(8,128)})) %all-reduce.5.cloned.1.call-update) | async-done | bytes 3145744 | tf_op jit(solution)/shard_map/psum | solution.py:160
  295.5 1.7 constant_dynamic-slice_fusion.3
  (296 shorter events, 109.0 us)
Async XLA Ops:
  7.2 288.3 %all-reduce.5.cloned.1.call-start = ((), (), s32[]{:S(2)}) async-start(), calls=%async_computation | async-start | bytes 6291456 | tf_op jit(solution)/shard_map/psum | solution.py:160
  11.4 8.9 %collective-permute-start.1 = (bf16[8,4,1,256]{3,2,1,0:T(2,128)(2,1)S(1)}, bf16[8,4,1,256]{3,2,1,0:T(2,128)(2,1)S(1)}, u32[]{:S(2)}, u32[]{:S(2)}) collective-permute-start(bf16[8,4,1,256]{3,2,1,0:T(2,128)(2,1)S(1)} %get-tuple-element.531), channel_id=1, source_target_pairs={{4,0},{8,4},{12,8},{5,1},{9,5},{13,9},{6,2},{10,6},{14,10},{7,3},{... | collective-permute-start | bytes 49160 | tf_op jit(solution)/shard_map/while/body/eval_jaxpr/ppermute | solution.py:23
  12.7 7.6 %collective-permute-start.2 = (bf16[8,4,1,256]{3,2,1,0:T(2,128)(2,1)S(1)}, bf16[8,4,1,256]{3,2,1,0:T(2,128)(2,1)S(1)}, u32[]{:S(2)}, u32[]{:S(2)}) collective-permute-start(bf16[8,4,1,256]{3,2,1,0:T(2,128)(2,1)S(1)} %get-tuple-element.532), channel_id=1, source_target_pairs={{0,4},{4,8},{8,12},{1,5},{5,9},{9,13},{2,6},{6,10},{10,14},{3,7},{... | collective-permute-start | bytes 49160 | tf_op jit(solution)/shard_map/while/body/eval_jaxpr/ppermute | solution.py:21
  18.9 10.4 %collective-permute-start = (bf16[8,4,4,256]{3,0,2,1:T(8,128)(2,1)}, bf16[8,4,4,256]{3,0,2,1:T(8,128)(2,1)}, u32[]{:S(2)}, u32[]{:S(2)}) collective-permute-start(bf16[8,4,4,256]{3,0,2,1:T(8,128)(2,1)} %copy.46), channel_id=1, source_target_pairs={{2,0},{3,1},{6,4},{7,5},{10,8},{11,9},{14,12},{15,13},{18,16},{19,... | collective-permute-start | bytes 196616 | tf_op jit(solution)/shard_map/while/body/eval_jaxpr/ppermute | solution.py:10
  20.3 4.5 %collective-permute-start.3 = (bf16[8,1,6,256]{3,2,1,0:T(8,128)(2,1)S(1)}, bf16[8,1,6,256]{3,2,1,0:T(8,128)(2,1)S(1)}, u32[]{:S(2)}, u32[]{:S(2)}) collective-permute-start(bf16[8,1,6,256]{3,2,1,0:T(8,128)(2,1)S(1)} %get-tuple-element.533), channel_id=1, source_target_pairs={{1,0},{3,2},{5,4},{7,6},{9,8},{11,10},{13,12},{15,14},{17,16},{19,... | collective-permute-start | bytes 73736 | tf_op jit(solution)/shard_map/while/body/eval_jaxpr/ppermute | solution.py:23
  21.6 3.9 %collective-permute-start.4 = (bf16[8,1,6,256]{3,2,1,0:T(8,128)(2,1)S(1)}, bf16[8,1,6,256]{3,2,1,0:T(8,128)(2,1)S(1)}, u32[]{:S(2)}, u32[]{:S(2)}) collective-permute-start(bf16[8,1,6,256]{3,2,1,0:T(8,128)(2,1)S(1)} %get-tuple-element.534), channel_id=1, source_target_pairs={{0,1},{2,3},{4,5},{6,7},{8,9},{10,11},{12,13},{14,15},{16,17},{18,... | collective-permute-start | bytes 73736 | tf_op jit(solution)/shard_map/while/body/eval_jaxpr/ppermute | solution.py:21
  32.1 2.6 copy-start.5
  35.8 6.9 %copy-start.4 = (bf16[128,256]{1,0:T(8,128)(2,1)}, bf16[128,256]{1,0:T(8,128)(2,1)S(1)}, u32[]{:S(2)}) copy-start(bf16[128,256]{1,0:T(8,128)(2,1)S(1)} %fusion.85) | copy-start | bytes 196612 | tf_op jit(solution)/shard_map/while
  35.8 6.9 %copy-start.2 = (bf16[8,4,4,256]{3,2,1,0:T(4,128)(2,1)}, bf16[8,4,4,256]{3,2,1,0:T(4,128)(2,1)S(1)}, u32[]{:S(2)}) copy-start(bf16[8,4,4,256]{3,2,1,0:T(4,128)(2,1)S(1)} %reshape.319) | copy-start | bytes 196612 | tf_op jit(solution)/shard_map/while
  35.9 7.9 %collective-permute-start.5 = (bf16[8,4,1,256]{3,2,1,0:T(2,128)(2,1)S(1)}, bf16[8,4,1,256]{3,2,1,0:T(2,128)(2,1)S(1)}, u32[]{:S(2)}, u32[]{:S(2)}) collective-permute-start(bf16[8,4,1,256]{3,2,1,0:T(2,128)(2,1)S(1)} %get-tuple-element.546), channel_id=1, source_target_pairs={{4,0},{8,4},{12,8},{5,1},{9,5},{13,9},{6,2},{10,6},{14,10},{7,3},{... | collective-permute-start | bytes 49160 | tf_op jit(solution)/shard_map/while/body/eval_jaxpr/ppermute | solution.py:23
  37.2 6.6 %collective-permute-start.6 = (bf16[8,4,1,256]{3,2,1,0:T(2,128)(2,1)S(1)}, bf16[8,4,1,256]{3,2,1,0:T(2,128)(2,1)S(1)}, u32[]{:S(2)}, u32[]{:S(2)}) collective-permute-start(bf16[8,4,1,256]{3,2,1,0:T(2,128)(2,1)S(1)} %get-tuple-element.547), channel_id=1, source_target_pairs={{0,4},{4,8},{8,12},{1,5},{5,9},{9,13},{2,6},{6,10},{10,14},{3,7},{... | collective-permute-start | bytes 49160 | tf_op jit(solution)/shard_map/while/body/eval_jaxpr/ppermute | solution.py:21
  43.8 29.3 %copy-start.1 = (bf16[2304,256]{1,0:T(8,128)(2,1)S(1)}, bf16[2304,256]{1,0:T(8,128)(2,1)}, u32[]{:S(2)}) copy-start(bf16[2304,256]{1,0:T(8,128)(2,1)} %get-tuple-element.602) | copy-start | bytes 3538948 | tf_op jit(solution)/shard_map/while
  43.8 5.4 %copy-start.6 = (bf16[8,4,1,256]{3,2,1,0:T(2,128)(2,1)}, bf16[8,4,1,256]{3,2,1,0:T(2,128)(2,1)S(1)}, u32[]{:S(2)}) copy-start(bf16[8,4,1,256]{3,2,1,0:T(2,128)(2,1)S(1)} %collective-permute-done.5) | copy-start | bytes 49156 | tf_op jit(solution)/shard_map/while
  43.8 5.4 %copy-start.7 = (bf16[8,4,1,256]{3,2,1,0:T(2,128)(2,1)}, bf16[8,4,1,256]{3,2,1,0:T(2,128)(2,1)S(1)}, u32[]{:S(2)}) copy-start(bf16[8,4,1,256]{3,2,1,0:T(2,128)(2,1)S(1)} %collective-permute-done.6) | copy-start | bytes 49156 | tf_op jit(solution)/shard_map/while
  44.5 7.6 %collective-permute-start.7 = (bf16[8,1,6,256]{3,2,1,0:T(8,128)(2,1)}, bf16[8,1,6,256]{3,2,1,0:T(8,128)(2,1)}, u32[]{:S(2)}, u32[]{:S(2)}) collective-permute-start(bf16[8,1,6,256]{3,2,1,0:T(8,128)(2,1)} %get-tuple-element.548), channel_id=1, source_target_pairs={{0,1},{2,3},{4,5},{6,7},{8,9},{10,11},{12,13},{14,15},{16,17},{18,... | collective-permute-start | bytes 73736 | tf_op jit(solution)/shard_map/while/body/eval_jaxpr/ppermute | solution.py:21
  47.1 5.1 %collective-permute-start.8 = (bf16[8,1,6,256]{3,2,1,0:T(8,128)(2,1)}, bf16[8,1,6,256]{3,2,1,0:T(8,128)(2,1)}, u32[]{:S(2)}, u32[]{:S(2)}) collective-permute-start(bf16[8,1,6,256]{3,2,1,0:T(8,128)(2,1)} %get-tuple-element.549), channel_id=1, source_target_pairs={{1,0},{3,2},{5,4},{7,6},{9,8},{11,10},{13,12},{15,14},{17,16},{19,... | collective-permute-start | bytes 73736 | tf_op jit(solution)/shard_map/while/body/eval_jaxpr/ppermute | solution.py:23
  79.1 7.8 %collective-permute-start.1 = (bf16[8,4,1,256]{3,2,1,0:T(2,128)(2,1)S(1)}, bf16[8,4,1,256]{3,2,1,0:T(2,128)(2,1)S(1)}, u32[]{:S(2)}, u32[]{:S(2)}) collective-permute-start(bf16[8,4,1,256]{3,2,1,0:T(2,128)(2,1)S(1)} %get-tuple-element.531), channel_id=1, source_target_pairs={{4,0},{8,4},{12,8},{5,1},{9,5},{13,9},{6,2},{10,6},{14,10},{7,3},{... | collective-permute-start | bytes 49160 | tf_op jit(solution)/shard_map/while/body/eval_jaxpr/ppermute | solution.py:23
  80.4 6.6 %collective-permute-start.2 = (bf16[8,4,1,256]{3,2,1,0:T(2,128)(2,1)S(1)}, bf16[8,4,1,256]{3,2,1,0:T(2,128)(2,1)S(1)}, u32[]{:S(2)}, u32[]{:S(2)}) collective-permute-start(bf16[8,4,1,256]{3,2,1,0:T(2,128)(2,1)S(1)} %get-tuple-element.532), channel_id=1, source_target_pairs={{0,4},{4,8},{8,12},{1,5},{5,9},{9,13},{2,6},{6,10},{10,14},{3,7},{... | collective-permute-start | bytes 49160 | tf_op jit(solution)/shard_map/while/body/eval_jaxpr/ppermute | solution.py:21
  85.6 10.6 %collective-permute-start = (bf16[8,4,4,256]{3,0,2,1:T(8,128)(2,1)}, bf16[8,4,4,256]{3,0,2,1:T(8,128)(2,1)}, u32[]{:S(2)}, u32[]{:S(2)}) collective-permute-start(bf16[8,4,4,256]{3,0,2,1:T(8,128)(2,1)} %copy.46), channel_id=1, source_target_pairs={{2,0},{3,1},{6,4},{7,5},{10,8},{11,9},{14,12},{15,13},{18,16},{19,... | collective-permute-start | bytes 196616 | tf_op jit(solution)/shard_map/while/body/eval_jaxpr/ppermute | solution.py:10
  87.0 4.7 %collective-permute-start.3 = (bf16[8,1,6,256]{3,2,1,0:T(8,128)(2,1)S(1)}, bf16[8,1,6,256]{3,2,1,0:T(8,128)(2,1)S(1)}, u32[]{:S(2)}, u32[]{:S(2)}) collective-permute-start(bf16[8,1,6,256]{3,2,1,0:T(8,128)(2,1)S(1)} %get-tuple-element.533), channel_id=1, source_target_pairs={{1,0},{3,2},{5,4},{7,6},{9,8},{11,10},{13,12},{15,14},{17,16},{19,... | collective-permute-start | bytes 73736 | tf_op jit(solution)/shard_map/while/body/eval_jaxpr/ppermute | solution.py:23
  88.3 4.1 %collective-permute-start.4 = (bf16[8,1,6,256]{3,2,1,0:T(8,128)(2,1)S(1)}, bf16[8,1,6,256]{3,2,1,0:T(8,128)(2,1)S(1)}, u32[]{:S(2)}, u32[]{:S(2)}) collective-permute-start(bf16[8,1,6,256]{3,2,1,0:T(8,128)(2,1)S(1)} %get-tuple-element.534), channel_id=1, source_target_pairs={{0,1},{2,3},{4,5},{6,7},{8,9},{10,11},{12,13},{14,15},{16,17},{18,... | collective-permute-start | bytes 73736 | tf_op jit(solution)/shard_map/while/body/eval_jaxpr/ppermute | solution.py:21
  99.0 2.6 copy-start.5
  102.7 6.9 %copy-start.4 = (bf16[128,256]{1,0:T(8,128)(2,1)}, bf16[128,256]{1,0:T(8,128)(2,1)S(1)}, u32[]{:S(2)}) copy-start(bf16[128,256]{1,0:T(8,128)(2,1)S(1)} %fusion.85) | copy-start | bytes 196612 | tf_op jit(solution)/shard_map/while
  102.8 6.9 %copy-start.2 = (bf16[8,4,4,256]{3,2,1,0:T(4,128)(2,1)}, bf16[8,4,4,256]{3,2,1,0:T(4,128)(2,1)S(1)}, u32[]{:S(2)}) copy-start(bf16[8,4,4,256]{3,2,1,0:T(4,128)(2,1)S(1)} %reshape.319) | copy-start | bytes 196612 | tf_op jit(solution)/shard_map/while
  102.8 9.1 %collective-permute-start.5 = (bf16[8,4,1,256]{3,2,1,0:T(2,128)(2,1)S(1)}, bf16[8,4,1,256]{3,2,1,0:T(2,128)(2,1)S(1)}, u32[]{:S(2)}, u32[]{:S(2)}) collective-permute-start(bf16[8,4,1,256]{3,2,1,0:T(2,128)(2,1)S(1)} %get-tuple-element.546), channel_id=1, source_target_pairs={{4,0},{8,4},{12,8},{5,1},{9,5},{13,9},{6,2},{10,6},{14,10},{7,3},{... | collective-permute-start | bytes 49160 | tf_op jit(solution)/shard_map/while/body/eval_jaxpr/ppermute | solution.py:23
  104.1 7.8 %collective-permute-start.6 = (bf16[8,4,1,256]{3,2,1,0:T(2,128)(2,1)S(1)}, bf16[8,4,1,256]{3,2,1,0:T(2,128)(2,1)S(1)}, u32[]{:S(2)}, u32[]{:S(2)}) collective-permute-start(bf16[8,4,1,256]{3,2,1,0:T(2,128)(2,1)S(1)} %get-tuple-element.547), channel_id=1, source_target_pairs={{0,4},{4,8},{8,12},{1,5},{5,9},{9,13},{2,6},{6,10},{10,14},{3,7},{... | collective-permute-start | bytes 49160 | tf_op jit(solution)/shard_map/while/body/eval_jaxpr/ppermute | solution.py:21
  109.7 2.2 copy-start.3
  111.9 29.0 %copy-start.1 = (bf16[2304,256]{1,0:T(8,128)(2,1)S(1)}, bf16[2304,256]{1,0:T(8,128)(2,1)}, u32[]{:S(2)}) copy-start(bf16[2304,256]{1,0:T(8,128)(2,1)} %get-tuple-element.602) | copy-start | bytes 3538948 | tf_op jit(solution)/shard_map/while
  111.9 5.1 %copy-start.6 = (bf16[8,4,1,256]{3,2,1,0:T(2,128)(2,1)}, bf16[8,4,1,256]{3,2,1,0:T(2,128)(2,1)S(1)}, u32[]{:S(2)}) copy-start(bf16[8,4,1,256]{3,2,1,0:T(2,128)(2,1)S(1)} %collective-permute-done.5) | copy-start | bytes 49156 | tf_op jit(solution)/shard_map/while
  111.9 5.1 %copy-start.7 = (bf16[8,4,1,256]{3,2,1,0:T(2,128)(2,1)}, bf16[8,4,1,256]{3,2,1,0:T(2,128)(2,1)S(1)}, u32[]{:S(2)}) copy-start(bf16[8,4,1,256]{3,2,1,0:T(2,128)(2,1)S(1)} %collective-permute-done.6) | copy-start | bytes 49156 | tf_op jit(solution)/shard_map/while
  112.6 7.4 %collective-permute-start.7 = (bf16[8,1,6,256]{3,2,1,0:T(8,128)(2,1)}, bf16[8,1,6,256]{3,2,1,0:T(8,128)(2,1)}, u32[]{:S(2)}, u32[]{:S(2)}) collective-permute-start(bf16[8,1,6,256]{3,2,1,0:T(8,128)(2,1)} %get-tuple-element.548), channel_id=1, source_target_pairs={{0,1},{2,3},{4,5},{6,7},{8,9},{10,11},{12,13},{14,15},{16,17},{18,... | collective-permute-start | bytes 73736 | tf_op jit(solution)/shard_map/while/body/eval_jaxpr/ppermute | solution.py:21
  114.9 5.1 %collective-permute-start.8 = (bf16[8,1,6,256]{3,2,1,0:T(8,128)(2,1)}, bf16[8,1,6,256]{3,2,1,0:T(8,128)(2,1)}, u32[]{:S(2)}, u32[]{:S(2)}) collective-permute-start(bf16[8,1,6,256]{3,2,1,0:T(8,128)(2,1)} %get-tuple-element.549), channel_id=1, source_target_pairs={{1,0},{3,2},{5,4},{7,6},{9,8},{11,10},{13,12},{15,14},{17,16},{19,... | collective-permute-start | bytes 73736 | tf_op jit(solution)/shard_map/while/body/eval_jaxpr/ppermute | solution.py:23
  146.9 7.8 %collective-permute-start.1 = (bf16[8,4,1,256]{3,2,1,0:T(2,128)(2,1)S(1)}, bf16[8,4,1,256]{3,2,1,0:T(2,128)(2,1)S(1)}, u32[]{:S(2)}, u32[]{:S(2)}) collective-permute-start(bf16[8,4,1,256]{3,2,1,0:T(2,128)(2,1)S(1)} %get-tuple-element.531), channel_id=1, source_target_pairs={{4,0},{8,4},{12,8},{5,1},{9,5},{13,9},{6,2},{10,6},{14,10},{7,3},{... | collective-permute-start | bytes 49160 | tf_op jit(solution)/shard_map/while/body/eval_jaxpr/ppermute | solution.py:23
  148.2 6.6 %collective-permute-start.2 = (bf16[8,4,1,256]{3,2,1,0:T(2,128)(2,1)S(1)}, bf16[8,4,1,256]{3,2,1,0:T(2,128)(2,1)S(1)}, u32[]{:S(2)}, u32[]{:S(2)}) collective-permute-start(bf16[8,4,1,256]{3,2,1,0:T(2,128)(2,1)S(1)} %get-tuple-element.532), channel_id=1, source_target_pairs={{0,4},{4,8},{8,12},{1,5},{5,9},{9,13},{2,6},{6,10},{10,14},{3,7},{... | collective-permute-start | bytes 49160 | tf_op jit(solution)/shard_map/while/body/eval_jaxpr/ppermute | solution.py:21
  153.4 10.5 %collective-permute-start = (bf16[8,4,4,256]{3,0,2,1:T(8,128)(2,1)}, bf16[8,4,4,256]{3,0,2,1:T(8,128)(2,1)}, u32[]{:S(2)}, u32[]{:S(2)}) collective-permute-start(bf16[8,4,4,256]{3,0,2,1:T(8,128)(2,1)} %copy.46), channel_id=1, source_target_pairs={{2,0},{3,1},{6,4},{7,5},{10,8},{11,9},{14,12},{15,13},{18,16},{19,... | collective-permute-start | bytes 196616 | tf_op jit(solution)/shard_map/while/body/eval_jaxpr/ppermute | solution.py:10
  154.8 4.7 %collective-permute-start.3 = (bf16[8,1,6,256]{3,2,1,0:T(8,128)(2,1)S(1)}, bf16[8,1,6,256]{3,2,1,0:T(8,128)(2,1)S(1)}, u32[]{:S(2)}, u32[]{:S(2)}) collective-permute-start(bf16[8,1,6,256]{3,2,1,0:T(8,128)(2,1)S(1)} %get-tuple-element.533), channel_id=1, source_target_pairs={{1,0},{3,2},{5,4},{7,6},{9,8},{11,10},{13,12},{15,14},{17,16},{19,... | collective-permute-start | bytes 73736 | tf_op jit(solution)/shard_map/while/body/eval_jaxpr/ppermute | solution.py:23
  156.1 4.0 %collective-permute-start.4 = (bf16[8,1,6,256]{3,2,1,0:T(8,128)(2,1)S(1)}, bf16[8,1,6,256]{3,2,1,0:T(8,128)(2,1)S(1)}, u32[]{:S(2)}, u32[]{:S(2)}) collective-permute-start(bf16[8,1,6,256]{3,2,1,0:T(8,128)(2,1)S(1)} %get-tuple-element.534), channel_id=1, source_target_pairs={{0,1},{2,3},{4,5},{6,7},{8,9},{10,11},{12,13},{14,15},{16,17},{18,... | collective-permute-start | bytes 73736 | tf_op jit(solution)/shard_map/while/body/eval_jaxpr/ppermute | solution.py:21
  166.8 2.6 copy-start.5
  170.5 6.9 %copy-start.4 = (bf16[128,256]{1,0:T(8,128)(2,1)}, bf16[128,256]{1,0:T(8,128)(2,1)S(1)}, u32[]{:S(2)}) copy-start(bf16[128,256]{1,0:T(8,128)(2,1)S(1)} %fusion.85) | copy-start | bytes 196612 | tf_op jit(solution)/shard_map/while
  170.5 6.9 %copy-start.2 = (bf16[8,4,4,256]{3,2,1,0:T(4,128)(2,1)}, bf16[8,4,4,256]{3,2,1,0:T(4,128)(2,1)S(1)}, u32[]{:S(2)}) copy-start(bf16[8,4,4,256]{3,2,1,0:T(4,128)(2,1)S(1)} %reshape.319) | copy-start | bytes 196612 | tf_op jit(solution)/shard_map/while
  170.6 9.1 %collective-permute-start.5 = (bf16[8,4,1,256]{3,2,1,0:T(2,128)(2,1)S(1)}, bf16[8,4,1,256]{3,2,1,0:T(2,128)(2,1)S(1)}, u32[]{:S(2)}, u32[]{:S(2)}) collective-permute-start(bf16[8,4,1,256]{3,2,1,0:T(2,128)(2,1)S(1)} %get-tuple-element.546), channel_id=1, source_target_pairs={{4,0},{8,4},{12,8},{5,1},{9,5},{13,9},{6,2},{10,6},{14,10},{7,3},{... | collective-permute-start | bytes 49160 | tf_op jit(solution)/shard_map/while/body/eval_jaxpr/ppermute | solution.py:23
  171.9 7.8 %collective-permute-start.6 = (bf16[8,4,1,256]{3,2,1,0:T(2,128)(2,1)S(1)}, bf16[8,4,1,256]{3,2,1,0:T(2,128)(2,1)S(1)}, u32[]{:S(2)}, u32[]{:S(2)}) collective-permute-start(bf16[8,4,1,256]{3,2,1,0:T(2,128)(2,1)S(1)} %get-tuple-element.547), channel_id=1, source_target_pairs={{0,4},{4,8},{8,12},{1,5},{5,9},{9,13},{2,6},{6,10},{10,14},{3,7},{... | collective-permute-start | bytes 49160 | tf_op jit(solution)/shard_map/while/body/eval_jaxpr/ppermute | solution.py:21
  177.5 2.2 copy-start.3
  179.7 29.0 %copy-start.1 = (bf16[2304,256]{1,0:T(8,128)(2,1)S(1)}, bf16[2304,256]{1,0:T(8,128)(2,1)}, u32[]{:S(2)}) copy-start(bf16[2304,256]{1,0:T(8,128)(2,1)} %get-tuple-element.602) | copy-start | bytes 3538948 | tf_op jit(solution)/shard_map/while
  179.7 5.1 %copy-start.6 = (bf16[8,4,1,256]{3,2,1,0:T(2,128)(2,1)}, bf16[8,4,1,256]{3,2,1,0:T(2,128)(2,1)S(1)}, u32[]{:S(2)}) copy-start(bf16[8,4,1,256]{3,2,1,0:T(2,128)(2,1)S(1)} %collective-permute-done.5) | copy-start | bytes 49156 | tf_op jit(solution)/shard_map/while
  179.7 5.1 %copy-start.7 = (bf16[8,4,1,256]{3,2,1,0:T(2,128)(2,1)}, bf16[8,4,1,256]{3,2,1,0:T(2,128)(2,1)S(1)}, u32[]{:S(2)}) copy-start(bf16[8,4,1,256]{3,2,1,0:T(2,128)(2,1)S(1)} %collective-permute-done.6) | copy-start | bytes 49156 | tf_op jit(solution)/shard_map/while
  180.4 7.4 %collective-permute-start.7 = (bf16[8,1,6,256]{3,2,1,0:T(8,128)(2,1)}, bf16[8,1,6,256]{3,2,1,0:T(8,128)(2,1)}, u32[]{:S(2)}, u32[]{:S(2)}) collective-permute-start(bf16[8,1,6,256]{3,2,1,0:T(8,128)(2,1)} %get-tuple-element.548), channel_id=1, source_target_pairs={{0,1},{2,3},{4,5},{6,7},{8,9},{10,11},{12,13},{14,15},{16,17},{18,... | collective-permute-start | bytes 73736 | tf_op jit(solution)/shard_map/while/body/eval_jaxpr/ppermute | solution.py:21
  182.7 5.1 %collective-permute-start.8 = (bf16[8,1,6,256]{3,2,1,0:T(8,128)(2,1)}, bf16[8,1,6,256]{3,2,1,0:T(8,128)(2,1)}, u32[]{:S(2)}, u32[]{:S(2)}) collective-permute-start(bf16[8,1,6,256]{3,2,1,0:T(8,128)(2,1)} %get-tuple-element.549), channel_id=1, source_target_pairs={{1,0},{3,2},{5,4},{7,6},{9,8},{11,10},{13,12},{15,14},{17,16},{19,... | collective-permute-start | bytes 73736 | tf_op jit(solution)/shard_map/while/body/eval_jaxpr/ppermute | solution.py:23
  (9 other events, 10.2 us)
Sparse Core Ops, SparseCore 0:
  215.3 80.1 all-reduce.4
where the time goes:
time: 311 us; the launch traced here: 306 us
  local copies, waits for them, and re-layouts  91.3 us (29%)
  waiting for transfers between devices  82.3 us (26%)
  starting transfers between devices  64.2 us (21%)
  matrix products  29.2 us (9%)
  other arithmetic  23.7 us (8%)
  between operations  14.1 us (5%)
    psum x1, waiting for transfers between devices, per_device(): totals_all = lax.psum((final_state[2], final_state[3]), ('chan', 'space'))  80.3 us
    ppermute x12, starting transfers between devices, extended(): lax.ppermute(tail, axis, [(i, (i + 1) % count) for i in range(ends)])  44.9 us
    reshape x24, local copies, waits for them, and re-layouts, back_columns(): return jnp.concatenate([grad_pad[:, 2 - row_tap:2 - row_tap + row_count,...  35.7 us
    while x105, local copies, waits for them, and re-layouts  25.1 us
    ppermute x12, starting transfers between devices, extended(): lax.ppermute(head, axis, [((i + 1) % count, i) for i in range(ends)])  15.5 us
    concatenate x18, other arithmetic, extended(): jnp.concatenate([lax.ppermute(tail, axis, [(i, (i + 1) % count) for i in...  11.2 us
    dot_general x9, matrix products, temporal_grad(): lax.dot_general(lagged, time_kernel[time_tap], (((1,), (1,)), ((), ())),...  9.92 us
    slice x6, local copies, waits for them, and re-layouts, back_columns(): grad_pad[:, 2 - row_tap:2 - row_tap + row_count, 2 - col_tap:2 - col_tap...  7.61 us
  transfers between devices with their start and end apart: 28, of which 4 were waited for; matrix products, arithmetic and copies ran while one was open for 11% of the time, Pallas kernels for 0%

commit v1 on v0

v1 whole, which is shorter than its diff:
```python
import functools

import jax
import jax.numpy as jnp
from jax import lax
from jax.experimental import pallas as pl
from jax.experimental.pallas import tpu as pltpu
from jax.sharding import PartitionSpec as P

F32 = jnp.float32
BF16 = jnp.bfloat16
VMEM_LIMIT = 50 * 1024 * 1024


def frame_shift(term, lag, frames):
    rows = term.shape[0]
    moved = pltpu.roll(term, rows - lag, 0)
    frame = lax.broadcasted_iota(jnp.int32, term.shape, 0) % frames
    return jnp.where(frame < frames - lag, moved, 0.0)


def fill_padded(padded, blocks, pad):
    rows_all, cols_all, steps, channels = padded.shape
    padded[0:pad] = jnp.zeros((pad, cols_all, steps, channels), padded.dtype)
    padded[rows_all - pad :] = jnp.zeros((pad, cols_all, steps, channels), padded.dtype)
    padded[:, 0:pad] = jnp.zeros((rows_all, pad, steps, channels), padded.dtype)
    padded[:, cols_all - pad :] = jnp.zeros((rows_all, pad, steps, channels), padded.dtype)
    space, chan, rows, cols = blocks.shape[:4]
    for i in range(space):
        for j in range(chan):
            padded[pad + i * rows : pad + (i + 1) * rows, pad + j * cols : pad + (j + 1) * cols] = (
                blocks[i, j]
            )


def slope_of(hidden):
    sig = jax.nn.sigmoid(hidden)
    return sig * (1.0 + hidden * (1.0 - sig))


def window_slope_kernel(x_ref, w_ref, slope_ref, xp_ref):
    space, chan, rows, cols, steps, channels = x_ref.shape
    fill_padded(xp_ref, x_ref, 2)
    r0 = lax.axis_index("space") * rows
    c0 = lax.axis_index("chan") * cols
    hidden = None
    for u in range(3):
        for v in range(3):
            piece = xp_ref[pl.ds(r0 + u, rows + 2), pl.ds(c0 + v, cols + 2)]
            term = jnp.dot(
                piece.reshape(-1, channels), w_ref[3 * u + v], preferred_element_type=F32
            )
            hidden = term if hidden is None else hidden + term
    slope_ref[...] = slope_of(hidden)


def own_window(gp_ref, slope_ref, wt_ref, twc_ref, out_ref, hg_ref, frames):
    rows, cols, steps, channels = out_ref.shape
    r0 = lax.axis_index("space") * rows
    c0 = lax.axis_index("chan") * cols
    window = gp_ref[pl.ds(r0, rows + 2), pl.ds(c0, cols + 2)].reshape(-1, channels)
    lagged = jnp.dot(window, twc_ref[...], preferred_element_type=F32)
    act = lagged[:, :channels]
    for lag in (1, 2):
        act = act + frame_shift(lagged[:, lag * channels : (lag + 1) * channels], lag, frames)
    hg_ref[...] = (act * slope_ref[...]).astype(BF16).reshape(hg_ref.shape)
    conv = None
    for u in range(3):
        for v in range(3):
            piece = hg_ref[2 - u : 2 - u + rows, 2 - v : 2 - v + cols]
            term = jnp.dot(
                piece.reshape(-1, channels), wt_ref[3 * u + v], preferred_element_type=F32
            )
            conv = term if conv is None else conv + term
    own = gp_ref[pl.ds(r0 + 1, rows), pl.ds(c0 + 1, cols)].reshape(-1, channels)
    out_ref[...] = (own.astype(F32) + conv).astype(BF16).reshape(out_ref.shape)


def tick_kernel(frames, g_ref, slope_ref, wt_ref, twc_ref, out_ref, gp_ref, hg_ref):
    fill_padded(gp_ref, g_ref, 1)
    own_window(gp_ref, slope_ref, wt_ref, twc_ref, out_ref, hg_ref, frames)


def tile_kernel(share, x_ref, w_ref, act_ref, xt_ref, slope_ref, xp_ref):
    space, chan, rows, cols, steps, channels = x_ref.shape
    fill_padded(xp_ref, x_ref, 1)
    width = chan * cols
    span = width * steps
    for i in range(space * rows):
        hidden = None
        for u in range(3):
            for v in range(3):
                piece = xp_ref[i + u, v : v + width].reshape(-1, channels)
                term = jnp.dot(piece, w_ref[3 * u + v], preferred_element_type=F32)
                hidden = term if hidden is None else hidden + term
        active = (hidden * jax.nn.sigmoid(hidden)).astype(BF16)
        act_ref[:, i * span : (i + 1) * span] = active.T
        slope_ref[i * span : (i + 1) * span, :] = slope_of(hidden[:, :share])
        xt_ref[:, i * span : (i + 1) * span] = xp_ref[i + 1, 1 : 1 + width].reshape(-1, channels).T


def final_kernel(
    frames,
    g_ref,
    slope_w_ref,
    slope_s_ref,
    act_ref,
    xt_ref,
    wt_ref,
    twc_ref,
    pick_ref,
    out_ref,
    space_ref,
    time_ref,
    gp_ref,
    hg_ref,
    hs_ref,
    hcols_ref,
    gcols_ref,
):
    space, chan, rows, cols, steps, channels = g_ref.shape
    share = slope_s_ref.shape[1]
    width = chan * cols
    height = space * rows
    span = width * steps
    fill_padded(gp_ref, g_ref, 1)
    own_window(gp_ref, slope_w_ref, wt_ref, twc_ref, out_ref, hg_ref, frames)
    hs_ref[...] = jnp.zeros(hs_ref.shape, BF16)
    for i in range(height):
        block = gp_ref[i + 1, 1 : 1 + width].reshape(-1, channels)
        mixed = jnp.dot(block, pick_ref[...], preferred_element_type=F32)
        act = mixed[:, :share]
        for lag in (1, 2):
            act = act + frame_shift(mixed[:, lag * share : (lag + 1) * share], lag, frames)
        grad = (act * slope_s_ref[i * span : (i + 1) * span, :]).astype(BF16)
        hs_ref[i + 1, 1 : 1 + width] = grad.reshape(width, steps, share)
        own = mixed[:, 3 * share :]
        for lag in range(3):
            shifted = own if lag == 0 else frame_shift(own, lag, frames)
            gcols_ref[i * span : (i + 1) * span, lag * share : (lag + 1) * share] = shifted.astype(
                BF16
            )
    for u in range(3):
        for v in range(3):
            tap = 3 * u + v
            for i in range(height):
                hcols_ref[i * span : (i + 1) * span, tap * share : (tap + 1) * share] = hs_ref[
                    i + 2 - u, 2 - v : 2 - v + width
                ].reshape(-1, share)
    time_sum = jnp.dot(act_ref[...], gcols_ref[...], preferred_element_type=F32)
    first = lax.axis_index("chan")
    for j in range(chan):
        place = pl.multiple_of(lax.rem(first + j, chan) * share, share)
        for lag in range(3):
            time_ref[lag, pl.ds(place, share), :] = time_sum[
                j * share : (j + 1) * share, lag * share : (lag + 1) * share
            ]
    space_sum = jnp.dot(xt_ref[...], hcols_ref[...], preferred_element_type=F32)
    for tap in range(9):
        space_ref[tap] = space_sum[:, tap * share : (tap + 1) * share]


def call(kernel, outs, scratch, flops, moved, *operands):
    return pl.pallas_call(
        kernel,
        out_shape=outs,
        scratch_shapes=scratch,
        compiler_params=pltpu.CompilerParams(vmem_limit_bytes=VMEM_LIMIT),
        cost_estimate=pl.CostEstimate(flops=flops, bytes_accessed=moved, transcendentals=0),
    )(*operands)


def per_device(activations, cotangent, space_weight, time_weight):
    clips, frames, rows, cols, channels = activations.shape[1:]
    steps = clips * frames
    space, chan = lax.axis_size("space"), lax.axis_size("chan")
    depth = lax.axis_size("pipe")
    stage = lax.axis_index("pipe")
    share = channels // chan
    height, width = space * rows, chan * cols
    count = height * width * steps
    win = (rows + 2) * (cols + 2) * steps
    first_col = lax.axis_index("chan") * share

    def cells(array):
        return jnp.transpose(array, (2, 3, 0, 1, 4)).reshape(rows, cols, steps, channels)

    def gathered(block):
        whole = lax.all_gather(block, ("space", "chan"), axis=0, tiled=False)
        return whole.reshape(space, chan, rows, cols, steps, channels)

    x_own = cells(activations[0])
    cot_own = cells(cotangent)
    x_all = gathered(x_own)
    up_all = gathered(cot_own)

    order = jnp.roll(space_weight[0].reshape(9, channels, channels), -first_col, axis=2)
    order_back = jnp.transpose(order, (0, 2, 1))
    time_rolled = jnp.roll(time_weight[0], -first_col, axis=1)
    time_back = jnp.transpose(time_rolled, (2, 0, 1))
    time_cat = time_back.reshape(channels, 3 * channels)
    chosen = jax.nn.one_hot(first_col + jnp.arange(share), channels, axis=0, dtype=BF16)
    pick = jnp.concatenate([time_back[:, k, :share] for k in range(3)] + [chosen], axis=1)

    cell = (steps, channels)
    slope_w = call(
        window_slope_kernel,
        jax.ShapeDtypeStruct((win, channels), F32),
        [pltpu.VMEM((height + 4, width + 4) + cell, BF16)],
        2 * win * 9 * channels * channels,
        4_000_000,
        x_all,
        order,
    )
    padded = pltpu.VMEM((height + 2, width + 2) + cell, BF16)
    hg_win = pltpu.VMEM((rows + 2, cols + 2) + cell, BF16)
    for _ in range(depth - 1):
        g_own = call(
            functools.partial(tick_kernel, frames),
            jax.ShapeDtypeStruct((rows, cols) + cell, BF16),
            [padded, hg_win],
            2 * win * 9 * channels * channels,
            4_000_000,
            up_all,
            slope_w,
            order_back,
            time_cat,
        )
        received = lax.ppermute(g_own, "pipe", [(i, i - 1) for i in range(1, depth)])
        up_all = gathered(jnp.where(stage == depth - 1, cot_own, received))
    act_t, x_t, slope_s = call(
        functools.partial(tile_kernel, share),
        (
            jax.ShapeDtypeStruct((channels, count), BF16),
            jax.ShapeDtypeStruct((channels, count), BF16),
            jax.ShapeDtypeStruct((count, share), F32),
        ),
        [padded],
        2 * count * 9 * channels * channels,
        6_000_000,
        x_all,
        order,
    )
    grads, space_grad, time_grad = call(
        functools.partial(final_kernel, frames),
        (
            jax.ShapeDtypeStruct((rows, cols) + cell, BF16),
            jax.ShapeDtypeStruct((9, channels, share), F32),
            jax.ShapeDtypeStruct((3, channels, share), F32),
        ),
        [
            padded,
            hg_win,
            pltpu.VMEM((height + 2, width + 2, steps, share), BF16),
            pltpu.VMEM((count, 9 * share), BF16),
            pltpu.VMEM((count, 3 * share), BF16),
        ],
        4 * win * 9 * channels * channels,
        8_000_000,
        up_all,
        slope_w,
        slope_s,
        act_t,
        x_t,
        order_back,
        time_cat,
        pick,
    )
    grads = jnp.transpose(
        grads.reshape(rows, cols, clips, frames, channels), (2, 3, 0, 1, 4)
    )
    return (
        grads[None],
        space_grad.reshape(3, 3, channels, share)[None],
        time_grad[None],
    )


def solution(mesh):
    return jax.shard_map(
        per_device,
        mesh=mesh,
        in_specs=(
            P("pipe", "groups", None, "space", "chan", None),
            P("groups", None, "space", "chan", None),
            P("pipe", None, None, None, None),
            P("pipe", None, None, None),
        ),
        out_specs=(
            P("pipe", "groups", None, "space", "chan", None),
            P("pipe", "groups", None, None, "chan"),
            P("pipe", "groups", None, "chan"),
        ),
        check_vma=False,
    )
```

time: 311 us -> 110 us (0.35); the launches traced: 306 us -> 109 us
  local copies, waits for them, and re-layouts: 91.3 us -> 17.3 us
  starting transfers between devices: 64.2 us -> 1.41 us
  matrix products: 29.2 us -> 0 us
  waiting for transfers between devices: 82.3 us -> 58.3 us
  other arithmetic: 23.7 us -> 5.03 us
  Pallas kernels: 0 us -> 13.4 us
    psum x1 -> x0, waiting for transfers between devices: 80.3 us -> none  [per_device(): totals_all = lax.psum((final_state[2], final_state[3]), ('chan', 'space'))]
    ppermute x27 -> x1, starting transfers between devices: 64.2 us -> 1.29 us  [per_device(): lax.ppermute(g_own, 'pipe', [(i, i - 1) for i in range(1, depth)])]
    all_gather x0 -> x3, waiting for transfers between devices: none -> 52 us  [gathered(): whole = lax.all_gather(block, ('space', 'chan'), axis=0, tiled=False)]
    reshape x72 -> x2, local copies, waits for them, and re-layouts: 41.2 us -> 0.89 us  [the longest x1 0.72 us: per_device(): grads.reshape(rows, cols, clips, frames, channels)]
    dot_general x27 -> x0, matrix products: 29.2 us -> none  [the longest x9 9.92 us: temporal_grad(): lax.dot_general(lagged, time_kernel[time_tap], (((1,), (1,)), ((), ())),...]
    while x105 -> x0, local copies, waits for them, and re-layouts: 25.1 us -> none
    pallas_call x0 -> x4, Pallas kernels: none -> 13.4 us  [call(): pl.pallas_call(kernel, out_shape=outs, scratch_shapes=scratch, compiler_p...]
    concatenate x18 -> x2, other arithmetic: 11.2 us -> 1.78 us  [the longest x1 1.66 us: per_device(): jnp.roll(space_weight[0].reshape(9, channels, channels), -first_col, axis=2)]
  transfers between devices with their start and end apart: 28 -> 4, of which waited for: 4 -> 4; matrix products, arithmetic and copies ran while one was open for 11% -> 9% of each run, Pallas kernels for 0% -> 5%
where the time goes in v1:
time: 110 us; the launch traced here: 109 us
  waiting for transfers between devices  58.3 us (53%)
  local copies, waits for them, and re-layouts  17.3 us (16%)
  between operations  14 us (13%)
  Pallas kernels  13.4 us (12%)
  other arithmetic  5.03 us (5%)
  starting transfers between devices  1.41 us (1%)
    all_gather x3, waiting for transfers between devices, gathered(): whole = lax.all_gather(block, ('space', 'chan'), axis=0, tiled=False)  52 us
    pallas_call x4, Pallas kernels, call(): pl.pallas_call(kernel, out_shape=outs, scratch_shapes=scratch, compiler_p...  13.4 us
    unnamed x28, local copies, waits for them, and re-layouts  11.4 us
    ppermute x1, waiting for transfers between devices, per_device(): lax.ppermute(g_own, 'pipe', [(i, i - 1) for i in range(1, depth)])  6.22 us
    transpose x2, local copies, waits for them, and re-layouts, cells(): jnp.transpose(array, (2, 3, 0, 1, 4)).reshape(rows, cols, steps, channels)  3.2 us
  transfers between devices with their start and end apart: 4, of which 4 were waited for; matrix products, arithmetic and copies ran while one was open for 9% of the time, Pallas kernels for 5%

profile of v1, /device:TPU:0, one launch (start us, length us, event | category | flops | bytes accessed | tf_op | source)
XLA Modules:
  0.0 109.3 jit_solution(17884591212161673823)
XLA Ops:
  7.2 0.0 all-gather.7.cloned.1.call-start
  7.2 1.6 %copy.48 = bf16[4,4,2,8,256]{4,3,2,1,0:T(8,128)(2,1)} copy(bf16[4,4,2,8,256]{4,1,0,3,2:T(4,128)(2,1)} %bitcast.51) | data formatting | bytes 262144 | tf_op jit(solution)/shard_map/transpose | solution.py:186
  8.8 0.0 all-gather.7.cloned.1.call-update
  8.8 0.0 all-gather.5.cloned.1.call-start
  8.9 1.6 %copy.49 = bf16[4,4,2,8,256]{4,3,2,1,0:T(8,128)(2,1)} copy(bf16[4,4,2,8,256]{4,1,0,3,2:T(4,128)(2,1)} %bitcast.47) | data formatting | bytes 262144 | tf_op jit(solution)/shard_map/transpose | solution.py:186
  10.5 0.0 all-gather.5.cloned.1.call-update
  10.5 0.0 all-gather.9.cloned.1.call-start
  10.6 1.2 %copy.35 = bf16[1,3,256,256]{2,3,1,0:T(8,128)(2,1)S(1)} copy(bf16[1,3,256,256]{3,2,1,0:T(8,128)(2,1)} %param.7) | data formatting | bytes 786432 | tf_op args[3]
  11.8 0.0 copy-start.10
  11.8 0.4 fusion.2
  12.1 0.0 copy-start.8
  12.2 0.2 copy.36
  12.3 0.6 copy-done.8
  12.9 0.2 copy.37.twc_ref
  13.1 0.0 copy-done.10
  13.1 0.7 copy.33
  13.8 0.0 copy-start.7
  13.8 1.7 %fusion = bf16[9,256,256]{1,2,0:T(8,128)(2,1)} fusion(s32[]{:T(128)S(6)} %select_n.29, bf16[9,256,256]{1,2,0:T(8,128)(2,1)S(1)} %bitcast.42), kind=kLoop, calls=%fused_computation.2 | loop fusion | flops 2359296 | bytes 2359300 | tf_op jit(solution)/shard_map/jit(_roll_dynamic)/concatenate | solution.py:197
  15.5 0.0 copy-done.7
  15.5 1.6 %copy.34.w_ref = bf16[9,256,256]{2,1,0:T(8,128)(2,1)S(1)} copy(bf16[9,256,256]{1,2,0:T(8,128)(2,1)} %fusion) | data formatting | bytes 2359296 | tf_op jit(solution)/shard_map/jit(_roll_dynamic)/dynamic_slice | solution.py:197
  17.1 0.0 copy-start.1
  17.1 2.2 %fusion.4.wt_ref = bf16[9,256,256]{2,1,0:T(8,128)(2,1)S(1)} fusion(s32[]{:T(128)S(6)} %select_n.29, bf16[9,256,256]{1,2,0:T(8,128)(2,1)} %bitcast.43), kind=kLoop, calls=%fused_computation.18 | loop fusion | flops 2359296 | bytes 2359300 | tf_op jit(solution)/shard_map/transpose | solution.py:198
  19.2 0.0 copy-start
  19.2 15.8 %all-gather.7.cloned.1.call-done = bf16[8,4,4,16,256]{4,3,2,1,0:T(8,128)(2,1)} async-done(((bf16[1,4,4,16,256]{4,3,2,1,0:T(8,128)(2,1)}), bf16[8,4,4,16,256]{4,3,2,1,0:T(8,128)(2,1)}) %all-gather.7.cloned.1.call-update) | async-done | bytes 1048592 | tf_op jit(solution)/shard_map/all_gather | solution.py:189
  35.0 0.0 copy-done.1
  35.0 1.2 %copy-done.6 = bf16[8,4,4,16,256]{4,3,2,1,0:T(8,128)(2,1)S(1)} copy-done((bf16[8,4,4,16,256]{4,3,2,1,0:T(8,128)(2,1)S(1)}, bf16[8,4,4,16,256]{4,3,2,1,0:T(8,128)(2,1)}, u32[]{:S(2)}) %copy-start.6) | copy-done | bytes 1048600
  36.2 1.0 shard_map.67.slope_ref.slope_w_ref
  37.2 21.7 %all-gather.5.cloned.1.call-done = bf16[8,4,4,16,256]{4,3,2,1,0:T(8,128)(2,1)} async-done(((bf16[1,4,4,16,256]{4,3,2,1,0:T(8,128)(2,1)}), bf16[8,4,4,16,256]{4,3,2,1,0:T(8,128)(2,1)}) %all-gather.5.cloned.1.call-update) | async-done | bytes 1048592 | tf_op jit(solution)/shard_map/all_gather | solution.py:189
  58.9 0.0 copy-done
  58.9 1.2 %copy-done.2 = bf16[8,4,4,16,256]{4,3,2,1,0:T(8,128)(2,1)S(1)} copy-done((bf16[8,4,4,16,256]{4,3,2,1,0:T(8,128)(2,1)S(1)}, bf16[8,4,4,16,256]{4,3,2,1,0:T(8,128)(2,1)}, u32[]{:S(2)}) %copy-start.2) | copy-done | bytes 1048600
  60.2 1.3 %shard_map.68 = bf16[4,4,16,256]{3,2,1,0:T(8,128)(2,1)S(1)} custom-call(bf16[2,4,4,4,16,256]{5,4,3,2,1,0:T(8,128)(2,1)S(1)} %bitcast.36, f32[576,256]{1,0:T(8,128)S(1)} %shard_map.67.slope_ref.slope_w_ref, bf16[9,256,256]{2,1,0:T(8,128)(2,1)S(1)} %fusion.4.wt_ref, bf16[256,768]{1,0:T(8,128)(2,1)S(1)} %copy.37.twc_ref), custom_call_target="tpu_custom_call" | custom-call | flops 679477248 | bytes 4000000 | tf_op jit(solution)/shard_map/pallas_call | solution.py:164
  61.5 1.3 %collective-permute-start = (bf16[4,4,16,256]{3,2,1,0:T(8,128)(2,1)S(1)}, bf16[4,4,16,256]{3,2,1,0:T(8,128)(2,1)S(1)}, u32[]{:S(2)}, u32[]{:S(2)}) collective-permute-start(bf16[4,4,16,256]{3,2,1,0:T(8,128)(2,1)S(1)} %shard_map.68), channel_id=1, source_target_pairs={{2,0},{3,1},{6,4},{7,5},{10,8},{11,9},{14,12},{15,13},{18,16},{19,... | collective-permute-start | bytes 393224 | tf_op jit(solution)/shard_map/ppermute | solution.py:229
  62.8 6.2 %collective-permute-done = bf16[4,4,16,256]{3,2,1,0:T(8,128)(2,1)S(1)} collective-permute-done((bf16[4,4,16,256]{3,2,1,0:T(8,128)(2,1)S(1)}, bf16[4,4,16,256]{3,2,1,0:T(8,128)(2,1)S(1)}, u32[]{:S(2)}, u32[]{:S(2)}) %collective-permute-start) | collective-permute-done | bytes 131104 | tf_op jit(solution)/shard_map/ppermute | solution.py:229
  69.0 0.0 copy-done.11
  69.0 0.7 bitcast_select_fusion
  69.7 0.0 all-gather.9.cloned.1.call-update
  69.8 0.0 copy-done.9
  69.8 0.1 pad_maximum_fusion.pick_ref
  69.9 4.4 %shard_map.69 = (bf16[256,2048]{1,0:T(8,128)(2,1)S(1)}, bf16[256,2048]{1,0:T(8,128)(2,1)S(1)}, f32[2048,64]{1,0:T(8,128)S(1)}) custom-call(bf16[2,4,4,4,16,256]{5,4,3,2,1,0:T(8,128)(2,1)} %bitcast.38, bf16[9,256,256]{2,1,0:T(8,128)(2,1)} %copy-done.1), custom_call_target="tpu_custom_call" | custom-call | flops 2415919104 | bytes 6000000 | tf_op jit(solution)/shard_map/pallas_call | solution.py:164
  74.3 0.0 copy-start.4
  74.3 1.0 copy-done.4
  75.3 1.0 copy-done.5
  76.3 14.5 %all-gather.9.cloned.1.call-done = bf16[32,4,16,256]{3,2,1,0:T(8,128)(2,1)} async-done(((bf16[4,4,16,256]{3,2,1,0:T(8,128)(2,1)}), bf16[32,4,16,256]{3,2,1,0:T(8,128)(2,1)}) %all-gather.9.cloned.1.call-update) | async-done | bytes 1048592 | tf_op jit(solution)/shard_map/all_gather | solution.py:189
  90.8 1.2 %copy-done.3 = bf16[32,4,16,256]{3,2,1,0:T(8,128)(2,1)S(1)} copy-done((bf16[32,4,16,256]{3,2,1,0:T(8,128)(2,1)S(1)}, bf16[32,4,16,256]{3,2,1,0:T(8,128)(2,1)}, u32[]{:S(2)}) %copy-start.3) | copy-done | bytes 1048600
  92.0 6.7 %shard_map.70 = (bf16[4,4,16,256]{3,2,1,0:T(8,128)(2,1)S(1)}, f32[9,256,64]{2,1,0:T(8,128)}, f32[3,256,64]{2,1,0:T(8,128)S(1)}) custom-call(bf16[2,4,4,4,16,256]{5,4,3,2,1,0:T(8,128)(2,1)S(1)} %bitcast.37, f32[576,256]{1,0:T(8,128)S(1)} %shard_map.67.slope_ref.slope_w_ref, f32[2048,64]{1,0:T(8,128)S(1)} %get-tuple-element.9.slope_s_ref, ...), custom_call_target="tpu_custom_call" | custom-call | flops 1358954496 | bytes 8000000 | tf_op jit(solution)/shard_map/pallas_call | solution.py:164
  98.8 0.7 copy.47
  99.5 2.4 %copy.41 = f32[1,3,3,256,64]{3,4,2,1,0:T(8,128)} copy(f32[1,3,3,256,64]{4,3,2,1,0:T(8,128)} %bitcast.46) | data formatting | bytes 1179648
  101.9 0.8 copy.42
  (9 shorter events, 0.1 us)
Async XLA Ops:
  7.2 27.8 %all-gather.7.cloned.1.call-start = ((), (), s32[]{:S(2)}) async-start(), calls=%async_computation.1 | async-start | bytes 1179648 | tf_op jit(solution)/shard_map/all_gather | solution.py:189
  8.8 50.1 %all-gather.5.cloned.1.call-start = ((), (), s32[]{:S(2)}) async-start(), calls=%async_computation | async-start | bytes 1179648 | tf_op jit(solution)/shard_map/all_gather | solution.py:189
  10.5 80.3 %all-gather.9.cloned.1.call-start = ((), (), s32[]{:S(2)}) async-start(), calls=%async_computation.2 | async-start | bytes 1179648 | tf_op jit(solution)/shard_map/all_gather | solution.py:189
  11.8 1.3 %copy-start.10 = (bf16[1,3,3,256,256]{4,3,2,1,0:T(8,128)(2,1)S(1)}, bf16[1,3,3,256,256]{4,3,2,1,0:T(8,128)(2,1)}, u32[]{:S(2)}) copy-start(bf16[1,3,3,256,256]{4,3,2,1,0:T(8,128)(2,1)} %param.6) | copy-start | bytes 3538948
  12.1 0.7 copy-start.8
  13.8 1.7 %copy-start.7 = (bf16[1,3,3,256,256]{3,4,2,1,0:T(8,128)(2,1)}, bf16[1,3,3,256,256]{3,4,2,1,0:T(8,128)(2,1)S(1)}, u32[]{:S(2)}) copy-start(bf16[1,3,3,256,256]{3,4,2,1,0:T(8,128)(2,1)S(1)} %copy.33) | copy-start | bytes 3538948
  17.1 17.9 %copy-start.1 = (bf16[9,256,256]{2,1,0:T(8,128)(2,1)}, bf16[9,256,256]{2,1,0:T(8,128)(2,1)S(1)}, u32[]{:S(2)}) copy-start(bf16[9,256,256]{2,1,0:T(8,128)(2,1)S(1)} %copy.34.w_ref) | copy-start | bytes 3538948
  19.2 39.7 %copy-start = (bf16[9,256,256]{2,1,0:T(8,128)(2,1)}, bf16[9,256,256]{2,1,0:T(8,128)(2,1)S(1)}, u32[]{:S(2)}) copy-start(bf16[9,256,256]{2,1,0:T(8,128)(2,1)S(1)} %fusion.4.wt_ref) | copy-start | bytes 3538948
  35.0 1.2 %copy-start.6 = (bf16[8,4,4,16,256]{4,3,2,1,0:T(8,128)(2,1)S(1)}, bf16[8,4,4,16,256]{4,3,2,1,0:T(8,128)(2,1)}, u32[]{:S(2)}) copy-start(bf16[8,4,4,16,256]{4,3,2,1,0:T(8,128)(2,1)} %all-gather.7.cloned.1.call-done) | copy-start | bytes 3145732
  58.9 1.2 %copy-start.2 = (bf16[8,4,4,16,256]{4,3,2,1,0:T(8,128)(2,1)S(1)}, bf16[8,4,4,16,256]{4,3,2,1,0:T(8,128)(2,1)}, u32[]{:S(2)}) copy-start(bf16[8,4,4,16,256]{4,3,2,1,0:T(8,128)(2,1)} %all-gather.5.cloned.1.call-done) | copy-start | bytes 3145732
  60.2 8.8 %copy-start.11 = (bf16[2,8,4,4,256]{4,3,2,1,0:T(4,128)(2,1)S(1)}, bf16[2,8,4,4,256]{4,3,2,1,0:T(4,128)(2,1)}, u32[]{:S(2)}) copy-start(bf16[2,8,4,4,256]{4,3,2,1,0:T(4,128)(2,1)} %param.5) | copy-start | bytes 393220
  60.2 9.6 %copy-start.9 = (bf16[256,3,256]{2,0,1:T(8,128)(2,1)S(1)}, bf16[256,3,256]{2,0,1:T(8,128)(2,1)}, u32[]{:S(2)}) copy-start(bf16[256,3,256]{2,0,1:T(8,128)(2,1)} %copy-done.8) | copy-start | bytes 1179652
  61.5 7.5 %collective-permute-start = (bf16[4,4,16,256]{3,2,1,0:T(8,128)(2,1)S(1)}, bf16[4,4,16,256]{3,2,1,0:T(8,128)(2,1)S(1)}, u32[]{:S(2)}, u32[]{:S(2)}) collective-permute-start(bf16[4,4,16,256]{3,2,1,0:T(8,128)(2,1)S(1)} %shard_map.68), channel_id=1, source_target_pairs={{2,0},{3,1},{6,4},{7,5},{10,8},{11,9},{14,12},{15,13},{18,16},{19,... | collective-permute-start | bytes 393224 | tf_op jit(solution)/shard_map/ppermute | solution.py:229
  74.3 1.0 copy-start.4
  75.3 1.0 copy-start.5
  90.8 1.2 %copy-start.3 = (bf16[32,4,16,256]{3,2,1,0:T(8,128)(2,1)S(1)}, bf16[32,4,16,256]{3,2,1,0:T(8,128)(2,1)}, u32[]{:S(2)}) copy-start(bf16[32,4,16,256]{3,2,1,0:T(8,128)(2,1)} %all-gather.9.cloned.1.call-done) | copy-start | bytes 3145732
Sparse Core Ops, SparseCore 0:
  10.2 24.7 all-gather.6
  37.2 21.7 all-gather.4
  69.8 20.9 all-gather.8

commit v2 on v1

--- a/solution.py
+++ b/solution.py
@@ -19,18 +19,18 @@
     return jnp.where(frame < frames - lag, moved, 0.0)
 
 
-def fill_padded(padded, blocks, pad):
+def fill_padded(padded, halves, pad):
     rows_all, cols_all, steps, channels = padded.shape
     padded[0:pad] = jnp.zeros((pad, cols_all, steps, channels), padded.dtype)
     padded[rows_all - pad :] = jnp.zeros((pad, cols_all, steps, channels), padded.dtype)
     padded[:, 0:pad] = jnp.zeros((rows_all, pad, steps, channels), padded.dtype)
     padded[:, cols_all - pad :] = jnp.zeros((rows_all, pad, steps, channels), padded.dtype)
-    space, chan, rows, cols = blocks.shape[:4]
-    for i in range(space):
+    first = lax.axis_index("space")
+    for k, half in enumerate(halves):
+        chan, rows, cols = half.shape[:3]
+        top = pad + lax.rem(first + k, len(halves)) * rows
         for j in range(chan):
-            padded[pad + i * rows : pad + (i + 1) * rows, pad + j * cols : pad + (j + 1) * cols] = (
-                blocks[i, j]
-            )
+            padded[pl.ds(top, rows), pad + j * cols : pad + (j + 1) * cols] = half[j]
 
 
 def slope_of(hidden):
@@ -38,9 +38,10 @@
     return sig * (1.0 + hidden * (1.0 - sig))
 
 
-def window_slope_kernel(x_ref, w_ref, slope_ref, xp_ref):
-    space, chan, rows, cols, steps, channels = x_ref.shape
-    fill_padded(xp_ref, x_ref, 2)
+def window_slope_kernel(space, *refs):
+    x_refs, (w_ref, slope_ref, xp_ref) = refs[:space], refs[space:]
+    chan, rows, cols, steps, channels = x_refs[0].shape
+    fill_padded(xp_ref, x_refs, 2)
     r0 = lax.axis_index("space") * rows
     c0 = lax.axis_index("chan") * cols
     hidden = None
@@ -76,14 +77,16 @@
     out_ref[...] = (own.astype(F32) + conv).astype(BF16).reshape(out_ref.shape)
 
 
-def tick_kernel(frames, g_ref, slope_ref, wt_ref, twc_ref, out_ref, gp_ref, hg_ref):
-    fill_padded(gp_ref, g_ref, 1)
+def tick_kernel(space, frames, *refs):
+    g_refs, (slope_ref, wt_ref, twc_ref, out_ref, gp_ref, hg_ref) = refs[:space], refs[space:]
+    fill_padded(gp_ref, g_refs, 1)
     own_window(gp_ref, slope_ref, wt_ref, twc_ref, out_ref, hg_ref, frames)
 
 
-def tile_kernel(share, x_ref, w_ref, act_ref, xt_ref, slope_ref, xp_ref):
-    space, chan, rows, cols, steps, channels = x_ref.shape
-    fill_padded(xp_ref, x_ref, 1)
+def tile_kernel(space, share, *refs):
+    x_refs, (w_ref, act_ref, xt_ref, slope_ref, xp_ref) = refs[:space], refs[space:]
+    chan, rows, cols, steps, channels = x_refs[0].shape
+    fill_padded(xp_ref, x_refs, 1)
     width = chan * cols
     span = width * steps
     for i in range(space * rows):
@@ -99,31 +102,16 @@
         xt_ref[:, i * span : (i + 1) * span] = xp_ref[i + 1, 1 : 1 + width].reshape(-1, channels).T
 
 
-def final_kernel(
-    frames,
-    g_ref,
-    slope_w_ref,
-    slope_s_ref,
-    act_ref,
-    xt_ref,
-    wt_ref,
-    twc_ref,
-    pick_ref,
-    out_ref,
-    space_ref,
-    time_ref,
-    gp_ref,
-    hg_ref,
-    hs_ref,
-    hcols_ref,
-    gcols_ref,
-):
-    space, chan, rows, cols, steps, channels = g_ref.shape
+def final_kernel(space, frames, *refs):
+    g_refs = refs[:space]
+    slope_w_ref, slope_s_ref, act_ref, xt_ref, wt_ref, twc_ref, pick_ref = refs[space : space + 7]
+    out_ref, space_ref, time_ref, gp_ref, hg_ref, hs_ref, hcols_ref, gcols_ref, roll_ref = refs[space + 7 :]
+    chan, rows, cols, steps, channels = g_refs[0].shape
     share = slope_s_ref.shape[1]
     width = chan * cols
     height = space * rows
     span = width * steps
-    fill_padded(gp_ref, g_ref, 1)
+    fill_padded(gp_ref, g_refs, 1)
     own_window(gp_ref, slope_w_ref, wt_ref, twc_ref, out_ref, hg_ref, frames)
     hs_ref[...] = jnp.zeros(hs_ref.shape, BF16)
     for i in range(height):
@@ -152,12 +140,13 @@
     for j in range(chan):
         place = pl.multiple_of(lax.rem(first + j, chan) * share, share)
         for lag in range(3):
-            time_ref[lag, pl.ds(place, share), :] = time_sum[
+            roll_ref[lag, pl.ds(place, share), :] = time_sum[
                 j * share : (j + 1) * share, lag * share : (lag + 1) * share
             ]
+    for lag in range(3):
+        time_ref[lag] = roll_ref[lag].T
     space_sum = jnp.dot(xt_ref[...], hcols_ref[...], preferred_element_type=F32)
-    for tap in range(9):
-        space_ref[tap] = space_sum[:, tap * share : (tap + 1) * share]
+    space_ref[...] = space_sum.T.reshape(space_ref.shape)
 
 
 def call(kernel, outs, scratch, flops, moved, *operands):
@@ -186,8 +175,11 @@
         return jnp.transpose(array, (2, 3, 0, 1, 4)).reshape(rows, cols, steps, channels)
 
     def gathered(block):
-        whole = lax.all_gather(block, ("space", "chan"), axis=0, tiled=False)
-        return whole.reshape(space, chan, rows, cols, steps, channels)
+        half = lax.all_gather(block, "chan", axis=0, tiled=False)
+        return [half] + [
+            lax.ppermute(half, "space", [((i + k) % space, i) for i in range(space)])
+            for k in range(1, space)
+        ]
 
     x_own = cells(activations[0])
     cot_own = cells(cotangent)
@@ -204,24 +196,24 @@
 
     cell = (steps, channels)
     slope_w = call(
-        window_slope_kernel,
+        functools.partial(window_slope_kernel, space),
         jax.ShapeDtypeStruct((win, channels), F32),
         [pltpu.VMEM((height + 4, width + 4) + cell, BF16)],
         2 * win * 9 * channels * channels,
         4_000_000,
-        x_all,
+        *x_all,
         order,
     )
     padded = pltpu.VMEM((height + 2, width + 2) + cell, BF16)
     hg_win = pltpu.VMEM((rows + 2, cols + 2) + cell, BF16)
     for _ in range(depth - 1):
         g_own = call(
-            functools.partial(tick_kernel, frames),
+            functools.partial(tick_kernel, space, frames),
             jax.ShapeDtypeStruct((rows, cols) + cell, BF16),
             [padded, hg_win],
             2 * win * 9 * channels * channels,
             4_000_000,
-            up_all,
+            *up_all,
             slope_w,
             order_back,
             time_cat,
@@ -229,7 +221,7 @@
         received = lax.ppermute(g_own, "pipe", [(i, i - 1) for i in range(1, depth)])
         up_all = gathered(jnp.where(stage == depth - 1, cot_own, received))
     act_t, x_t, slope_s = call(
-        functools.partial(tile_kernel, share),
+        functools.partial(tile_kernel, space, share),
         (
             jax.ShapeDtypeStruct((channels, count), BF16),
             jax.ShapeDtypeStruct((channels, count), BF16),
@@ -238,15 +230,15 @@
         [padded],
         2 * count * 9 * channels * channels,
         6_000_000,
-        x_all,
+        *x_all,
         order,
     )
     grads, space_grad, time_grad = call(
-        functools.partial(final_kernel, frames),
+        functools.partial(final_kernel, space, frames),
         (
             jax.ShapeDtypeStruct((rows, cols) + cell, BF16),
-            jax.ShapeDtypeStruct((9, channels, share), F32),
-            jax.ShapeDtypeStruct((3, channels, share), F32),
+            jax.ShapeDtypeStruct((9, share, channels), F32),
+            jax.ShapeDtypeStruct((3, share, channels), F32),
         ),
         [
             padded,
@@ -254,10 +246,11 @@
             pltpu.VMEM((height + 2, width + 2, steps, share), BF16),
             pltpu.VMEM((count, 9 * share), BF16),
             pltpu.VMEM((count, 3 * share), BF16),
+            pltpu.VMEM((3, channels, share), F32),
         ],
         4 * win * 9 * channels * channels,
         8_000_000,
-        up_all,
+        *up_all,
         slope_w,
         slope_s,
         act_t,
@@ -271,8 +264,8 @@
     )
     return (
         grads[None],
-        space_grad.reshape(3, 3, channels, share)[None],
-        time_grad[None],
+        jnp.swapaxes(space_grad, 1, 2).reshape(3, 3, channels, share)[None],
+        jnp.swapaxes(time_grad, 1, 2)[None],
     )
 
 

time: 110 us -> 91.7 us (0.83)
  waiting for transfers between devices: 58.3 us -> 6.45 us
  blocking collectives: 0 us -> 50.8 us
  between operations: 14 us -> 0.86 us
  local copies, waits for them, and re-layouts: 17.3 us -> 10.7 us
  Pallas kernels: 13.4 us -> 16.6 us
    all_gather x3 -> x0, waiting for transfers between devices: 52 us -> none  [gathered(): whole = lax.all_gather(block, ('space', 'chan'), axis=0, tiled=False)]
    all_gather x0 -> x3, blocking collectives: none -> 50.8 us  [gathered(): half = lax.all_gather(block, 'chan', axis=0, tiled=False)]
    unnamed x28 -> x24, local copies, waits for them, and re-layouts: 11.4 us -> 5.97 us
    pallas_call x4, Pallas kernels: 13.4 us -> 16.6 us  [call(): pl.pallas_call(kernel, out_shape=outs, scratch_shapes=scratch, compiler_p...]
    transpose x2, local copies, waits for them, and re-layouts: 3.2 us -> 2.06 us  [cells(): jnp.transpose(array, (2, 3, 0, 1, 4)).reshape(rows, cols, steps, channels)]
  transfers between devices with their start and end apart: 4 -> 4, of which waited for: 4 -> 1; matrix products, arithmetic and copies ran while one was open for 9% -> 10% of each run, Pallas kernels for 5% -> 8%
where the time goes in v2:
time: 91.7 us; the launch traced here: 91.2 us
  blocking collectives  50.8 us (55%)
  Pallas kernels  16.6 us (18%)
  local copies, waits for them, and re-layouts  10.7 us (12%)
  waiting for transfers between devices  6.45 us (7%)
  other arithmetic  4.39 us (5%)
  starting transfers between devices  1.43 us (2%)
    all_gather x3, blocking collectives, gathered(): half = lax.all_gather(block, 'chan', axis=0, tiled=False)  50.8 us
    pallas_call x4, Pallas kernels, call(): pl.pallas_call(kernel, out_shape=outs, scratch_shapes=scratch, compiler_p...  16.6 us
    ppermute x1, waiting for transfers between devices, per_device(): lax.ppermute(g_own, 'pipe', [(i, i - 1) for i in range(1, depth)])  6.44 us
    unnamed x24, local copies, waits for them, and re-layouts  5.97 us
    transpose x1, other arithmetic, per_device(): order_back = jnp.transpose(order, (0, 2, 1))  2.19 us
    transpose x2, local copies, waits for them, and re-layouts, cells(): jnp.transpose(array, (2, 3, 0, 1, 4)).reshape(rows, cols, steps, channels)  2.06 us
  transfers between devices with their start and end apart: 4, of which 1 were waited for; matrix products, arithmetic and copies ran while one was open for 10% of the time, Pallas kernels for 8%

profile of v2, /device:TPU:0, one launch (start us, length us, event | category | flops | bytes accessed | tf_op | source)
XLA Modules:
  0.0 91.2 jit_solution(1833186736516111868)
XLA Ops:
  0.6 0.0 copy-start.10
  0.6 1.0 %copy.42 = bf16[4,4,2,8,256]{4,3,2,1,0:T(8,128)(2,1)S(1)} copy(bf16[4,4,2,8,256]{4,1,0,3,2:T(4,128)(2,1)} %bitcast.49) | data formatting | bytes 262144 | tf_op jit(solution)/shard_map/transpose | solution.py:175
  1.6 17.4 %all_gather.13.refs_0_ = bf16[4,4,4,16,256]{4,3,2,1,0:T(8,128)(2,1)S(1)} all-gather(bf16[1,4,4,16,256]{4,3,2,1,0:T(8,128)(2,1)S(1)} %bitcast.45), channel_id=1, replica_groups=mesh['groups'=2,'chan'=4,'pipe'=2,'space'=2] {'chan'}, dimensions={0}, use_global_device_ids=true | all-gather | bytes 655360 | tf_op jit(solution)/shard_map/all_gather | solution.py:178
  19.0 0.0 copy-start.2
  19.0 0.0 collective-permute-start.1
  19.0 1.1 %copy.43 = bf16[4,4,2,8,256]{4,3,2,1,0:T(8,128)(2,1)S(1)} copy(bf16[4,4,2,8,256]{4,1,0,3,2:T(4,128)(2,1)} %bitcast.47) | data formatting | bytes 262144 | tf_op jit(solution)/shard_map/transpose | solution.py:175
  20.1 17.3 %all_gather.12.refs_0_ = bf16[4,4,4,16,256]{4,3,2,1,0:T(8,128)(2,1)} all-gather(bf16[1,4,4,16,256]{4,3,2,1,0:T(8,128)(2,1)S(1)} %bitcast.46), channel_id=1, replica_groups=mesh['groups'=2,'chan'=4,'pipe'=2,'space'=2] {'chan'}, dimensions={0}, use_global_device_ids=true | all-gather | bytes 655360 | tf_op jit(solution)/shard_map/all_gather | solution.py:178
  37.4 0.0 collective-permute-start
  37.4 0.0 copy-done.10
  37.4 0.2 copy.31
  37.6 0.4 fusion.2
  37.9 0.0 copy-done.2
  37.9 0.2 copy.32
  38.1 0.2 copy.33.refs_4_.refs_7_
  38.3 1.6 %copy.29 = bf16[1,3,3,256,256]{3,4,2,1,0:T(8,128)(2,1)S(1)} copy(bf16[1,3,3,256,256]{4,3,2,1,0:T(8,128)(2,1)} %param.6) | data formatting | bytes 2359296 | tf_op args[2]
  39.9 0.0 copy-start.8
  39.9 1.0 %copy-done.8 = bf16[1,3,3,256,256]{3,4,2,1,0:T(8,128)(2,1)} copy-done((bf16[1,3,3,256,256]{3,4,2,1,0:T(8,128)(2,1)}, bf16[1,3,3,256,256]{3,4,2,1,0:T(8,128)(2,1)S(1)}, u32[]{:S(2)}) %copy-start.8) | copy-done | bytes 1179672
  40.9 1.6 %fusion = bf16[9,256,256]{1,2,0:T(8,128)(2,1)} fusion(s32[]{:T(128)S(6)} %select_n.29, bf16[9,256,256]{1,2,0:T(8,128)(2,1)S(1)} %bitcast.41), kind=kLoop, calls=%fused_computation.2 | loop fusion | flops 2359296 | bytes 2359300 | tf_op jit(solution)/shard_map/jit(_roll_dynamic)/concatenate | solution.py:189
  42.6 1.6 %copy.30.refs_2_ = bf16[9,256,256]{2,1,0:T(8,128)(2,1)S(1)} copy(bf16[9,256,256]{1,2,0:T(8,128)(2,1)} %fusion) | data formatting | bytes 2359296 | tf_op jit(solution)/shard_map/jit(_roll_dynamic)/dynamic_slice | solution.py:189
  44.1 0.0 copy-start.1
  44.1 0.0 copy-start.3
  44.2 2.2 %fusion.4.refs_3_.refs_6_ = bf16[9,256,256]{2,1,0:T(8,128)(2,1)S(1)} fusion(s32[]{:T(128)S(6)} %select_n.29, bf16[9,256,256]{1,2,0:T(8,128)(2,1)} %bitcast.42), kind=kLoop, calls=%fused_computation.18 | loop fusion | flops 2359296 | bytes 2359300 | tf_op jit(solution)/shard_map/transpose | solution.py:190
  46.4 0.0 copy-start
  46.4 0.0 collective-permute-done.1.refs_1_
  46.4 0.0 copy-done.1
  46.4 0.0 copy-done.3
  46.4 2.4 %shard_map.67.refs_2_ = f32[576,256]{1,0:T(8,128)S(1)} custom-call(bf16[4,4,4,16,256]{4,3,2,1,0:T(8,128)(2,1)S(1)} %copy-done.3, bf16[4,4,4,16,256]{4,3,2,1,0:T(8,128)(2,1)} %collective-permute-done.1.refs_1_, bf16[9,256,256]{2,1,0:T(8,128)(2,1)S(1)} %copy.30.refs_2_), custom_call_target="tpu_custom_call" | custom-call | flops 679477248 | bytes 4000000 | tf_op jit(solution)/shard_map/pallas_call | solution.py:153
  48.8 0.0 copy-start.9
  48.8 0.0 collective-permute-done.refs_1_
  48.8 0.0 copy-done
  48.8 2.5 %shard_map.68 = bf16[4,4,16,256]{3,2,1,0:T(8,128)(2,1)S(1)} custom-call(bf16[4,4,4,16,256]{4,3,2,1,0:T(8,128)(2,1)} %all_gather.12.refs_0_, bf16[4,4,4,16,256]{4,3,2,1,0:T(8,128)(2,1)} %collective-permute-done.refs_1_, f32[576,256]{1,0:T(8,128)S(1)} %shard_map.67.refs_2_, bf16[9,256,256]{2,1,0:T(8,128)(2,1)S(1)} %fusion.4.refs_3_.refs_6_, ...), custom_call_target="tpu_custom_call" | custom-call | flops 679477248 | bytes 4000000 | tf_op jit(solution)/shard_map/pallas_call | solution.py:153
  51.3 0.0 copy-start.4
  51.4 1.4 %collective-permute-start.2 = (bf16[4,4,16,256]{3,2,1,0:T(8,128)(2,1)S(1)}, bf16[4,4,16,256]{3,2,1,0:T(8,128)(2,1)S(1)}, u32[]{:S(2)}, u32[]{:S(2)}) collective-permute-start(bf16[4,4,16,256]{3,2,1,0:T(8,128)(2,1)S(1)} %shard_map.68), channel_id=1, source_target_pairs={{2,0},{3,1},{6,4},{7,5},{10,8},{11,9},{14,12},{15,13},{18,16},{19,... | collective-permute-start | bytes 393224 | tf_op jit(solution)/shard_map/ppermute | solution.py:221
  52.9 6.4 %collective-permute-done.2 = bf16[4,4,16,256]{3,2,1,0:T(8,128)(2,1)S(1)} collective-permute-done((bf16[4,4,16,256]{3,2,1,0:T(8,128)(2,1)S(1)}, bf16[4,4,16,256]{3,2,1,0:T(8,128)(2,1)S(1)}, u32[]{:S(2)}, u32[]{:S(2)}) %collective-permute-start.2) | collective-permute-done | bytes 131104 | tf_op jit(solution)/shard_map/ppermute | solution.py:221
  59.3 0.0 copy-done.9
  59.3 16.1 %all-gather = bf16[16,4,16,256]{3,2,1,0:T(8,128)(2,1)S(1)} all-gather(bf16[4,4,16,256]{3,2,1,0:T(8,128)(2,1)S(1)} %bitcast_select_fusion), channel_id=2, replica_groups=mesh['groups'=2,'chan'=4,'pipe'=2,'space'=2] {'chan'}, dimensions={0}, use_global_device_ids=true | all-gather | bytes 655360 | tf_op jit(solution)/shard_map/all_gather | solution.py:178
  75.5 0.0 collective-permute-start.3
  75.5 0.1 pad_maximum_fusion.refs_8_
  75.6 0.0 copy-done.4
  75.7 5.2 %shard_map.69 = (bf16[256,2048]{1,0:T(8,128)(2,1)S(1)}, bf16[256,2048]{1,0:T(8,128)(2,1)S(1)}, f32[2048,64]{1,0:T(8,128)}) custom-call(bf16[4,4,4,16,256]{4,3,2,1,0:T(8,128)(2,1)S(1)} %copy-done.4, bf16[4,4,4,16,256]{4,3,2,1,0:T(8,128)(2,1)} %collective-permute-done.1.refs_1_, bf16[9,256,256]{2,1,0:T(8,128)(2,1)} %copy-done.1), custom_call_target="tpu_custom_call" | custom-call | flops 2415919104 | bytes 6000000 | tf_op jit(solution)/shard_map/pallas_call | solution.py:153
  80.8 0.0 copy-start.5
  80.8 1.0 %copy-done.5 = bf16[256,2048]{1,0:T(8,128)(2,1)} copy-done((bf16[256,2048]{1,0:T(8,128)(2,1)}, bf16[256,2048]{1,0:T(8,128)(2,1)S(1)}, u32[]{:S(2)}) %copy-start.5) | copy-done | bytes 1048600
  81.8 0.0 copy-start.6
  81.8 1.0 %copy-done.6 = bf16[256,2048]{1,0:T(8,128)(2,1)} copy-done((bf16[256,2048]{1,0:T(8,128)(2,1)}, bf16[256,2048]{1,0:T(8,128)(2,1)S(1)}, u32[]{:S(2)}) %copy-start.6) | copy-done | bytes 1048600
  82.8 0.0 collective-permute-done.3.refs_1_
  82.8 1.2 %copy-done.7 = f32[2048,64]{1,0:T(8,128)S(1)} copy-done((f32[2048,64]{1,0:T(8,128)S(1)}, f32[2048,64]{1,0:T(8,128)}, u32[]{:S(2)}) %copy-start.7) | copy-done | bytes 524312
  84.0 6.5 %shard_map.70 = (bf16[4,4,16,256]{3,2,1,0:T(8,128)(2,1)S(1)}, f32[9,64,256]{2,1,0:T(8,128)}, f32[3,64,256]{2,1,0:T(8,128)}) custom-call(bf16[4,4,4,16,256]{4,3,2,1,0:T(8,128)(2,1)S(1)} %bitcast.39, bf16[4,4,4,16,256]{4,3,2,1,0:T(8,128)(2,1)S(1)} %collective-permute-done.3.refs_1_, f32[576,256]{1,0:T(8,128)S(1)} %shard_map.67.refs_2_, ...), custom_call_target="tpu_custom_call" | custom-call | flops 1358954496 | bytes 8000000 | tf_op jit(solution)/shard_map/pallas_call | solution.py:153
  90.5 0.7 copy.41
  (5 shorter events, 0.1 us)
Async XLA Ops:
  0.6 36.8 %copy-start.10 = (bf16[1,3,256,256]{3,2,1,0:T(8,128)(2,1)S(1)}, bf16[1,3,256,256]{3,2,1,0:T(8,128)(2,1)}, u32[]{:S(2)}) copy-start(bf16[1,3,256,256]{3,2,1,0:T(8,128)(2,1)} %param.7) | copy-start | bytes 1179652
  19.0 18.9 %copy-start.2 = (bf16[4,4,4,16,256]{4,3,2,1,0:T(8,128)(2,1)}, bf16[4,4,4,16,256]{4,3,2,1,0:T(8,128)(2,1)S(1)}, u32[]{:S(2)}) copy-start(bf16[4,4,4,16,256]{4,3,2,1,0:T(8,128)(2,1)S(1)} %all_gather.13.refs_0_) | copy-start | bytes 1572868
  19.0 27.4 %collective-permute-start.1 = (bf16[4,4,4,16,256]{4,3,2,1,0:T(8,128)(2,1)S(1)}, bf16[4,4,4,16,256]{4,3,2,1,0:T(8,128)(2,1)}, u32[]{:S(2)}, u32[]{:S(2)}) collective-permute-start(bf16[4,4,4,16,256]{4,3,2,1,0:T(8,128)(2,1)S(1)} %all_gather.13.refs_0_), channel_id=1, source_target_pairs={{1,0},{0,1},{3,2},{2,3},{5,4},{4,5},{7,6},{6,7},{9,8},{8,9},{11,10... | collective-permute-start | bytes 1572872 | tf_op jit(solution)/shard_map/ppermute | solution.py:180
  37.4 11.4 %collective-permute-start = (bf16[4,4,4,16,256]{4,3,2,1,0:T(8,128)(2,1)}, bf16[4,4,4,16,256]{4,3,2,1,0:T(8,128)(2,1)}, u32[]{:S(2)}, u32[]{:S(2)}) collective-permute-start(bf16[4,4,4,16,256]{4,3,2,1,0:T(8,128)(2,1)} %all_gather.12.refs_0_), channel_id=1, source_target_pairs={{1,0},{0,1},{3,2},{2,3},{5,4},{4,5},{7,6},{6,7},{9,8},{8,9},{11,10... | collective-permute-start | bytes 1572872 | tf_op jit(solution)/shard_map/ppermute | solution.py:180
  39.9 1.0 %copy-start.8 = (bf16[1,3,3,256,256]{3,4,2,1,0:T(8,128)(2,1)}, bf16[1,3,3,256,256]{3,4,2,1,0:T(8,128)(2,1)S(1)}, u32[]{:S(2)}) copy-start(bf16[1,3,3,256,256]{3,4,2,1,0:T(8,128)(2,1)S(1)} %copy.29) | copy-start | bytes 3538948
  44.1 2.2 %copy-start.1 = (bf16[9,256,256]{2,1,0:T(8,128)(2,1)}, bf16[9,256,256]{2,1,0:T(8,128)(2,1)S(1)}, u32[]{:S(2)}) copy-start(bf16[9,256,256]{2,1,0:T(8,128)(2,1)S(1)} %copy.30.refs_2_) | copy-start | bytes 3538948
  44.1 2.2 %copy-start.3 = (bf16[4,4,4,16,256]{4,3,2,1,0:T(8,128)(2,1)S(1)}, bf16[4,4,4,16,256]{4,3,2,1,0:T(8,128)(2,1)}, u32[]{:S(2)}) copy-start(bf16[4,4,4,16,256]{4,3,2,1,0:T(8,128)(2,1)} %copy-done.2) | copy-start | bytes 1572868
  46.4 2.5 %copy-start = (bf16[9,256,256]{2,1,0:T(8,128)(2,1)}, bf16[9,256,256]{2,1,0:T(8,128)(2,1)S(1)}, u32[]{:S(2)}) copy-start(bf16[9,256,256]{2,1,0:T(8,128)(2,1)S(1)} %fusion.4.refs_3_.refs_6_) | copy-start | bytes 3538948
  48.8 10.5 %copy-start.9 = (bf16[2,8,4,4,256]{4,3,2,1,0:T(4,128)(2,1)S(1)}, bf16[2,8,4,4,256]{4,3,2,1,0:T(4,128)(2,1)}, u32[]{:S(2)}) copy-start(bf16[2,8,4,4,256]{4,3,2,1,0:T(4,128)(2,1)} %param.5) | copy-start | bytes 393220
  51.3 24.3 %copy-start.4 = (bf16[4,4,4,16,256]{4,3,2,1,0:T(8,128)(2,1)S(1)}, bf16[4,4,4,16,256]{4,3,2,1,0:T(8,128)(2,1)}, u32[]{:S(2)}) copy-start(bf16[4,4,4,16,256]{4,3,2,1,0:T(8,128)(2,1)} %copy-done.2) | copy-start | bytes 1572868
  51.4 7.9 %collective-permute-start.2 = (bf16[4,4,16,256]{3,2,1,0:T(8,128)(2,1)S(1)}, bf16[4,4,16,256]{3,2,1,0:T(8,128)(2,1)S(1)}, u32[]{:S(2)}, u32[]{:S(2)}) collective-permute-start(bf16[4,4,16,256]{3,2,1,0:T(8,128)(2,1)S(1)} %shard_map.68), channel_id=1, source_target_pairs={{2,0},{3,1},{6,4},{7,5},{10,8},{11,9},{14,12},{15,13},{18,16},{19,... | collective-permute-start | bytes 393224 | tf_op jit(solution)/shard_map/ppermute | solution.py:221
  75.5 7.3 %collective-permute-start.3 = (bf16[4,4,4,16,256]{4,3,2,1,0:T(8,128)(2,1)S(1)}, bf16[4,4,4,16,256]{4,3,2,1,0:T(8,128)(2,1)S(1)}, u32[]{:S(2)}, u32[]{:S(2)}) collective-permute-start(bf16[4,4,4,16,256]{4,3,2,1,0:T(8,128)(2,1)S(1)} %bitcast.38), channel_id=1, source_target_pairs={{1,0},{0,1},{3,2},{2,3},{5,4},{4,5},{7,6},{6,7},{9,8},{8,9},{11,10... | collective-permute-start | bytes 1572872 | tf_op jit(solution)/shard_map/ppermute | solution.py:180
  80.8 1.0 %copy-start.5 = (bf16[256,2048]{1,0:T(8,128)(2,1)}, bf16[256,2048]{1,0:T(8,128)(2,1)S(1)}, u32[]{:S(2)}) copy-start(bf16[256,2048]{1,0:T(8,128)(2,1)S(1)} %get-tuple-element.10.refs_4_) | copy-start | bytes 3145732
  81.8 1.0 %copy-start.6 = (bf16[256,2048]{1,0:T(8,128)(2,1)}, bf16[256,2048]{1,0:T(8,128)(2,1)S(1)}, u32[]{:S(2)}) copy-start(bf16[256,2048]{1,0:T(8,128)(2,1)S(1)} %get-tuple-element.11.refs_5_) | copy-start | bytes 3145732
  82.8 1.2 %copy-start.7 = (f32[2048,64]{1,0:T(8,128)S(1)}, f32[2048,64]{1,0:T(8,128)}, u32[]{:S(2)}) copy-start(f32[2048,64]{1,0:T(8,128)} %get-tuple-element.9.refs_3_) | copy-start | bytes 1572868

commit v3 on v2

v3 whole, which is shorter than its diff:
```python
import functools

import jax
import jax.numpy as jnp
from jax import lax
from jax.experimental import pallas as pl
from jax.experimental.pallas import tpu as pltpu
from jax.sharding import PartitionSpec as P

F32 = jnp.float32
BF16 = jnp.bfloat16
MIB = 1024 * 1024
ROWS_IN = (((1,), (1,)), ((), ()))


def dot(left, right):
    return jnp.dot(left, right, preferred_element_type=F32)


def dot_back(left, right):
    return lax.dot_general(left, right, ROWS_IN, preferred_element_type=F32)


def frame_shift(term, lag, frames):
    rows = term.shape[0]
    moved = pltpu.roll(term, rows - lag, 0)
    frame = lax.broadcasted_iota(jnp.int32, term.shape, 0) % frames
    return jnp.where(frame < frames - lag, moved, 0.0)


def slope_of(hidden):
    sig = jax.nn.sigmoid(hidden)
    return sig * (1.0 + hidden * (1.0 - sig))


def pack_kernel(x_ref, cot_ref, xc_ref, cc_ref, right_ref, left_ref, side_ref, dr_ref, dl_ref):
    rows, cols, steps, channels = xc_ref.shape
    for src, dst in ((x_ref, xc_ref), (cot_ref, cc_ref)):
        for r in range(rows):
            dst[r] = jnp.swapaxes(src[:, :, r].reshape(steps, cols, channels), 0, 1)
    cells = rows * cols
    for msg, col in ((right_ref, cols - 1), (left_ref, 0)):
        msg[:cells] = xc_ref[...].reshape(cells, steps, channels)
        for r in range(rows):
            msg[cells + r] = cc_ref[r, col]
    top = lax.axis_index("space") == 0
    for here, row, edge in ((top, rows - 2, rows - 1), (jnp.logical_not(top), 0, 0)):

        @pl.when(here)
        def _(row=row, edge=edge):
            side_ref[:2] = xc_ref[row : row + 2]
            side_ref[2] = cc_ref[edge]
            for msg, col, last in ((dr_ref, cols - 2, cols - 1), (dl_ref, 0, 0)):
                for i in range(2):
                    msg[2 * i : 2 * i + 2] = xc_ref[row + i, col : col + 2]
                msg[4] = cc_ref[edge, last]


def conv_back(hg_ref, w_ref, rows, cols):
    channels = w_ref.shape[-1]
    conv = None
    for u in range(3):
        for v in range(3):
            piece = hg_ref[2 - u : 2 - u + rows, 2 - v : 2 - v + cols]
            term = dot_back(piece.reshape(-1, channels), w_ref[3 * u + v])
            conv = term if conv is None else conv + term
    return conv


def window_grad(window, slope_ref, tw_ref, hg_ref, frames):
    act = dot_back(window, tw_ref[0])
    for lag in (1, 2):
        act = act + frame_shift(dot_back(window, tw_ref[lag]), lag, frames)
    hg_ref[...] = (act * slope_ref[...]).astype(BF16).reshape(hg_ref.shape)


def send_on(out_ref, own, conv, cot_ref):
    first = lax.axis_index("pipe") == 0

    @pl.when(first)
    def _():
        out_ref[...] = cot_ref[...]

    @pl.when(jnp.logical_not(first))
    def _():
        out_ref[...] = (own.astype(F32) + conv).astype(BF16).reshape(out_ref.shape)


def first_kernel(
    frames, x_ref, cot_ref, l_ref, r_ref, s_ref, dl_ref, dr_ref, w_ref, tw_ref,
    slope_ref, out_ref, xw_ref, cw_ref, hg_ref,
):
    rows, cols, steps, channels = x_ref.shape
    cells = rows * cols
    bottom = lax.axis_index("space")
    xw_ref[2 : 2 + rows, 2 : 2 + cols] = x_ref[...]
    cw_ref[1 : 1 + rows, 1 : 1 + cols] = cot_ref[...]
    for r in range(rows):
        xw_ref[2 + r, 0:2] = l_ref[r * cols + cols - 2 : r * cols + cols]
        xw_ref[2 + r, cols + 2 : cols + 4] = r_ref[r * cols : r * cols + 2]
        cw_ref[1 + r, 0] = l_ref[cells + r]
        cw_ref[1 + r, cols + 1] = r_ref[cells + r]
    near = (1 - bottom) * (rows + 2)
    far = bottom * (rows + 2)
    for i in range(2):
        xw_ref[near + i, 2 : 2 + cols] = s_ref[i]
        xw_ref[near + i, 0:2] = dl_ref[2 * i : 2 * i + 2]
        xw_ref[near + i, cols + 2 : cols + 4] = dr_ref[2 * i : 2 * i + 2]
        xw_ref[far + i] = jnp.zeros(xw_ref.shape[1:], BF16)
    near = (1 - bottom) * (rows + 1)
    far = bottom * (rows + 1)
    cw_ref[near, 1 : 1 + cols] = s_ref[2]
    cw_ref[near, 0] = dl_ref[4]
    cw_ref[near, cols + 1] = dr_ref[4]
    cw_ref[far] = jnp.zeros(cw_ref.shape[1:], BF16)
    hidden = None
    for u in range(3):
        for v in range(3):
            piece = xw_ref[u : u + rows + 2, v : v + cols + 2]
            term = dot(piece.reshape(-1, channels), w_ref[3 * u + v])
            hidden = term if hidden is None else hidden + term
    slope_ref[...] = slope_of(hidden)
    window_grad(cw_ref[...].reshape(-1, channels), slope_ref, tw_ref, hg_ref, frames)
    conv = conv_back(hg_ref, w_ref, rows, cols)
    send_on(out_ref, cot_ref[...].reshape(-1, channels), conv, cot_ref)


def collect_kernel(wrapped, *refs):
    pieces, out_ref = refs[:-1], refs[-1]
    chan = len(pieces) - wrapped
    rows, cols, steps, channels = pieces[0].shape
    me = lax.axis_index("chan")

    def put(d, piece):
        place = lax.rem(me - d + chan, chan) * cols
        for r in range(rows):
            out_ref[r, pl.ds(place, cols)] = (
                piece[r] if piece.ndim == 4 else piece[r * cols : (r + 1) * cols]
            )

    for d in range(chan):
        if not wrapped or d not in (1, chan - 1):
            put(d, pieces[d])
    if wrapped:
        edge = pieces[chan]
        for d, at in ((1, 0), (chan - 1, chan - 1)):
            pl.when(me == at)(functools.partial(put, d, edge))
            pl.when(me != at)(functools.partial(put, d, pieces[d]))


def fill_padded(padded, own, other):
    rows_all, cols_all, steps, channels = padded.shape
    zero_row = jnp.zeros((1, cols_all, steps, channels), padded.dtype)
    padded[0:1] = zero_row
    padded[rows_all - 1 :] = zero_row
    for r in range(1, rows_all - 1):
        for c in (0, cols_all - 1):
            padded[r, c] = jnp.zeros((steps, channels), padded.dtype)
    rows = own.shape[0]
    bottom = lax.axis_index("space")
    for half, top in ((own, bottom * rows), (other, (1 - bottom) * rows)):
        padded[pl.ds(1 + top, rows), 1 : cols_all - 1] = half[...]


def own_window(gp_ref, slope_ref, w_ref, tw_ref, hg_ref, frames, rows, cols):
    channels = w_ref.shape[-1]
    r0 = lax.axis_index("space") * rows
    c0 = lax.axis_index("chan") * cols
    window = gp_ref[pl.ds(r0, rows + 2), pl.ds(c0, cols + 2)].reshape(-1, channels)
    window_grad(window, slope_ref, tw_ref, hg_ref, frames)
    own = gp_ref[pl.ds(r0 + 1, rows), pl.ds(c0 + 1, cols)].reshape(-1, channels)
    return own, conv_back(hg_ref, w_ref, rows, cols)


def tick_kernel(
    frames, g_ref, other_ref, cot_ref, slope_ref, w_ref, tw_ref, out_ref, gp_ref, hg_ref
):
    rows, cols = cot_ref.shape[:2]
    fill_padded(gp_ref, g_ref, other_ref)
    own, conv = own_window(gp_ref, slope_ref, w_ref, tw_ref, hg_ref, frames, rows, cols)
    send_on(out_ref, own, conv, cot_ref)


def tile_kernel(share, x_ref, other_ref, w_ref, act_ref, xt_ref, slope_ref, xp_ref):
    rows, width, steps, channels = x_ref.shape
    fill_padded(xp_ref, x_ref, other_ref)
    span = width * steps
    turn = lax.rem(channels - lax.axis_index("chan") * share, channels)
    for i in range(2 * rows):
        hidden = None
        for u in range(3):
            for v in range(3):
                piece = xp_ref[i + u, v : v + width].reshape(-1, channels)
                term = dot(piece, w_ref[3 * u + v])
                hidden = term if hidden is None else hidden + term
        active = (hidden * jax.nn.sigmoid(hidden)).astype(BF16)
        act_ref[:, i * span : (i + 1) * span] = active.T
        slope_ref[i * span : (i + 1) * span, :] = slope_of(pltpu.roll(hidden, turn, 1)[:, :share])
        xt_ref[:, i * span : (i + 1) * span] = xp_ref[i + 1, 1 : 1 + width].reshape(-1, channels).T


def final_kernel(
    frames, g_ref, other_ref, slope_w_ref, slope_s_ref, act_ref, xt_ref, w_ref, tw_ref,
    out_ref, space_ref, time_ref, gp_ref, hg_ref, hs_ref, hcols_ref, gcols_ref, pick_ref,
):
    rows, width, steps, channels = g_ref.shape
    clips, _, _, cols, _ = out_ref.shape
    share = slope_s_ref.shape[1]
    height = 2 * rows
    span = width * steps
    fill_padded(gp_ref, g_ref, other_ref)
    first = pl.multiple_of(lax.axis_index("chan") * share, share)
    for lag in range(3):
        pick_ref[lag * share : (lag + 1) * share, :] = tw_ref[lag, pl.ds(first, share), :]
    at = lax.broadcasted_iota(jnp.int32, (share, channels), 1) - first
    chosen = at == lax.broadcasted_iota(jnp.int32, (share, channels), 0)
    pick_ref[3 * share :, :] = jnp.where(chosen, 1.0, 0.0).astype(BF16)
    hs_ref[...] = jnp.zeros(hs_ref.shape, BF16)
    for i in range(height):
        block = gp_ref[i + 1, 1 : 1 + width].reshape(-1, channels)
        mixed = dot_back(block, pick_ref[...])
        act = mixed[:, :share]
        for lag in (1, 2):
            act = act + frame_shift(mixed[:, lag * share : (lag + 1) * share], lag, frames)
        grad = (act * slope_s_ref[i * span : (i + 1) * span, :]).astype(BF16)
        hs_ref[i + 1, 1 : 1 + width] = grad.reshape(width, steps, share)
        own = mixed[:, 3 * share :]
        for lag in range(3):
            shifted = own if lag == 0 else frame_shift(own, lag, frames)
            gcols_ref[i * span : (i + 1) * span, lag * share : (lag + 1) * share] = shifted.astype(
                BF16
            )
    for u in range(3):
        for v in range(3):
            tap = 3 * u + v
            for i in range(height):
                hcols_ref[i * span : (i + 1) * span, tap * share : (tap + 1) * share] = hs_ref[
                    i + 2 - u, 2 - v : 2 - v + width
                ].reshape(-1, share)
    time_ref[...] = dot(act_ref[...], gcols_ref[...]).T.reshape(time_ref.shape)
    space_ref[...] = dot(xt_ref[...], hcols_ref[...]).T.reshape(space_ref.shape)
    own, conv = own_window(gp_ref, slope_w_ref, w_ref, tw_ref, hg_ref, frames, rows, cols)
    grads = (own.astype(F32) + conv).astype(BF16).reshape(rows, cols, steps, channels)
    for r in range(rows):
        out_ref[:, :, r] = jnp.swapaxes(grads[r], 0, 1).reshape(clips, frames, cols, channels)


def call(kernel, outs, scratch, limit, flops, moved, *operands):
    return pl.pallas_call(
        kernel,
        out_shape=outs,
        scratch_shapes=scratch,
        compiler_params=pltpu.CompilerParams(vmem_limit_bytes=limit * MIB),
        cost_estimate=pl.CostEstimate(flops=flops, bytes_accessed=moved, transcendentals=0),
    )(*operands)


def per_device(activations, cotangent, space_weight, time_weight):
    clips, frames, rows, cols, channels = activations.shape[1:]
    steps = clips * frames
    chan, depth = lax.axis_size("chan"), lax.axis_size("pipe")
    share = channels // chan
    height, width = 2 * rows, chan * cols
    count = height * width * steps
    win = (rows + 2) * (cols + 2) * steps
    large = 24 if chan <= 4 else 56
    w = space_weight[0].reshape(9, channels, channels)
    tw = time_weight[0]
    cell = (steps, channels)

    def bf16(*shape):
        return jax.ShapeDtypeStruct(shape + cell, BF16)

    x_own, cot_own, to_right, to_left, to_side, to_dr, to_dl = call(
        pack_kernel,
        (
            bf16(rows, cols), bf16(rows, cols), bf16(rows * cols + rows),
            bf16(rows * cols + rows), bf16(3, cols), bf16(5), bf16(5),
        ),
        [],
        16,
        1_000_000,
        1_000_000,
        activations[0],
        cotangent,
    )

    def moved(message, by, flip):
        pairs = [
            (2 * c + s, 2 * (c + by) + (1 - s if flip else s))
            for c in range(chan)
            for s in range(2)
            if 0 <= c + by < chan
        ]
        return lax.ppermute(message, ("chan", "space"), pairs)

    from_left = moved(to_right, 1, False)
    from_right = moved(to_left, -1, False)
    from_dl = moved(to_dr, 1, True)
    from_dr = moved(to_dl, -1, True)
    from_side = moved(to_side, 0, True)
    pieces = [x_own, from_left]
    for d in range(2, chan - 1):
        pieces.append(lax.ppermute(x_own, "chan", [(i, (i + d) % chan) for i in range(chan)]))
    pieces.append(from_right)
    pieces.append(lax.ppermute(x_own, "chan", [(0, chan - 1), (chan - 1, 0)]))

    def gathered(wrapped, parts):
        half = call(
            functools.partial(collect_kernel, wrapped),
            bf16(rows, width),
            [],
            16,
            1_000_000,
            1_000_000,
            *parts,
        )
        return half, lax.ppermute(half, "space", [(0, 1), (1, 0)])

    slope_w, payload = call(
        functools.partial(first_kernel, frames),
        (jax.ShapeDtypeStruct((win, channels), F32), bf16(rows, cols)),
        [
            pltpu.VMEM((rows + 4, cols + 4) + cell, BF16),
            pltpu.VMEM((rows + 2, cols + 2) + cell, BF16),
            pltpu.VMEM((rows + 2, cols + 2) + cell, BF16),
        ],
        20,
        2 * win * 18 * channels * channels,
        4_000_000,
        x_own, cot_own, from_left, from_right, from_side, from_dl, from_dr, w, tw,
    )

    padded = pltpu.VMEM((height + 2, width + 2) + cell, BF16)
    hg_win = pltpu.VMEM((rows + 2, cols + 2) + cell, BF16)
    for tick in range(depth - 1):
        if tick:
            payload = call(
                functools.partial(tick_kernel, frames),
                bf16(rows, cols),
                [padded, hg_win],
                large,
                2 * win * 12 * channels * channels,
                4_000_000,
                *g_all, cot_own, slope_w, w, tw,
            )
        arrived = []
        for d in range(chan):
            pairs = [
                (c * depth + p, (c + d) % chan * depth + (p - 1) % depth)
                for p in range(depth)
                for c in range(chan)
            ]
            arrived.append(lax.ppermute(payload, ("chan", "pipe"), pairs))
        g_all = gathered(0, arrived)

    x_all = gathered(1, pieces)
    act_t, x_t, slope_s = call(
        functools.partial(tile_kernel, share),
        (
            jax.ShapeDtypeStruct((channels, count), BF16),
            jax.ShapeDtypeStruct((channels, count), BF16),
            jax.ShapeDtypeStruct((count, share), F32),
        ),
        [padded],
        large,
        2 * count * 9 * channels * channels,
        6_000_000,
        *x_all,
        w,
    )
    grads, space_grad, time_grad = call(
        functools.partial(final_kernel, frames),
        (
            jax.ShapeDtypeStruct((clips, frames, rows, cols, channels), BF16),
            jax.ShapeDtypeStruct((9, share, channels), F32),
            jax.ShapeDtypeStruct((3, share, channels), F32),
        ),
        [
            padded,
            hg_win,
            pltpu.VMEM((height + 2, width + 2, steps, share), BF16),
            pltpu.VMEM((count, 9 * share), BF16),
            pltpu.VMEM((count, 3 * share), BF16),
            pltpu.VMEM((4 * share, channels), BF16),
        ],
        large,
        4 * win * 9 * channels * channels,
        8_000_000,
        *g_all, slope_w, slope_s, act_t, x_t, w, tw,
    )
    return (
        grads[None],
        jnp.swapaxes(space_grad, 1, 2).reshape(3, 3, channels, share)[None],
        jnp.swapaxes(time_grad, 1, 2)[None],
    )


def solution(mesh):
    return jax.shard_map(
        per_device,
        mesh=mesh,
        in_specs=(
            P("pipe", "groups", None, "space", "chan", None),
            P("groups", None, "space", "chan", None),
            P("pipe", None, None, None, None),
            P("pipe", None, None, None),
        ),
        out_specs=(
            P("pipe", "groups", None, "space", "chan", None),
            P("pipe", "groups", None, None, "chan"),
            P("pipe", "groups", None, "chan"),
        ),
        check_vma=False,
    )
```

time: 91.7 us -> 52.2 us (0.57)
  the two profiles are of different devices: /device:TPU:0 before, /device:TPU:9 now
where the time goes in v3:
time: 52.2 us; the launch traced here: 51.9 us
  starting transfers between devices  21.8 us (42%)
  waiting for transfers between devices  15.6 us (30%)
  Pallas kernels  10.8 us (21%)
  local copies, waits for them, and re-layouts  2.9 us (6%)
  between operations  0.78 us (1%)
    ppermute x5, starting transfers between devices, moved(): return lax.ppermute(message, ('chan', 'space'), pairs)  12.8 us
    ppermute x4, waiting for transfers between devices, per_device(): arrived.append(lax.ppermute(payload, ('chan', 'pipe'), pairs))  11.4 us
    pallas_call x6, Pallas kernels, call(): pl.pallas_call(kernel, out_shape=outs, scratch_shapes=scratch, compiler_p...  10.8 us
    ppermute x4, starting transfers between devices, per_device(): arrived.append(lax.ppermute(payload, ('chan', 'pipe'), pairs))  4.77 us
    ppermute x5, waiting for transfers between devices, moved(): return lax.ppermute(message, ('chan', 'space'), pairs)  3.38 us
    unnamed x10, local copies, waits for them, and re-layouts  2.9 us
    ppermute x1, starting transfers between devices, per_device(): lax.ppermute(x_own, 'chan', [(i, (i + d) % chan) for i in range(chan)])  2.37 us
    ppermute x2, starting transfers between devices, gathered(): return (half, lax.ppermute(half, 'space', [(0, 1), (1, 0)]))  1.21 us
  transfers between devices with their start and end apart: 13, of which 6 were waited for; matrix products, arithmetic and copies ran while one was open for 0% of the time, Pallas kernels for 10%

profile of v3, /device:TPU:9, one launch (start us, length us, event | category | flops | bytes accessed | tf_op | source)
XLA Modules:
  0.0 51.9 jit_solution(8000623796471375782)
XLA Ops:
  0.6 0.0 copy-start
  0.6 0.0 copy-start.3
  0.7 1.0 %copy-done.3 = bf16[1,2,8,4,4,256]{5,4,3,2,1,0:T(4,128)(2,1)S(1)} copy-done((bf16[1,2,8,4,4,256]{5,4,3,2,1,0:T(4,128)(2,1)S(1)}, bf16[1,2,8,4,4,256]{5,4,3,2,1,0:T(4,128)(2,1)}, u32[]{:S(2)}) %copy-start.3) | copy-done | bytes 131096
  1.6 0.0 copy-start.4
  1.6 0.9 %copy-done.4 = bf16[2,8,4,4,256]{4,3,2,1,0:T(4,128)(2,1)S(1)} copy-done((bf16[2,8,4,4,256]{4,3,2,1,0:T(4,128)(2,1)S(1)}, bf16[2,8,4,4,256]{4,3,2,1,0:T(4,128)(2,1)}, u32[]{:S(2)}) %copy-start.4) | copy-done | bytes 131096
  2.5 0.1 shard_map.67
  2.7 2.4 %collective-permute-start.10 = (bf16[4,4,16,256]{3,2,1,0:T(8,128)(2,1)S(1)}, bf16[4,4,16,256]{3,2,1,0:T(8,128)(2,1)S(1)}, u32[]{:S(2)}, u32[]{:S(2)}) collective-permute-start(bf16[4,4,16,256]{3,2,1,0:T(8,128)(2,1)S(1)} %get-tuple-element.18.x_ref.refs_0_), channel_id=1, source_target_pairs={{0,8},{4,12},{8,0},{12,4},{1,9},{5,13},{9,1},{13,5},{2,10},{6,14},... | collective-permute-start | bytes 393224 | tf_op jit(solution)/shard_map/ppermute | solution.py:304
  5.0 0.7 %collective-permute-start.11 = (bf16[4,4,16,256]{3,2,1,0:T(8,128)(2,1)S(1)}, bf16[4,4,16,256]{3,2,1,0:T(8,128)(2,1)S(1)}, u32[]{:S(2)}, u32[]{:S(2)}) collective-permute-start(bf16[4,4,16,256]{3,2,1,0:T(8,128)(2,1)S(1)} %get-tuple-element.18.x_ref.refs_0_), channel_id=1, source_target_pairs={{0,12},{12,0},{1,13},{13,1},{2,14},{14,2},{3,15},{15,3},{16,28},{2... | collective-permute-start | bytes 393224 | tf_op jit(solution)/shard_map/ppermute | solution.py:306
  5.7 1.9 %collective-permute-start = (bf16[20,16,256]{2,1,0:T(8,128)(2,1)S(1)}, bf16[20,16,256]{2,1,0:T(8,128)(2,1)S(1)}, u32[]{:S(2)}, u32[]{:S(2)}) collective-permute-start(bf16[20,16,256]{2,1,0:T(8,128)(2,1)S(1)} %get-tuple-element.20), channel_id=1, source_target_pairs={{0,4},{1,5},{4,8},{5,9},{8,12},{9,13},{2,6},{3,7},{6,10},{7,11},{1... | collective-permute-start | bytes 491528 | tf_op jit(solution)/shard_map/ppermute | solution.py:295
  7.6 3.8 %collective-permute-start.1 = (bf16[20,16,256]{2,1,0:T(8,128)(2,1)S(1)}, bf16[20,16,256]{2,1,0:T(8,128)(2,1)S(1)}, u32[]{:S(2)}, u32[]{:S(2)}) collective-permute-start(bf16[20,16,256]{2,1,0:T(8,128)(2,1)S(1)} %get-tuple-element.21), channel_id=1, source_target_pairs={{4,0},{5,1},{8,4},{9,5},{12,8},{13,9},{6,2},{7,3},{10,6},{11,7},{1... | collective-permute-start | bytes 491528 | tf_op jit(solution)/shard_map/ppermute | solution.py:295
  11.4 1.6 %collective-permute-start.2 = (bf16[3,4,16,256]{3,2,1,0:T(8,128)(2,1)S(1)}, bf16[3,4,16,256]{3,2,1,0:T(8,128)(2,1)S(1)}, u32[]{:S(2)}, u32[]{:S(2)}) collective-permute-start(bf16[3,4,16,256]{3,2,1,0:T(8,128)(2,1)S(1)} %get-tuple-element.22), channel_id=1, source_target_pairs={{0,1},{1,0},{4,5},{5,4},{8,9},{9,8},{12,13},{13,12},{2,3},{3,2},{6... | collective-permute-start | bytes 294920 | tf_op jit(solution)/shard_map/ppermute | solution.py:295
  13.0 0.8 %collective-permute-done.10.refs_2_ = bf16[4,4,16,256]{3,2,1,0:T(8,128)(2,1)S(1)} collective-permute-done((bf16[4,4,16,256]{3,2,1,0:T(8,128)(2,1)S(1)}, bf16[4,4,16,256]{3,2,1,0:T(8,128)(2,1)S(1)}, u32[]{:S(2)}, u32[]{:S(2)}) %collective-permute-start.10) | collective-permute-done | bytes 131104 | tf_op jit(solution)/shard_map/ppermute | solution.py:304
  13.8 2.9 %collective-permute-start.3 = (bf16[5,16,256]{2,1,0:T(8,128)(2,1)S(1)}, bf16[5,16,256]{2,1,0:T(8,128)(2,1)S(1)}, u32[]{:S(2)}, u32[]{:S(2)}) collective-permute-start(bf16[5,16,256]{2,1,0:T(8,128)(2,1)S(1)} %get-tuple-element.23), channel_id=1, source_target_pairs={{0,5},{1,4},{4,9},{5,8},{8,13},{9,12},{2,7},{3,6},{6,11},{7,10},{1... | collective-permute-start | bytes 122888 | tf_op jit(solution)/shard_map/ppermute | solution.py:295
  16.7 0.0 collective-permute-done.11.refs_4_
  16.7 2.6 %collective-permute-start.4 = (bf16[5,16,256]{2,1,0:T(8,128)(2,1)S(1)}, bf16[5,16,256]{2,1,0:T(8,128)(2,1)S(1)}, u32[]{:S(2)}, u32[]{:S(2)}) collective-permute-start(bf16[5,16,256]{2,1,0:T(8,128)(2,1)S(1)} %get-tuple-element.24), channel_id=1, source_target_pairs={{4,1},{5,0},{8,5},{9,4},{12,9},{13,8},{6,3},{7,2},{10,7},{11,6},{1... | collective-permute-start | bytes 122888 | tf_op jit(solution)/shard_map/ppermute | solution.py:295
  19.4 0.0 collective-permute-done.l_ref.refs_1_
  19.4 0.0 collective-permute-done.1.r_ref.refs_3_
  19.4 0.1 shard_map.70.x_ref
  19.5 0.7 %collective-permute-start.12 = (bf16[4,16,16,256]{3,2,1,0:T(8,128)(2,1)S(1)}, bf16[4,16,16,256]{3,2,1,0:T(8,128)(2,1)S(1)}, u32[]{:S(2)}, u32[]{:S(2)}) collective-permute-start(bf16[4,16,16,256]{3,2,1,0:T(8,128)(2,1)S(1)} %shard_map.70.x_ref), channel_id=1, source_target_pairs={{0,1},{1,0},{2,3},{3,2},{4,5},{5,4},{6,7},{7,6},{8,9},{9,8},{10,11... | collective-permute-start | bytes 1572872 | tf_op jit(solution)/shard_map/ppermute | solution.py:318
  20.1 0.0 collective-permute-done.3.dl_ref
  20.1 3.4 %collective-permute-done.4.dr_ref = bf16[5,16,256]{2,1,0:T(8,128)(2,1)S(1)} collective-permute-done((bf16[5,16,256]{2,1,0:T(8,128)(2,1)S(1)}, bf16[5,16,256]{2,1,0:T(8,128)(2,1)S(1)}, u32[]{:S(2)}, u32[]{:S(2)}) %collective-permute-start.4) | collective-permute-done | bytes 40992 | tf_op jit(solution)/shard_map/ppermute | solution.py:295
  23.5 0.0 collective-permute-done.2.s_ref
  23.5 0.0 copy-done
  23.5 0.0 copy-start.1
  23.5 1.0 %copy-done.1 = bf16[1,3,256,256]{3,2,1,0:T(8,128)(2,1)S(1)} copy-done((bf16[1,3,256,256]{3,2,1,0:T(8,128)(2,1)S(1)}, bf16[1,3,256,256]{3,2,1,0:T(8,128)(2,1)}, u32[]{:S(2)}) %copy-start.1) | copy-done | bytes 393240
  24.5 2.1 %shard_map.68 = (f32[576,256]{1,0:T(8,128)S(1)}, bf16[4,4,16,256]{3,2,1,0:T(8,128)(2,1)S(1)}) custom-call(bf16[4,4,16,256]{3,2,1,0:T(8,128)(2,1)S(1)} %get-tuple-element.18.x_ref.refs_0_, bf16[4,4,16,256]{3,2,1,0:T(8,128)(2,1)S(1)} %get-tuple-element.19.cot_ref, bf16[20,16,256]{2,1,0:T(8,128)(2,1)S(1)} %collective-permute-done.l_ref.refs_1_, ...), custom_call_target="tpu_custom_call" | custom-call | flops 1358954496 | bytes 4000000 | tf_op jit(solution)/shard_map/pallas_call | solution.py:249
  26.6 1.3 %collective-permute-start.5 = (bf16[4,4,16,256]{3,2,1,0:T(8,128)(2,1)S(1)}, bf16[4,4,16,256]{3,2,1,0:T(8,128)(2,1)S(1)}, u32[]{:S(2)}, u32[]{:S(2)}) collective-permute-start(bf16[4,4,16,256]{3,2,1,0:T(8,128)(2,1)S(1)} %get-tuple-element.25), channel_id=1, source_target_pairs={{0,2},{4,6},{8,10},{12,14},{2,0},{6,4},{10,8},{14,12},{1,3},{5,7},... | collective-permute-start | bytes 393224 | tf_op jit(solution)/shard_map/ppermute | solution.py:354
  27.9 1.4 %collective-permute-start.6 = (bf16[4,4,16,256]{3,2,1,0:T(8,128)(2,1)S(1)}, bf16[4,4,16,256]{3,2,1,0:T(8,128)(2,1)S(1)}, u32[]{:S(2)}, u32[]{:S(2)}) collective-permute-start(bf16[4,4,16,256]{3,2,1,0:T(8,128)(2,1)S(1)} %get-tuple-element.25), channel_id=1, source_target_pairs={{0,6},{4,10},{8,14},{12,2},{2,4},{6,8},{10,12},{14,0},{1,7},{5,11}... | collective-permute-start | bytes 393224 | tf_op jit(solution)/shard_map/ppermute | solution.py:354
  29.2 1.1 %collective-permute-start.7 = (bf16[4,4,16,256]{3,2,1,0:T(8,128)(2,1)S(1)}, bf16[4,4,16,256]{3,2,1,0:T(8,128)(2,1)S(1)}, u32[]{:S(2)}, u32[]{:S(2)}) collective-permute-start(bf16[4,4,16,256]{3,2,1,0:T(8,128)(2,1)S(1)} %get-tuple-element.25), channel_id=1, source_target_pairs={{0,10},{4,14},{8,2},{12,6},{2,8},{6,12},{10,0},{14,4},{1,11},{5,15... | collective-permute-start | bytes 393224 | tf_op jit(solution)/shard_map/ppermute | solution.py:354
  30.3 1.0 %collective-permute-start.8 = (bf16[4,4,16,256]{3,2,1,0:T(8,128)(2,1)S(1)}, bf16[4,4,16,256]{3,2,1,0:T(8,128)(2,1)S(1)}, u32[]{:S(2)}, u32[]{:S(2)}) collective-permute-start(bf16[4,4,16,256]{3,2,1,0:T(8,128)(2,1)S(1)} %get-tuple-element.25), channel_id=1, source_target_pairs={{0,14},{4,2},{8,6},{12,10},{2,12},{6,0},{10,4},{14,8},{1,15},{5,3}... | collective-permute-start | bytes 393224 | tf_op jit(solution)/shard_map/ppermute | solution.py:354
  31.4 1.0 %collective-permute-done.5.refs_0_ = bf16[4,4,16,256]{3,2,1,0:T(8,128)(2,1)S(1)} collective-permute-done((bf16[4,4,16,256]{3,2,1,0:T(8,128)(2,1)S(1)}, bf16[4,4,16,256]{3,2,1,0:T(8,128)(2,1)S(1)}, u32[]{:S(2)}, u32[]{:S(2)}) %collective-permute-start.5) | collective-permute-done | bytes 131104 | tf_op jit(solution)/shard_map/ppermute | solution.py:354
  32.3 0.9 %collective-permute-done.6.refs_1_ = bf16[4,4,16,256]{3,2,1,0:T(8,128)(2,1)S(1)} collective-permute-done((bf16[4,4,16,256]{3,2,1,0:T(8,128)(2,1)S(1)}, bf16[4,4,16,256]{3,2,1,0:T(8,128)(2,1)S(1)}, u32[]{:S(2)}, u32[]{:S(2)}) %collective-permute-start.6) | collective-permute-done | bytes 131104 | tf_op jit(solution)/shard_map/ppermute | solution.py:354
  33.2 7.2 %collective-permute-done.7.refs_2_ = bf16[4,4,16,256]{3,2,1,0:T(8,128)(2,1)S(1)} collective-permute-done((bf16[4,4,16,256]{3,2,1,0:T(8,128)(2,1)S(1)}, bf16[4,4,16,256]{3,2,1,0:T(8,128)(2,1)S(1)}, u32[]{:S(2)}, u32[]{:S(2)}) %collective-permute-start.7) | collective-permute-done | bytes 131104 | tf_op jit(solution)/shard_map/ppermute | solution.py:354
  40.4 2.3 %collective-permute-done.8.refs_3_ = bf16[4,4,16,256]{3,2,1,0:T(8,128)(2,1)S(1)} collective-permute-done((bf16[4,4,16,256]{3,2,1,0:T(8,128)(2,1)S(1)}, bf16[4,4,16,256]{3,2,1,0:T(8,128)(2,1)S(1)}, u32[]{:S(2)}, u32[]{:S(2)}) %collective-permute-start.8) | collective-permute-done | bytes 131104 | tf_op jit(solution)/shard_map/ppermute | solution.py:354
  42.8 0.0 copy-start.2
  42.8 0.6 %collective-permute-start.9 = (bf16[4,16,16,256]{3,2,1,0:T(8,128)(2,1)S(1)}, bf16[4,16,16,256]{3,2,1,0:T(8,128)(2,1)S(1)}, u32[]{:S(2)}, u32[]{:S(2)}) collective-permute-start(bf16[4,16,16,256]{3,2,1,0:T(8,128)(2,1)S(1)} %shard_map.69.g_ref), channel_id=1, source_target_pairs={{0,1},{1,0},{2,3},{3,2},{4,5},{5,4},{6,7},{7,6},{8,9},{9,8},{10,11... | collective-permute-start | bytes 1572872 | tf_op jit(solution)/shard_map/ppermute | solution.py:318
  43.3 0.0 collective-permute-done.12.other_ref
  43.3 2.9 %shard_map.71 = (bf16[256,2048]{1,0:T(8,128)(2,1)S(1)}, bf16[256,2048]{1,0:T(8,128)(2,1)S(1)}, f32[2048,64]{1,0:T(8,128)S(1)}) custom-call(bf16[4,16,16,256]{3,2,1,0:T(8,128)(2,1)S(1)} %shard_map.70.x_ref, bf16[4,16,16,256]{3,2,1,0:T(8,128)(2,1)S(1)} %collective-permute-done.12.other_ref, bf16[9,256,256]{2,1,0:T(8,128)(2,1)S(1)} %bitcast.11), custom_call_target="tpu_custom_call" | custom-call | flops 2415919104 | bytes 6000000 | tf_op jit(solution)/shard_map/pallas_call | solution.py:249
  46.3 0.0 collective-permute-done.9.other_ref
  46.3 0.0 copy-done.2
  46.3 5.6 %shard_map.72 = (bf16[2,8,4,4,256]{4,3,2,1,0:T(4,128)(2,1)}, f32[9,64,256]{2,1,0:T(8,128)}, f32[3,64,256]{2,1,0:T(8,128)}) custom-call(bf16[4,16,16,256]{3,2,1,0:T(8,128)(2,1)S(1)} %shard_map.69.g_ref, bf16[4,16,16,256]{3,2,1,0:T(8,128)(2,1)S(1)} %collective-permute-done.9.other_ref, f32[576,256]{1,0:T(8,128)S(1)} %get-tuple-element.26.slope_w_ref, ...), custom_call_target="tpu_custom_call" | custom-call | flops 1358954496 | bytes 8000000 | tf_op jit(solution)/shard_map/pallas_call | solution.py:249
  (1 shorter events, 0.0 us)
Async XLA Ops:
  0.6 22.9 %copy-start = (bf16[1,3,3,256,256]{4,3,2,1,0:T(8,128)(2,1)S(1)}, bf16[1,3,3,256,256]{4,3,2,1,0:T(8,128)(2,1)}, u32[]{:S(2)}) copy-start(bf16[1,3,3,256,256]{4,3,2,1,0:T(8,128)(2,1)} %param.6) | copy-start | bytes 3538948
  0.6 1.0 %copy-start.3 = (bf16[1,2,8,4,4,256]{5,4,3,2,1,0:T(4,128)(2,1)S(1)}, bf16[1,2,8,4,4,256]{5,4,3,2,1,0:T(4,128)(2,1)}, u32[]{:S(2)}) copy-start(bf16[1,2,8,4,4,256]{5,4,3,2,1,0:T(4,128)(2,1)} %param.4) | copy-start | bytes 393220
  1.6 0.9 %copy-start.4 = (bf16[2,8,4,4,256]{4,3,2,1,0:T(4,128)(2,1)S(1)}, bf16[2,8,4,4,256]{4,3,2,1,0:T(4,128)(2,1)}, u32[]{:S(2)}) copy-start(bf16[2,8,4,4,256]{4,3,2,1,0:T(4,128)(2,1)} %cot_ref.1) | copy-start | bytes 393220
  2.7 11.1 %collective-permute-start.10 = (bf16[4,4,16,256]{3,2,1,0:T(8,128)(2,1)S(1)}, bf16[4,4,16,256]{3,2,1,0:T(8,128)(2,1)S(1)}, u32[]{:S(2)}, u32[]{:S(2)}) collective-permute-start(bf16[4,4,16,256]{3,2,1,0:T(8,128)(2,1)S(1)} %get-tuple-element.18.x_ref.refs_0_), channel_id=1, source_target_pairs={{0,8},{4,12},{8,0},{12,4},{1,9},{5,13},{9,1},{13,5},{2,10},{6,14},... | collective-permute-start | bytes 393224 | tf_op jit(solution)/shard_map/ppermute | solution.py:304
  5.0 11.7 %collective-permute-start.11 = (bf16[4,4,16,256]{3,2,1,0:T(8,128)(2,1)S(1)}, bf16[4,4,16,256]{3,2,1,0:T(8,128)(2,1)S(1)}, u32[]{:S(2)}, u32[]{:S(2)}) collective-permute-start(bf16[4,4,16,256]{3,2,1,0:T(8,128)(2,1)S(1)} %get-tuple-element.18.x_ref.refs_0_), channel_id=1, source_target_pairs={{0,12},{12,0},{1,13},{13,1},{2,14},{14,2},{3,15},{15,3},{16,28},{2... | collective-permute-start | bytes 393224 | tf_op jit(solution)/shard_map/ppermute | solution.py:306
  5.7 13.7 %collective-permute-start = (bf16[20,16,256]{2,1,0:T(8,128)(2,1)S(1)}, bf16[20,16,256]{2,1,0:T(8,128)(2,1)S(1)}, u32[]{:S(2)}, u32[]{:S(2)}) collective-permute-start(bf16[20,16,256]{2,1,0:T(8,128)(2,1)S(1)} %get-tuple-element.20), channel_id=1, source_target_pairs={{0,4},{1,5},{4,8},{5,9},{8,12},{9,13},{2,6},{3,7},{6,10},{7,11},{1... | collective-permute-start | bytes 491528 | tf_op jit(solution)/shard_map/ppermute | solution.py:295
  7.6 11.8 %collective-permute-start.1 = (bf16[20,16,256]{2,1,0:T(8,128)(2,1)S(1)}, bf16[20,16,256]{2,1,0:T(8,128)(2,1)S(1)}, u32[]{:S(2)}, u32[]{:S(2)}) collective-permute-start(bf16[20,16,256]{2,1,0:T(8,128)(2,1)S(1)} %get-tuple-element.21), channel_id=1, source_target_pairs={{4,0},{5,1},{8,4},{9,5},{12,8},{13,9},{6,2},{7,3},{10,6},{11,7},{1... | collective-permute-start | bytes 491528 | tf_op jit(solution)/shard_map/ppermute | solution.py:295
  11.4 12.1 %collective-permute-start.2 = (bf16[3,4,16,256]{3,2,1,0:T(8,128)(2,1)S(1)}, bf16[3,4,16,256]{3,2,1,0:T(8,128)(2,1)S(1)}, u32[]{:S(2)}, u32[]{:S(2)}) collective-permute-start(bf16[3,4,16,256]{3,2,1,0:T(8,128)(2,1)S(1)} %get-tuple-element.22), channel_id=1, source_target_pairs={{0,1},{1,0},{4,5},{5,4},{8,9},{9,8},{12,13},{13,12},{2,3},{3,2},{6... | collective-permute-start | bytes 294920 | tf_op jit(solution)/shard_map/ppermute | solution.py:295
  13.8 6.3 %collective-permute-start.3 = (bf16[5,16,256]{2,1,0:T(8,128)(2,1)S(1)}, bf16[5,16,256]{2,1,0:T(8,128)(2,1)S(1)}, u32[]{:S(2)}, u32[]{:S(2)}) collective-permute-start(bf16[5,16,256]{2,1,0:T(8,128)(2,1)S(1)} %get-tuple-element.23), channel_id=1, source_target_pairs={{0,5},{1,4},{4,9},{5,8},{8,13},{9,12},{2,7},{3,6},{6,11},{7,10},{1... | collective-permute-start | bytes 122888 | tf_op jit(solution)/shard_map/ppermute | solution.py:295
  16.7 6.8 %collective-permute-start.4 = (bf16[5,16,256]{2,1,0:T(8,128)(2,1)S(1)}, bf16[5,16,256]{2,1,0:T(8,128)(2,1)S(1)}, u32[]{:S(2)}, u32[]{:S(2)}) collective-permute-start(bf16[5,16,256]{2,1,0:T(8,128)(2,1)S(1)} %get-tuple-element.24), channel_id=1, source_target_pairs={{4,1},{5,0},{8,5},{9,4},{12,9},{13,8},{6,3},{7,2},{10,7},{11,6},{1... | collective-permute-start | bytes 122888 | tf_op jit(solution)/shard_map/ppermute | solution.py:295
  19.5 23.9 %collective-permute-start.12 = (bf16[4,16,16,256]{3,2,1,0:T(8,128)(2,1)S(1)}, bf16[4,16,16,256]{3,2,1,0:T(8,128)(2,1)S(1)}, u32[]{:S(2)}, u32[]{:S(2)}) collective-permute-start(bf16[4,16,16,256]{3,2,1,0:T(8,128)(2,1)S(1)} %shard_map.70.x_ref), channel_id=1, source_target_pairs={{0,1},{1,0},{2,3},{3,2},{4,5},{5,4},{6,7},{7,6},{8,9},{9,8},{10,11... | collective-permute-start | bytes 1572872 | tf_op jit(solution)/shard_map/ppermute | solution.py:318
  23.5 1.0 %copy-start.1 = (bf16[1,3,256,256]{3,2,1,0:T(8,128)(2,1)S(1)}, bf16[1,3,256,256]{3,2,1,0:T(8,128)(2,1)}, u32[]{:S(2)}) copy-start(bf16[1,3,256,256]{3,2,1,0:T(8,128)(2,1)} %param.7) | copy-start | bytes 1179652
  26.6 5.8 %collective-permute-start.5 = (bf16[4,4,16,256]{3,2,1,0:T(8,128)(2,1)S(1)}, bf16[4,4,16,256]{3,2,1,0:T(8,128)(2,1)S(1)}, u32[]{:S(2)}, u32[]{:S(2)}) collective-permute-start(bf16[4,4,16,256]{3,2,1,0:T(8,128)(2,1)S(1)} %get-tuple-element.25), channel_id=1, source_target_pairs={{0,2},{4,6},{8,10},{12,14},{2,0},{6,4},{10,8},{14,12},{1,3},{5,7},... | collective-permute-start | bytes 393224 | tf_op jit(solution)/shard_map/ppermute | solution.py:354
  27.9 5.4 %collective-permute-start.6 = (bf16[4,4,16,256]{3,2,1,0:T(8,128)(2,1)S(1)}, bf16[4,4,16,256]{3,2,1,0:T(8,128)(2,1)S(1)}, u32[]{:S(2)}, u32[]{:S(2)}) collective-permute-start(bf16[4,4,16,256]{3,2,1,0:T(8,128)(2,1)S(1)} %get-tuple-element.25), channel_id=1, source_target_pairs={{0,6},{4,10},{8,14},{12,2},{2,4},{6,8},{10,12},{14,0},{1,7},{5,11}... | collective-permute-start | bytes 393224 | tf_op jit(solution)/shard_map/ppermute | solution.py:354
  29.2 11.2 %collective-permute-start.7 = (bf16[4,4,16,256]{3,2,1,0:T(8,128)(2,1)S(1)}, bf16[4,4,16,256]{3,2,1,0:T(8,128)(2,1)S(1)}, u32[]{:S(2)}, u32[]{:S(2)}) collective-permute-start(bf16[4,4,16,256]{3,2,1,0:T(8,128)(2,1)S(1)} %get-tuple-element.25), channel_id=1, source_target_pairs={{0,10},{4,14},{8,2},{12,6},{2,8},{6,12},{10,0},{14,4},{1,11},{5,15... | collective-permute-start | bytes 393224 | tf_op jit(solution)/shard_map/ppermute | solution.py:354
  30.3 12.4 %collective-permute-start.8 = (bf16[4,4,16,256]{3,2,1,0:T(8,128)(2,1)S(1)}, bf16[4,4,16,256]{3,2,1,0:T(8,128)(2,1)S(1)}, u32[]{:S(2)}, u32[]{:S(2)}) collective-permute-start(bf16[4,4,16,256]{3,2,1,0:T(8,128)(2,1)S(1)} %get-tuple-element.25), channel_id=1, source_target_pairs={{0,14},{4,2},{8,6},{12,10},{2,12},{6,0},{10,4},{14,8},{1,15},{5,3}... | collective-permute-start | bytes 393224 | tf_op jit(solution)/shard_map/ppermute | solution.py:354
  42.8 3.5 %copy-start.2 = (bf16[1,3,256,256]{3,2,1,0:T(8,128)(2,1)S(1)}, bf16[1,3,256,256]{3,2,1,0:T(8,128)(2,1)}, u32[]{:S(2)}) copy-start(bf16[1,3,256,256]{3,2,1,0:T(8,128)(2,1)} %param.7) | copy-start | bytes 1179652
  42.8 3.5 %collective-permute-start.9 = (bf16[4,16,16,256]{3,2,1,0:T(8,128)(2,1)S(1)}, bf16[4,16,16,256]{3,2,1,0:T(8,128)(2,1)S(1)}, u32[]{:S(2)}, u32[]{:S(2)}) collective-permute-start(bf16[4,16,16,256]{3,2,1,0:T(8,128)(2,1)S(1)} %shard_map.69.g_ref), channel_id=1, source_target_pairs={{0,1},{1,0},{2,3},{3,2},{4,5},{5,4},{6,7},{7,6},{8,9},{9,8},{10,11... | collective-permute-start | bytes 1572872 | tf_op jit(solution)/shard_map/ppermute | solution.py:318

commit v4 on v3

--- a/solution.py
+++ b/solution.py
@@ -33,27 +33,45 @@
     return sig * (1.0 + hidden * (1.0 - sig))
 
 
-def pack_kernel(x_ref, cot_ref, xc_ref, cc_ref, right_ref, left_ref, side_ref, dr_ref, dl_ref):
+def pack_kernel(both_ref, xc_ref, cc_ref, right_ref, left_ref):
     rows, cols, steps, channels = xc_ref.shape
-    for src, dst in ((x_ref, xc_ref), (cot_ref, cc_ref)):
+    for n, dst in enumerate((xc_ref, cc_ref)):
         for r in range(rows):
-            dst[r] = jnp.swapaxes(src[:, :, r].reshape(steps, cols, channels), 0, 1)
+            dst[r] = jnp.swapaxes(both_ref[n, :, :, r].reshape(steps, cols, channels), 0, 1)
     cells = rows * cols
     for msg, col in ((right_ref, cols - 1), (left_ref, 0)):
         msg[:cells] = xc_ref[...].reshape(cells, steps, channels)
         for r in range(rows):
             msg[cells + r] = cc_ref[r, col]
-    top = lax.axis_index("space") == 0
-    for here, row, edge in ((top, rows - 2, rows - 1), (jnp.logical_not(top), 0, 0)):
-
-        @pl.when(here)
-        def _(row=row, edge=edge):
-            side_ref[:2] = xc_ref[row : row + 2]
-            side_ref[2] = cc_ref[edge]
-            for msg, col, last in ((dr_ref, cols - 2, cols - 1), (dl_ref, 0, 0)):
-                for i in range(2):
-                    msg[2 * i : 2 * i + 2] = xc_ref[row + i, col : col + 2]
-                msg[4] = cc_ref[edge, last]
+
+
+def weights_kernel(share, w_in, tw_in, after_ref, w_ref, tw_ref, pick_ref):
+    channels = w_ref.shape[-1]
+    w_ref[...] = w_in[...]
+    tw_ref[...] = tw_in[...]
+    first = pl.multiple_of(lax.axis_index("chan") * share, share)
+    for lag in range(3):
+        pick_ref[lag * share : (lag + 1) * share, :] = tw_in[lag, pl.ds(first, share), :]
+    at = lax.broadcasted_iota(jnp.int32, (share, channels), 1) - first
+    chosen = at == lax.broadcasted_iota(jnp.int32, (share, channels), 0)
+    pick_ref[3 * share :, :] = jnp.where(chosen, 1.0, 0.0).astype(BF16)
+
+
+def side_kernel(x_ref, cot_ref, l_ref, r_ref, after_ref, side_ref):
+    rows, cols = x_ref.shape[:2]
+    cells = rows * cols
+    bottom = lax.axis_index("space")
+    for i in range(2):
+        row = (1 - bottom) * (rows - 2) + i
+        base = i * (cols + 4)
+        side_ref[base : base + 2] = l_ref[pl.ds(row * cols + cols - 2, 2)]
+        side_ref[base + 2 : base + 2 + cols] = x_ref[row]
+        side_ref[base + 2 + cols : base + 4 + cols] = r_ref[pl.ds(row * cols, 2)]
+    row = (1 - bottom) * (rows - 1)
+    base = 2 * (cols + 4)
+    side_ref[base] = l_ref[cells + row]
+    side_ref[base + 1 : base + 1 + cols] = cot_ref[row]
+    side_ref[base + 1 + cols] = r_ref[cells + row]
 
 
 def conv_back(hg_ref, w_ref, rows, cols):
@@ -87,7 +105,7 @@
 
 
 def first_kernel(
-    frames, x_ref, cot_ref, l_ref, r_ref, s_ref, dl_ref, dr_ref, w_ref, tw_ref,
+    frames, x_ref, cot_ref, l_ref, r_ref, side_ref, w_ref, tw_ref,
     slope_ref, out_ref, xw_ref, cw_ref, hg_ref,
 ):
     rows, cols, steps, channels = x_ref.shape
@@ -103,15 +121,11 @@
     near = (1 - bottom) * (rows + 2)
     far = bottom * (rows + 2)
     for i in range(2):
-        xw_ref[near + i, 2 : 2 + cols] = s_ref[i]
-        xw_ref[near + i, 0:2] = dl_ref[2 * i : 2 * i + 2]
-        xw_ref[near + i, cols + 2 : cols + 4] = dr_ref[2 * i : 2 * i + 2]
+        xw_ref[near + i] = side_ref[i * (cols + 4) : (i + 1) * (cols + 4)]
         xw_ref[far + i] = jnp.zeros(xw_ref.shape[1:], BF16)
     near = (1 - bottom) * (rows + 1)
     far = bottom * (rows + 1)
-    cw_ref[near, 1 : 1 + cols] = s_ref[2]
-    cw_ref[near, 0] = dl_ref[4]
-    cw_ref[near, cols + 1] = dr_ref[4]
+    cw_ref[near] = side_ref[2 * (cols + 4) :]
     cw_ref[far] = jnp.zeros(cw_ref.shape[1:], BF16)
     hidden = None
     for u in range(3):
@@ -125,8 +139,8 @@
     send_on(out_ref, cot_ref[...].reshape(-1, channels), conv, cot_ref)
 
 
-def collect_kernel(wrapped, *refs):
-    pieces, out_ref = refs[:-1], refs[-1]
+def collect_kernel(wrapped, extra, *refs):
+    pieces, out_ref = refs[: -1 - extra], refs[-1]
     chan = len(pieces) - wrapped
     rows, cols, steps, channels = pieces[0].shape
     me = lax.axis_index("chan")
@@ -181,7 +195,7 @@
     send_on(out_ref, own, conv, cot_ref)
 
 
-def tile_kernel(share, x_ref, other_ref, w_ref, act_ref, xt_ref, slope_ref, xp_ref):
+def tile_kernel(share, x_ref, other_ref, w_ref, after_ref, act_ref, xt_ref, slope_ref, xp_ref):
     rows, width, steps, channels = x_ref.shape
     fill_padded(xp_ref, x_ref, other_ref)
     span = width * steps
@@ -200,8 +214,8 @@
 
 
 def final_kernel(
-    frames, g_ref, other_ref, slope_w_ref, slope_s_ref, act_ref, xt_ref, w_ref, tw_ref,
-    out_ref, space_ref, time_ref, gp_ref, hg_ref, hs_ref, hcols_ref, gcols_ref, pick_ref,
+    frames, g_ref, other_ref, slope_w_ref, slope_s_ref, act_ref, xt_ref, w_ref, tw_ref, pick_ref,
+    out_ref, space_ref, time_ref, gp_ref, hg_ref, hs_ref, hcols_ref, gcols_ref,
 ):
     rows, width, steps, channels = g_ref.shape
     clips, _, _, cols, _ = out_ref.shape
@@ -209,12 +223,6 @@
     height = 2 * rows
     span = width * steps
     fill_padded(gp_ref, g_ref, other_ref)
-    first = pl.multiple_of(lax.axis_index("chan") * share, share)
-    for lag in range(3):
-        pick_ref[lag * share : (lag + 1) * share, :] = tw_ref[lag, pl.ds(first, share), :]
-    at = lax.broadcasted_iota(jnp.int32, (share, channels), 1) - first
-    chosen = at == lax.broadcasted_iota(jnp.int32, (share, channels), 0)
-    pick_ref[3 * share :, :] = jnp.where(chosen, 1.0, 0.0).astype(BF16)
     hs_ref[...] = jnp.zeros(hs_ref.shape, BF16)
     for i in range(height):
         block = gp_ref[i + 1, 1 : 1 + width].reshape(-1, channels)
@@ -245,10 +253,15 @@
         out_ref[:, :, r] = jnp.swapaxes(grads[r], 0, 1).reshape(clips, frames, cols, channels)
 
 
-def call(kernel, outs, scratch, limit, flops, moved, *operands):
+VM = pltpu.VMEM
+
+
+def call(kernel, outs, scratch, limit, flops, moved, *operands, places=None):
+    places = places or [VM] * len(operands)
     return pl.pallas_call(
         kernel,
         out_shape=outs,
+        in_specs=[pl.BlockSpec(memory_space=place) for place in places],
         scratch_shapes=scratch,
         compiler_params=pltpu.CompilerParams(vmem_limit_bytes=limit * MIB),
         cost_estimate=pl.CostEstimate(flops=flops, bytes_accessed=moved, transcendentals=0),
@@ -264,56 +277,73 @@
     count = height * width * steps
     win = (rows + 2) * (cols + 2) * steps
     large = 24 if chan <= 4 else 56
-    w = space_weight[0].reshape(9, channels, channels)
-    tw = time_weight[0]
     cell = (steps, channels)
 
     def bf16(*shape):
         return jax.ShapeDtypeStruct(shape + cell, BF16)
 
-    x_own, cot_own, to_right, to_left, to_side, to_dr, to_dl = call(
+    beside = rows * cols + rows
+    x_own, cot_own, to_right, to_left = call(
         pack_kernel,
+        (bf16(rows, cols), bf16(rows, cols), bf16(beside), bf16(beside)),
+        [],
+        16,
+        1_000_000,
+        1_000_000,
+        jnp.stack([activations[0], cotangent]),
+    )
+    w, tw, pick = call(
+        functools.partial(weights_kernel, share),
         (
-            bf16(rows, cols), bf16(rows, cols), bf16(rows * cols + rows),
-            bf16(rows * cols + rows), bf16(3, cols), bf16(5), bf16(5),
+            jax.ShapeDtypeStruct((9, channels, channels), BF16),
+            jax.ShapeDtypeStruct((3, channels, channels), BF16),
+            jax.ShapeDtypeStruct((4 * share, channels), BF16),
         ),
         [],
         16,
         1_000_000,
-        1_000_000,
-        activations[0],
-        cotangent,
-    )
-
-    def moved(message, by, flip):
-        pairs = [
-            (2 * c + s, 2 * (c + by) + (1 - s if flip else s))
-            for c in range(chan)
-            for s in range(2)
-            if 0 <= c + by < chan
-        ]
-        return lax.ppermute(message, ("chan", "space"), pairs)
-
-    from_left = moved(to_right, 1, False)
-    from_right = moved(to_left, -1, False)
-    from_dl = moved(to_dr, 1, True)
-    from_dr = moved(to_dl, -1, True)
-    from_side = moved(to_side, 0, True)
+        3_000_000,
+        space_weight[0].reshape(9, channels, channels),
+        time_weight[0],
+        x_own,
+        places=[VM, VM, pl.ANY],
+    )
+
+    def along(message, by):
+        return lax.ppermute(
+            message, "chan", [(c, c + by) for c in range(chan) if 0 <= c + by < chan]
+        )
+
+    from_left = along(to_right, 1)
+    from_right = along(to_left, -1)
     pieces = [x_own, from_left]
     for d in range(2, chan - 1):
         pieces.append(lax.ppermute(x_own, "chan", [(i, (i + d) % chan) for i in range(chan)]))
     pieces.append(from_right)
     pieces.append(lax.ppermute(x_own, "chan", [(0, chan - 1), (chan - 1, 0)]))
-
-    def gathered(wrapped, parts):
+    to_side = call(
+        side_kernel,
+        bf16(2 * (cols + 4) + cols + 2),
+        [],
+        16,
+        1_000_000,
+        1_000_000,
+        x_own, cot_own, from_left, from_right, pick,
+        places=[VM] * 4 + [pl.ANY],
+    )
+    from_side = lax.ppermute(to_side, "space", [(0, 1), (1, 0)])
+
+    def gathered(wrapped, parts, after=()):
         half = call(
-            functools.partial(collect_kernel, wrapped),
+            functools.partial(collect_kernel, wrapped, len(after)),
             bf16(rows, width),
             [],
             16,
             1_000_000,
             1_000_000,
             *parts,
+            *after,
+            places=[VM] * len(parts) + [pl.ANY] * len(after),
         )
         return half, lax.ppermute(half, "space", [(0, 1), (1, 0)])
 
@@ -328,7 +358,7 @@
         20,
         2 * win * 18 * channels * channels,
         4_000_000,
-        x_own, cot_own, from_left, from_right, from_side, from_dl, from_dr, w, tw,
+        x_own, cot_own, from_left, from_right, from_side, w, tw,
     )
 
     padded = pltpu.VMEM((height + 2, width + 2) + cell, BF16)
@@ -352,23 +382,25 @@
                 for c in range(chan)
             ]
             arrived.append(lax.ppermute(payload, ("chan", "pipe"), pairs))
-        g_all = gathered(0, arrived)
-
-    x_all = gathered(1, pieces)
-    act_t, x_t, slope_s = call(
-        functools.partial(tile_kernel, share),
-        (
-            jax.ShapeDtypeStruct((channels, count), BF16),
-            jax.ShapeDtypeStruct((channels, count), BF16),
-            jax.ShapeDtypeStruct((count, share), F32),
-        ),
-        [padded],
-        large,
-        2 * count * 9 * channels * channels,
-        6_000_000,
-        *x_all,
-        w,
-    )
+        if not tick:
+            x_all = gathered(1, pieces, (payload,))
+            act_t, x_t, slope_s = call(
+                functools.partial(tile_kernel, share),
+                (
+                    jax.ShapeDtypeStruct((channels, count), BF16),
+                    jax.ShapeDtypeStruct((channels, count), BF16),
+                    jax.ShapeDtypeStruct((count, share), F32),
+                ),
+                [padded],
+                large,
+                2 * count * 9 * channels * channels,
+                6_000_000,
+                *x_all,
+                w,
+                arrived[0],
+                places=[VM, VM, VM, pl.ANY],
+            )
+        g_all = gathered(0, arrived, () if tick else (slope_s,))
     grads, space_grad, time_grad = call(
         functools.partial(final_kernel, frames),
         (
@@ -382,12 +414,11 @@
             pltpu.VMEM((height + 2, width + 2, steps, share), BF16),
             pltpu.VMEM((count, 9 * share), BF16),
             pltpu.VMEM((count, 3 * share), BF16),
-            pltpu.VMEM((4 * share, channels), BF16),
         ],
         large,
         4 * win * 9 * channels * channels,
         8_000_000,
-        *g_all, slope_w, slope_s, act_t, x_t, w, tw,
+        *g_all, slope_w, slope_s, act_t, x_t, w, tw, pick,
     )
     return (
         grads[None],

time: 52.2 us -> 53.2 us (1.019)
  the two profiles are of different devices: /device:TPU:9 before, /device:TPU:0 now
where the time goes in v4:
time: 53.2 us; the launch traced here: 52.9 us
  waiting for transfers between devices  23.4 us (44%)
  starting transfers between devices  14.6 us (27%)
  Pallas kernels  10.7 us (20%)
  local copies, waits for them, and re-layouts  2.26 us (4%)
  other arithmetic  1.16 us (2%)
  between operations  0.75 us (1%)
    pallas_call x8, Pallas kernels, call(): pl.pallas_call(kernel, out_shape=outs, in_specs=[pl.BlockSpec(memory_spac...  10.7 us
    ppermute x4, waiting for transfers between devices, per_device(): arrived.append(lax.ppermute(payload, ('chan', 'pipe'), pairs))  8.15 us
    ppermute x2, starting transfers between devices, along(): lax.ppermute(message, 'chan', [(c, c + by) for c in range(chan) if 0 <= c...  6.23 us
    ppermute x1, waiting for transfers between devices, per_device(): lax.ppermute(x_own, 'chan', [(i, (i + d) % chan) for i in range(chan)])  5.11 us
    ppermute x4, starting transfers between devices, per_device(): arrived.append(lax.ppermute(payload, ('chan', 'pipe'), pairs))  4.56 us
    ppermute x1, waiting for transfers between devices, per_device(): pieces.append(lax.ppermute(x_own, 'chan', [(0, chan - 1), (chan - 1, 0)]))  4.42 us
    ppermute x2, waiting for transfers between devices, along(): lax.ppermute(message, 'chan', [(c, c + by) for c in range(chan) if 0 <= c...  3.86 us
    ppermute x1, starting transfers between devices, per_device(): pieces.append(lax.ppermute(x_own, 'chan', [(0, chan - 1), (chan - 1, 0)]))  3.47 us
  transfers between devices with their start and end apart: 11, of which 6 were waited for; matrix products, arithmetic and copies ran while one was open for 0% of the time, Pallas kernels for 10%

profile of v4, /device:TPU:0, one launch (start us, length us, event | category | flops | bytes accessed | tf_op | source)
XLA Modules:
  0.0 52.9 jit_solution(16103051035838565003)
XLA Ops:
  0.6 1.2 %pad_maximum_fusion.both_ref = bf16[2,2,8,4,4,256]{5,4,3,2,1,0:T(4,128)(2,1)S(1)} fusion(bf16[1,2,8,4,4,256]{5,4,3,2,1,0:T(4,128)(2,1)} %bitcast.12, bf16[1,2,8,4,4,256]{5,4,3,2,1,0:T(4,128)(2,1)} %param.4), kind=kLoop, calls=%fused_computation | loop fusion | flops 131072 | bytes 524288 | tf_op jit(solution)/shard_map/stack | solution.py:293
  1.8 0.1 shard_map.67
  1.9 4.9 %collective-permute-start = (bf16[20,16,256]{2,1,0:T(8,128)(2,1)S(1)}, bf16[20,16,256]{2,1,0:T(8,128)(2,1)S(1)}, u32[]{:S(2)}, u32[]{:S(2)}) collective-permute-start(bf16[20,16,256]{2,1,0:T(8,128)(2,1)S(1)} %get-tuple-element.20), channel_id=1, source_target_pairs={{0,4},{4,8},{8,12},{1,5},{5,9},{9,13},{2,6},{6,10},{10,14},{3,7},{... | collective-permute-start | bytes 491528 | tf_op jit(solution)/shard_map/ppermute | solution.py:313
  6.8 1.3 %collective-permute-start.1 = (bf16[20,16,256]{2,1,0:T(8,128)(2,1)S(1)}, bf16[20,16,256]{2,1,0:T(8,128)(2,1)S(1)}, u32[]{:S(2)}, u32[]{:S(2)}) collective-permute-start(bf16[20,16,256]{2,1,0:T(8,128)(2,1)S(1)} %get-tuple-element.21), channel_id=1, source_target_pairs={{4,0},{8,4},{12,8},{5,1},{9,5},{13,9},{6,2},{10,6},{14,10},{7,3},{... | collective-permute-start | bytes 491528 | tf_op jit(solution)/shard_map/ppermute | solution.py:313
  8.1 0.0 copy-start
  8.2 1.3 %copy-done = bf16[1,3,3,256,256]{4,3,2,1,0:T(8,128)(2,1)S(1)} copy-done((bf16[1,3,3,256,256]{4,3,2,1,0:T(8,128)(2,1)S(1)}, bf16[1,3,3,256,256]{4,3,2,1,0:T(8,128)(2,1)}, u32[]{:S(2)}) %copy-start) | copy-done | bytes 1179672
  9.4 0.0 copy-start.1
  9.4 1.0 %copy-done.1 = bf16[1,3,256,256]{3,2,1,0:T(8,128)(2,1)S(1)} copy-done((bf16[1,3,256,256]{3,2,1,0:T(8,128)(2,1)S(1)}, bf16[1,3,256,256]{3,2,1,0:T(8,128)(2,1)}, u32[]{:S(2)}) %copy-start.1) | copy-done | bytes 393240
  10.4 0.1 shard_map.68
  10.5 0.0 collective-permute-done.l_ref.refs_1_
  10.5 3.9 %collective-permute-done.1.r_ref.refs_3_ = bf16[20,16,256]{2,1,0:T(8,128)(2,1)S(1)} collective-permute-done((bf16[20,16,256]{2,1,0:T(8,128)(2,1)S(1)}, bf16[20,16,256]{2,1,0:T(8,128)(2,1)S(1)}, u32[]{:S(2)}, u32[]{:S(2)}) %collective-permute-start.1) | collective-permute-done | bytes 163872 | tf_op jit(solution)/shard_map/ppermute | solution.py:313
  14.4 0.1 collective-permute-start.2
  14.5 3.5 %collective-permute-start.8 = (bf16[4,4,16,256]{3,2,1,0:T(8,128)(2,1)S(1)}, bf16[4,4,16,256]{3,2,1,0:T(8,128)(2,1)S(1)}, u32[]{:S(2)}, u32[]{:S(2)}) collective-permute-start(bf16[4,4,16,256]{3,2,1,0:T(8,128)(2,1)S(1)} %get-tuple-element.18.after_ref.x_ref.refs_0_), channel_id=1, source_target_pairs={{0,12},{12,0},{1,13},{13,1},{2,14},{14,2},{3,15},{15,3},{16,28},{2... | collective-permute-start | bytes 393224 | tf_op jit(solution)/shard_map/ppermute | solution.py:323
  18.0 0.1 collective-permute-start.7
  18.0 0.0 collective-permute-done.2.side_ref
  18.1 2.1 %shard_map.70 = (f32[576,256]{1,0:T(8,128)S(1)}, bf16[4,4,16,256]{3,2,1,0:T(8,128)(2,1)S(1)}) custom-call(bf16[4,4,16,256]{3,2,1,0:T(8,128)(2,1)S(1)} %get-tuple-element.18.after_ref.x_ref.refs_0_, bf16[4,4,16,256]{3,2,1,0:T(8,128)(2,1)S(1)} %get-tuple-element.19.cot_ref, bf16[20,16,256]{2,1,0:T(8,128)(2,1)S(1)} %collective-permute-done.l_ref.refs_1_, ...), custom_call_target="tpu_custom_call" | custom-call | flops 1358954496 | bytes 4000000 | tf_op jit(solution)/shard_map/pallas_call | solution.py:261
  20.2 4.4 %collective-permute-done.8.refs_4_ = bf16[4,4,16,256]{3,2,1,0:T(8,128)(2,1)S(1)} collective-permute-done((bf16[4,4,16,256]{3,2,1,0:T(8,128)(2,1)S(1)}, bf16[4,4,16,256]{3,2,1,0:T(8,128)(2,1)S(1)}, u32[]{:S(2)}, u32[]{:S(2)}) %collective-permute-start.8) | collective-permute-done | bytes 131104 | tf_op jit(solution)/shard_map/ppermute | solution.py:323
  24.6 5.1 %collective-permute-done.7.refs_2_ = bf16[4,4,16,256]{3,2,1,0:T(8,128)(2,1)S(1)} collective-permute-done((bf16[4,4,16,256]{3,2,1,0:T(8,128)(2,1)S(1)}, bf16[4,4,16,256]{3,2,1,0:T(8,128)(2,1)S(1)}, u32[]{:S(2)}, u32[]{:S(2)}) %collective-permute-start.7) | collective-permute-done | bytes 131104 | tf_op jit(solution)/shard_map/ppermute | solution.py:321
  29.7 0.1 shard_map.71.x_ref
  29.8 0.1 collective-permute-start.9
  29.9 1.5 %collective-permute-start.3 = (bf16[4,4,16,256]{3,2,1,0:T(8,128)(2,1)S(1)}, bf16[4,4,16,256]{3,2,1,0:T(8,128)(2,1)S(1)}, u32[]{:S(2)}, u32[]{:S(2)}) collective-permute-start(bf16[4,4,16,256]{3,2,1,0:T(8,128)(2,1)S(1)} %get-tuple-element.25.refs_5_), channel_id=1, source_target_pairs={{0,2},{4,6},{8,10},{12,14},{2,0},{6,4},{10,8},{14,12},{1,3},{5,7},... | collective-permute-start | bytes 393224 | tf_op jit(solution)/shard_map/ppermute | solution.py:384
  31.4 1.5 %collective-permute-start.6 = (bf16[4,4,16,256]{3,2,1,0:T(8,128)(2,1)S(1)}, bf16[4,4,16,256]{3,2,1,0:T(8,128)(2,1)S(1)}, u32[]{:S(2)}, u32[]{:S(2)}) collective-permute-start(bf16[4,4,16,256]{3,2,1,0:T(8,128)(2,1)S(1)} %get-tuple-element.25.refs_5_), channel_id=1, source_target_pairs={{0,14},{4,2},{8,6},{12,10},{2,12},{6,0},{10,4},{14,8},{1,15},{5,3}... | collective-permute-start | bytes 393224 | tf_op jit(solution)/shard_map/ppermute | solution.py:384
  32.9 0.0 collective-permute-start.5
  32.9 1.5 %collective-permute-start.4 = (bf16[4,4,16,256]{3,2,1,0:T(8,128)(2,1)S(1)}, bf16[4,4,16,256]{3,2,1,0:T(8,128)(2,1)S(1)}, u32[]{:S(2)}, u32[]{:S(2)}) collective-permute-start(bf16[4,4,16,256]{3,2,1,0:T(8,128)(2,1)S(1)} %get-tuple-element.25.refs_5_), channel_id=1, source_target_pairs={{0,6},{4,10},{8,14},{12,2},{2,4},{6,8},{10,12},{14,0},{1,7},{5,11}... | collective-permute-start | bytes 393224 | tf_op jit(solution)/shard_map/ppermute | solution.py:384
  34.4 4.2 %collective-permute-done.3.after_ref.refs_0_ = bf16[4,4,16,256]{3,2,1,0:T(8,128)(2,1)S(1)} collective-permute-done((bf16[4,4,16,256]{3,2,1,0:T(8,128)(2,1)S(1)}, bf16[4,4,16,256]{3,2,1,0:T(8,128)(2,1)S(1)}, u32[]{:S(2)}, u32[]{:S(2)}) %collective-permute-start.3) | collective-permute-done | bytes 131104 | tf_op jit(solution)/shard_map/ppermute | solution.py:384
  38.7 0.0 collective-permute-done.9.other_ref
  38.7 2.9 %shard_map.72 = (bf16[256,2048]{1,0:T(8,128)(2,1)S(1)}, bf16[256,2048]{1,0:T(8,128)(2,1)S(1)}, f32[2048,64]{1,0:T(8,128)S(1)}) custom-call(bf16[4,16,16,256]{3,2,1,0:T(8,128)(2,1)S(1)} %shard_map.71.x_ref, bf16[4,16,16,256]{3,2,1,0:T(8,128)(2,1)S(1)} %collective-permute-done.9.other_ref, bf16[9,256,256]{2,1,0:T(8,128)(2,1)S(1)} %get-tuple-element.23.w_ref, ...), custom_call_target="tpu_custom_call" | custom-call | flops 2415919104 | bytes 6000000 | tf_op jit(solution)/shard_map/pallas_call | solution.py:261
  41.6 0.0 collective-permute-done.6.refs_3_
  41.6 3.9 %collective-permute-done.5.refs_2_ = bf16[4,4,16,256]{3,2,1,0:T(8,128)(2,1)S(1)} collective-permute-done((bf16[4,4,16,256]{3,2,1,0:T(8,128)(2,1)S(1)}, bf16[4,4,16,256]{3,2,1,0:T(8,128)(2,1)S(1)}, u32[]{:S(2)}, u32[]{:S(2)}) %collective-permute-start.5) | collective-permute-done | bytes 131104 | tf_op jit(solution)/shard_map/ppermute | solution.py:384
  45.5 0.0 collective-permute-done.4.refs_1_
  45.6 0.1 collective-permute-start.10
  45.7 1.9 %collective-permute-done.10.other_ref = bf16[4,16,16,256]{3,2,1,0:T(8,128)(2,1)S(1)} collective-permute-done((bf16[4,16,16,256]{3,2,1,0:T(8,128)(2,1)S(1)}, bf16[4,16,16,256]{3,2,1,0:T(8,128)(2,1)S(1)}, u32[]{:S(2)}, u32[]{:S(2)}) %collective-permute-start.10) | collective-permute-done | bytes 524320 | tf_op jit(solution)/shard_map/ppermute | solution.py:348
  47.6 5.4 %shard_map.74 = (bf16[2,8,4,4,256]{4,3,2,1,0:T(4,128)(2,1)}, f32[9,64,256]{2,1,0:T(8,128)}, f32[3,64,256]{2,1,0:T(8,128)}) custom-call(bf16[4,16,16,256]{3,2,1,0:T(8,128)(2,1)S(1)} %shard_map.73.g_ref, bf16[4,16,16,256]{3,2,1,0:T(8,128)(2,1)S(1)} %collective-permute-done.10.other_ref, f32[576,256]{1,0:T(8,128)S(1)} %get-tuple-element.27.slope_w_ref, ...), custom_call_target="tpu_custom_call" | custom-call | flops 1358954496 | bytes 8000000 | tf_op jit(solution)/shard_map/pallas_call | solution.py:261
  (2 shorter events, 0.1 us)
Async XLA Ops:
  1.9 8.6 %collective-permute-start = (bf16[20,16,256]{2,1,0:T(8,128)(2,1)S(1)}, bf16[20,16,256]{2,1,0:T(8,128)(2,1)S(1)}, u32[]{:S(2)}, u32[]{:S(2)}) collective-permute-start(bf16[20,16,256]{2,1,0:T(8,128)(2,1)S(1)} %get-tuple-element.20), channel_id=1, source_target_pairs={{0,4},{4,8},{8,12},{1,5},{5,9},{9,13},{2,6},{6,10},{10,14},{3,7},{... | collective-permute-start | bytes 491528 | tf_op jit(solution)/shard_map/ppermute | solution.py:313
  6.8 7.6 %collective-permute-start.1 = (bf16[20,16,256]{2,1,0:T(8,128)(2,1)S(1)}, bf16[20,16,256]{2,1,0:T(8,128)(2,1)S(1)}, u32[]{:S(2)}, u32[]{:S(2)}) collective-permute-start(bf16[20,16,256]{2,1,0:T(8,128)(2,1)S(1)} %get-tuple-element.21), channel_id=1, source_target_pairs={{4,0},{8,4},{12,8},{5,1},{9,5},{13,9},{6,2},{10,6},{14,10},{7,3},{... | collective-permute-start | bytes 491528 | tf_op jit(solution)/shard_map/ppermute | solution.py:313
  8.1 1.3 %copy-start = (bf16[1,3,3,256,256]{4,3,2,1,0:T(8,128)(2,1)S(1)}, bf16[1,3,3,256,256]{4,3,2,1,0:T(8,128)(2,1)}, u32[]{:S(2)}) copy-start(bf16[1,3,3,256,256]{4,3,2,1,0:T(8,128)(2,1)} %param.6) | copy-start | bytes 3538948
  9.4 1.0 %copy-start.1 = (bf16[1,3,256,256]{3,2,1,0:T(8,128)(2,1)S(1)}, bf16[1,3,256,256]{3,2,1,0:T(8,128)(2,1)}, u32[]{:S(2)}) copy-start(bf16[1,3,256,256]{3,2,1,0:T(8,128)(2,1)} %param.7) | copy-start | bytes 1179652
  14.4 3.6 %collective-permute-start.2 = (bf16[22,16,256]{2,1,0:T(8,128)(2,1)S(1)}, bf16[22,16,256]{2,1,0:T(8,128)(2,1)S(1)}, u32[]{:S(2)}, u32[]{:S(2)}) collective-permute-start(bf16[22,16,256]{2,1,0:T(8,128)(2,1)S(1)} %shard_map.69), channel_id=1, source_target_pairs={{0,1},{1,0},{2,3},{3,2},{4,5},{5,4},{6,7},{7,6},{8,9},{9,8},{10,11... | collective-permute-start | bytes 540680 | tf_op jit(solution)/shard_map/ppermute | solution.py:334
  14.5 10.1 %collective-permute-start.8 = (bf16[4,4,16,256]{3,2,1,0:T(8,128)(2,1)S(1)}, bf16[4,4,16,256]{3,2,1,0:T(8,128)(2,1)S(1)}, u32[]{:S(2)}, u32[]{:S(2)}) collective-permute-start(bf16[4,4,16,256]{3,2,1,0:T(8,128)(2,1)S(1)} %get-tuple-element.18.after_ref.x_ref.refs_0_), channel_id=1, source_target_pairs={{0,12},{12,0},{1,13},{13,1},{2,14},{14,2},{3,15},{15,3},{16,28},{2... | collective-permute-start | bytes 393224 | tf_op jit(solution)/shard_map/ppermute | solution.py:323
  18.0 11.7 %collective-permute-start.7 = (bf16[4,4,16,256]{3,2,1,0:T(8,128)(2,1)S(1)}, bf16[4,4,16,256]{3,2,1,0:T(8,128)(2,1)S(1)}, u32[]{:S(2)}, u32[]{:S(2)}) collective-permute-start(bf16[4,4,16,256]{3,2,1,0:T(8,128)(2,1)S(1)} %get-tuple-element.18.after_ref.x_ref.refs_0_), channel_id=1, source_target_pairs={{0,8},{4,12},{8,0},{12,4},{1,9},{5,13},{9,1},{13,5},{2,10},{6,14},... | collective-permute-start | bytes 393224 | tf_op jit(solution)/shard_map/ppermute | solution.py:321
  29.8 8.9 %collective-permute-start.9 = (bf16[4,16,16,256]{3,2,1,0:T(8,128)(2,1)S(1)}, bf16[4,16,16,256]{3,2,1,0:T(8,128)(2,1)S(1)}, u32[]{:S(2)}, u32[]{:S(2)}) collective-permute-start(bf16[4,16,16,256]{3,2,1,0:T(8,128)(2,1)S(1)} %shard_map.71.x_ref), channel_id=1, source_target_pairs={{0,1},{1,0},{2,3},{3,2},{4,5},{5,4},{6,7},{7,6},{8,9},{9,8},{10,11... | collective-permute-start | bytes 1572872 | tf_op jit(solution)/shard_map/ppermute | solution.py:348
  29.9 8.8 %collective-permute-start.3 = (bf16[4,4,16,256]{3,2,1,0:T(8,128)(2,1)S(1)}, bf16[4,4,16,256]{3,2,1,0:T(8,128)(2,1)S(1)}, u32[]{:S(2)}, u32[]{:S(2)}) collective-permute-start(bf16[4,4,16,256]{3,2,1,0:T(8,128)(2,1)S(1)} %get-tuple-element.25.refs_5_), channel_id=1, source_target_pairs={{0,2},{4,6},{8,10},{12,14},{2,0},{6,4},{10,8},{14,12},{1,3},{5,7},... | collective-permute-start | bytes 393224 | tf_op jit(solution)/shard_map/ppermute | solution.py:384
  31.4 10.2 %collective-permute-start.6 = (bf16[4,4,16,256]{3,2,1,0:T(8,128)(2,1)S(1)}, bf16[4,4,16,256]{3,2,1,0:T(8,128)(2,1)S(1)}, u32[]{:S(2)}, u32[]{:S(2)}) collective-permute-start(bf16[4,4,16,256]{3,2,1,0:T(8,128)(2,1)S(1)} %get-tuple-element.25.refs_5_), channel_id=1, source_target_pairs={{0,14},{4,2},{8,6},{12,10},{2,12},{6,0},{10,4},{14,8},{1,15},{5,3}... | collective-permute-start | bytes 393224 | tf_op jit(solution)/shard_map/ppermute | solution.py:384
  32.9 12.6 %collective-permute-start.5 = (bf16[4,4,16,256]{3,2,1,0:T(8,128)(2,1)S(1)}, bf16[4,4,16,256]{3,2,1,0:T(8,128)(2,1)S(1)}, u32[]{:S(2)}, u32[]{:S(2)}) collective-permute-start(bf16[4,4,16,256]{3,2,1,0:T(8,128)(2,1)S(1)} %get-tuple-element.25.refs_5_), channel_id=1, source_target_pairs={{0,10},{4,14},{8,2},{12,6},{2,8},{6,12},{10,0},{14,4},{1,11},{5,15... | collective-permute-start | bytes 393224 | tf_op jit(solution)/shard_map/ppermute | solution.py:384
  32.9 12.6 %collective-permute-start.4 = (bf16[4,4,16,256]{3,2,1,0:T(8,128)(2,1)S(1)}, bf16[4,4,16,256]{3,2,1,0:T(8,128)(2,1)S(1)}, u32[]{:S(2)}, u32[]{:S(2)}) collective-permute-start(bf16[4,4,16,256]{3,2,1,0:T(8,128)(2,1)S(1)} %get-tuple-element.25.refs_5_), channel_id=1, source_target_pairs={{0,6},{4,10},{8,14},{12,2},{2,4},{6,8},{10,12},{14,0},{1,7},{5,11}... | collective-permute-start | bytes 393224 | tf_op jit(solution)/shard_map/ppermute | solution.py:384
  45.6 2.0 %collective-permute-start.10 = (bf16[4,16,16,256]{3,2,1,0:T(8,128)(2,1)S(1)}, bf16[4,16,16,256]{3,2,1,0:T(8,128)(2,1)S(1)}, u32[]{:S(2)}, u32[]{:S(2)}) collective-permute-start(bf16[4,16,16,256]{3,2,1,0:T(8,128)(2,1)S(1)} %shard_map.73.g_ref), channel_id=1, source_target_pairs={{0,1},{1,0},{2,3},{3,2},{4,5},{5,4},{6,7},{7,6},{8,9},{9,8},{10,11... | collective-permute-start | bytes 1572872 | tf_op jit(solution)/shard_map/ppermute | solution.py:348

commit v5 on v4

--- a/solution.py
+++ b/solution.py
@@ -57,21 +57,18 @@
     pick_ref[3 * share :, :] = jnp.where(chosen, 1.0, 0.0).astype(BF16)
 
 
-def side_kernel(x_ref, cot_ref, l_ref, r_ref, after_ref, side_ref):
-    rows, cols = x_ref.shape[:2]
+def side_kernel(*refs):
+    pieces, (cot_ref, _, side_ref) = refs[:-3], refs[-3:]
+    rows, cols, steps, channels = pieces[0].shape
     cells = rows * cols
-    bottom = lax.axis_index("space")
-    for i in range(2):
-        row = (1 - bottom) * (rows - 2) + i
-        base = i * (cols + 4)
-        side_ref[base : base + 2] = l_ref[pl.ds(row * cols + cols - 2, 2)]
-        side_ref[base + 2 : base + 2 + cols] = x_ref[row]
-        side_ref[base + 2 + cols : base + 4 + cols] = r_ref[pl.ds(row * cols, 2)]
-    row = (1 - bottom) * (rows - 1)
-    base = 2 * (cols + 4)
-    side_ref[base] = l_ref[cells + row]
+    for d, piece in enumerate(pieces):
+        block = piece[...].reshape(cells, steps, channels) if d == 0 else piece[:cells]
+        side_ref[d * cells : (d + 1) * cells] = block
+    row = (1 - lax.axis_index("space")) * (rows - 1)
+    base = len(pieces) * cells
+    side_ref[base] = pieces[1][cells + row]
     side_ref[base + 1 : base + 1 + cols] = cot_ref[row]
-    side_ref[base + 1 + cols] = r_ref[cells + row]
+    side_ref[base + 1 + cols] = pieces[-1][cells + row]
 
 
 def conv_back(hg_ref, w_ref, rows, cols):
@@ -110,6 +107,7 @@
 ):
     rows, cols, steps, channels = x_ref.shape
     cells = rows * cols
+    chan = side_ref.shape[0] // cells
     bottom = lax.axis_index("space")
     xw_ref[2 : 2 + rows, 2 : 2 + cols] = x_ref[...]
     cw_ref[1 : 1 + rows, 1 : 1 + cols] = cot_ref[...]
@@ -121,12 +119,24 @@
     near = (1 - bottom) * (rows + 2)
     far = bottom * (rows + 2)
     for i in range(2):
-        xw_ref[near + i] = side_ref[i * (cols + 4) : (i + 1) * (cols + 4)]
+        at = (bottom * (rows - 2) + i) * cols
+        xw_ref[near + i, 2 : 2 + cols] = side_ref[pl.ds(at, cols)]
+        xw_ref[near + i, 0:2] = side_ref[pl.ds(cells + at + cols - 2, 2)]
+        xw_ref[near + i, cols + 2 : cols + 4] = side_ref[pl.ds((chan - 1) * cells + at, 2)]
         xw_ref[far + i] = jnp.zeros(xw_ref.shape[1:], BF16)
     near = (1 - bottom) * (rows + 1)
     far = bottom * (rows + 1)
-    cw_ref[near] = side_ref[2 * (cols + 4) :]
+    cw_ref[near] = side_ref[chan * cells :]
     cw_ref[far] = jnp.zeros(cw_ref.shape[1:], BF16)
+    me = lax.axis_index("chan")
+    for end, c in ((0, 0), (chan - 1, cols + 2)):
+
+        @pl.when(me == end)
+        def _(c=c):
+            xw_ref[:, c : c + 2] = jnp.zeros((rows + 4, 2, steps, channels), BF16)
+            edge = min(c, cols + 1)
+            cw_ref[:, edge : edge + 1] = jnp.zeros((rows + 2, 1, steps, channels), BF16)
+
     hidden = None
     for u in range(3):
         for v in range(3):
@@ -139,30 +149,16 @@
     send_on(out_ref, cot_ref[...].reshape(-1, channels), conv, cot_ref)
 
 
-def collect_kernel(wrapped, extra, *refs):
+def collect_kernel(extra, *refs):
     pieces, out_ref = refs[: -1 - extra], refs[-1]
-    chan = len(pieces) - wrapped
+    chan = len(pieces)
     rows, cols, steps, channels = pieces[0].shape
     me = lax.axis_index("chan")
-
-    def put(d, piece):
-        place = lax.rem(me - d + chan, chan) * cols
-        for r in range(rows):
-            out_ref[r, pl.ds(place, cols)] = (
-                piece[r] if piece.ndim == 4 else piece[r * cols : (r + 1) * cols]
-            )
-
-    for d in range(chan):
-        if not wrapped or d not in (1, chan - 1):
-            put(d, pieces[d])
-    if wrapped:
-        edge = pieces[chan]
-        for d, at in ((1, 0), (chan - 1, chan - 1)):
-            pl.when(me == at)(functools.partial(put, d, edge))
-            pl.when(me != at)(functools.partial(put, d, pieces[d]))
-
-
-def fill_padded(padded, own, other):
+    for d, piece in enumerate(pieces):
+        out_ref[:, pl.ds(lax.rem(me - d + chan, chan) * cols, cols)] = piece[...]
+
+
+def clear_rim(padded):
     rows_all, cols_all, steps, channels = padded.shape
     zero_row = jnp.zeros((1, cols_all, steps, channels), padded.dtype)
     padded[0:1] = zero_row
@@ -170,10 +166,28 @@
     for r in range(1, rows_all - 1):
         for c in (0, cols_all - 1):
             padded[r, c] = jnp.zeros((steps, channels), padded.dtype)
-    rows = own.shape[0]
+
+
+def fill_padded(padded, own, other):
+    clear_rim(padded)
+    rows, cols = own.shape[0], own.shape[1]
     bottom = lax.axis_index("space")
     for half, top in ((own, bottom * rows), (other, (1 - bottom) * rows)):
-        padded[pl.ds(1 + top, rows), 1 : cols_all - 1] = half[...]
+        padded[pl.ds(1 + top, rows), 1 : 1 + cols] = half[...]
+
+
+def fill_from_pieces(padded, rows, cols, pieces, side):
+    clear_rim(padded)
+    chan, cells = len(pieces), rows * cols
+    me = lax.axis_index("chan")
+    bottom = lax.axis_index("space")
+    for d, piece in enumerate(pieces):
+        place = 1 + lax.rem(me - d + chan, chan) * cols
+        for r in range(rows):
+            near = piece[r] if d == 0 else piece[r * cols : (r + 1) * cols]
+            padded[1 + bottom * rows + r, pl.ds(place, cols)] = near
+            at = d * cells + r * cols
+            padded[1 + (1 - bottom) * rows + r, pl.ds(place, cols)] = side[at : at + cols]
 
 
 def own_window(gp_ref, slope_ref, w_ref, tw_ref, hg_ref, frames, rows, cols):
@@ -195,9 +209,16 @@
     send_on(out_ref, own, conv, cot_ref)
 
 
-def tile_kernel(share, x_ref, other_ref, w_ref, after_ref, act_ref, xt_ref, slope_ref, xp_ref):
-    rows, width, steps, channels = x_ref.shape
-    fill_padded(xp_ref, x_ref, other_ref)
+def tile_kernel(chan, *refs):
+    pieces, (side, w_ref), (act_ref, xt_ref, slope_ref, xp_ref) = (
+        refs[:chan],
+        refs[chan : chan + 2],
+        refs[-4:],
+    )
+    rows, cols, steps, channels = pieces[0].shape
+    width = chan * cols
+    share = channels // chan
+    fill_from_pieces(xp_ref, rows, cols, pieces, side)
     span = width * steps
     turn = lax.rem(channels - lax.axis_index("chan") * share, channels)
     for i in range(2 * rows):
@@ -309,33 +330,32 @@
         places=[VM, VM, pl.ANY],
     )
 
-    def along(message, by):
-        return lax.ppermute(
-            message, "chan", [(c, c + by) for c in range(chan) if 0 <= c + by < chan]
-        )
-
-    from_left = along(to_right, 1)
-    from_right = along(to_left, -1)
-    pieces = [x_own, from_left]
-    for d in range(2, chan - 1):
-        pieces.append(lax.ppermute(x_own, "chan", [(i, (i + d) % chan) for i in range(chan)]))
-    pieces.append(from_right)
-    pieces.append(lax.ppermute(x_own, "chan", [(0, chan - 1), (chan - 1, 0)]))
+    def turned(message, by):
+        return lax.ppermute(message, "chan", [(i, (i + by) % chan) for i in range(chan)])
+
+    x_flat = x_own.reshape((rows * cols,) + cell)
+    pieces = [
+        x_own,
+        turned(to_right, 1),
+        *[turned(x_flat, d) for d in range(2, chan - 1)],
+        turned(to_left, chan - 1),
+    ]
+    swap = [(0, 1), (1, 0)]
     to_side = call(
         side_kernel,
-        bf16(2 * (cols + 4) + cols + 2),
+        bf16(chan * rows * cols + cols + 2),
         [],
         16,
         1_000_000,
         1_000_000,
-        x_own, cot_own, from_left, from_right, pick,
-        places=[VM] * 4 + [pl.ANY],
-    )
-    from_side = lax.ppermute(to_side, "space", [(0, 1), (1, 0)])
-
-    def gathered(wrapped, parts, after=()):
+        *pieces, cot_own, pick,
+        places=[VM] * (chan + 1) + [pl.ANY],
+    )
+    from_side = lax.ppermute(to_side, "space", swap)
+
+    def gathered(parts, after=()):
         half = call(
-            functools.partial(collect_kernel, wrapped, len(after)),
+            functools.partial(collect_kernel, len(after)),
             bf16(rows, width),
             [],
             16,
@@ -345,7 +365,7 @@
             *after,
             places=[VM] * len(parts) + [pl.ANY] * len(after),
         )
-        return half, lax.ppermute(half, "space", [(0, 1), (1, 0)])
+        return half, lax.ppermute(half, "space", swap)
 
     slope_w, payload = call(
         functools.partial(first_kernel, frames),
@@ -358,7 +378,7 @@
         20,
         2 * win * 18 * channels * channels,
         4_000_000,
-        x_own, cot_own, from_left, from_right, from_side, w, tw,
+        x_own, cot_own, pieces[1], pieces[-1], from_side, w, tw,
     )
 
     padded = pltpu.VMEM((height + 2, width + 2) + cell, BF16)
@@ -383,9 +403,9 @@
             ]
             arrived.append(lax.ppermute(payload, ("chan", "pipe"), pairs))
         if not tick:
-            x_all = gathered(1, pieces, (payload,))
+            operands = [*pieces, from_side, w]
             act_t, x_t, slope_s = call(
-                functools.partial(tile_kernel, share),
+                functools.partial(tile_kernel, chan),
                 (
                     jax.ShapeDtypeStruct((channels, count), BF16),
                     jax.ShapeDtypeStruct((channels, count), BF16),
@@ -395,12 +415,11 @@
                 large,
                 2 * count * 9 * channels * channels,
                 6_000_000,
-                *x_all,
-                w,
+                *operands,
                 arrived[0],
-                places=[VM, VM, VM, pl.ANY],
+                places=[VM] * len(operands) + [pl.ANY],
             )
-        g_all = gathered(0, arrived, () if tick else (slope_s,))
+        g_all = gathered(arrived, () if tick else (slope_s,))
     grads, space_grad, time_grad = call(
         functools.partial(final_kernel, frames),
         (

time: 53.2 us -> 47.6 us (0.89)
  starting transfers between devices: 14.6 us -> 10.9 us
  waiting for transfers between devices: 23.4 us -> 21.6 us
    ppermute x7 -> x5, starting transfers between devices: 10 us -> 6.28 us  [the longest x3 6.11 us: turned(): lax.ppermute(message, 'chan', [(i, (i + by) % chan) for i in range(chan)])]
    ppermute x7 -> x5, waiting for transfers between devices: 15.3 us -> 13.8 us  [the longest x3 9.94 us: turned(): lax.ppermute(message, 'chan', [(i, (i + by) % chan) for i in range(chan)])]
    pallas_call x8 -> x7, Pallas kernels: 10.7 us -> 10.8 us  [call(): pl.pallas_call(kernel, out_shape=outs, in_specs=[pl.BlockSpec(memory_spac...]
  transfers between devices with their start and end apart: 11 -> 9, of which waited for: 6 -> 5; matrix products, arithmetic and copies ran while one was open for 0% -> 0% of each run, Pallas kernels for 10% -> 6%
where the time goes in v5:
time: 47.6 us; the launch traced here: 47.4 us
  waiting for transfers between devices  21.6 us (45%)
  starting transfers between devices  10.9 us (23%)
  Pallas kernels  10.8 us (23%)
  local copies, waits for them, and re-layouts  2.27 us (5%)
  other arithmetic  1.16 us (2%)
  between operations  0.68 us (1%)
    pallas_call x7, Pallas kernels, call(): pl.pallas_call(kernel, out_shape=outs, in_specs=[pl.BlockSpec(memory_spac...  10.8 us
    ppermute x3, waiting for transfers between devices, turned(): lax.ppermute(message, 'chan', [(i, (i + by) % chan) for i in range(chan)])  9.94 us
    ppermute x4, waiting for transfers between devices, per_device(): arrived.append(lax.ppermute(payload, ('chan', 'pipe'), pairs))  7.78 us
    ppermute x3, starting transfers between devices, turned(): lax.ppermute(message, 'chan', [(i, (i + by) % chan) for i in range(chan)])  6.11 us
    ppermute x4, starting transfers between devices, per_device(): arrived.append(lax.ppermute(payload, ('chan', 'pipe'), pairs))  4.66 us
    unnamed x4, local copies, waits for them, and re-layouts  2.27 us
    ppermute x1, waiting for transfers between devices, per_device(): from_side = lax.ppermute(to_side, 'space', swap)  1.96 us
    ppermute x1, waiting for transfers between devices, gathered(): return (half, lax.ppermute(half, 'space', swap))  1.89 us
  transfers between devices with their start and end apart: 9, of which 5 were waited for; matrix products, arithmetic and copies ran while one was open for 0% of the time, Pallas kernels for 6%

profile of v5, /device:TPU:0, one launch (start us, length us, event | category | flops | bytes accessed | tf_op | source)
XLA Modules:
  0.0 47.4 jit_solution(2596551022482457363)
XLA Ops:
  0.6 1.2 %pad_maximum_fusion.both_ref = bf16[2,2,8,4,4,256]{5,4,3,2,1,0:T(4,128)(2,1)S(1)} fusion(bf16[1,2,8,4,4,256]{5,4,3,2,1,0:T(4,128)(2,1)} %bitcast.14, bf16[1,2,8,4,4,256]{5,4,3,2,1,0:T(4,128)(2,1)} %param.4), kind=kLoop, calls=%fused_computation | loop fusion | flops 131072 | bytes 524288 | tf_op jit(solution)/shard_map/stack | solution.py:314
  1.8 0.1 shard_map.67
  1.9 3.1 %collective-permute-start = (bf16[20,16,256]{2,1,0:T(8,128)(2,1)S(1)}, bf16[20,16,256]{2,1,0:T(8,128)(2,1)S(1)}, u32[]{:S(2)}, u32[]{:S(2)}) collective-permute-start(bf16[20,16,256]{2,1,0:T(8,128)(2,1)S(1)} %get-tuple-element.20), channel_id=1, source_target_pairs={{0,4},{4,8},{8,12},{12,0},{1,5},{5,9},{9,13},{13,1},{2,6},{6,10},{... | collective-permute-start | bytes 491528 | tf_op jit(solution)/shard_map/ppermute | solution.py:334
  5.0 2.1 %collective-permute-start.1 = (bf16[20,16,256]{2,1,0:T(8,128)(2,1)S(1)}, bf16[20,16,256]{2,1,0:T(8,128)(2,1)S(1)}, u32[]{:S(2)}, u32[]{:S(2)}) collective-permute-start(bf16[20,16,256]{2,1,0:T(8,128)(2,1)S(1)} %get-tuple-element.21), channel_id=1, source_target_pairs={{0,12},{4,0},{8,4},{12,8},{1,13},{5,1},{9,5},{13,9},{2,14},{6,2},{... | collective-permute-start | bytes 491528 | tf_op jit(solution)/shard_map/ppermute | solution.py:334
  7.1 0.9 %collective-permute-start.2 = (bf16[16,16,256]{2,1,0:T(8,128)(2,1)S(1)}, bf16[16,16,256]{2,1,0:T(8,128)(2,1)S(1)}, u32[]{:S(2)}, u32[]{:S(2)}) collective-permute-start(bf16[16,16,256]{2,1,0:T(8,128)(2,1)S(1)} %bitcast.12), channel_id=1, source_target_pairs={{0,8},{4,12},{8,0},{12,4},{1,9},{5,13},{9,1},{13,5},{2,10},{6,14},... | collective-permute-start | bytes 393224 | tf_op jit(solution)/shard_map/ppermute | solution.py:334
  8.0 0.0 copy-start
  8.0 1.3 %copy-done = bf16[1,3,3,256,256]{4,3,2,1,0:T(8,128)(2,1)S(1)} copy-done((bf16[1,3,3,256,256]{4,3,2,1,0:T(8,128)(2,1)S(1)}, bf16[1,3,3,256,256]{4,3,2,1,0:T(8,128)(2,1)}, u32[]{:S(2)}) %copy-start) | copy-done | bytes 1179672
  9.3 0.0 copy-start.1
  9.3 1.0 %copy-done.1 = bf16[1,3,256,256]{3,2,1,0:T(8,128)(2,1)S(1)} copy-done((bf16[1,3,256,256]{3,2,1,0:T(8,128)(2,1)S(1)}, bf16[1,3,256,256]{3,2,1,0:T(8,128)(2,1)}, u32[]{:S(2)}) %copy-start.1) | copy-done | bytes 393240
  10.3 0.1 shard_map.68
  10.4 9.9 %collective-permute-done.2.refs_2_ = bf16[16,16,256]{2,1,0:T(8,128)(2,1)S(1)} collective-permute-done((bf16[16,16,256]{2,1,0:T(8,128)(2,1)S(1)}, bf16[16,16,256]{2,1,0:T(8,128)(2,1)S(1)}, u32[]{:S(2)}, u32[]{:S(2)}) %collective-permute-start.2) | collective-permute-done | bytes 131104 | tf_op jit(solution)/shard_map/ppermute | solution.py:334
  20.3 0.0 collective-permute-done.refs_1_.l_ref
  20.3 0.0 collective-permute-done.1.refs_3_.r_ref
  20.4 0.1 collective-permute-start.3
  20.5 2.0 %collective-permute-done.3.side_ref.refs_4_ = bf16[70,16,256]{2,1,0:T(8,128)(2,1)S(1)} collective-permute-done((bf16[70,16,256]{2,1,0:T(8,128)(2,1)S(1)}, bf16[70,16,256]{2,1,0:T(8,128)(2,1)S(1)}, u32[]{:S(2)}, u32[]{:S(2)}) %collective-permute-start.3) | collective-permute-done | bytes 573472 | tf_op jit(solution)/shard_map/ppermute | solution.py:354
  22.4 2.1 %shard_map.70 = (f32[576,256]{1,0:T(8,128)S(1)}, bf16[4,4,16,256]{3,2,1,0:T(8,128)(2,1)S(1)}) custom-call(bf16[4,4,16,256]{3,2,1,0:T(8,128)(2,1)S(1)} %get-tuple-element.18.after_ref.refs_0_.x_ref, bf16[4,4,16,256]{3,2,1,0:T(8,128)(2,1)S(1)} %get-tuple-element.19.refs_4_.cot_ref, bf16[20,16,256]{2,1,0:T(8,128)(2,1)S(1)} %collective-permute-done.refs_1_.l_ref, ...), custom_call_target="tpu_custom_call" | custom-call | flops 1358954496 | bytes 4000000 | tf_op jit(solution)/shard_map/pallas_call | solution.py:282
  24.6 1.6 %collective-permute-start.4 = (bf16[4,4,16,256]{3,2,1,0:T(8,128)(2,1)S(1)}, bf16[4,4,16,256]{3,2,1,0:T(8,128)(2,1)S(1)}, u32[]{:S(2)}, u32[]{:S(2)}) collective-permute-start(bf16[4,4,16,256]{3,2,1,0:T(8,128)(2,1)S(1)} %get-tuple-element.25), channel_id=1, source_target_pairs={{0,2},{4,6},{8,10},{12,14},{2,0},{6,4},{10,8},{14,12},{1,3},{5,7},... | collective-permute-start | bytes 393224 | tf_op jit(solution)/shard_map/ppermute | solution.py:404
  26.1 1.6 %collective-permute-start.7 = (bf16[4,4,16,256]{3,2,1,0:T(8,128)(2,1)S(1)}, bf16[4,4,16,256]{3,2,1,0:T(8,128)(2,1)S(1)}, u32[]{:S(2)}, u32[]{:S(2)}) collective-permute-start(bf16[4,4,16,256]{3,2,1,0:T(8,128)(2,1)S(1)} %get-tuple-element.25), channel_id=1, source_target_pairs={{0,14},{4,2},{8,6},{12,10},{2,12},{6,0},{10,4},{14,8},{1,15},{5,3}... | collective-permute-start | bytes 393224 | tf_op jit(solution)/shard_map/ppermute | solution.py:404
  27.7 0.0 collective-permute-start.6
  27.7 1.5 %collective-permute-start.5 = (bf16[4,4,16,256]{3,2,1,0:T(8,128)(2,1)S(1)}, bf16[4,4,16,256]{3,2,1,0:T(8,128)(2,1)S(1)}, u32[]{:S(2)}, u32[]{:S(2)}) collective-permute-start(bf16[4,4,16,256]{3,2,1,0:T(8,128)(2,1)S(1)} %get-tuple-element.25), channel_id=1, source_target_pairs={{0,6},{4,10},{8,14},{12,2},{2,4},{6,8},{10,12},{14,0},{1,7},{5,11}... | collective-permute-start | bytes 393224 | tf_op jit(solution)/shard_map/ppermute | solution.py:404
  29.2 3.9 %collective-permute-done.4.refs_6_.refs_0_ = bf16[4,4,16,256]{3,2,1,0:T(8,128)(2,1)S(1)} collective-permute-done((bf16[4,4,16,256]{3,2,1,0:T(8,128)(2,1)S(1)}, bf16[4,4,16,256]{3,2,1,0:T(8,128)(2,1)S(1)}, u32[]{:S(2)}, u32[]{:S(2)}) %collective-permute-start.4) | collective-permute-done | bytes 131104 | tf_op jit(solution)/shard_map/ppermute | solution.py:404
  33.2 2.9 %shard_map.71 = (bf16[256,2048]{1,0:T(8,128)(2,1)S(1)}, bf16[256,2048]{1,0:T(8,128)(2,1)S(1)}, f32[2048,64]{1,0:T(8,128)S(1)}) custom-call(bf16[4,4,16,256]{3,2,1,0:T(8,128)(2,1)S(1)} %get-tuple-element.18.after_ref.refs_0_.x_ref, bf16[20,16,256]{2,1,0:T(8,128)(2,1)S(1)} %collective-permute-done.refs_1_.l_ref, ...), custom_call_target="tpu_custom_call" | custom-call | flops 2415919104 | bytes 6000000 | tf_op jit(solution)/shard_map/pallas_call | solution.py:282
  36.1 0.0 collective-permute-done.7.refs_3_
  36.1 3.8 %collective-permute-done.6.refs_2_ = bf16[4,4,16,256]{3,2,1,0:T(8,128)(2,1)S(1)} collective-permute-done((bf16[4,4,16,256]{3,2,1,0:T(8,128)(2,1)S(1)}, bf16[4,4,16,256]{3,2,1,0:T(8,128)(2,1)S(1)}, u32[]{:S(2)}, u32[]{:S(2)}) %collective-permute-start.6) | collective-permute-done | bytes 131104 | tf_op jit(solution)/shard_map/ppermute | solution.py:404
  40.0 0.0 collective-permute-done.5.refs_1_
  40.0 0.1 collective-permute-start.8
  40.1 1.9 %collective-permute-done.8.other_ref = bf16[4,16,16,256]{3,2,1,0:T(8,128)(2,1)S(1)} collective-permute-done((bf16[4,16,16,256]{3,2,1,0:T(8,128)(2,1)S(1)}, bf16[4,16,16,256]{3,2,1,0:T(8,128)(2,1)S(1)}, u32[]{:S(2)}, u32[]{:S(2)}) %collective-permute-start.8) | collective-permute-done | bytes 524320 | tf_op jit(solution)/shard_map/ppermute | solution.py:368
  42.0 5.4 %shard_map.73 = (bf16[2,8,4,4,256]{4,3,2,1,0:T(4,128)(2,1)}, f32[9,64,256]{2,1,0:T(8,128)}, f32[3,64,256]{2,1,0:T(8,128)}) custom-call(bf16[4,16,16,256]{3,2,1,0:T(8,128)(2,1)S(1)} %shard_map.72.g_ref, bf16[4,16,16,256]{3,2,1,0:T(8,128)(2,1)S(1)} %collective-permute-done.8.other_ref, f32[576,256]{1,0:T(8,128)S(1)} %get-tuple-element.27.slope_w_ref, ...), custom_call_target="tpu_custom_call" | custom-call | flops 1358954496 | bytes 8000000 | tf_op jit(solution)/shard_map/pallas_call | solution.py:282
  (2 shorter events, 0.1 us)
Async XLA Ops:
  1.9 18.4 %collective-permute-start = (bf16[20,16,256]{2,1,0:T(8,128)(2,1)S(1)}, bf16[20,16,256]{2,1,0:T(8,128)(2,1)S(1)}, u32[]{:S(2)}, u32[]{:S(2)}) collective-permute-start(bf16[20,16,256]{2,1,0:T(8,128)(2,1)S(1)} %get-tuple-element.20), channel_id=1, source_target_pairs={{0,4},{4,8},{8,12},{12,0},{1,5},{5,9},{9,13},{13,1},{2,6},{6,10},{... | collective-permute-start | bytes 491528 | tf_op jit(solution)/shard_map/ppermute | solution.py:334
  5.0 15.4 %collective-permute-start.1 = (bf16[20,16,256]{2,1,0:T(8,128)(2,1)S(1)}, bf16[20,16,256]{2,1,0:T(8,128)(2,1)S(1)}, u32[]{:S(2)}, u32[]{:S(2)}) collective-permute-start(bf16[20,16,256]{2,1,0:T(8,128)(2,1)S(1)} %get-tuple-element.21), channel_id=1, source_target_pairs={{0,12},{4,0},{8,4},{12,8},{1,13},{5,1},{9,5},{13,9},{2,14},{6,2},{... | collective-permute-start | bytes 491528 | tf_op jit(solution)/shard_map/ppermute | solution.py:334
  7.1 13.3 %collective-permute-start.2 = (bf16[16,16,256]{2,1,0:T(8,128)(2,1)S(1)}, bf16[16,16,256]{2,1,0:T(8,128)(2,1)S(1)}, u32[]{:S(2)}, u32[]{:S(2)}) collective-permute-start(bf16[16,16,256]{2,1,0:T(8,128)(2,1)S(1)} %bitcast.12), channel_id=1, source_target_pairs={{0,8},{4,12},{8,0},{12,4},{1,9},{5,13},{9,1},{13,5},{2,10},{6,14},... | collective-permute-start | bytes 393224 | tf_op jit(solution)/shard_map/ppermute | solution.py:334
  8.0 1.3 %copy-start = (bf16[1,3,3,256,256]{4,3,2,1,0:T(8,128)(2,1)S(1)}, bf16[1,3,3,256,256]{4,3,2,1,0:T(8,128)(2,1)}, u32[]{:S(2)}) copy-start(bf16[1,3,3,256,256]{4,3,2,1,0:T(8,128)(2,1)} %param.6) | copy-start | bytes 3538948
  9.3 1.0 %copy-start.1 = (bf16[1,3,256,256]{3,2,1,0:T(8,128)(2,1)S(1)}, bf16[1,3,256,256]{3,2,1,0:T(8,128)(2,1)}, u32[]{:S(2)}) copy-start(bf16[1,3,256,256]{3,2,1,0:T(8,128)(2,1)} %param.7) | copy-start | bytes 1179652
  20.4 2.0 %collective-permute-start.3 = (bf16[70,16,256]{2,1,0:T(8,128)(2,1)S(1)}, bf16[70,16,256]{2,1,0:T(8,128)(2,1)S(1)}, u32[]{:S(2)}, u32[]{:S(2)}) collective-permute-start(bf16[70,16,256]{2,1,0:T(8,128)(2,1)S(1)} %shard_map.69), channel_id=1, source_target_pairs={{0,1},{1,0},{2,3},{3,2},{4,5},{5,4},{6,7},{7,6},{8,9},{9,8},{10,11... | collective-permute-start | bytes 1720328 | tf_op jit(solution)/shard_map/ppermute | solution.py:354
  24.6 8.6 %collective-permute-start.4 = (bf16[4,4,16,256]{3,2,1,0:T(8,128)(2,1)S(1)}, bf16[4,4,16,256]{3,2,1,0:T(8,128)(2,1)S(1)}, u32[]{:S(2)}, u32[]{:S(2)}) collective-permute-start(bf16[4,4,16,256]{3,2,1,0:T(8,128)(2,1)S(1)} %get-tuple-element.25), channel_id=1, source_target_pairs={{0,2},{4,6},{8,10},{12,14},{2,0},{6,4},{10,8},{14,12},{1,3},{5,7},... | collective-permute-start | bytes 393224 | tf_op jit(solution)/shard_map/ppermute | solution.py:404
  26.1 10.0 %collective-permute-start.7 = (bf16[4,4,16,256]{3,2,1,0:T(8,128)(2,1)S(1)}, bf16[4,4,16,256]{3,2,1,0:T(8,128)(2,1)S(1)}, u32[]{:S(2)}, u32[]{:S(2)}) collective-permute-start(bf16[4,4,16,256]{3,2,1,0:T(8,128)(2,1)S(1)} %get-tuple-element.25), channel_id=1, source_target_pairs={{0,14},{4,2},{8,6},{12,10},{2,12},{6,0},{10,4},{14,8},{1,15},{5,3}... | collective-permute-start | bytes 393224 | tf_op jit(solution)/shard_map/ppermute | solution.py:404
  27.7 12.2 %collective-permute-start.6 = (bf16[4,4,16,256]{3,2,1,0:T(8,128)(2,1)S(1)}, bf16[4,4,16,256]{3,2,1,0:T(8,128)(2,1)S(1)}, u32[]{:S(2)}, u32[]{:S(2)}) collective-permute-start(bf16[4,4,16,256]{3,2,1,0:T(8,128)(2,1)S(1)} %get-tuple-element.25), channel_id=1, source_target_pairs={{0,10},{4,14},{8,2},{12,6},{2,8},{6,12},{10,0},{14,4},{1,11},{5,15... | collective-permute-start | bytes 393224 | tf_op jit(solution)/shard_map/ppermute | solution.py:404
  27.7 12.2 %collective-permute-start.5 = (bf16[4,4,16,256]{3,2,1,0:T(8,128)(2,1)S(1)}, bf16[4,4,16,256]{3,2,1,0:T(8,128)(2,1)S(1)}, u32[]{:S(2)}, u32[]{:S(2)}) collective-permute-start(bf16[4,4,16,256]{3,2,1,0:T(8,128)(2,1)S(1)} %get-tuple-element.25), channel_id=1, source_target_pairs={{0,6},{4,10},{8,14},{12,2},{2,4},{6,8},{10,12},{14,0},{1,7},{5,11}... | collective-permute-start | bytes 393224 | tf_op jit(solution)/shard_map/ppermute | solution.py:404
  40.0 2.0 %collective-permute-start.8 = (bf16[4,16,16,256]{3,2,1,0:T(8,128)(2,1)S(1)}, bf16[4,16,16,256]{3,2,1,0:T(8,128)(2,1)S(1)}, u32[]{:S(2)}, u32[]{:S(2)}) collective-permute-start(bf16[4,16,16,256]{3,2,1,0:T(8,128)(2,1)S(1)} %shard_map.72.g_ref), channel_id=1, source_target_pairs={{0,1},{1,0},{2,3},{3,2},{4,5},{5,4},{6,7},{7,6},{8,9},{9,8},{10,11... | collective-permute-start | bytes 1572872 | tf_op jit(solution)/shard_map/ppermute | solution.py:368

commit v6 on v5

--- a/solution.py
+++ b/solution.py
@@ -57,18 +57,35 @@
     pick_ref[3 * share :, :] = jnp.where(chosen, 1.0, 0.0).astype(BF16)
 
 
-def side_kernel(*refs):
-    pieces, (cot_ref, _, side_ref) = refs[:-3], refs[-3:]
-    rows, cols, steps, channels = pieces[0].shape
+def side_kernel(x_ref, l_ref, r_ref, cot_ref, after_ref, *side_refs):
+    rows, cols = x_ref.shape[:2]
     cells = rows * cols
-    for d, piece in enumerate(pieces):
-        block = piece[...].reshape(cells, steps, channels) if d == 0 else piece[:cells]
-        side_ref[d * cells : (d + 1) * cells] = block
-    row = (1 - lax.axis_index("space")) * (rows - 1)
-    base = len(pieces) * cells
-    side_ref[base] = pieces[1][cells + row]
-    side_ref[base + 1 : base + 1 + cols] = cot_ref[row]
-    side_ref[base + 1 + cols] = pieces[-1][cells + row]
+    bottom = lax.axis_index("space")
+    out = [side.at[i] for side in side_refs for i in range(side.shape[0])]
+    for i in range(2):
+        at = ((1 - bottom) * (rows - 2) + i) * cols
+        line = out[i * (cols + 4) : (i + 1) * (cols + 4)]
+        for c in range(cols):
+            line[2 + c][...] = x_ref[(1 - bottom) * (rows - 2) + i, c]
+        for c in range(2):
+            line[c][...] = l_ref[at + cols - 2 + c]
+            line[2 + cols + c][...] = r_ref[at + c]
+    row = (1 - bottom) * (rows - 1)
+    line = out[2 * (cols + 4) :]
+    line[0][...] = l_ref[cells + row]
+    line[1 + cols][...] = r_ref[cells + row]
+    for c in range(cols):
+        line[1 + c][...] = cot_ref[row, c]
+
+
+def late_kernel(payload_ref, x_ref, *refs):
+    pieces, (out_ref, late_ref) = refs[:-2], refs[-2:]
+    out_ref[...] = payload_ref[...]
+    rows, cols, steps, channels = x_ref.shape
+    cells = rows * cols
+    late_ref[:cells] = x_ref[...].reshape(cells, steps, channels)
+    for n, piece in enumerate(pieces):
+        late_ref[(n + 1) * cells : (n + 2) * cells] = piece[:cells]
 
 
 def conv_back(hg_ref, w_ref, rows, cols):
@@ -102,12 +119,12 @@
 
 
 def first_kernel(
-    frames, x_ref, cot_ref, l_ref, r_ref, side_ref, w_ref, tw_ref,
+    frames, x_ref, cot_ref, l_ref, r_ref, side_ref, side2_ref, w_ref, tw_ref,
     slope_ref, out_ref, xw_ref, cw_ref, hg_ref,
 ):
     rows, cols, steps, channels = x_ref.shape
     cells = rows * cols
-    chan = side_ref.shape[0] // cells
+    chan = lax.axis_size("chan")
     bottom = lax.axis_index("space")
     xw_ref[2 : 2 + rows, 2 : 2 + cols] = x_ref[...]
     cw_ref[1 : 1 + rows, 1 : 1 + cols] = cot_ref[...]
@@ -118,15 +135,15 @@
         cw_ref[1 + r, cols + 1] = r_ref[cells + r]
     near = (1 - bottom) * (rows + 2)
     far = bottom * (rows + 2)
+    line = [side.at[i] for side in (side_ref, side2_ref) for i in range(side.shape[0])]
     for i in range(2):
-        at = (bottom * (rows - 2) + i) * cols
-        xw_ref[near + i, 2 : 2 + cols] = side_ref[pl.ds(at, cols)]
-        xw_ref[near + i, 0:2] = side_ref[pl.ds(cells + at + cols - 2, 2)]
-        xw_ref[near + i, cols + 2 : cols + 4] = side_ref[pl.ds((chan - 1) * cells + at, 2)]
+        for c in range(cols + 4):
+            xw_ref[near + i, c] = line[i * (cols + 4) + c][...]
         xw_ref[far + i] = jnp.zeros(xw_ref.shape[1:], BF16)
     near = (1 - bottom) * (rows + 1)
     far = bottom * (rows + 1)
-    cw_ref[near] = side_ref[chan * cells :]
+    for c in range(cols + 2):
+        cw_ref[near, c] = line[2 * (cols + 4) + c][...]
     cw_ref[far] = jnp.zeros(cw_ref.shape[1:], BF16)
     me = lax.axis_index("chan")
     for end, c in ((0, 0), (chan - 1, cols + 2)):
@@ -176,7 +193,7 @@
         padded[pl.ds(1 + top, rows), 1 : 1 + cols] = half[...]
 
 
-def fill_from_pieces(padded, rows, cols, pieces, side):
+def fill_from_pieces(padded, rows, cols, pieces, late):
     clear_rim(padded)
     chan, cells = len(pieces), rows * cols
     me = lax.axis_index("chan")
@@ -187,7 +204,7 @@
             near = piece[r] if d == 0 else piece[r * cols : (r + 1) * cols]
             padded[1 + bottom * rows + r, pl.ds(place, cols)] = near
             at = d * cells + r * cols
-            padded[1 + (1 - bottom) * rows + r, pl.ds(place, cols)] = side[at : at + cols]
+            padded[1 + (1 - bottom) * rows + r, pl.ds(place, cols)] = late[at : at + cols]
 
 
 def own_window(gp_ref, slope_ref, w_ref, tw_ref, hg_ref, frames, rows, cols):
@@ -210,15 +227,12 @@
 
 
 def tile_kernel(chan, *refs):
-    pieces, (side, w_ref), (act_ref, xt_ref, slope_ref, xp_ref) = (
-        refs[:chan],
-        refs[chan : chan + 2],
-        refs[-4:],
-    )
+    pieces, (late, w_ref) = refs[:chan], refs[chan : chan + 2]
+    act_ref, xt_ref, slope_ref, xp_ref = refs[-4:]
     rows, cols, steps, channels = pieces[0].shape
     width = chan * cols
     share = channels // chan
-    fill_from_pieces(xp_ref, rows, cols, pieces, side)
+    fill_from_pieces(xp_ref, rows, cols, pieces, late)
     span = width * steps
     turn = lax.rem(channels - lax.axis_index("chan") * share, channels)
     for i in range(2 * rows):
@@ -341,17 +355,18 @@
         turned(to_left, chan - 1),
     ]
     swap = [(0, 1), (1, 0)]
+    half_side = (2 * (cols + 4) + cols + 2) // 2
     to_side = call(
         side_kernel,
-        bf16(chan * rows * cols + cols + 2),
+        (bf16(half_side), bf16(2 * (cols + 4) + cols + 2 - half_side)),
         [],
         16,
         1_000_000,
         1_000_000,
-        *pieces, cot_own, pick,
-        places=[VM] * (chan + 1) + [pl.ANY],
-    )
-    from_side = lax.ppermute(to_side, "space", swap)
+        x_own, pieces[1], pieces[-1], cot_own, pick,
+        places=[VM] * 4 + [pl.ANY],
+    )
+    from_side = [lax.ppermute(part, "space", swap) for part in to_side]
 
     def gathered(parts, after=()):
         half = call(
@@ -376,9 +391,9 @@
             pltpu.VMEM((rows + 2, cols + 2) + cell, BF16),
         ],
         20,
-        2 * win * 18 * channels * channels,
-        4_000_000,
-        x_own, cot_own, pieces[1], pieces[-1], from_side, w, tw,
+        1,
+        1,
+        x_own, cot_own, pieces[1], pieces[-1], *from_side, w, tw,
     )
 
     padded = pltpu.VMEM((height + 2, width + 2) + cell, BF16)
@@ -394,6 +409,18 @@
                 4_000_000,
                 *g_all, cot_own, slope_w, w, tw,
             )
+        if not tick:
+            payload, to_late = call(
+                late_kernel,
+                (bf16(rows, cols), bf16(chan * rows * cols)),
+                [],
+                16,
+                1_000_000,
+                1_000_000,
+                payload,
+                *pieces,
+            )
+            from_late = lax.ppermute(to_late, "space", swap)
         arrived = []
         for d in range(chan):
             pairs = [
@@ -403,7 +430,7 @@
             ]
             arrived.append(lax.ppermute(payload, ("chan", "pipe"), pairs))
         if not tick:
-            operands = [*pieces, from_side, w]
+            operands = [*pieces, from_late, w]
             act_t, x_t, slope_s = call(
                 functools.partial(tile_kernel, chan),
                 (

time: 47.6 us -> 44.8 us (0.941)
  waiting for transfers between devices: 21.6 us -> 15.4 us
  starting transfers between devices: 10.9 us -> 14.3 us
    ppermute x3, waiting for transfers between devices: 9.94 us -> 6.24 us  [turned(): lax.ppermute(message, 'chan', [(i, (i + by) % chan) for i in range(chan)])]
    ppermute x4, starting transfers between devices: 4.66 us -> 7.45 us  [per_device(): arrived.append(lax.ppermute(payload, ('chan', 'pipe'), pairs))]
    ppermute x4, waiting for transfers between devices: 7.78 us -> 6.33 us  [per_device(): arrived.append(lax.ppermute(payload, ('chan', 'pipe'), pairs))]
    ppermute x1 -> x3, waiting for transfers between devices: 1.96 us -> 0.94 us  [the longest x2 0.93 us: per_device(): from_side = [lax.ppermute(part, 'space', swap) for part in to_side]]
    ppermute x1 -> x3, starting transfers between devices: 0.08 us -> 0.65 us  [the longest x2 0.57 us: per_device(): from_side = [lax.ppermute(part, 'space', swap) for part in to_side]]
    pallas_call x7 -> x8, Pallas kernels: 10.8 us -> 10.8 us  [call(): pl.pallas_call(kernel, out_shape=outs, in_specs=[pl.BlockSpec(memory_spac...]
  transfers between devices with their start and end apart: 9 -> 11, of which waited for: 5 -> 8; matrix products, arithmetic and copies ran while one was open for 0% -> 0% of each run, Pallas kernels for 6% -> 12%
where the time goes in v6:
time: 44.8 us; the launch traced here: 44.6 us
  waiting for transfers between devices  15.4 us (34%)
  starting transfers between devices  14.3 us (32%)
  Pallas kernels  10.8 us (24%)
  local copies, waits for them, and re-layouts  2.27 us (5%)
  other arithmetic  1.16 us (3%)
  between operations  0.7 us (2%)
    pallas_call x8, Pallas kernels, call(): pl.pallas_call(kernel, out_shape=outs, in_specs=[pl.BlockSpec(memory_spac...  10.8 us
    ppermute x4, starting transfers between devices, per_device(): arrived.append(lax.ppermute(payload, ('chan', 'pipe'), pairs))  7.45 us
    ppermute x4, waiting for transfers between devices, per_device(): arrived.append(lax.ppermute(payload, ('chan', 'pipe'), pairs))  6.33 us
    ppermute x3, waiting for transfers between devices, turned(): lax.ppermute(message, 'chan', [(i, (i + by) % chan) for i in range(chan)])  6.24 us
    ppermute x3, starting transfers between devices, turned(): lax.ppermute(message, 'chan', [(i, (i + by) % chan) for i in range(chan)])  6.11 us
    unnamed x4, local copies, waits for them, and re-layouts  2.27 us
    ppermute x1, waiting for transfers between devices, gathered(): return (half, lax.ppermute(half, 'space', swap))  1.9 us
    another operation x1, other arithmetic, per_device(): jnp.stack([activations[0], cotangent])  1.16 us
  transfers between devices with their start and end apart: 11, of which 8 were waited for; matrix products, arithmetic and copies ran while one was open for 0% of the time, Pallas kernels for 12%

profile of v6, /device:TPU:0, one launch (start us, length us, event | category | flops | bytes accessed | tf_op | source)
XLA Modules:
  0.0 44.6 jit_solution(13098744434187126930)
XLA Ops:
  0.6 1.2 %pad_maximum_fusion.both_ref = bf16[2,2,8,4,4,256]{5,4,3,2,1,0:T(4,128)(2,1)S(1)} fusion(bf16[1,2,8,4,4,256]{5,4,3,2,1,0:T(4,128)(2,1)} %bitcast.14, bf16[1,2,8,4,4,256]{5,4,3,2,1,0:T(4,128)(2,1)} %param.4), kind=kLoop, calls=%fused_computation | loop fusion | flops 131072 | bytes 524288 | tf_op jit(solution)/shard_map/stack | solution.py:328
  1.8 0.1 shard_map.67
  1.9 3.1 %collective-permute-start = (bf16[20,16,256]{2,1,0:T(8,128)(2,1)S(1)}, bf16[20,16,256]{2,1,0:T(8,128)(2,1)S(1)}, u32[]{:S(2)}, u32[]{:S(2)}) collective-permute-start(bf16[20,16,256]{2,1,0:T(8,128)(2,1)S(1)} %get-tuple-element.24), channel_id=1, source_target_pairs={{0,4},{4,8},{8,12},{12,0},{1,5},{5,9},{9,13},{13,1},{2,6},{6,10},{... | collective-permute-start | bytes 491528 | tf_op jit(solution)/shard_map/ppermute | solution.py:348
  5.0 2.1 %collective-permute-start.1 = (bf16[20,16,256]{2,1,0:T(8,128)(2,1)S(1)}, bf16[20,16,256]{2,1,0:T(8,128)(2,1)S(1)}, u32[]{:S(2)}, u32[]{:S(2)}) collective-permute-start(bf16[20,16,256]{2,1,0:T(8,128)(2,1)S(1)} %get-tuple-element.25), channel_id=1, source_target_pairs={{0,12},{4,0},{8,4},{12,8},{1,13},{5,1},{9,5},{13,9},{2,14},{6,2},{... | collective-permute-start | bytes 491528 | tf_op jit(solution)/shard_map/ppermute | solution.py:348
  7.1 0.9 %collective-permute-start.4 = (bf16[16,16,256]{2,1,0:T(8,128)(2,1)S(1)}, bf16[16,16,256]{2,1,0:T(8,128)(2,1)S(1)}, u32[]{:S(2)}, u32[]{:S(2)}) collective-permute-start(bf16[16,16,256]{2,1,0:T(8,128)(2,1)S(1)} %bitcast.11), channel_id=1, source_target_pairs={{0,8},{4,12},{8,0},{12,4},{1,9},{5,13},{9,1},{13,5},{2,10},{6,14},... | collective-permute-start | bytes 393224 | tf_op jit(solution)/shard_map/ppermute | solution.py:348
  8.0 0.0 copy-start
  8.0 1.3 %copy-done = bf16[1,3,3,256,256]{4,3,2,1,0:T(8,128)(2,1)S(1)} copy-done((bf16[1,3,3,256,256]{4,3,2,1,0:T(8,128)(2,1)S(1)}, bf16[1,3,3,256,256]{4,3,2,1,0:T(8,128)(2,1)}, u32[]{:S(2)}) %copy-start) | copy-done | bytes 1179672
  9.3 0.0 copy-start.1
  9.3 1.0 %copy-done.1 = bf16[1,3,256,256]{3,2,1,0:T(8,128)(2,1)S(1)} copy-done((bf16[1,3,256,256]{3,2,1,0:T(8,128)(2,1)S(1)}, bf16[1,3,256,256]{3,2,1,0:T(8,128)(2,1)}, u32[]{:S(2)}) %copy-start.1) | copy-done | bytes 393240
  10.3 0.1 shard_map.68
  10.4 1.7 %collective-permute-done.l_ref.refs_0_.refs_1_ = bf16[20,16,256]{2,1,0:T(8,128)(2,1)S(1)} collective-permute-done((bf16[20,16,256]{2,1,0:T(8,128)(2,1)S(1)}, bf16[20,16,256]{2,1,0:T(8,128)(2,1)S(1)}, u32[]{:S(2)}, u32[]{:S(2)}) %collective-permute-start) | collective-permute-done | bytes 163872 | tf_op jit(solution)/shard_map/ppermute | solution.py:348
  12.1 2.1 %collective-permute-done.1.r_ref.refs_2_.refs_3_ = bf16[20,16,256]{2,1,0:T(8,128)(2,1)S(1)} collective-permute-done((bf16[20,16,256]{2,1,0:T(8,128)(2,1)S(1)}, bf16[20,16,256]{2,1,0:T(8,128)(2,1)S(1)}, u32[]{:S(2)}, u32[]{:S(2)}) %collective-permute-start.1) | collective-permute-done | bytes 163872 | tf_op jit(solution)/shard_map/ppermute | solution.py:348
  14.2 0.1 collective-permute-start.2
  14.2 0.5 %collective-permute-start.3 = (bf16[11,16,256]{2,1,0:T(8,128)(2,1)S(1)}, bf16[11,16,256]{2,1,0:T(8,128)(2,1)S(1)}, u32[]{:S(2)}, u32[]{:S(2)}) collective-permute-start(bf16[11,16,256]{2,1,0:T(8,128)(2,1)S(1)} %get-tuple-element.28), channel_id=1, source_target_pairs={{0,1},{1,0},{2,3},{3,2},{4,5},{5,4},{6,7},{7,6},{8,9},{9,8},{10,11... | collective-permute-start | bytes 270344 | tf_op jit(solution)/shard_map/ppermute | solution.py:369
  14.7 0.8 %collective-permute-done.2.side_ref = bf16[11,16,256]{2,1,0:T(8,128)(2,1)S(1)} collective-permute-done((bf16[11,16,256]{2,1,0:T(8,128)(2,1)S(1)}, bf16[11,16,256]{2,1,0:T(8,128)(2,1)S(1)}, u32[]{:S(2)}, u32[]{:S(2)}) %collective-permute-start.2) | collective-permute-done | bytes 90144 | tf_op jit(solution)/shard_map/ppermute | solution.py:369
  15.5 0.2 collective-permute-done.3.side2_ref
  15.7 2.2 %shard_map.70 = (f32[576,256]{1,0:T(8,128)S(1)}, bf16[4,4,16,256]{3,2,1,0:T(8,128)(2,1)S(1)}) custom-call(bf16[4,4,16,256]{3,2,1,0:T(8,128)(2,1)S(1)} %get-tuple-element.22.after_ref.x_ref.refs_0_, bf16[4,4,16,256]{3,2,1,0:T(8,128)(2,1)S(1)} %get-tuple-element.23.cot_ref, bf16[20,16,256]{2,1,0:T(8,128)(2,1)S(1)} %collective-permute-done.l_ref.refs_0_.refs_1_, ...), custom_call_target="tpu_custom_call" | custom-call | flops 1 | bytes 1 | tf_op jit(solution)/shard_map/pallas_call | solution.py:296
  17.8 2.5 %collective-permute-done.4.refs_1_.refs_2_ = bf16[16,16,256]{2,1,0:T(8,128)(2,1)S(1)} collective-permute-done((bf16[16,16,256]{2,1,0:T(8,128)(2,1)S(1)}, bf16[16,16,256]{2,1,0:T(8,128)(2,1)S(1)}, u32[]{:S(2)}, u32[]{:S(2)}) %collective-permute-start.4) | collective-permute-done | bytes 131104 | tf_op jit(solution)/shard_map/ppermute | solution.py:348
  20.4 0.1 collective-permute-start.9
  20.5 1.6 %collective-permute-start.5 = (bf16[4,4,16,256]{3,2,1,0:T(8,128)(2,1)S(1)}, bf16[4,4,16,256]{3,2,1,0:T(8,128)(2,1)S(1)}, u32[]{:S(2)}, u32[]{:S(2)}) collective-permute-start(bf16[4,4,16,256]{3,2,1,0:T(8,128)(2,1)S(1)} %get-tuple-element.32), channel_id=1, source_target_pairs={{0,2},{4,6},{8,10},{12,14},{2,0},{6,4},{10,8},{14,12},{1,3},{5,7},... | collective-permute-start | bytes 393224 | tf_op jit(solution)/shard_map/ppermute | solution.py:431
  22.0 1.6 %collective-permute-start.8 = (bf16[4,4,16,256]{3,2,1,0:T(8,128)(2,1)S(1)}, bf16[4,4,16,256]{3,2,1,0:T(8,128)(2,1)S(1)}, u32[]{:S(2)}, u32[]{:S(2)}) collective-permute-start(bf16[4,4,16,256]{3,2,1,0:T(8,128)(2,1)S(1)} %get-tuple-element.32), channel_id=1, source_target_pairs={{0,14},{4,2},{8,6},{12,10},{2,12},{6,0},{10,4},{14,8},{1,15},{5,3}... | collective-permute-start | bytes 393224 | tf_op jit(solution)/shard_map/ppermute | solution.py:431
  23.6 1.9 %collective-permute-start.7 = (bf16[4,4,16,256]{3,2,1,0:T(8,128)(2,1)S(1)}, bf16[4,4,16,256]{3,2,1,0:T(8,128)(2,1)S(1)}, u32[]{:S(2)}, u32[]{:S(2)}) collective-permute-start(bf16[4,4,16,256]{3,2,1,0:T(8,128)(2,1)S(1)} %get-tuple-element.32), channel_id=1, source_target_pairs={{0,10},{4,14},{8,2},{12,6},{2,8},{6,12},{10,0},{14,4},{1,11},{5,15... | collective-permute-start | bytes 393224 | tf_op jit(solution)/shard_map/ppermute | solution.py:431
  25.5 2.4 %collective-permute-start.6 = (bf16[4,4,16,256]{3,2,1,0:T(8,128)(2,1)S(1)}, bf16[4,4,16,256]{3,2,1,0:T(8,128)(2,1)S(1)}, u32[]{:S(2)}, u32[]{:S(2)}) collective-permute-start(bf16[4,4,16,256]{3,2,1,0:T(8,128)(2,1)S(1)} %get-tuple-element.32), channel_id=1, source_target_pairs={{0,6},{4,10},{8,14},{12,2},{2,4},{6,8},{10,12},{14,0},{1,7},{5,11}... | collective-permute-start | bytes 393224 | tf_op jit(solution)/shard_map/ppermute | solution.py:431
  27.9 2.5 %collective-permute-done.5.refs_6_.refs_0_ = bf16[4,4,16,256]{3,2,1,0:T(8,128)(2,1)S(1)} collective-permute-done((bf16[4,4,16,256]{3,2,1,0:T(8,128)(2,1)S(1)}, bf16[4,4,16,256]{3,2,1,0:T(8,128)(2,1)S(1)}, u32[]{:S(2)}, u32[]{:S(2)}) %collective-permute-start.5) | collective-permute-done | bytes 131104 | tf_op jit(solution)/shard_map/ppermute | solution.py:431
  30.4 0.0 collective-permute-done.9.refs_4_
  30.4 2.9 %shard_map.72 = (bf16[256,2048]{1,0:T(8,128)(2,1)S(1)}, bf16[256,2048]{1,0:T(8,128)(2,1)S(1)}, f32[2048,64]{1,0:T(8,128)S(1)}) custom-call(bf16[4,4,16,256]{3,2,1,0:T(8,128)(2,1)S(1)} %get-tuple-element.22.after_ref.x_ref.refs_0_, bf16[20,16,256]{2,1,0:T(8,128)(2,1)S(1)} %collective-permute-done.l_ref.refs_0_.refs_1_, ...), custom_call_target="tpu_custom_call" | custom-call | flops 2415919104 | bytes 6000000 | tf_op jit(solution)/shard_map/pallas_call | solution.py:296
  33.4 0.0 collective-permute-done.8.refs_3_
  33.4 3.8 %collective-permute-done.7.refs_2_ = bf16[4,4,16,256]{3,2,1,0:T(8,128)(2,1)S(1)} collective-permute-done((bf16[4,4,16,256]{3,2,1,0:T(8,128)(2,1)S(1)}, bf16[4,4,16,256]{3,2,1,0:T(8,128)(2,1)S(1)}, u32[]{:S(2)}, u32[]{:S(2)}) %collective-permute-start.7) | collective-permute-done | bytes 131104 | tf_op jit(solution)/shard_map/ppermute | solution.py:431
  37.2 0.0 collective-permute-done.6.refs_1_
  37.2 0.1 collective-permute-start.10
  37.3 1.9 %collective-permute-done.10.other_ref = bf16[4,16,16,256]{3,2,1,0:T(8,128)(2,1)S(1)} collective-permute-done((bf16[4,16,16,256]{3,2,1,0:T(8,128)(2,1)S(1)}, bf16[4,16,16,256]{3,2,1,0:T(8,128)(2,1)S(1)}, u32[]{:S(2)}, u32[]{:S(2)}) %collective-permute-start.10) | collective-permute-done | bytes 524320 | tf_op jit(solution)/shard_map/ppermute | solution.py:383
  39.2 5.4 %shard_map.74 = (bf16[2,8,4,4,256]{4,3,2,1,0:T(4,128)(2,1)}, f32[9,64,256]{2,1,0:T(8,128)}, f32[3,64,256]{2,1,0:T(8,128)}) custom-call(bf16[4,16,16,256]{3,2,1,0:T(8,128)(2,1)S(1)} %shard_map.73.g_ref, bf16[4,16,16,256]{3,2,1,0:T(8,128)(2,1)S(1)} %collective-permute-done.10.other_ref, f32[576,256]{1,0:T(8,128)S(1)} %get-tuple-element.35.slope_w_ref, ...), custom_call_target="tpu_custom_call" | custom-call | flops 1358954496 | bytes 8000000 | tf_op jit(solution)/shard_map/pallas_call | solution.py:296
  (3 shorter events, 0.1 us)
Async XLA Ops:
  1.9 10.2 %collective-permute-start = (bf16[20,16,256]{2,1,0:T(8,128)(2,1)S(1)}, bf16[20,16,256]{2,1,0:T(8,128)(2,1)S(1)}, u32[]{:S(2)}, u32[]{:S(2)}) collective-permute-start(bf16[20,16,256]{2,1,0:T(8,128)(2,1)S(1)} %get-tuple-element.24), channel_id=1, source_target_pairs={{0,4},{4,8},{8,12},{12,0},{1,5},{5,9},{9,13},{13,1},{2,6},{6,10},{... | collective-permute-start | bytes 491528 | tf_op jit(solution)/shard_map/ppermute | solution.py:348
  5.0 9.2 %collective-permute-start.1 = (bf16[20,16,256]{2,1,0:T(8,128)(2,1)S(1)}, bf16[20,16,256]{2,1,0:T(8,128)(2,1)S(1)}, u32[]{:S(2)}, u32[]{:S(2)}) collective-permute-start(bf16[20,16,256]{2,1,0:T(8,128)(2,1)S(1)} %get-tuple-element.25), channel_id=1, source_target_pairs={{0,12},{4,0},{8,4},{12,8},{1,13},{5,1},{9,5},{13,9},{2,14},{6,2},{... | collective-permute-start | bytes 491528 | tf_op jit(solution)/shard_map/ppermute | solution.py:348
  7.1 13.3 %collective-permute-start.4 = (bf16[16,16,256]{2,1,0:T(8,128)(2,1)S(1)}, bf16[16,16,256]{2,1,0:T(8,128)(2,1)S(1)}, u32[]{:S(2)}, u32[]{:S(2)}) collective-permute-start(bf16[16,16,256]{2,1,0:T(8,128)(2,1)S(1)} %bitcast.11), channel_id=1, source_target_pairs={{0,8},{4,12},{8,0},{12,4},{1,9},{5,13},{9,1},{13,5},{2,10},{6,14},... | collective-permute-start | bytes 393224 | tf_op jit(solution)/shard_map/ppermute | solution.py:348
  8.0 1.3 %copy-start = (bf16[1,3,3,256,256]{4,3,2,1,0:T(8,128)(2,1)S(1)}, bf16[1,3,3,256,256]{4,3,2,1,0:T(8,128)(2,1)}, u32[]{:S(2)}) copy-start(bf16[1,3,3,256,256]{4,3,2,1,0:T(8,128)(2,1)} %param.6) | copy-start | bytes 3538948
  9.3 1.0 %copy-start.1 = (bf16[1,3,256,256]{3,2,1,0:T(8,128)(2,1)S(1)}, bf16[1,3,256,256]{3,2,1,0:T(8,128)(2,1)}, u32[]{:S(2)}) copy-start(bf16[1,3,256,256]{3,2,1,0:T(8,128)(2,1)} %param.7) | copy-start | bytes 1179652
  14.2 1.4 %collective-permute-start.2 = (bf16[11,16,256]{2,1,0:T(8,128)(2,1)S(1)}, bf16[11,16,256]{2,1,0:T(8,128)(2,1)S(1)}, u32[]{:S(2)}, u32[]{:S(2)}) collective-permute-start(bf16[11,16,256]{2,1,0:T(8,128)(2,1)S(1)} %get-tuple-element.27), channel_id=1, source_target_pairs={{0,1},{1,0},{2,3},{3,2},{4,5},{5,4},{6,7},{7,6},{8,9},{9,8},{10,11... | collective-permute-start | bytes 270344 | tf_op jit(solution)/shard_map/ppermute | solution.py:369
  14.2 1.4 %collective-permute-start.3 = (bf16[11,16,256]{2,1,0:T(8,128)(2,1)S(1)}, bf16[11,16,256]{2,1,0:T(8,128)(2,1)S(1)}, u32[]{:S(2)}, u32[]{:S(2)}) collective-permute-start(bf16[11,16,256]{2,1,0:T(8,128)(2,1)S(1)} %get-tuple-element.28), channel_id=1, source_target_pairs={{0,1},{1,0},{2,3},{3,2},{4,5},{5,4},{6,7},{7,6},{8,9},{9,8},{10,11... | collective-permute-start | bytes 270344 | tf_op jit(solution)/shard_map/ppermute | solution.py:369
  20.4 10.1 %collective-permute-start.9 = (bf16[64,16,256]{2,1,0:T(8,128)(2,1)S(1)}, bf16[64,16,256]{2,1,0:T(8,128)(2,1)S(1)}, u32[]{:S(2)}, u32[]{:S(2)}) collective-permute-start(bf16[64,16,256]{2,1,0:T(8,128)(2,1)S(1)} %get-tuple-element.33), channel_id=1, source_target_pairs={{0,1},{1,0},{2,3},{3,2},{4,5},{5,4},{6,7},{7,6},{8,9},{9,8},{10,11... | collective-permute-start | bytes 1572872 | tf_op jit(solution)/shard_map/ppermute | solution.py:423
  20.5 10.0 %collective-permute-start.5 = (bf16[4,4,16,256]{3,2,1,0:T(8,128)(2,1)S(1)}, bf16[4,4,16,256]{3,2,1,0:T(8,128)(2,1)S(1)}, u32[]{:S(2)}, u32[]{:S(2)}) collective-permute-start(bf16[4,4,16,256]{3,2,1,0:T(8,128)(2,1)S(1)} %get-tuple-element.32), channel_id=1, source_target_pairs={{0,2},{4,6},{8,10},{12,14},{2,0},{6,4},{10,8},{14,12},{1,3},{5,7},... | collective-permute-start | bytes 393224 | tf_op jit(solution)/shard_map/ppermute | solution.py:431
  22.0 11.4 %collective-permute-start.8 = (bf16[4,4,16,256]{3,2,1,0:T(8,128)(2,1)S(1)}, bf16[4,4,16,256]{3,2,1,0:T(8,128)(2,1)S(1)}, u32[]{:S(2)}, u32[]{:S(2)}) collective-permute-start(bf16[4,4,16,256]{3,2,1,0:T(8,128)(2,1)S(1)} %get-tuple-element.32), channel_id=1, source_target_pairs={{0,14},{4,2},{8,6},{12,10},{2,12},{6,0},{10,4},{14,8},{1,15},{5,3}... | collective-permute-start | bytes 393224 | tf_op jit(solution)/shard_map/ppermute | solution.py:431
  23.6 13.6 %collective-permute-start.7 = (bf16[4,4,16,256]{3,2,1,0:T(8,128)(2,1)S(1)}, bf16[4,4,16,256]{3,2,1,0:T(8,128)(2,1)S(1)}, u32[]{:S(2)}, u32[]{:S(2)}) collective-permute-start(bf16[4,4,16,256]{3,2,1,0:T(8,128)(2,1)S(1)} %get-tuple-element.32), channel_id=1, source_target_pairs={{0,10},{4,14},{8,2},{12,6},{2,8},{6,12},{10,0},{14,4},{1,11},{5,15... | collective-permute-start | bytes 393224 | tf_op jit(solution)/shard_map/ppermute | solution.py:431
  25.5 11.7 %collective-permute-start.6 = (bf16[4,4,16,256]{3,2,1,0:T(8,128)(2,1)S(1)}, bf16[4,4,16,256]{3,2,1,0:T(8,128)(2,1)S(1)}, u32[]{:S(2)}, u32[]{:S(2)}) collective-permute-start(bf16[4,4,16,256]{3,2,1,0:T(8,128)(2,1)S(1)} %get-tuple-element.32), channel_id=1, source_target_pairs={{0,6},{4,10},{8,14},{12,2},{2,4},{6,8},{10,12},{14,0},{1,7},{5,11}... | collective-permute-start | bytes 393224 | tf_op jit(solution)/shard_map/ppermute | solution.py:431
  37.2 2.0 %collective-permute-start.10 = (bf16[4,16,16,256]{3,2,1,0:T(8,128)(2,1)S(1)}, bf16[4,16,16,256]{3,2,1,0:T(8,128)(2,1)S(1)}, u32[]{:S(2)}, u32[]{:S(2)}) collective-permute-start(bf16[4,16,16,256]{3,2,1,0:T(8,128)(2,1)S(1)} %shard_map.73.g_ref), channel_id=1, source_target_pairs={{0,1},{1,0},{2,3},{3,2},{4,5},{5,4},{6,7},{7,6},{8,9},{9,8},{10,11... | collective-permute-start | bytes 1572872 | tf_op jit(solution)/shard_map/ppermute | solution.py:383

commit v7 on v5

--- a/solution.py
+++ b/solution.py
@@ -57,18 +57,23 @@
     pick_ref[3 * share :, :] = jnp.where(chosen, 1.0, 0.0).astype(BF16)
 
 
-def side_kernel(*refs):
-    pieces, (cot_ref, _, side_ref) = refs[:-3], refs[-3:]
-    rows, cols, steps, channels = pieces[0].shape
+def side_kernel(x_ref, l_ref, r_ref, cot_ref, after_ref, side_ref):
+    rows, cols, steps, channels = x_ref.shape
     cells = rows * cols
-    for d, piece in enumerate(pieces):
-        block = piece[...].reshape(cells, steps, channels) if d == 0 else piece[:cells]
-        side_ref[d * cells : (d + 1) * cells] = block
+    side_ref[:cells] = x_ref[...].reshape(cells, steps, channels)
+    side_ref[cells : 2 * cells] = l_ref[:cells]
+    side_ref[2 * cells : 3 * cells] = r_ref[:cells]
     row = (1 - lax.axis_index("space")) * (rows - 1)
-    base = len(pieces) * cells
-    side_ref[base] = pieces[1][cells + row]
-    side_ref[base + 1 : base + 1 + cols] = cot_ref[row]
-    side_ref[base + 1 + cols] = pieces[-1][cells + row]
+    side_ref[3 * cells] = l_ref[cells + row]
+    side_ref[3 * cells + 1 : 3 * cells + 1 + cols] = cot_ref[row]
+    side_ref[3 * cells + 1 + cols] = r_ref[cells + row]
+
+
+def late_kernel(count, *refs):
+    pieces, late_ref = refs[:count], refs[-1]
+    cells = pieces[0].shape[0]
+    for n, piece in enumerate(pieces):
+        late_ref[n * cells : (n + 1) * cells] = piece[...]
 
 
 def conv_back(hg_ref, w_ref, rows, cols):
@@ -107,7 +112,7 @@
 ):
     rows, cols, steps, channels = x_ref.shape
     cells = rows * cols
-    chan = side_ref.shape[0] // cells
+    chan = lax.axis_size("chan")
     bottom = lax.axis_index("space")
     xw_ref[2 : 2 + rows, 2 : 2 + cols] = x_ref[...]
     cw_ref[1 : 1 + rows, 1 : 1 + cols] = cot_ref[...]
@@ -122,11 +127,11 @@
         at = (bottom * (rows - 2) + i) * cols
         xw_ref[near + i, 2 : 2 + cols] = side_ref[pl.ds(at, cols)]
         xw_ref[near + i, 0:2] = side_ref[pl.ds(cells + at + cols - 2, 2)]
-        xw_ref[near + i, cols + 2 : cols + 4] = side_ref[pl.ds((chan - 1) * cells + at, 2)]
+        xw_ref[near + i, cols + 2 : cols + 4] = side_ref[pl.ds(2 * cells + at, 2)]
         xw_ref[far + i] = jnp.zeros(xw_ref.shape[1:], BF16)
     near = (1 - bottom) * (rows + 1)
     far = bottom * (rows + 1)
-    cw_ref[near] = side_ref[chan * cells :]
+    cw_ref[near] = side_ref[3 * cells :]
     cw_ref[far] = jnp.zeros(cw_ref.shape[1:], BF16)
     me = lax.axis_index("chan")
     for end, c in ((0, 0), (chan - 1, cols + 2)):
@@ -176,7 +181,7 @@
         padded[pl.ds(1 + top, rows), 1 : 1 + cols] = half[...]
 
 
-def fill_from_pieces(padded, rows, cols, pieces, side):
+def fill_from_pieces(padded, rows, cols, pieces, side, late):
     clear_rim(padded)
     chan, cells = len(pieces), rows * cols
     me = lax.axis_index("chan")
@@ -186,8 +191,13 @@
         for r in range(rows):
             near = piece[r] if d == 0 else piece[r * cols : (r + 1) * cols]
             padded[1 + bottom * rows + r, pl.ds(place, cols)] = near
-            at = d * cells + r * cols
-            padded[1 + (1 - bottom) * rows + r, pl.ds(place, cols)] = side[at : at + cols]
+            source, n = (late, d - 2) if 1 < d < chan - 1 else (side, min(d, 2))
+            at = n * cells + r * cols
+            far = 1 + (1 - bottom) * rows + r
+            if source is late:
+                padded[far, pl.ds(place, cols)] = late[1 - bottom, at : at + cols]
+            else:
+                padded[far, pl.ds(place, cols)] = side[at : at + cols]
 
 
 def own_window(gp_ref, slope_ref, w_ref, tw_ref, hg_ref, frames, rows, cols):
@@ -210,15 +220,12 @@
 
 
 def tile_kernel(chan, *refs):
-    pieces, (side, w_ref), (act_ref, xt_ref, slope_ref, xp_ref) = (
-        refs[:chan],
-        refs[chan : chan + 2],
-        refs[-4:],
-    )
+    pieces, (side, late, w_ref) = refs[:chan], refs[chan : chan + 3]
+    act_ref, xt_ref, slope_ref, xp_ref = refs[-4:]
     rows, cols, steps, channels = pieces[0].shape
     width = chan * cols
     share = channels // chan
-    fill_from_pieces(xp_ref, rows, cols, pieces, side)
+    fill_from_pieces(xp_ref, rows, cols, pieces, side, late)
     span = width * steps
     turn = lax.rem(channels - lax.axis_index("chan") * share, channels)
     for i in range(2 * rows):
@@ -343,13 +350,13 @@
     swap = [(0, 1), (1, 0)]
     to_side = call(
         side_kernel,
-        bf16(chan * rows * cols + cols + 2),
+        bf16(3 * rows * cols + cols + 2),
         [],
         16,
         1_000_000,
         1_000_000,
-        *pieces, cot_own, pick,
-        places=[VM] * (chan + 1) + [pl.ANY],
+        x_own, pieces[1], pieces[-1], cot_own, pick,
+        places=[VM] * 4 + [pl.ANY],
     )
     from_side = lax.ppermute(to_side, "space", swap)
 
@@ -376,8 +383,8 @@
             pltpu.VMEM((rows + 2, cols + 2) + cell, BF16),
         ],
         20,
-        2 * win * 18 * channels * channels,
-        4_000_000,
+        1,
+        1,
         x_own, cot_own, pieces[1], pieces[-1], from_side, w, tw,
     )
 
@@ -394,6 +401,20 @@
                 4_000_000,
                 *g_all, cot_own, slope_w, w, tw,
             )
+        if not tick:
+            far = pieces[2:-1]
+            to_late = call(
+                functools.partial(late_kernel, len(far)),
+                bf16(len(far) * rows * cols),
+                [],
+                16,
+                1,
+                1,
+                *far,
+                payload,
+                places=[VM] * len(far) + [pl.ANY],
+            )
+            from_late = lax.all_gather(to_late, "space", axis=0, tiled=False)
         arrived = []
         for d in range(chan):
             pairs = [
@@ -403,7 +424,7 @@
             ]
             arrived.append(lax.ppermute(payload, ("chan", "pipe"), pairs))
         if not tick:
-            operands = [*pieces, from_side, w]
+            operands = [*pieces, from_side, from_late, w]
             act_t, x_t, slope_s = call(
                 functools.partial(tile_kernel, chan),
                 (
@@ -413,8 +434,8 @@
                 ),
                 [padded],
                 large,
-                2 * count * 9 * channels * channels,
-                6_000_000,
+                1,
+                1,
                 *operands,
                 arrived[0],
                 places=[VM] * len(operands) + [pl.ANY],

time: 47.6 us -> 43.7 us (0.918)
  waiting for transfers between devices: 21.6 us -> 14.2 us
  blocking collectives: 0 us -> 1.99 us
  starting transfers between devices: 10.9 us -> 12.4 us
    ppermute x3, waiting for transfers between devices: 9.94 us -> 5.09 us  [turned(): lax.ppermute(message, 'chan', [(i, (i + by) % chan) for i in range(chan)])]
    all_gather x0 -> x1, blocking collectives: none -> 1.99 us  [per_device(): from_late = lax.all_gather(to_late, 'space', axis=0, tiled=False)]
    ppermute x1, waiting for transfers between devices: 1.96 us -> 0.42 us  [per_device(): from_side = lax.ppermute(to_side, 'space', swap)]
    ppermute x4, starting transfers between devices: 4.66 us -> 5.74 us  [per_device(): arrived.append(lax.ppermute(payload, ('chan', 'pipe'), pairs))]
    ppermute x4, waiting for transfers between devices: 7.78 us -> 6.76 us  [per_device(): arrived.append(lax.ppermute(payload, ('chan', 'pipe'), pairs))]
    pallas_call x7 -> x8, Pallas kernels: 10.8 us -> 10.8 us  [call(): pl.pallas_call(kernel, out_shape=outs, in_specs=[pl.BlockSpec(memory_spac...]
  transfers between devices with their start and end apart: 9 -> 9, of which waited for: 5 -> 6; matrix products, arithmetic and copies ran while one was open for 0% -> 0% of each run, Pallas kernels for 6% -> 12%
where the time goes in v7:
time: 43.7 us; the launch traced here: 43.5 us
  waiting for transfers between devices  14.2 us (32%)
  starting transfers between devices  12.4 us (28%)
  Pallas kernels  10.8 us (25%)
  local copies, waits for them, and re-layouts  2.27 us (5%)
  blocking collectives  1.99 us (5%)
  other arithmetic  1.16 us (3%)
  between operations  0.7 us (2%)
    pallas_call x8, Pallas kernels, call(): pl.pallas_call(kernel, out_shape=outs, in_specs=[pl.BlockSpec(memory_spac...  10.8 us
    ppermute x4, waiting for transfers between devices, per_device(): arrived.append(lax.ppermute(payload, ('chan', 'pipe'), pairs))  6.76 us
    ppermute x3, starting transfers between devices, turned(): lax.ppermute(message, 'chan', [(i, (i + by) % chan) for i in range(chan)])  6.53 us
    ppermute x4, starting transfers between devices, per_device(): arrived.append(lax.ppermute(payload, ('chan', 'pipe'), pairs))  5.74 us
    ppermute x3, waiting for transfers between devices, turned(): lax.ppermute(message, 'chan', [(i, (i + by) % chan) for i in range(chan)])  5.09 us
    unnamed x4, local copies, waits for them, and re-layouts  2.27 us
    all_gather x1, blocking collectives, per_device(): from_late = lax.all_gather(to_late, 'space', axis=0, tiled=False)  1.99 us
    ppermute x1, waiting for transfers between devices, gathered(): return (half, lax.ppermute(half, 'space', swap))  1.9 us
  transfers between devices with their start and end apart: 9, of which 6 were waited for; matrix products, arithmetic and copies ran while one was open for 0% of the time, Pallas kernels for 12%

profile of v7, /device:TPU:0, one launch (start us, length us, event | category | flops | bytes accessed | tf_op | source)
XLA Modules:
  0.0 43.5 jit_solution(10640068873939864015)
XLA Ops:
  0.6 1.2 %pad_maximum_fusion.both_ref = bf16[2,2,8,4,4,256]{5,4,3,2,1,0:T(4,128)(2,1)S(1)} fusion(bf16[1,2,8,4,4,256]{5,4,3,2,1,0:T(4,128)(2,1)} %bitcast.16, bf16[1,2,8,4,4,256]{5,4,3,2,1,0:T(4,128)(2,1)} %param.4), kind=kLoop, calls=%fused_computation | loop fusion | flops 131072 | bytes 524288 | tf_op jit(solution)/shard_map/stack | solution.py:321
  1.8 0.1 shard_map.67
  1.9 3.1 %collective-permute-start = (bf16[20,16,256]{2,1,0:T(8,128)(2,1)S(1)}, bf16[20,16,256]{2,1,0:T(8,128)(2,1)S(1)}, u32[]{:S(2)}, u32[]{:S(2)}) collective-permute-start(bf16[20,16,256]{2,1,0:T(8,128)(2,1)S(1)} %get-tuple-element.20), channel_id=1, source_target_pairs={{0,4},{4,8},{8,12},{12,0},{1,5},{5,9},{9,13},{13,1},{2,6},{6,10},{... | collective-permute-start | bytes 491528 | tf_op jit(solution)/shard_map/ppermute | solution.py:341
  5.0 2.1 %collective-permute-start.1 = (bf16[20,16,256]{2,1,0:T(8,128)(2,1)S(1)}, bf16[20,16,256]{2,1,0:T(8,128)(2,1)S(1)}, u32[]{:S(2)}, u32[]{:S(2)}) collective-permute-start(bf16[20,16,256]{2,1,0:T(8,128)(2,1)S(1)} %get-tuple-element.21), channel_id=1, source_target_pairs={{0,12},{4,0},{8,4},{12,8},{1,13},{5,1},{9,5},{13,9},{2,14},{6,2},{... | collective-permute-start | bytes 491528 | tf_op jit(solution)/shard_map/ppermute | solution.py:341
  7.1 0.0 copy-start
  7.1 1.3 %copy-done = bf16[1,3,3,256,256]{4,3,2,1,0:T(8,128)(2,1)S(1)} copy-done((bf16[1,3,3,256,256]{4,3,2,1,0:T(8,128)(2,1)S(1)}, bf16[1,3,3,256,256]{4,3,2,1,0:T(8,128)(2,1)}, u32[]{:S(2)}) %copy-start) | copy-done | bytes 1179672
  8.3 0.0 copy-start.1
  8.3 1.0 %copy-done.1 = bf16[1,3,256,256]{3,2,1,0:T(8,128)(2,1)S(1)} copy-done((bf16[1,3,256,256]{3,2,1,0:T(8,128)(2,1)S(1)}, bf16[1,3,256,256]{3,2,1,0:T(8,128)(2,1)}, u32[]{:S(2)}) %copy-start.1) | copy-done | bytes 393240
  9.3 0.1 shard_map.68
  9.4 2.6 %collective-permute-done.l_ref.refs_1_ = bf16[20,16,256]{2,1,0:T(8,128)(2,1)S(1)} collective-permute-done((bf16[20,16,256]{2,1,0:T(8,128)(2,1)S(1)}, bf16[20,16,256]{2,1,0:T(8,128)(2,1)S(1)}, u32[]{:S(2)}, u32[]{:S(2)}) %collective-permute-start) | collective-permute-done | bytes 163872 | tf_op jit(solution)/shard_map/ppermute | solution.py:341
  12.1 2.1 %collective-permute-done.1.r_ref.refs_3_ = bf16[20,16,256]{2,1,0:T(8,128)(2,1)S(1)} collective-permute-done((bf16[20,16,256]{2,1,0:T(8,128)(2,1)S(1)}, bf16[20,16,256]{2,1,0:T(8,128)(2,1)S(1)}, u32[]{:S(2)}, u32[]{:S(2)}) %collective-permute-start.1) | collective-permute-done | bytes 163872 | tf_op jit(solution)/shard_map/ppermute | solution.py:341
  14.2 0.1 collective-permute-start.2
  14.3 1.4 %collective-permute-start.7 = (bf16[16,16,256]{2,1,0:T(8,128)(2,1)S(1)}, bf16[16,16,256]{2,1,0:T(8,128)(2,1)S(1)}, u32[]{:S(2)}, u32[]{:S(2)}) collective-permute-start(bf16[16,16,256]{2,1,0:T(8,128)(2,1)S(1)} %bitcast.12), channel_id=1, source_target_pairs={{0,8},{4,12},{8,0},{12,4},{1,9},{5,13},{9,1},{13,5},{2,10},{6,14},... | collective-permute-start | bytes 393224 | tf_op jit(solution)/shard_map/ppermute | solution.py:341
  15.6 0.4 collective-permute-done.2.side_ref.refs_4_
  16.0 2.1 %shard_map.70 = (f32[576,256]{1,0:T(8,128)S(1)}, bf16[4,4,16,256]{3,2,1,0:T(8,128)(2,1)S(1)}) custom-call(bf16[4,4,16,256]{3,2,1,0:T(8,128)(2,1)S(1)} %get-tuple-element.18.after_ref.x_ref.refs_0_, bf16[4,4,16,256]{3,2,1,0:T(8,128)(2,1)S(1)} %get-tuple-element.19.cot_ref, bf16[20,16,256]{2,1,0:T(8,128)(2,1)S(1)} %collective-permute-done.l_ref.refs_1_, ...), custom_call_target="tpu_custom_call" | custom-call | flops 1 | bytes 1 | tf_op jit(solution)/shard_map/pallas_call | solution.py:289
  18.2 1.6 %collective-permute-start.3 = (bf16[4,4,16,256]{3,2,1,0:T(8,128)(2,1)S(1)}, bf16[4,4,16,256]{3,2,1,0:T(8,128)(2,1)S(1)}, u32[]{:S(2)}, u32[]{:S(2)}) collective-permute-start(bf16[4,4,16,256]{3,2,1,0:T(8,128)(2,1)S(1)} %get-tuple-element.25.refs_1_), channel_id=1, source_target_pairs={{0,2},{4,6},{8,10},{12,14},{2,0},{6,4},{10,8},{14,12},{1,3},{5,7},... | collective-permute-start | bytes 393224 | tf_op jit(solution)/shard_map/ppermute | solution.py:425
  19.8 2.3 %collective-permute-start.6 = (bf16[4,4,16,256]{3,2,1,0:T(8,128)(2,1)S(1)}, bf16[4,4,16,256]{3,2,1,0:T(8,128)(2,1)S(1)}, u32[]{:S(2)}, u32[]{:S(2)}) collective-permute-start(bf16[4,4,16,256]{3,2,1,0:T(8,128)(2,1)S(1)} %get-tuple-element.25.refs_1_), channel_id=1, source_target_pairs={{0,14},{4,2},{8,6},{12,10},{2,12},{6,0},{10,4},{14,8},{1,15},{5,3}... | collective-permute-start | bytes 393224 | tf_op jit(solution)/shard_map/ppermute | solution.py:425
  22.0 1.2 %collective-permute-start.5 = (bf16[4,4,16,256]{3,2,1,0:T(8,128)(2,1)S(1)}, bf16[4,4,16,256]{3,2,1,0:T(8,128)(2,1)S(1)}, u32[]{:S(2)}, u32[]{:S(2)}) collective-permute-start(bf16[4,4,16,256]{3,2,1,0:T(8,128)(2,1)S(1)} %get-tuple-element.25.refs_1_), channel_id=1, source_target_pairs={{0,10},{4,14},{8,2},{12,6},{2,8},{6,12},{10,0},{14,4},{1,11},{5,15... | collective-permute-start | bytes 393224 | tf_op jit(solution)/shard_map/ppermute | solution.py:425
  23.3 0.7 %collective-permute-start.4 = (bf16[4,4,16,256]{3,2,1,0:T(8,128)(2,1)S(1)}, bf16[4,4,16,256]{3,2,1,0:T(8,128)(2,1)S(1)}, u32[]{:S(2)}, u32[]{:S(2)}) collective-permute-start(bf16[4,4,16,256]{3,2,1,0:T(8,128)(2,1)S(1)} %get-tuple-element.25.refs_1_), channel_id=1, source_target_pairs={{0,6},{4,10},{8,14},{12,2},{2,4},{6,8},{10,12},{14,0},{1,7},{5,11}... | collective-permute-start | bytes 393224 | tf_op jit(solution)/shard_map/ppermute | solution.py:425
  23.9 0.4 collective-permute-done.7.refs_0_.refs_2_
  24.3 2.0 %all-gather = bf16[32,16,256]{2,1,0:T(8,128)(2,1)S(1)} all-gather(bf16[16,16,256]{2,1,0:T(8,128)(2,1)S(1)} %shard_map.71), channel_id=2, replica_groups=mesh['groups'=2,'chan'=4,'pipe'=2,'space'=2] {'space'}, dimensions={0}, use_global_device_ids=true | all-gather | bytes 393216 | tf_op jit(solution)/shard_map/all_gather | solution.py:417
  26.3 0.0 collective-permute-done.3.refs_7_.refs_0_
  26.3 2.9 %shard_map.72 = (bf16[256,2048]{1,0:T(8,128)(2,1)S(1)}, bf16[256,2048]{1,0:T(8,128)(2,1)S(1)}, f32[2048,64]{1,0:T(8,128)S(1)}) custom-call(bf16[4,4,16,256]{3,2,1,0:T(8,128)(2,1)S(1)} %get-tuple-element.18.after_ref.x_ref.refs_0_, bf16[20,16,256]{2,1,0:T(8,128)(2,1)S(1)} %collective-permute-done.l_ref.refs_1_, ...), custom_call_target="tpu_custom_call" | custom-call | flops 1 | bytes 1 | tf_op jit(solution)/shard_map/pallas_call | solution.py:289
  29.3 0.0 collective-permute-done.6.refs_3_
  29.3 6.8 %collective-permute-done.5.refs_2_ = bf16[4,4,16,256]{3,2,1,0:T(8,128)(2,1)S(1)} collective-permute-done((bf16[4,4,16,256]{3,2,1,0:T(8,128)(2,1)S(1)}, bf16[4,4,16,256]{3,2,1,0:T(8,128)(2,1)S(1)}, u32[]{:S(2)}, u32[]{:S(2)}) %collective-permute-start.5) | collective-permute-done | bytes 131104 | tf_op jit(solution)/shard_map/ppermute | solution.py:425
  36.0 0.0 collective-permute-done.4.refs_1_
  36.1 0.1 collective-permute-start.8
  36.2 1.9 %collective-permute-done.8.other_ref = bf16[4,16,16,256]{3,2,1,0:T(8,128)(2,1)S(1)} collective-permute-done((bf16[4,16,16,256]{3,2,1,0:T(8,128)(2,1)S(1)}, bf16[4,16,16,256]{3,2,1,0:T(8,128)(2,1)S(1)}, u32[]{:S(2)}, u32[]{:S(2)}) %collective-permute-start.8) | collective-permute-done | bytes 524320 | tf_op jit(solution)/shard_map/ppermute | solution.py:375
  38.1 5.4 %shard_map.74 = (bf16[2,8,4,4,256]{4,3,2,1,0:T(4,128)(2,1)}, f32[9,64,256]{2,1,0:T(8,128)}, f32[3,64,256]{2,1,0:T(8,128)}) custom-call(bf16[4,16,16,256]{3,2,1,0:T(8,128)(2,1)S(1)} %shard_map.73.g_ref, bf16[4,16,16,256]{3,2,1,0:T(8,128)(2,1)S(1)} %collective-permute-done.8.other_ref, f32[576,256]{1,0:T(8,128)S(1)} %get-tuple-element.27.slope_w_ref, ...), custom_call_target="tpu_custom_call" | custom-call | flops 1358954496 | bytes 8000000 | tf_op jit(solution)/shard_map/pallas_call | solution.py:289
  (3 shorter events, 0.1 us)
Async XLA Ops:
  1.9 10.2 %collective-permute-start = (bf16[20,16,256]{2,1,0:T(8,128)(2,1)S(1)}, bf16[20,16,256]{2,1,0:T(8,128)(2,1)S(1)}, u32[]{:S(2)}, u32[]{:S(2)}) collective-permute-start(bf16[20,16,256]{2,1,0:T(8,128)(2,1)S(1)} %get-tuple-element.20), channel_id=1, source_target_pairs={{0,4},{4,8},{8,12},{12,0},{1,5},{5,9},{9,13},{13,1},{2,6},{6,10},{... | collective-permute-start | bytes 491528 | tf_op jit(solution)/shard_map/ppermute | solution.py:341
  5.0 9.2 %collective-permute-start.1 = (bf16[20,16,256]{2,1,0:T(8,128)(2,1)S(1)}, bf16[20,16,256]{2,1,0:T(8,128)(2,1)S(1)}, u32[]{:S(2)}, u32[]{:S(2)}) collective-permute-start(bf16[20,16,256]{2,1,0:T(8,128)(2,1)S(1)} %get-tuple-element.21), channel_id=1, source_target_pairs={{0,12},{4,0},{8,4},{12,8},{1,13},{5,1},{9,5},{13,9},{2,14},{6,2},{... | collective-permute-start | bytes 491528 | tf_op jit(solution)/shard_map/ppermute | solution.py:341
  7.1 1.3 %copy-start = (bf16[1,3,3,256,256]{4,3,2,1,0:T(8,128)(2,1)S(1)}, bf16[1,3,3,256,256]{4,3,2,1,0:T(8,128)(2,1)}, u32[]{:S(2)}) copy-start(bf16[1,3,3,256,256]{4,3,2,1,0:T(8,128)(2,1)} %param.6) | copy-start | bytes 3538948
  8.3 1.0 %copy-start.1 = (bf16[1,3,256,256]{3,2,1,0:T(8,128)(2,1)S(1)}, bf16[1,3,256,256]{3,2,1,0:T(8,128)(2,1)}, u32[]{:S(2)}) copy-start(bf16[1,3,256,256]{3,2,1,0:T(8,128)(2,1)} %param.7) | copy-start | bytes 1179652
  14.2 1.9 %collective-permute-start.2 = (bf16[54,16,256]{2,1,0:T(8,128)(2,1)S(1)}, bf16[54,16,256]{2,1,0:T(8,128)(2,1)S(1)}, u32[]{:S(2)}, u32[]{:S(2)}) collective-permute-start(bf16[54,16,256]{2,1,0:T(8,128)(2,1)S(1)} %shard_map.69), channel_id=1, source_target_pairs={{0,1},{1,0},{2,3},{3,2},{4,5},{5,4},{6,7},{7,6},{8,9},{9,8},{10,11... | collective-permute-start | bytes 1327112 | tf_op jit(solution)/shard_map/ppermute | solution.py:361
  14.3 10.1 %collective-permute-start.7 = (bf16[16,16,256]{2,1,0:T(8,128)(2,1)S(1)}, bf16[16,16,256]{2,1,0:T(8,128)(2,1)S(1)}, u32[]{:S(2)}, u32[]{:S(2)}) collective-permute-start(bf16[16,16,256]{2,1,0:T(8,128)(2,1)S(1)} %bitcast.12), channel_id=1, source_target_pairs={{0,8},{4,12},{8,0},{12,4},{1,9},{5,13},{9,1},{13,5},{2,10},{6,14},... | collective-permute-start | bytes 393224 | tf_op jit(solution)/shard_map/ppermute | solution.py:341
  18.2 8.1 %collective-permute-start.3 = (bf16[4,4,16,256]{3,2,1,0:T(8,128)(2,1)S(1)}, bf16[4,4,16,256]{3,2,1,0:T(8,128)(2,1)S(1)}, u32[]{:S(2)}, u32[]{:S(2)}) collective-permute-start(bf16[4,4,16,256]{3,2,1,0:T(8,128)(2,1)S(1)} %get-tuple-element.25.refs_1_), channel_id=1, source_target_pairs={{0,2},{4,6},{8,10},{12,14},{2,0},{6,4},{10,8},{14,12},{1,3},{5,7},... | collective-permute-start | bytes 393224 | tf_op jit(solution)/shard_map/ppermute | solution.py:425
  19.8 9.5 %collective-permute-start.6 = (bf16[4,4,16,256]{3,2,1,0:T(8,128)(2,1)S(1)}, bf16[4,4,16,256]{3,2,1,0:T(8,128)(2,1)S(1)}, u32[]{:S(2)}, u32[]{:S(2)}) collective-permute-start(bf16[4,4,16,256]{3,2,1,0:T(8,128)(2,1)S(1)} %get-tuple-element.25.refs_1_), channel_id=1, source_target_pairs={{0,14},{4,2},{8,6},{12,10},{2,12},{6,0},{10,4},{14,8},{1,15},{5,3}... | collective-permute-start | bytes 393224 | tf_op jit(solution)/shard_map/ppermute | solution.py:425
  22.0 14.0 %collective-permute-start.5 = (bf16[4,4,16,256]{3,2,1,0:T(8,128)(2,1)S(1)}, bf16[4,4,16,256]{3,2,1,0:T(8,128)(2,1)S(1)}, u32[]{:S(2)}, u32[]{:S(2)}) collective-permute-start(bf16[4,4,16,256]{3,2,1,0:T(8,128)(2,1)S(1)} %get-tuple-element.25.refs_1_), channel_id=1, source_target_pairs={{0,10},{4,14},{8,2},{12,6},{2,8},{6,12},{10,0},{14,4},{1,11},{5,15... | collective-permute-start | bytes 393224 | tf_op jit(solution)/shard_map/ppermute | solution.py:425
  23.3 12.8 %collective-permute-start.4 = (bf16[4,4,16,256]{3,2,1,0:T(8,128)(2,1)S(1)}, bf16[4,4,16,256]{3,2,1,0:T(8,128)(2,1)S(1)}, u32[]{:S(2)}, u32[]{:S(2)}) collective-permute-start(bf16[4,4,16,256]{3,2,1,0:T(8,128)(2,1)S(1)} %get-tuple-element.25.refs_1_), channel_id=1, source_target_pairs={{0,6},{4,10},{8,14},{12,2},{2,4},{6,8},{10,12},{14,0},{1,7},{5,11}... | collective-permute-start | bytes 393224 | tf_op jit(solution)/shard_map/ppermute | solution.py:425
  36.1 2.0 %collective-permute-start.8 = (bf16[4,16,16,256]{3,2,1,0:T(8,128)(2,1)S(1)}, bf16[4,16,16,256]{3,2,1,0:T(8,128)(2,1)S(1)}, u32[]{:S(2)}, u32[]{:S(2)}) collective-permute-start(bf16[4,16,16,256]{3,2,1,0:T(8,128)(2,1)S(1)} %shard_map.73.g_ref), channel_id=1, source_target_pairs={{0,1},{1,0},{2,3},{3,2},{4,5},{5,4},{6,7},{7,6},{8,9},{9,8},{10,11... | collective-permute-start | bytes 1572872 | tf_op jit(solution)/shard_map/ppermute | solution.py:375

commit v8 on v7

--- a/solution.py
+++ b/solution.py
@@ -112,7 +112,6 @@
 ):
     rows, cols, steps, channels = x_ref.shape
     cells = rows * cols
-    chan = lax.axis_size("chan")
     bottom = lax.axis_index("space")
     xw_ref[2 : 2 + rows, 2 : 2 + cols] = x_ref[...]
     cw_ref[1 : 1 + rows, 1 : 1 + cols] = cot_ref[...]
@@ -133,15 +132,6 @@
     far = bottom * (rows + 1)
     cw_ref[near] = side_ref[3 * cells :]
     cw_ref[far] = jnp.zeros(cw_ref.shape[1:], BF16)
-    me = lax.axis_index("chan")
-    for end, c in ((0, 0), (chan - 1, cols + 2)):
-
-        @pl.when(me == end)
-        def _(c=c):
-            xw_ref[:, c : c + 2] = jnp.zeros((rows + 4, 2, steps, channels), BF16)
-            edge = min(c, cols + 1)
-            cw_ref[:, edge : edge + 1] = jnp.zeros((rows + 2, 1, steps, channels), BF16)
-
     hidden = None
     for u in range(3):
         for v in range(3):
@@ -181,23 +171,34 @@
         padded[pl.ds(1 + top, rows), 1 : 1 + cols] = half[...]
 
 
-def fill_from_pieces(padded, rows, cols, pieces, side, late):
+def fill_from_pieces(padded, rows, cols, pieces, wrap, side, late):
     clear_rim(padded)
     chan, cells = len(pieces), rows * cols
     me = lax.axis_index("chan")
     bottom = lax.axis_index("space")
-    for d, piece in enumerate(pieces):
+
+    def put(d, near, far, n):
         place = 1 + lax.rem(me - d + chan, chan) * cols
         for r in range(rows):
-            near = piece[r] if d == 0 else piece[r * cols : (r + 1) * cols]
-            padded[1 + bottom * rows + r, pl.ds(place, cols)] = near
-            source, n = (late, d - 2) if 1 < d < chan - 1 else (side, min(d, 2))
+            padded[1 + bottom * rows + r, pl.ds(place, cols)] = (
+                near[r] if d == 0 else near[r * cols : (r + 1) * cols]
+            )
             at = n * cells + r * cols
-            far = 1 + (1 - bottom) * rows + r
-            if source is late:
-                padded[far, pl.ds(place, cols)] = late[1 - bottom, at : at + cols]
-            else:
-                padded[far, pl.ds(place, cols)] = side[at : at + cols]
+            padded[1 + (1 - bottom) * rows + r, pl.ds(place, cols)] = far[at : at + cols]
+
+    other = late.at[1 - bottom]
+    put(0, pieces[0], side, 0)
+    for d in range(2, chan - 1):
+        put(d, pieces[d], other, d - 2)
+    for d, end, n in ((1, 0, 1), (chan - 1, chan - 1, 2)):
+
+        @pl.when(me == end)
+        def _(d=d):
+            put(d, wrap, other, chan - 3)
+
+        @pl.when(me != end)
+        def _(d=d, n=n):
+            put(d, pieces[d], side, n)
 
 
 def own_window(gp_ref, slope_ref, w_ref, tw_ref, hg_ref, frames, rows, cols):
@@ -220,12 +221,12 @@
 
 
 def tile_kernel(chan, *refs):
-    pieces, (side, late, w_ref) = refs[:chan], refs[chan : chan + 3]
+    pieces, (wrap, side, late, w_ref) = refs[:chan], refs[chan : chan + 4]
     act_ref, xt_ref, slope_ref, xp_ref = refs[-4:]
     rows, cols, steps, channels = pieces[0].shape
     width = chan * cols
     share = channels // chan
-    fill_from_pieces(xp_ref, rows, cols, pieces, side, late)
+    fill_from_pieces(xp_ref, rows, cols, pieces, wrap, side, late)
     span = width * steps
     turn = lax.rem(channels - lax.axis_index("chan") * share, channels)
     for i in range(2 * rows):
@@ -343,10 +344,11 @@
     x_flat = x_own.reshape((rows * cols,) + cell)
     pieces = [
         x_own,
-        turned(to_right, 1),
+        lax.ppermute(to_right, "chan", [(i, i + 1) for i in range(chan - 1)]),
         *[turned(x_flat, d) for d in range(2, chan - 1)],
-        turned(to_left, chan - 1),
+        lax.ppermute(to_left, "chan", [(i + 1, i) for i in range(chan - 1)]),
     ]
+    wrap = lax.ppermute(x_flat, "chan", [(0, chan - 1), (chan - 1, 0)])
     swap = [(0, 1), (1, 0)]
     to_side = call(
         side_kernel,
@@ -402,7 +404,7 @@
                 *g_all, cot_own, slope_w, w, tw,
             )
         if not tick:
-            far = pieces[2:-1]
+            far = [*pieces[2:-1], wrap]
             to_late = call(
                 functools.partial(late_kernel, len(far)),
                 bf16(len(far) * rows * cols),
@@ -424,7 +426,7 @@
             ]
             arrived.append(lax.ppermute(payload, ("chan", "pipe"), pairs))
         if not tick:
-            operands = [*pieces, from_side, from_late, w]
+            operands = [*pieces, wrap, from_side, from_late, w]
             act_t, x_t, slope_s = call(
                 functools.partial(tile_kernel, chan),
                 (

time: 43.7 us -> 45.6 us (1.043)
  starting transfers between devices: 12.4 us -> 19.6 us
  waiting for transfers between devices: 14.2 us -> 8.58 us
    ppermute x0 -> x3, starting transfers between devices: none -> 9.47 us  [the longest x1 4.94 us: per_device(): lax.ppermute(to_right, 'chan', [(i, i + 1) for i in range(chan - 1)])]
    ppermute x3 -> x1, waiting for transfers between devices: 5.09 us -> 0.01 us  [turned(): lax.ppermute(message, 'chan', [(i, (i + by) % chan) for i in range(chan)])]
    ppermute x4, waiting for transfers between devices: 6.76 us -> 2.81 us  [per_device(): arrived.append(lax.ppermute(payload, ('chan', 'pipe'), pairs))]
    ppermute x3 -> x1, starting transfers between devices: 6.53 us -> 2.65 us  [turned(): lax.ppermute(message, 'chan', [(i, (i + by) % chan) for i in range(chan)])]
    ppermute x0 -> x3, waiting for transfers between devices: none -> 3.86 us  [the longest x1 3.86 us: per_device(): lax.ppermute(to_left, 'chan', [(i + 1, i) for i in range(chan - 1)])]
    ppermute x4, starting transfers between devices: 5.74 us -> 7.36 us  [per_device(): arrived.append(lax.ppermute(payload, ('chan', 'pipe'), pairs))]
  transfers between devices with their start and end apart: 9 -> 10, of which waited for: 6 -> 3; matrix products, arithmetic and copies ran while one was open for 0% -> 0% of each run, Pallas kernels for 12% -> 11%
where the time goes in v8:
time: 45.6 us; the launch traced here: 45.3 us
  starting transfers between devices  19.6 us (43%)
  Pallas kernels  10.8 us (24%)
  waiting for transfers between devices  8.58 us (19%)
  local copies, waits for them, and re-layouts  2.26 us (5%)
  blocking collectives  2.18 us (5%)
  other arithmetic  1.16 us (3%)
  between operations  0.76 us (2%)
    pallas_call x8, Pallas kernels, call(): pl.pallas_call(kernel, out_shape=outs, in_specs=[pl.BlockSpec(memory_spac...  10.8 us
    ppermute x4, starting transfers between devices, per_device(): arrived.append(lax.ppermute(payload, ('chan', 'pipe'), pairs))  7.36 us
    ppermute x1, starting transfers between devices, per_device(): lax.ppermute(to_right, 'chan', [(i, i + 1) for i in range(chan - 1)])  4.94 us
    ppermute x1, waiting for transfers between devices, per_device(): lax.ppermute(to_left, 'chan', [(i + 1, i) for i in range(chan - 1)])  3.86 us
    ppermute x1, starting transfers between devices, per_device(): wrap = lax.ppermute(x_flat, 'chan', [(0, chan - 1), (chan - 1, 0)])  3.24 us
    ppermute x4, waiting for transfers between devices, per_device(): arrived.append(lax.ppermute(payload, ('chan', 'pipe'), pairs))  2.81 us
    ppermute x1, starting transfers between devices, turned(): lax.ppermute(message, 'chan', [(i, (i + by) % chan) for i in range(chan)])  2.65 us
    unnamed x4, local copies, waits for them, and re-layouts  2.26 us
  transfers between devices with their start and end apart: 10, of which 3 were waited for; matrix products, arithmetic and copies ran while one was open for 0% of the time, Pallas kernels for 11%

profile of v8, /device:TPU:0, one launch (start us, length us, event | category | flops | bytes accessed | tf_op | source)
XLA Modules:
  0.0 45.3 jit_solution(11612503340365439292)
XLA Ops:
  0.6 1.2 %pad_maximum_fusion.both_ref = bf16[2,2,8,4,4,256]{5,4,3,2,1,0:T(4,128)(2,1)S(1)} fusion(bf16[1,2,8,4,4,256]{5,4,3,2,1,0:T(4,128)(2,1)} %bitcast.17, bf16[1,2,8,4,4,256]{5,4,3,2,1,0:T(4,128)(2,1)} %param.4), kind=kLoop, calls=%fused_computation | loop fusion | flops 131072 | bytes 524288 | tf_op jit(solution)/shard_map/stack | solution.py:322
  1.8 0.1 shard_map.67
  1.9 4.9 %collective-permute-start = (bf16[20,16,256]{2,1,0:T(8,128)(2,1)S(1)}, bf16[20,16,256]{2,1,0:T(8,128)(2,1)S(1)}, u32[]{:S(2)}, u32[]{:S(2)}) collective-permute-start(bf16[20,16,256]{2,1,0:T(8,128)(2,1)S(1)} %get-tuple-element.20), channel_id=1, source_target_pairs={{0,4},{4,8},{8,12},{1,5},{5,9},{9,13},{2,6},{6,10},{10,14},{3,7},{... | collective-permute-start | bytes 491528 | tf_op jit(solution)/shard_map/ppermute | solution.py:347
  6.8 1.3 %collective-permute-start.1 = (bf16[20,16,256]{2,1,0:T(8,128)(2,1)S(1)}, bf16[20,16,256]{2,1,0:T(8,128)(2,1)S(1)}, u32[]{:S(2)}, u32[]{:S(2)}) collective-permute-start(bf16[20,16,256]{2,1,0:T(8,128)(2,1)S(1)} %get-tuple-element.21), channel_id=1, source_target_pairs={{4,0},{8,4},{12,8},{5,1},{9,5},{13,9},{6,2},{10,6},{14,10},{7,3},{... | collective-permute-start | bytes 491528 | tf_op jit(solution)/shard_map/ppermute | solution.py:349
  8.1 0.0 copy-start
  8.2 1.3 %copy-done = bf16[1,3,3,256,256]{4,3,2,1,0:T(8,128)(2,1)S(1)} copy-done((bf16[1,3,3,256,256]{4,3,2,1,0:T(8,128)(2,1)S(1)}, bf16[1,3,3,256,256]{4,3,2,1,0:T(8,128)(2,1)}, u32[]{:S(2)}) %copy-start) | copy-done | bytes 1179672
  9.4 0.0 copy-start.1
  9.4 1.0 %copy-done.1 = bf16[1,3,256,256]{3,2,1,0:T(8,128)(2,1)S(1)} copy-done((bf16[1,3,256,256]{3,2,1,0:T(8,128)(2,1)S(1)}, bf16[1,3,256,256]{3,2,1,0:T(8,128)(2,1)}, u32[]{:S(2)}) %copy-start.1) | copy-done | bytes 393240
  10.4 0.1 shard_map.68
  10.5 0.0 collective-permute-done.l_ref.refs_1_
  10.5 3.9 %collective-permute-done.1.r_ref.refs_3_ = bf16[20,16,256]{2,1,0:T(8,128)(2,1)S(1)} collective-permute-done((bf16[20,16,256]{2,1,0:T(8,128)(2,1)S(1)}, bf16[20,16,256]{2,1,0:T(8,128)(2,1)S(1)}, u32[]{:S(2)}, u32[]{:S(2)}) %collective-permute-start.1) | collective-permute-done | bytes 163872 | tf_op jit(solution)/shard_map/ppermute | solution.py:349
  14.4 0.1 collective-permute-start.2
  14.5 2.6 %collective-permute-start.7 = (bf16[16,16,256]{2,1,0:T(8,128)(2,1)S(1)}, bf16[16,16,256]{2,1,0:T(8,128)(2,1)S(1)}, u32[]{:S(2)}, u32[]{:S(2)}) collective-permute-start(bf16[16,16,256]{2,1,0:T(8,128)(2,1)S(1)} %bitcast.12), channel_id=1, source_target_pairs={{0,8},{4,12},{8,0},{12,4},{1,9},{5,13},{9,1},{13,5},{2,10},{6,14},... | collective-permute-start | bytes 393224 | tf_op jit(solution)/shard_map/ppermute | solution.py:342
  17.2 3.2 %collective-permute-start.8 = (bf16[16,16,256]{2,1,0:T(8,128)(2,1)S(1)}, bf16[16,16,256]{2,1,0:T(8,128)(2,1)S(1)}, u32[]{:S(2)}, u32[]{:S(2)}) collective-permute-start(bf16[16,16,256]{2,1,0:T(8,128)(2,1)S(1)} %bitcast.13), channel_id=1, source_target_pairs={{0,12},{12,0},{1,13},{13,1},{2,14},{14,2},{3,15},{15,3},{16,28},{2... | collective-permute-start | bytes 393224 | tf_op jit(solution)/shard_map/ppermute | solution.py:351
  20.4 0.0 collective-permute-done.2.side_ref.refs_5_
  20.4 2.1 %shard_map.70 = (f32[576,256]{1,0:T(8,128)S(1)}, bf16[4,4,16,256]{3,2,1,0:T(8,128)(2,1)S(1)}) custom-call(bf16[4,4,16,256]{3,2,1,0:T(8,128)(2,1)S(1)} %get-tuple-element.18.after_ref.x_ref.refs_0_, bf16[4,4,16,256]{3,2,1,0:T(8,128)(2,1)S(1)} %get-tuple-element.19.cot_ref, bf16[20,16,256]{2,1,0:T(8,128)(2,1)S(1)} %collective-permute-done.l_ref.refs_1_, ...), custom_call_target="tpu_custom_call" | custom-call | flops 1 | bytes 1 | tf_op jit(solution)/shard_map/pallas_call | solution.py:290
  22.5 1.6 %collective-permute-start.3 = (bf16[4,4,16,256]{3,2,1,0:T(8,128)(2,1)S(1)}, bf16[4,4,16,256]{3,2,1,0:T(8,128)(2,1)S(1)}, u32[]{:S(2)}, u32[]{:S(2)}) collective-permute-start(bf16[4,4,16,256]{3,2,1,0:T(8,128)(2,1)S(1)} %get-tuple-element.25.refs_2_), channel_id=1, source_target_pairs={{0,2},{4,6},{8,10},{12,14},{2,0},{6,4},{10,8},{14,12},{1,3},{5,7},... | collective-permute-start | bytes 393224 | tf_op jit(solution)/shard_map/ppermute | solution.py:427
  24.1 0.0 collective-permute-start.4
  24.1 3.9 %collective-permute-start.5 = (bf16[4,4,16,256]{3,2,1,0:T(8,128)(2,1)S(1)}, bf16[4,4,16,256]{3,2,1,0:T(8,128)(2,1)S(1)}, u32[]{:S(2)}, u32[]{:S(2)}) collective-permute-start(bf16[4,4,16,256]{3,2,1,0:T(8,128)(2,1)S(1)} %get-tuple-element.25.refs_2_), channel_id=1, source_target_pairs={{0,10},{4,14},{8,2},{12,6},{2,8},{6,12},{10,0},{14,4},{1,11},{5,15... | collective-permute-start | bytes 393224 | tf_op jit(solution)/shard_map/ppermute | solution.py:427
  28.0 0.0 collective-permute-done.7.refs_0_.refs_2_
  28.0 1.8 %collective-permute-start.6 = (bf16[4,4,16,256]{3,2,1,0:T(8,128)(2,1)S(1)}, bf16[4,4,16,256]{3,2,1,0:T(8,128)(2,1)S(1)}, u32[]{:S(2)}, u32[]{:S(2)}) collective-permute-start(bf16[4,4,16,256]{3,2,1,0:T(8,128)(2,1)S(1)} %get-tuple-element.25.refs_2_), channel_id=1, source_target_pairs={{0,14},{4,2},{8,6},{12,10},{2,12},{6,0},{10,4},{14,8},{1,15},{5,3}... | collective-permute-start | bytes 393224 | tf_op jit(solution)/shard_map/ppermute | solution.py:427
  29.9 0.0 collective-permute-done.8.refs_1_.refs_4_
  29.9 2.2 %all-gather = bf16[64,16,256]{2,1,0:T(8,128)(2,1)S(1)} all-gather(bf16[32,16,256]{2,1,0:T(8,128)(2,1)S(1)} %shard_map.71), channel_id=2, replica_groups=mesh['groups'=2,'chan'=4,'pipe'=2,'space'=2] {'space'}, dimensions={0}, use_global_device_ids=true | all-gather | bytes 786432 | tf_op jit(solution)/shard_map/all_gather | solution.py:419
  32.1 2.8 %collective-permute-done.3.refs_8_.refs_0_ = bf16[4,4,16,256]{3,2,1,0:T(8,128)(2,1)S(1)} collective-permute-done((bf16[4,4,16,256]{3,2,1,0:T(8,128)(2,1)S(1)}, bf16[4,4,16,256]{3,2,1,0:T(8,128)(2,1)S(1)}, u32[]{:S(2)}, u32[]{:S(2)}) %collective-permute-start.3) | collective-permute-done | bytes 131104 | tf_op jit(solution)/shard_map/ppermute | solution.py:427
  34.9 3.0 %shard_map.72 = (bf16[256,2048]{1,0:T(8,128)(2,1)S(1)}, bf16[256,2048]{1,0:T(8,128)(2,1)S(1)}, f32[2048,64]{1,0:T(8,128)S(1)}) custom-call(bf16[4,4,16,256]{3,2,1,0:T(8,128)(2,1)S(1)} %get-tuple-element.18.after_ref.x_ref.refs_0_, bf16[20,16,256]{2,1,0:T(8,128)(2,1)S(1)} %collective-permute-done.l_ref.refs_1_, ...), custom_call_target="tpu_custom_call" | custom-call | flops 1 | bytes 1 | tf_op jit(solution)/shard_map/pallas_call | solution.py:290
  37.9 0.0 collective-permute-done.4.refs_1_
  37.9 0.0 collective-permute-done.5.refs_2_
  37.9 0.0 collective-permute-done.6.refs_3_
  38.0 0.1 collective-permute-start.9
  38.0 1.9 %collective-permute-done.9.other_ref = bf16[4,16,16,256]{3,2,1,0:T(8,128)(2,1)S(1)} collective-permute-done((bf16[4,16,16,256]{3,2,1,0:T(8,128)(2,1)S(1)}, bf16[4,16,16,256]{3,2,1,0:T(8,128)(2,1)S(1)}, u32[]{:S(2)}, u32[]{:S(2)}) %collective-permute-start.9) | collective-permute-done | bytes 524320 | tf_op jit(solution)/shard_map/ppermute | solution.py:377
  39.9 5.4 %shard_map.74 = (bf16[2,8,4,4,256]{4,3,2,1,0:T(4,128)(2,1)}, f32[9,64,256]{2,1,0:T(8,128)}, f32[3,64,256]{2,1,0:T(8,128)}) custom-call(bf16[4,16,16,256]{3,2,1,0:T(8,128)(2,1)S(1)} %shard_map.73.g_ref, bf16[4,16,16,256]{3,2,1,0:T(8,128)(2,1)S(1)} %collective-permute-done.9.other_ref, f32[576,256]{1,0:T(8,128)S(1)} %get-tuple-element.27.slope_w_ref, ...), custom_call_target="tpu_custom_call" | custom-call | flops 1358954496 | bytes 8000000 | tf_op jit(solution)/shard_map/pallas_call | solution.py:290
  (3 shorter events, 0.1 us)
Async XLA Ops:
  1.9 8.6 %collective-permute-start = (bf16[20,16,256]{2,1,0:T(8,128)(2,1)S(1)}, bf16[20,16,256]{2,1,0:T(8,128)(2,1)S(1)}, u32[]{:S(2)}, u32[]{:S(2)}) collective-permute-start(bf16[20,16,256]{2,1,0:T(8,128)(2,1)S(1)} %get-tuple-element.20), channel_id=1, source_target_pairs={{0,4},{4,8},{8,12},{1,5},{5,9},{9,13},{2,6},{6,10},{10,14},{3,7},{... | collective-permute-start | bytes 491528 | tf_op jit(solution)/shard_map/ppermute | solution.py:347
  6.8 7.6 %collective-permute-start.1 = (bf16[20,16,256]{2,1,0:T(8,128)(2,1)S(1)}, bf16[20,16,256]{2,1,0:T(8,128)(2,1)S(1)}, u32[]{:S(2)}, u32[]{:S(2)}) collective-permute-start(bf16[20,16,256]{2,1,0:T(8,128)(2,1)S(1)} %get-tuple-element.21), channel_id=1, source_target_pairs={{4,0},{8,4},{12,8},{5,1},{9,5},{13,9},{6,2},{10,6},{14,10},{7,3},{... | collective-permute-start | bytes 491528 | tf_op jit(solution)/shard_map/ppermute | solution.py:349
  8.1 1.3 %copy-start = (bf16[1,3,3,256,256]{4,3,2,1,0:T(8,128)(2,1)S(1)}, bf16[1,3,3,256,256]{4,3,2,1,0:T(8,128)(2,1)}, u32[]{:S(2)}) copy-start(bf16[1,3,3,256,256]{4,3,2,1,0:T(8,128)(2,1)} %param.6) | copy-start | bytes 3538948
  9.4 1.0 %copy-start.1 = (bf16[1,3,256,256]{3,2,1,0:T(8,128)(2,1)S(1)}, bf16[1,3,256,256]{3,2,1,0:T(8,128)(2,1)}, u32[]{:S(2)}) copy-start(bf16[1,3,256,256]{3,2,1,0:T(8,128)(2,1)} %param.7) | copy-start | bytes 1179652
  14.4 6.0 %collective-permute-start.2 = (bf16[54,16,256]{2,1,0:T(8,128)(2,1)S(1)}, bf16[54,16,256]{2,1,0:T(8,128)(2,1)S(1)}, u32[]{:S(2)}, u32[]{:S(2)}) collective-permute-start(bf16[54,16,256]{2,1,0:T(8,128)(2,1)S(1)} %shard_map.69), channel_id=1, source_target_pairs={{0,1},{1,0},{2,3},{3,2},{4,5},{5,4},{6,7},{7,6},{8,9},{9,8},{10,11... | collective-permute-start | bytes 1327112 | tf_op jit(solution)/shard_map/ppermute | solution.py:363
  14.5 13.5 %collective-permute-start.7 = (bf16[16,16,256]{2,1,0:T(8,128)(2,1)S(1)}, bf16[16,16,256]{2,1,0:T(8,128)(2,1)S(1)}, u32[]{:S(2)}, u32[]{:S(2)}) collective-permute-start(bf16[16,16,256]{2,1,0:T(8,128)(2,1)S(1)} %bitcast.12), channel_id=1, source_target_pairs={{0,8},{4,12},{8,0},{12,4},{1,9},{5,13},{9,1},{13,5},{2,10},{6,14},... | collective-permute-start | bytes 393224 | tf_op jit(solution)/shard_map/ppermute | solution.py:342
  17.2 12.7 %collective-permute-start.8 = (bf16[16,16,256]{2,1,0:T(8,128)(2,1)S(1)}, bf16[16,16,256]{2,1,0:T(8,128)(2,1)S(1)}, u32[]{:S(2)}, u32[]{:S(2)}) collective-permute-start(bf16[16,16,256]{2,1,0:T(8,128)(2,1)S(1)} %bitcast.13), channel_id=1, source_target_pairs={{0,12},{12,0},{1,13},{13,1},{2,14},{14,2},{3,15},{15,3},{16,28},{2... | collective-permute-start | bytes 393224 | tf_op jit(solution)/shard_map/ppermute | solution.py:351
  22.5 12.4 %collective-permute-start.3 = (bf16[4,4,16,256]{3,2,1,0:T(8,128)(2,1)S(1)}, bf16[4,4,16,256]{3,2,1,0:T(8,128)(2,1)S(1)}, u32[]{:S(2)}, u32[]{:S(2)}) collective-permute-start(bf16[4,4,16,256]{3,2,1,0:T(8,128)(2,1)S(1)} %get-tuple-element.25.refs_2_), channel_id=1, source_target_pairs={{0,2},{4,6},{8,10},{12,14},{2,0},{6,4},{10,8},{14,12},{1,3},{5,7},... | collective-permute-start | bytes 393224 | tf_op jit(solution)/shard_map/ppermute | solution.py:427
  24.1 13.8 %collective-permute-start.4 = (bf16[4,4,16,256]{3,2,1,0:T(8,128)(2,1)S(1)}, bf16[4,4,16,256]{3,2,1,0:T(8,128)(2,1)S(1)}, u32[]{:S(2)}, u32[]{:S(2)}) collective-permute-start(bf16[4,4,16,256]{3,2,1,0:T(8,128)(2,1)S(1)} %get-tuple-element.25.refs_2_), channel_id=1, source_target_pairs={{0,6},{4,10},{8,14},{12,2},{2,4},{6,8},{10,12},{14,0},{1,7},{5,11}... | collective-permute-start | bytes 393224 | tf_op jit(solution)/shard_map/ppermute | solution.py:427
  24.1 13.8 %collective-permute-start.5 = (bf16[4,4,16,256]{3,2,1,0:T(8,128)(2,1)S(1)}, bf16[4,4,16,256]{3,2,1,0:T(8,128)(2,1)S(1)}, u32[]{:S(2)}, u32[]{:S(2)}) collective-permute-start(bf16[4,4,16,256]{3,2,1,0:T(8,128)(2,1)S(1)} %get-tuple-element.25.refs_2_), channel_id=1, source_target_pairs={{0,10},{4,14},{8,2},{12,6},{2,8},{6,12},{10,0},{14,4},{1,11},{5,15... | collective-permute-start | bytes 393224 | tf_op jit(solution)/shard_map/ppermute | solution.py:427
  28.0 9.9 %collective-permute-start.6 = (bf16[4,4,16,256]{3,2,1,0:T(8,128)(2,1)S(1)}, bf16[4,4,16,256]{3,2,1,0:T(8,128)(2,1)S(1)}, u32[]{:S(2)}, u32[]{:S(2)}) collective-permute-start(bf16[4,4,16,256]{3,2,1,0:T(8,128)(2,1)S(1)} %get-tuple-element.25.refs_2_), channel_id=1, source_target_pairs={{0,14},{4,2},{8,6},{12,10},{2,12},{6,0},{10,4},{14,8},{1,15},{5,3}... | collective-permute-start | bytes 393224 | tf_op jit(solution)/shard_map/ppermute | solution.py:427
  38.0 2.0 %collective-permute-start.9 = (bf16[4,16,16,256]{3,2,1,0:T(8,128)(2,1)S(1)}, bf16[4,16,16,256]{3,2,1,0:T(8,128)(2,1)S(1)}, u32[]{:S(2)}, u32[]{:S(2)}) collective-permute-start(bf16[4,16,16,256]{3,2,1,0:T(8,128)(2,1)S(1)} %shard_map.73.g_ref), channel_id=1, source_target_pairs={{0,1},{1,0},{2,3},{3,2},{4,5},{5,4},{6,7},{7,6},{8,9},{9,8},{10,11... | collective-permute-start | bytes 1572872 | tf_op jit(solution)/shard_map/ppermute | solution.py:377

commit v9 on v7

--- a/solution.py
+++ b/solution.py
@@ -33,13 +33,14 @@
     return sig * (1.0 + hidden * (1.0 - sig))
 
 
-def pack_kernel(both_ref, xc_ref, cc_ref, right_ref, left_ref):
+def pack_kernel(both_ref, xc_ref, cc_ref, one_ref, two_ref):
     rows, cols, steps, channels = xc_ref.shape
     for n, dst in enumerate((xc_ref, cc_ref)):
         for r in range(rows):
             dst[r] = jnp.swapaxes(both_ref[n, :, :, r].reshape(steps, cols, channels), 0, 1)
     cells = rows * cols
-    for msg, col in ((right_ref, cols - 1), (left_ref, 0)):
+    odd = lax.rem(lax.axis_index("chan"), 2)
+    for msg, col in ((one_ref, (1 - odd) * (cols - 1)), (two_ref, odd * (cols - 1))):
         msg[:cells] = xc_ref[...].reshape(cells, steps, channels)
         for r in range(rows):
             msg[cells + r] = cc_ref[r, col]
@@ -57,16 +58,26 @@
     pick_ref[3 * share :, :] = jnp.where(chosen, 1.0, 0.0).astype(BF16)
 
 
-def side_kernel(x_ref, l_ref, r_ref, cot_ref, after_ref, side_ref):
+def by_parity(body, one, two):
+    odd = lax.rem(lax.axis_index("chan"), 2)
+    pl.when(odd == 0)(functools.partial(body, two, one))
+    pl.when(odd == 1)(functools.partial(body, one, two))
+
+
+def side_kernel(x_ref, one_ref, two_ref, cot_ref, after_ref, side_ref):
     rows, cols, steps, channels = x_ref.shape
     cells = rows * cols
     side_ref[:cells] = x_ref[...].reshape(cells, steps, channels)
-    side_ref[cells : 2 * cells] = l_ref[:cells]
-    side_ref[2 * cells : 3 * cells] = r_ref[:cells]
+    side_ref[cells : 2 * cells] = one_ref[:cells]
+    side_ref[2 * cells : 3 * cells] = two_ref[:cells]
     row = (1 - lax.axis_index("space")) * (rows - 1)
-    side_ref[3 * cells] = l_ref[cells + row]
     side_ref[3 * cells + 1 : 3 * cells + 1 + cols] = cot_ref[row]
-    side_ref[3 * cells + 1 + cols] = r_ref[cells + row]
+
+    def ends(left, right):
+        side_ref[3 * cells] = left[cells + row]
+        side_ref[3 * cells + 1 + cols] = right[cells + row]
+
+    by_parity(ends, one_ref, two_ref)
 
 
 def late_kernel(count, *refs):
@@ -107,40 +118,46 @@
 
 
 def first_kernel(
-    frames, x_ref, cot_ref, l_ref, r_ref, side_ref, w_ref, tw_ref,
+    frames, x_ref, cot_ref, one_ref, two_ref, side_ref, w_ref, tw_ref,
     slope_ref, out_ref, xw_ref, cw_ref, hg_ref,
 ):
     rows, cols, steps, channels = x_ref.shape
     cells = rows * cols
-    chan = lax.axis_size("chan")
     bottom = lax.axis_index("space")
+    near = (1 - bottom) * (rows + 2)
+    edge = (1 - bottom) * (rows + 1)
     xw_ref[2 : 2 + rows, 2 : 2 + cols] = x_ref[...]
     cw_ref[1 : 1 + rows, 1 : 1 + cols] = cot_ref[...]
-    for r in range(rows):
-        xw_ref[2 + r, 0:2] = l_ref[r * cols + cols - 2 : r * cols + cols]
-        xw_ref[2 + r, cols + 2 : cols + 4] = r_ref[r * cols : r * cols + 2]
-        cw_ref[1 + r, 0] = l_ref[cells + r]
-        cw_ref[1 + r, cols + 1] = r_ref[cells + r]
-    near = (1 - bottom) * (rows + 2)
-    far = bottom * (rows + 2)
+
+    def beside(left, right):
+        for r in range(rows):
+            xw_ref[2 + r, 0:2] = left[r * cols + cols - 2 : r * cols + cols]
+            xw_ref[2 + r, cols + 2 : cols + 4] = right[r * cols : r * cols + 2]
+            cw_ref[1 + r, 0] = left[cells + r]
+            cw_ref[1 + r, cols + 1] = right[cells + r]
+
+    def corners(left, right):
+        for i in range(2):
+            at = (bottom * (rows - 2) + i) * cols
+            xw_ref[near + i, 0:2] = side_ref[pl.ds(left * cells + at + cols - 2, 2)]
+            xw_ref[near + i, cols + 2 : cols + 4] = side_ref[pl.ds(right * cells + at, 2)]
+
+    by_parity(beside, one_ref, two_ref)
+    by_parity(corners, 1, 2)
     for i in range(2):
         at = (bottom * (rows - 2) + i) * cols
         xw_ref[near + i, 2 : 2 + cols] = side_ref[pl.ds(at, cols)]
-        xw_ref[near + i, 0:2] = side_ref[pl.ds(cells + at + cols - 2, 2)]
-        xw_ref[near + i, cols + 2 : cols + 4] = side_ref[pl.ds(2 * cells + at, 2)]
-        xw_ref[far + i] = jnp.zeros(xw_ref.shape[1:], BF16)
-    near = (1 - bottom) * (rows + 1)
-    far = bottom * (rows + 1)
-    cw_ref[near] = side_ref[3 * cells :]
-    cw_ref[far] = jnp.zeros(cw_ref.shape[1:], BF16)
+        xw_ref[bottom * (rows + 2) + i] = jnp.zeros(xw_ref.shape[1:], BF16)
+    cw_ref[edge] = side_ref[3 * cells :]
+    cw_ref[bottom * (rows + 1)] = jnp.zeros(cw_ref.shape[1:], BF16)
     me = lax.axis_index("chan")
-    for end, c in ((0, 0), (chan - 1, cols + 2)):
+    for end, c in ((0, 0), (lax.axis_size("chan") - 1, cols + 2)):
 
         @pl.when(me == end)
         def _(c=c):
             xw_ref[:, c : c + 2] = jnp.zeros((rows + 4, 2, steps, channels), BF16)
-            edge = min(c, cols + 1)
-            cw_ref[:, edge : edge + 1] = jnp.zeros((rows + 2, 1, steps, channels), BF16)
+            last = min(c, cols + 1)
+            cw_ref[:, last : last + 1] = jnp.zeros((rows + 2, 1, steps, channels), BF16)
 
     hidden = None
     for u in range(3):
@@ -185,19 +202,17 @@
     clear_rim(padded)
     chan, cells = len(pieces), rows * cols
     me = lax.axis_index("chan")
+    turn = 1 - 2 * lax.rem(me, 2)
     bottom = lax.axis_index("space")
-    for d, piece in enumerate(pieces):
-        place = 1 + lax.rem(me - d + chan, chan) * cols
+    for n, piece in enumerate(pieces):
+        place = 1 + lax.rem(me + (0, turn, -turn, *range(-2, 1 - chan, -1))[n] + chan, chan) * cols
         for r in range(rows):
-            near = piece[r] if d == 0 else piece[r * cols : (r + 1) * cols]
+            near = piece[r] if n == 0 else piece[r * cols : (r + 1) * cols]
             padded[1 + bottom * rows + r, pl.ds(place, cols)] = near
-            source, n = (late, d - 2) if 1 < d < chan - 1 else (side, min(d, 2))
-            at = n * cells + r * cols
-            far = 1 + (1 - bottom) * rows + r
-            if source is late:
-                padded[far, pl.ds(place, cols)] = late[1 - bottom, at : at + cols]
-            else:
-                padded[far, pl.ds(place, cols)] = side[at : at + cols]
+            at = r * cols + (n if n < 3 else n - 3) * cells
+            span = pl.ds(at, cols)
+            other = side[span] if n < 3 else late[1 - bottom, span]
+            padded[1 + (1 - bottom) * rows + r, pl.ds(place, cols)] = other
 
 
 def own_window(gp_ref, slope_ref, w_ref, tw_ref, hg_ref, frames, rows, cols):
@@ -311,7 +326,7 @@
         return jax.ShapeDtypeStruct(shape + cell, BF16)
 
     beside = rows * cols + rows
-    x_own, cot_own, to_right, to_left = call(
+    x_own, cot_own, first_msg, second_msg = call(
         pack_kernel,
         (bf16(rows, cols), bf16(rows, cols), bf16(beside), bf16(beside)),
         [],
@@ -341,12 +356,10 @@
         return lax.ppermute(message, "chan", [(i, (i + by) % chan) for i in range(chan)])
 
     x_flat = x_own.reshape((rows * cols,) + cell)
-    pieces = [
-        x_own,
-        turned(to_right, 1),
-        *[turned(x_flat, d) for d in range(2, chan - 1)],
-        turned(to_left, chan - 1),
-    ]
+    one = lax.ppermute(first_msg, "chan", [(i, i ^ 1) for i in range(chan)])
+    two = lax.ppermute(second_msg, "chan", [(i, (i + 2 * (i % 2) - 1) % chan) for i in range(chan)])
+    far = [turned(x_flat, d) for d in range(2, chan - 1)]
+    pieces = [x_own, one, two, *far]
     swap = [(0, 1), (1, 0)]
     to_side = call(
         side_kernel,
@@ -355,7 +368,7 @@
         16,
         1_000_000,
         1_000_000,
-        x_own, pieces[1], pieces[-1], cot_own, pick,
+        x_own, one, two, cot_own, pick,
         places=[VM] * 4 + [pl.ANY],
     )
     from_side = lax.ppermute(to_side, "space", swap)
@@ -385,7 +398,7 @@
         20,
         1,
         1,
-        x_own, cot_own, pieces[1], pieces[-1], from_side, w, tw,
+        x_own, cot_own, one, two, from_side, w, tw,
     )
 
     padded = pltpu.VMEM((height + 2, width + 2) + cell, BF16)
@@ -402,7 +415,6 @@
                 *g_all, cot_own, slope_w, w, tw,
             )
         if not tick:
-            far = pieces[2:-1]
             to_late = call(
                 functools.partial(late_kernel, len(far)),
                 bf16(len(far) * rows * cols),

time: 43.7 us -> 44.5 us (1.018)
  starting transfers between devices: 12.4 us -> 13.7 us
  waiting for transfers between devices: 14.2 us -> 13.7 us
    ppermute x0 -> x2, starting transfers between devices: none -> 5.56 us  [the longest x1 3.09 us: per_device(): one = lax.ppermute(first_msg, 'chan', [(i, i ^ 1) for i in range(chan)])]
    ppermute x0 -> x2, waiting for transfers between devices: none -> 5.14 us  [the longest x1 5.14 us: per_device(): lax.ppermute(second_msg, 'chan', [(i, (i + 2 * (i % 2) - 1) % chan) for i...]
    ppermute x3 -> x1, waiting for transfers between devices: 5.09 us -> 0.01 us  [turned(): lax.ppermute(message, 'chan', [(i, (i + by) % chan) for i in range(chan)])]
    ppermute x3 -> x1, starting transfers between devices: 6.53 us -> 1.83 us  [turned(): lax.ppermute(message, 'chan', [(i, (i + by) % chan) for i in range(chan)])]
  transfers between devices with their start and end apart: 9 -> 9, of which waited for: 6 -> 3; matrix products, arithmetic and copies ran while one was open for 0% -> 0% of each run, Pallas kernels for 12% -> 12%
where the time goes in v9:
time: 44.5 us; the launch traced here: 44.3 us
  starting transfers between devices  13.7 us (31%)
  waiting for transfers between devices  13.7 us (31%)
  Pallas kernels  10.8 us (24%)
  local copies, waits for them, and re-layouts  2.27 us (5%)
  blocking collectives  1.99 us (4%)
  other arithmetic  1.16 us (3%)
  between operations  0.71 us (2%)
    pallas_call x8, Pallas kernels, call(): pl.pallas_call(kernel, out_shape=outs, in_specs=[pl.BlockSpec(memory_spac...  10.8 us
    ppermute x4, waiting for transfers between devices, per_device(): arrived.append(lax.ppermute(payload, ('chan', 'pipe'), pairs))  6.68 us
    ppermute x4, starting transfers between devices, per_device(): arrived.append(lax.ppermute(payload, ('chan', 'pipe'), pairs))  6.15 us
    ppermute x1, waiting for transfers between devices, per_device(): lax.ppermute(second_msg, 'chan', [(i, (i + 2 * (i % 2) - 1) % chan) for i...  5.14 us
    ppermute x1, starting transfers between devices, per_device(): one = lax.ppermute(first_msg, 'chan', [(i, i ^ 1) for i in range(chan)])  3.09 us
    ppermute x1, starting transfers between devices, per_device(): lax.ppermute(second_msg, 'chan', [(i, (i + 2 * (i % 2) - 1) % chan) for i...  2.47 us
    unnamed x4, local copies, waits for them, and re-layouts  2.27 us
    all_gather x1, blocking collectives, per_device(): from_late = lax.all_gather(to_late, 'space', axis=0, tiled=False)  1.99 us
  transfers between devices with their start and end apart: 9, of which 3 were waited for; matrix products, arithmetic and copies ran while one was open for 0% of the time, Pallas kernels for 12%

profile of v9, /device:TPU:0, one launch (start us, length us, event | category | flops | bytes accessed | tf_op | source)
XLA Modules:
  0.0 44.3 jit_solution(14013379599617092522)
XLA Ops:
  0.6 1.2 %pad_maximum_fusion.both_ref = bf16[2,2,8,4,4,256]{5,4,3,2,1,0:T(4,128)(2,1)S(1)} fusion(bf16[1,2,8,4,4,256]{5,4,3,2,1,0:T(4,128)(2,1)} %bitcast.16, bf16[1,2,8,4,4,256]{5,4,3,2,1,0:T(4,128)(2,1)} %param.4), kind=kLoop, calls=%fused_computation | loop fusion | flops 131072 | bytes 524288 | tf_op jit(solution)/shard_map/stack | solution.py:336
  1.8 0.1 shard_map.67
  1.9 3.1 %collective-permute-start = (bf16[20,16,256]{2,1,0:T(8,128)(2,1)S(1)}, bf16[20,16,256]{2,1,0:T(8,128)(2,1)S(1)}, u32[]{:S(2)}, u32[]{:S(2)}) collective-permute-start(bf16[20,16,256]{2,1,0:T(8,128)(2,1)S(1)} %get-tuple-element.20), channel_id=1, source_target_pairs={{0,4},{4,0},{8,12},{12,8},{1,5},{5,1},{9,13},{13,9},{2,6},{6,2},{1... | collective-permute-start | bytes 491528 | tf_op jit(solution)/shard_map/ppermute | solution.py:359
  5.0 2.5 %collective-permute-start.1 = (bf16[20,16,256]{2,1,0:T(8,128)(2,1)S(1)}, bf16[20,16,256]{2,1,0:T(8,128)(2,1)S(1)}, u32[]{:S(2)}, u32[]{:S(2)}) collective-permute-start(bf16[20,16,256]{2,1,0:T(8,128)(2,1)S(1)} %get-tuple-element.21), channel_id=1, source_target_pairs={{0,12},{4,8},{8,4},{12,0},{1,13},{5,9},{9,5},{13,1},{2,14},{6,10},... | collective-permute-start | bytes 491528 | tf_op jit(solution)/shard_map/ppermute | solution.py:360
  7.5 0.0 copy-start
  7.5 1.3 %copy-done = bf16[1,3,3,256,256]{4,3,2,1,0:T(8,128)(2,1)S(1)} copy-done((bf16[1,3,3,256,256]{4,3,2,1,0:T(8,128)(2,1)S(1)}, bf16[1,3,3,256,256]{4,3,2,1,0:T(8,128)(2,1)}, u32[]{:S(2)}) %copy-start) | copy-done | bytes 1179672
  8.7 0.0 copy-start.1
  8.7 1.0 %copy-done.1 = bf16[1,3,256,256]{3,2,1,0:T(8,128)(2,1)S(1)} copy-done((bf16[1,3,256,256]{3,2,1,0:T(8,128)(2,1)S(1)}, bf16[1,3,256,256]{3,2,1,0:T(8,128)(2,1)}, u32[]{:S(2)}) %copy-start.1) | copy-done | bytes 393240
  9.7 0.1 shard_map.68
  9.8 0.0 collective-permute-done.one_ref.refs_1_
  9.8 5.1 %collective-permute-done.1.two_ref.refs_2_ = bf16[20,16,256]{2,1,0:T(8,128)(2,1)S(1)} collective-permute-done((bf16[20,16,256]{2,1,0:T(8,128)(2,1)S(1)}, bf16[20,16,256]{2,1,0:T(8,128)(2,1)S(1)}, u32[]{:S(2)}, u32[]{:S(2)}) %collective-permute-start.1) | collective-permute-done | bytes 163872 | tf_op jit(solution)/shard_map/ppermute | solution.py:360
  15.0 0.1 collective-permute-start.2
  15.1 1.8 %collective-permute-start.7 = (bf16[16,16,256]{2,1,0:T(8,128)(2,1)S(1)}, bf16[16,16,256]{2,1,0:T(8,128)(2,1)S(1)}, u32[]{:S(2)}, u32[]{:S(2)}) collective-permute-start(bf16[16,16,256]{2,1,0:T(8,128)(2,1)S(1)} %bitcast.12), channel_id=1, source_target_pairs={{0,8},{4,12},{8,0},{12,4},{1,9},{5,13},{9,1},{13,5},{2,10},{6,14},... | collective-permute-start | bytes 393224 | tf_op jit(solution)/shard_map/ppermute | solution.py:356
  16.9 0.0 collective-permute-done.2.side_ref.refs_4_
  16.9 2.2 %shard_map.70 = (f32[576,256]{1,0:T(8,128)S(1)}, bf16[4,4,16,256]{3,2,1,0:T(8,128)(2,1)S(1)}) custom-call(bf16[4,4,16,256]{3,2,1,0:T(8,128)(2,1)S(1)} %get-tuple-element.18.after_ref.x_ref.refs_0_, bf16[4,4,16,256]{3,2,1,0:T(8,128)(2,1)S(1)} %get-tuple-element.19.cot_ref, bf16[20,16,256]{2,1,0:T(8,128)(2,1)S(1)} %collective-permute-done.one_ref.refs_1_, ...), custom_call_target="tpu_custom_call" | custom-call | flops 1 | bytes 1 | tf_op jit(solution)/shard_map/pallas_call | solution.py:304
  19.1 1.6 %collective-permute-start.3 = (bf16[4,4,16,256]{3,2,1,0:T(8,128)(2,1)S(1)}, bf16[4,4,16,256]{3,2,1,0:T(8,128)(2,1)S(1)}, u32[]{:S(2)}, u32[]{:S(2)}) collective-permute-start(bf16[4,4,16,256]{3,2,1,0:T(8,128)(2,1)S(1)} %get-tuple-element.25.refs_1_), channel_id=1, source_target_pairs={{0,2},{4,6},{8,10},{12,14},{2,0},{6,4},{10,8},{14,12},{1,3},{5,7},... | collective-permute-start | bytes 393224 | tf_op jit(solution)/shard_map/ppermute | solution.py:437
  20.7 1.4 %collective-permute-start.6 = (bf16[4,4,16,256]{3,2,1,0:T(8,128)(2,1)S(1)}, bf16[4,4,16,256]{3,2,1,0:T(8,128)(2,1)S(1)}, u32[]{:S(2)}, u32[]{:S(2)}) collective-permute-start(bf16[4,4,16,256]{3,2,1,0:T(8,128)(2,1)S(1)} %get-tuple-element.25.refs_1_), channel_id=1, source_target_pairs={{0,14},{4,2},{8,6},{12,10},{2,12},{6,0},{10,4},{14,8},{1,15},{5,3}... | collective-permute-start | bytes 393224 | tf_op jit(solution)/shard_map/ppermute | solution.py:437
  22.0 1.5 %collective-permute-start.5 = (bf16[4,4,16,256]{3,2,1,0:T(8,128)(2,1)S(1)}, bf16[4,4,16,256]{3,2,1,0:T(8,128)(2,1)S(1)}, u32[]{:S(2)}, u32[]{:S(2)}) collective-permute-start(bf16[4,4,16,256]{3,2,1,0:T(8,128)(2,1)S(1)} %get-tuple-element.25.refs_1_), channel_id=1, source_target_pairs={{0,10},{4,14},{8,2},{12,6},{2,8},{6,12},{10,0},{14,4},{1,11},{5,15... | collective-permute-start | bytes 393224 | tf_op jit(solution)/shard_map/ppermute | solution.py:437
  23.5 1.7 %collective-permute-start.4 = (bf16[4,4,16,256]{3,2,1,0:T(8,128)(2,1)S(1)}, bf16[4,4,16,256]{3,2,1,0:T(8,128)(2,1)S(1)}, u32[]{:S(2)}, u32[]{:S(2)}) collective-permute-start(bf16[4,4,16,256]{3,2,1,0:T(8,128)(2,1)S(1)} %get-tuple-element.25.refs_1_), channel_id=1, source_target_pairs={{0,6},{4,10},{8,14},{12,2},{2,4},{6,8},{10,12},{14,0},{1,7},{5,11}... | collective-permute-start | bytes 393224 | tf_op jit(solution)/shard_map/ppermute | solution.py:437
  25.2 0.0 collective-permute-done.7.refs_0_.refs_3_
  25.3 2.0 %all-gather = bf16[32,16,256]{2,1,0:T(8,128)(2,1)S(1)} all-gather(bf16[16,16,256]{2,1,0:T(8,128)(2,1)S(1)} %shard_map.71), channel_id=2, replica_groups=mesh['groups'=2,'chan'=4,'pipe'=2,'space'=2] {'space'}, dimensions={0}, use_global_device_ids=true | all-gather | bytes 393216 | tf_op jit(solution)/shard_map/all_gather | solution.py:429
  27.3 0.0 collective-permute-done.3.refs_7_.refs_0_
  27.3 2.9 %shard_map.72 = (bf16[256,2048]{1,0:T(8,128)(2,1)S(1)}, bf16[256,2048]{1,0:T(8,128)(2,1)S(1)}, f32[2048,64]{1,0:T(8,128)S(1)}) custom-call(bf16[4,4,16,256]{3,2,1,0:T(8,128)(2,1)S(1)} %get-tuple-element.18.after_ref.x_ref.refs_0_, bf16[20,16,256]{2,1,0:T(8,128)(2,1)S(1)} %collective-permute-done.one_ref.refs_1_, ...), custom_call_target="tpu_custom_call" | custom-call | flops 1 | bytes 1 | tf_op jit(solution)/shard_map/pallas_call | solution.py:304
  30.2 0.0 collective-permute-done.6.refs_3_
  30.2 6.7 %collective-permute-done.5.refs_2_ = bf16[4,4,16,256]{3,2,1,0:T(8,128)(2,1)S(1)} collective-permute-done((bf16[4,4,16,256]{3,2,1,0:T(8,128)(2,1)S(1)}, bf16[4,4,16,256]{3,2,1,0:T(8,128)(2,1)S(1)}, u32[]{:S(2)}, u32[]{:S(2)}) %collective-permute-start.5) | collective-permute-done | bytes 131104 | tf_op jit(solution)/shard_map/ppermute | solution.py:437
  36.9 0.0 collective-permute-done.4.refs_1_
  36.9 0.1 collective-permute-start.8
  37.0 1.9 %collective-permute-done.8.other_ref = bf16[4,16,16,256]{3,2,1,0:T(8,128)(2,1)S(1)} collective-permute-done((bf16[4,16,16,256]{3,2,1,0:T(8,128)(2,1)S(1)}, bf16[4,16,16,256]{3,2,1,0:T(8,128)(2,1)S(1)}, u32[]{:S(2)}, u32[]{:S(2)}) %collective-permute-start.8) | collective-permute-done | bytes 524320 | tf_op jit(solution)/shard_map/ppermute | solution.py:388
  38.9 5.4 %shard_map.74 = (bf16[2,8,4,4,256]{4,3,2,1,0:T(4,128)(2,1)}, f32[9,64,256]{2,1,0:T(8,128)}, f32[3,64,256]{2,1,0:T(8,128)}) custom-call(bf16[4,16,16,256]{3,2,1,0:T(8,128)(2,1)S(1)} %shard_map.73.g_ref, bf16[4,16,16,256]{3,2,1,0:T(8,128)(2,1)S(1)} %collective-permute-done.8.other_ref, f32[576,256]{1,0:T(8,128)S(1)} %get-tuple-element.27.slope_w_ref, ...), custom_call_target="tpu_custom_call" | custom-call | flops 1358954496 | bytes 8000000 | tf_op jit(solution)/shard_map/pallas_call | solution.py:304
  (3 shorter events, 0.1 us)
Async XLA Ops:
  1.9 7.9 %collective-permute-start = (bf16[20,16,256]{2,1,0:T(8,128)(2,1)S(1)}, bf16[20,16,256]{2,1,0:T(8,128)(2,1)S(1)}, u32[]{:S(2)}, u32[]{:S(2)}) collective-permute-start(bf16[20,16,256]{2,1,0:T(8,128)(2,1)S(1)} %get-tuple-element.20), channel_id=1, source_target_pairs={{0,4},{4,0},{8,12},{12,8},{1,5},{5,1},{9,13},{13,9},{2,6},{6,2},{1... | collective-permute-start | bytes 491528 | tf_op jit(solution)/shard_map/ppermute | solution.py:359
  5.0 10.0 %collective-permute-start.1 = (bf16[20,16,256]{2,1,0:T(8,128)(2,1)S(1)}, bf16[20,16,256]{2,1,0:T(8,128)(2,1)S(1)}, u32[]{:S(2)}, u32[]{:S(2)}) collective-permute-start(bf16[20,16,256]{2,1,0:T(8,128)(2,1)S(1)} %get-tuple-element.21), channel_id=1, source_target_pairs={{0,12},{4,8},{8,4},{12,0},{1,13},{5,9},{9,5},{13,1},{2,14},{6,10},... | collective-permute-start | bytes 491528 | tf_op jit(solution)/shard_map/ppermute | solution.py:360
  7.5 1.3 %copy-start = (bf16[1,3,3,256,256]{4,3,2,1,0:T(8,128)(2,1)S(1)}, bf16[1,3,3,256,256]{4,3,2,1,0:T(8,128)(2,1)}, u32[]{:S(2)}) copy-start(bf16[1,3,3,256,256]{4,3,2,1,0:T(8,128)(2,1)} %param.6) | copy-start | bytes 3538948
  8.7 1.0 %copy-start.1 = (bf16[1,3,256,256]{3,2,1,0:T(8,128)(2,1)S(1)}, bf16[1,3,256,256]{3,2,1,0:T(8,128)(2,1)}, u32[]{:S(2)}) copy-start(bf16[1,3,256,256]{3,2,1,0:T(8,128)(2,1)} %param.7) | copy-start | bytes 1179652
  15.0 1.9 %collective-permute-start.2 = (bf16[54,16,256]{2,1,0:T(8,128)(2,1)S(1)}, bf16[54,16,256]{2,1,0:T(8,128)(2,1)S(1)}, u32[]{:S(2)}, u32[]{:S(2)}) collective-permute-start(bf16[54,16,256]{2,1,0:T(8,128)(2,1)S(1)} %shard_map.69), channel_id=1, source_target_pairs={{0,1},{1,0},{2,3},{3,2},{4,5},{5,4},{6,7},{7,6},{8,9},{9,8},{10,11... | collective-permute-start | bytes 1327112 | tf_op jit(solution)/shard_map/ppermute | solution.py:374
  15.1 10.2 %collective-permute-start.7 = (bf16[16,16,256]{2,1,0:T(8,128)(2,1)S(1)}, bf16[16,16,256]{2,1,0:T(8,128)(2,1)S(1)}, u32[]{:S(2)}, u32[]{:S(2)}) collective-permute-start(bf16[16,16,256]{2,1,0:T(8,128)(2,1)S(1)} %bitcast.12), channel_id=1, source_target_pairs={{0,8},{4,12},{8,0},{12,4},{1,9},{5,13},{9,1},{13,5},{2,10},{6,14},... | collective-permute-start | bytes 393224 | tf_op jit(solution)/shard_map/ppermute | solution.py:356
  19.1 8.2 %collective-permute-start.3 = (bf16[4,4,16,256]{3,2,1,0:T(8,128)(2,1)S(1)}, bf16[4,4,16,256]{3,2,1,0:T(8,128)(2,1)S(1)}, u32[]{:S(2)}, u32[]{:S(2)}) collective-permute-start(bf16[4,4,16,256]{3,2,1,0:T(8,128)(2,1)S(1)} %get-tuple-element.25.refs_1_), channel_id=1, source_target_pairs={{0,2},{4,6},{8,10},{12,14},{2,0},{6,4},{10,8},{14,12},{1,3},{5,7},... | collective-permute-start | bytes 393224 | tf_op jit(solution)/shard_map/ppermute | solution.py:437
  20.7 9.5 %collective-permute-start.6 = (bf16[4,4,16,256]{3,2,1,0:T(8,128)(2,1)S(1)}, bf16[4,4,16,256]{3,2,1,0:T(8,128)(2,1)S(1)}, u32[]{:S(2)}, u32[]{:S(2)}) collective-permute-start(bf16[4,4,16,256]{3,2,1,0:T(8,128)(2,1)S(1)} %get-tuple-element.25.refs_1_), channel_id=1, source_target_pairs={{0,14},{4,2},{8,6},{12,10},{2,12},{6,0},{10,4},{14,8},{1,15},{5,3}... | collective-permute-start | bytes 393224 | tf_op jit(solution)/shard_map/ppermute | solution.py:437
  22.0 14.8 %collective-permute-start.5 = (bf16[4,4,16,256]{3,2,1,0:T(8,128)(2,1)S(1)}, bf16[4,4,16,256]{3,2,1,0:T(8,128)(2,1)S(1)}, u32[]{:S(2)}, u32[]{:S(2)}) collective-permute-start(bf16[4,4,16,256]{3,2,1,0:T(8,128)(2,1)S(1)} %get-tuple-element.25.refs_1_), channel_id=1, source_target_pairs={{0,10},{4,14},{8,2},{12,6},{2,8},{6,12},{10,0},{14,4},{1,11},{5,15... | collective-permute-start | bytes 393224 | tf_op jit(solution)/shard_map/ppermute | solution.py:437
  23.5 13.3 %collective-permute-start.4 = (bf16[4,4,16,256]{3,2,1,0:T(8,128)(2,1)S(1)}, bf16[4,4,16,256]{3,2,1,0:T(8,128)(2,1)S(1)}, u32[]{:S(2)}, u32[]{:S(2)}) collective-permute-start(bf16[4,4,16,256]{3,2,1,0:T(8,128)(2,1)S(1)} %get-tuple-element.25.refs_1_), channel_id=1, source_target_pairs={{0,6},{4,10},{8,14},{12,2},{2,4},{6,8},{10,12},{14,0},{1,7},{5,11}... | collective-permute-start | bytes 393224 | tf_op jit(solution)/shard_map/ppermute | solution.py:437
  36.9 2.0 %collective-permute-start.8 = (bf16[4,16,16,256]{3,2,1,0:T(8,128)(2,1)S(1)}, bf16[4,16,16,256]{3,2,1,0:T(8,128)(2,1)S(1)}, u32[]{:S(2)}, u32[]{:S(2)}) collective-permute-start(bf16[4,16,16,256]{3,2,1,0:T(8,128)(2,1)S(1)} %shard_map.73.g_ref), channel_id=1, source_target_pairs={{0,1},{1,0},{2,3},{3,2},{4,5},{5,4},{6,7},{7,6},{8,9},{9,8},{10,11... | collective-permute-start | bytes 1572872 | tf_op jit(solution)/shard_map/ppermute | solution.py:388

commit v10 on v7

--- a/solution.py
+++ b/solution.py
@@ -160,7 +160,7 @@
     rows, cols, steps, channels = pieces[0].shape
     me = lax.axis_index("chan")
     for d, piece in enumerate(pieces):
-        out_ref[:, pl.ds(lax.rem(me - d + chan, chan) * cols, cols)] = piece[...]
+        out_ref[:, pl.ds((me ^ d) * cols, cols)] = piece[...]
 
 
 def clear_rim(padded):
@@ -418,7 +418,7 @@
         arrived = []
         for d in range(chan):
             pairs = [
-                (c * depth + p, (c + d) % chan * depth + (p - 1) % depth)
+                (c * depth + p, (c ^ d) * depth + (p - 1) % depth)
                 for p in range(depth)
                 for c in range(chan)
             ]

time: 43.7 us -> 45.2 us (1.034)
  starting transfers between devices: 12.4 us -> 13.5 us
    ppermute x3, waiting for transfers between devices: 5.09 us -> 8.86 us  [turned(): lax.ppermute(message, 'chan', [(i, (i + by) % chan) for i in range(chan)])]
    ppermute x4, waiting for transfers between devices: 6.76 us -> 3.42 us  [per_device(): arrived.append(lax.ppermute(payload, ('chan', 'pipe'), pairs))]
    ppermute x4, starting transfers between devices: 5.74 us -> 6.81 us  [per_device(): arrived.append(lax.ppermute(payload, ('chan', 'pipe'), pairs))]
where the time goes in v10:
time: 45.2 us; the launch traced here: 45 us
  waiting for transfers between devices  14.6 us (32%)
  starting transfers between devices  13.5 us (30%)
  Pallas kernels  10.8 us (24%)
  local copies, waits for them, and re-layouts  2.27 us (5%)
  blocking collectives  1.99 us (4%)
  other arithmetic  1.16 us (3%)
  between operations  0.7 us (2%)
    pallas_call x8, Pallas kernels, call(): pl.pallas_call(kernel, out_shape=outs, in_specs=[pl.BlockSpec(memory_spac...  10.8 us
    ppermute x3, waiting for transfers between devices, turned(): lax.ppermute(message, 'chan', [(i, (i + by) % chan) for i in range(chan)])  8.86 us
    ppermute x4, starting transfers between devices, per_device(): arrived.append(lax.ppermute(payload, ('chan', 'pipe'), pairs))  6.81 us
    ppermute x3, starting transfers between devices, turned(): lax.ppermute(message, 'chan', [(i, (i + by) % chan) for i in range(chan)])  6.53 us
    ppermute x4, waiting for transfers between devices, per_device(): arrived.append(lax.ppermute(payload, ('chan', 'pipe'), pairs))  3.42 us
    unnamed x4, local copies, waits for them, and re-layouts  2.27 us
    all_gather x1, blocking collectives, per_device(): from_late = lax.all_gather(to_late, 'space', axis=0, tiled=False)  1.99 us
    ppermute x1, waiting for transfers between devices, gathered(): return (half, lax.ppermute(half, 'space', swap))  1.9 us
  transfers between devices with their start and end apart: 9, of which 6 were waited for; matrix products, arithmetic and copies ran while one was open for 0% of the time, Pallas kernels for 12%

profile of v10, /device:TPU:0, one launch (start us, length us, event | category | flops | bytes accessed | tf_op | source)
XLA Modules:
  0.0 45.0 jit_solution(10823902612984554937)
XLA Ops:
  0.6 1.2 %pad_maximum_fusion.both_ref = bf16[2,2,8,4,4,256]{5,4,3,2,1,0:T(4,128)(2,1)S(1)} fusion(bf16[1,2,8,4,4,256]{5,4,3,2,1,0:T(4,128)(2,1)} %bitcast.16, bf16[1,2,8,4,4,256]{5,4,3,2,1,0:T(4,128)(2,1)} %param.4), kind=kLoop, calls=%fused_computation | loop fusion | flops 131072 | bytes 524288 | tf_op jit(solution)/shard_map/stack | solution.py:321
  1.8 0.1 shard_map.67
  1.9 3.1 %collective-permute-start = (bf16[20,16,256]{2,1,0:T(8,128)(2,1)S(1)}, bf16[20,16,256]{2,1,0:T(8,128)(2,1)S(1)}, u32[]{:S(2)}, u32[]{:S(2)}) collective-permute-start(bf16[20,16,256]{2,1,0:T(8,128)(2,1)S(1)} %get-tuple-element.20), channel_id=1, source_target_pairs={{0,4},{4,8},{8,12},{12,0},{1,5},{5,9},{9,13},{13,1},{2,6},{6,10},{... | collective-permute-start | bytes 491528 | tf_op jit(solution)/shard_map/ppermute | solution.py:341
  5.0 2.1 %collective-permute-start.1 = (bf16[20,16,256]{2,1,0:T(8,128)(2,1)S(1)}, bf16[20,16,256]{2,1,0:T(8,128)(2,1)S(1)}, u32[]{:S(2)}, u32[]{:S(2)}) collective-permute-start(bf16[20,16,256]{2,1,0:T(8,128)(2,1)S(1)} %get-tuple-element.21), channel_id=1, source_target_pairs={{0,12},{4,0},{8,4},{12,8},{1,13},{5,1},{9,5},{13,9},{2,14},{6,2},{... | collective-permute-start | bytes 491528 | tf_op jit(solution)/shard_map/ppermute | solution.py:341
  7.1 0.0 copy-start
  7.1 1.3 %copy-done = bf16[1,3,3,256,256]{4,3,2,1,0:T(8,128)(2,1)S(1)} copy-done((bf16[1,3,3,256,256]{4,3,2,1,0:T(8,128)(2,1)S(1)}, bf16[1,3,3,256,256]{4,3,2,1,0:T(8,128)(2,1)}, u32[]{:S(2)}) %copy-start) | copy-done | bytes 1179672
  8.3 0.0 copy-start.1
  8.3 1.0 %copy-done.1 = bf16[1,3,256,256]{3,2,1,0:T(8,128)(2,1)S(1)} copy-done((bf16[1,3,256,256]{3,2,1,0:T(8,128)(2,1)S(1)}, bf16[1,3,256,256]{3,2,1,0:T(8,128)(2,1)}, u32[]{:S(2)}) %copy-start.1) | copy-done | bytes 393240
  9.3 0.1 shard_map.68
  9.4 2.6 %collective-permute-done.l_ref.refs_1_ = bf16[20,16,256]{2,1,0:T(8,128)(2,1)S(1)} collective-permute-done((bf16[20,16,256]{2,1,0:T(8,128)(2,1)S(1)}, bf16[20,16,256]{2,1,0:T(8,128)(2,1)S(1)}, u32[]{:S(2)}, u32[]{:S(2)}) %collective-permute-start) | collective-permute-done | bytes 163872 | tf_op jit(solution)/shard_map/ppermute | solution.py:341
  12.1 2.1 %collective-permute-done.1.r_ref.refs_3_ = bf16[20,16,256]{2,1,0:T(8,128)(2,1)S(1)} collective-permute-done((bf16[20,16,256]{2,1,0:T(8,128)(2,1)S(1)}, bf16[20,16,256]{2,1,0:T(8,128)(2,1)S(1)}, u32[]{:S(2)}, u32[]{:S(2)}) %collective-permute-start.1) | collective-permute-done | bytes 163872 | tf_op jit(solution)/shard_map/ppermute | solution.py:341
  14.2 0.1 collective-permute-start.2
  14.3 1.4 %collective-permute-start.7 = (bf16[16,16,256]{2,1,0:T(8,128)(2,1)S(1)}, bf16[16,16,256]{2,1,0:T(8,128)(2,1)S(1)}, u32[]{:S(2)}, u32[]{:S(2)}) collective-permute-start(bf16[16,16,256]{2,1,0:T(8,128)(2,1)S(1)} %bitcast.12), channel_id=1, source_target_pairs={{0,8},{4,12},{8,0},{12,4},{1,9},{5,13},{9,1},{13,5},{2,10},{6,14},... | collective-permute-start | bytes 393224 | tf_op jit(solution)/shard_map/ppermute | solution.py:341
  15.6 0.4 collective-permute-done.2.side_ref.refs_4_
  16.0 2.1 %shard_map.70 = (f32[576,256]{1,0:T(8,128)S(1)}, bf16[4,4,16,256]{3,2,1,0:T(8,128)(2,1)S(1)}) custom-call(bf16[4,4,16,256]{3,2,1,0:T(8,128)(2,1)S(1)} %get-tuple-element.18.after_ref.x_ref.refs_0_, bf16[4,4,16,256]{3,2,1,0:T(8,128)(2,1)S(1)} %get-tuple-element.19.cot_ref, bf16[20,16,256]{2,1,0:T(8,128)(2,1)S(1)} %collective-permute-done.l_ref.refs_1_, ...), custom_call_target="tpu_custom_call" | custom-call | flops 1 | bytes 1 | tf_op jit(solution)/shard_map/pallas_call | solution.py:289
  18.2 1.6 %collective-permute-start.3 = (bf16[4,4,16,256]{3,2,1,0:T(8,128)(2,1)S(1)}, bf16[4,4,16,256]{3,2,1,0:T(8,128)(2,1)S(1)}, u32[]{:S(2)}, u32[]{:S(2)}) collective-permute-start(bf16[4,4,16,256]{3,2,1,0:T(8,128)(2,1)S(1)} %get-tuple-element.25.refs_1_), channel_id=1, source_target_pairs={{0,2},{4,6},{8,10},{12,14},{2,0},{6,4},{10,8},{14,12},{1,3},{5,7},... | collective-permute-start | bytes 393224 | tf_op jit(solution)/shard_map/ppermute | solution.py:425
  19.8 2.3 %collective-permute-start.6 = (bf16[4,4,16,256]{3,2,1,0:T(8,128)(2,1)S(1)}, bf16[4,4,16,256]{3,2,1,0:T(8,128)(2,1)S(1)}, u32[]{:S(2)}, u32[]{:S(2)}) collective-permute-start(bf16[4,4,16,256]{3,2,1,0:T(8,128)(2,1)S(1)} %get-tuple-element.25.refs_1_), channel_id=1, source_target_pairs={{0,14},{4,10},{8,6},{12,2},{2,12},{6,8},{10,4},{14,0},{1,15},{5,11... | collective-permute-start | bytes 393224 | tf_op jit(solution)/shard_map/ppermute | solution.py:425
  22.0 1.2 %collective-permute-start.5 = (bf16[4,4,16,256]{3,2,1,0:T(8,128)(2,1)S(1)}, bf16[4,4,16,256]{3,2,1,0:T(8,128)(2,1)S(1)}, u32[]{:S(2)}, u32[]{:S(2)}) collective-permute-start(bf16[4,4,16,256]{3,2,1,0:T(8,128)(2,1)S(1)} %get-tuple-element.25.refs_1_), channel_id=1, source_target_pairs={{0,10},{4,14},{8,2},{12,6},{2,8},{6,12},{10,0},{14,4},{1,11},{5,15... | collective-permute-start | bytes 393224 | tf_op jit(solution)/shard_map/ppermute | solution.py:425
  23.3 1.7 %collective-permute-start.4 = (bf16[4,4,16,256]{3,2,1,0:T(8,128)(2,1)S(1)}, bf16[4,4,16,256]{3,2,1,0:T(8,128)(2,1)S(1)}, u32[]{:S(2)}, u32[]{:S(2)}) collective-permute-start(bf16[4,4,16,256]{3,2,1,0:T(8,128)(2,1)S(1)} %get-tuple-element.25.refs_1_), channel_id=1, source_target_pairs={{0,6},{4,2},{8,14},{12,10},{2,4},{6,0},{10,12},{14,8},{1,7},{5,3},... | collective-permute-start | bytes 393224 | tf_op jit(solution)/shard_map/ppermute | solution.py:425
  25.0 4.2 %collective-permute-done.7.refs_0_.refs_2_ = bf16[16,16,256]{2,1,0:T(8,128)(2,1)S(1)} collective-permute-done((bf16[16,16,256]{2,1,0:T(8,128)(2,1)S(1)}, bf16[16,16,256]{2,1,0:T(8,128)(2,1)S(1)}, u32[]{:S(2)}, u32[]{:S(2)}) %collective-permute-start.7) | collective-permute-done | bytes 131104 | tf_op jit(solution)/shard_map/ppermute | solution.py:341
  29.2 2.0 %all-gather = bf16[32,16,256]{2,1,0:T(8,128)(2,1)S(1)} all-gather(bf16[16,16,256]{2,1,0:T(8,128)(2,1)S(1)} %shard_map.71), channel_id=2, replica_groups=mesh['groups'=2,'chan'=4,'pipe'=2,'space'=2] {'space'}, dimensions={0}, use_global_device_ids=true | all-gather | bytes 393216 | tf_op jit(solution)/shard_map/all_gather | solution.py:417
  31.2 0.0 collective-permute-done.3.refs_7_.refs_0_
  31.2 2.9 %shard_map.72 = (bf16[256,2048]{1,0:T(8,128)(2,1)S(1)}, bf16[256,2048]{1,0:T(8,128)(2,1)S(1)}, f32[2048,64]{1,0:T(8,128)S(1)}) custom-call(bf16[4,4,16,256]{3,2,1,0:T(8,128)(2,1)S(1)} %get-tuple-element.18.after_ref.x_ref.refs_0_, bf16[20,16,256]{2,1,0:T(8,128)(2,1)S(1)} %collective-permute-done.l_ref.refs_1_, ...), custom_call_target="tpu_custom_call" | custom-call | flops 1 | bytes 1 | tf_op jit(solution)/shard_map/pallas_call | solution.py:289
  34.1 0.0 collective-permute-done.6.refs_3_
  34.1 3.4 %collective-permute-done.5.refs_2_ = bf16[4,4,16,256]{3,2,1,0:T(8,128)(2,1)S(1)} collective-permute-done((bf16[4,4,16,256]{3,2,1,0:T(8,128)(2,1)S(1)}, bf16[4,4,16,256]{3,2,1,0:T(8,128)(2,1)S(1)}, u32[]{:S(2)}, u32[]{:S(2)}) %collective-permute-start.5) | collective-permute-done | bytes 131104 | tf_op jit(solution)/shard_map/ppermute | solution.py:425
  37.5 0.0 collective-permute-done.4.refs_1_
  37.6 0.1 collective-permute-start.8
  37.7 1.9 %collective-permute-done.8.other_ref = bf16[4,16,16,256]{3,2,1,0:T(8,128)(2,1)S(1)} collective-permute-done((bf16[4,16,16,256]{3,2,1,0:T(8,128)(2,1)S(1)}, bf16[4,16,16,256]{3,2,1,0:T(8,128)(2,1)S(1)}, u32[]{:S(2)}, u32[]{:S(2)}) %collective-permute-start.8) | collective-permute-done | bytes 524320 | tf_op jit(solution)/shard_map/ppermute | solution.py:375
  39.6 5.4 %shard_map.74 = (bf16[2,8,4,4,256]{4,3,2,1,0:T(4,128)(2,1)}, f32[9,64,256]{2,1,0:T(8,128)}, f32[3,64,256]{2,1,0:T(8,128)}) custom-call(bf16[4,16,16,256]{3,2,1,0:T(8,128)(2,1)S(1)} %shard_map.73.g_ref, bf16[4,16,16,256]{3,2,1,0:T(8,128)(2,1)S(1)} %collective-permute-done.8.other_ref, f32[576,256]{1,0:T(8,128)S(1)} %get-tuple-element.27.slope_w_ref, ...), custom_call_target="tpu_custom_call" | custom-call | flops 1358954496 | bytes 8000000 | tf_op jit(solution)/shard_map/pallas_call | solution.py:289
  (3 shorter events, 0.1 us)
Async XLA Ops:
  1.9 10.2 %collective-permute-start = (bf16[20,16,256]{2,1,0:T(8,128)(2,1)S(1)}, bf16[20,16,256]{2,1,0:T(8,128)(2,1)S(1)}, u32[]{:S(2)}, u32[]{:S(2)}) collective-permute-start(bf16[20,16,256]{2,1,0:T(8,128)(2,1)S(1)} %get-tuple-element.20), channel_id=1, source_target_pairs={{0,4},{4,8},{8,12},{12,0},{1,5},{5,9},{9,13},{13,1},{2,6},{6,10},{... | collective-permute-start | bytes 491528 | tf_op jit(solution)/shard_map/ppermute | solution.py:341
  5.0 9.2 %collective-permute-start.1 = (bf16[20,16,256]{2,1,0:T(8,128)(2,1)S(1)}, bf16[20,16,256]{2,1,0:T(8,128)(2,1)S(1)}, u32[]{:S(2)}, u32[]{:S(2)}) collective-permute-start(bf16[20,16,256]{2,1,0:T(8,128)(2,1)S(1)} %get-tuple-element.21), channel_id=1, source_target_pairs={{0,12},{4,0},{8,4},{12,8},{1,13},{5,1},{9,5},{13,9},{2,14},{6,2},{... | collective-permute-start | bytes 491528 | tf_op jit(solution)/shard_map/ppermute | solution.py:341
  7.1 1.3 %copy-start = (bf16[1,3,3,256,256]{4,3,2,1,0:T(8,128)(2,1)S(1)}, bf16[1,3,3,256,256]{4,3,2,1,0:T(8,128)(2,1)}, u32[]{:S(2)}) copy-start(bf16[1,3,3,256,256]{4,3,2,1,0:T(8,128)(2,1)} %param.6) | copy-start | bytes 3538948
  8.3 1.0 %copy-start.1 = (bf16[1,3,256,256]{3,2,1,0:T(8,128)(2,1)S(1)}, bf16[1,3,256,256]{3,2,1,0:T(8,128)(2,1)}, u32[]{:S(2)}) copy-start(bf16[1,3,256,256]{3,2,1,0:T(8,128)(2,1)} %param.7) | copy-start | bytes 1179652
  14.2 1.9 %collective-permute-start.2 = (bf16[54,16,256]{2,1,0:T(8,128)(2,1)S(1)}, bf16[54,16,256]{2,1,0:T(8,128)(2,1)S(1)}, u32[]{:S(2)}, u32[]{:S(2)}) collective-permute-start(bf16[54,16,256]{2,1,0:T(8,128)(2,1)S(1)} %shard_map.69), channel_id=1, source_target_pairs={{0,1},{1,0},{2,3},{3,2},{4,5},{5,4},{6,7},{7,6},{8,9},{9,8},{10,11... | collective-permute-start | bytes 1327112 | tf_op jit(solution)/shard_map/ppermute | solution.py:361
  14.3 14.9 %collective-permute-start.7 = (bf16[16,16,256]{2,1,0:T(8,128)(2,1)S(1)}, bf16[16,16,256]{2,1,0:T(8,128)(2,1)S(1)}, u32[]{:S(2)}, u32[]{:S(2)}) collective-permute-start(bf16[16,16,256]{2,1,0:T(8,128)(2,1)S(1)} %bitcast.12), channel_id=1, source_target_pairs={{0,8},{4,12},{8,0},{12,4},{1,9},{5,13},{9,1},{13,5},{2,10},{6,14},... | collective-permute-start | bytes 393224 | tf_op jit(solution)/shard_map/ppermute | solution.py:341
  18.2 13.0 %collective-permute-start.3 = (bf16[4,4,16,256]{3,2,1,0:T(8,128)(2,1)S(1)}, bf16[4,4,16,256]{3,2,1,0:T(8,128)(2,1)S(1)}, u32[]{:S(2)}, u32[]{:S(2)}) collective-permute-start(bf16[4,4,16,256]{3,2,1,0:T(8,128)(2,1)S(1)} %get-tuple-element.25.refs_1_), channel_id=1, source_target_pairs={{0,2},{4,6},{8,10},{12,14},{2,0},{6,4},{10,8},{14,12},{1,3},{5,7},... | collective-permute-start | bytes 393224 | tf_op jit(solution)/shard_map/ppermute | solution.py:425
  19.8 14.4 %collective-permute-start.6 = (bf16[4,4,16,256]{3,2,1,0:T(8,128)(2,1)S(1)}, bf16[4,4,16,256]{3,2,1,0:T(8,128)(2,1)S(1)}, u32[]{:S(2)}, u32[]{:S(2)}) collective-permute-start(bf16[4,4,16,256]{3,2,1,0:T(8,128)(2,1)S(1)} %get-tuple-element.25.refs_1_), channel_id=1, source_target_pairs={{0,14},{4,10},{8,6},{12,2},{2,12},{6,8},{10,4},{14,0},{1,15},{5,11... | collective-permute-start | bytes 393224 | tf_op jit(solution)/shard_map/ppermute | solution.py:425
  22.0 15.5 %collective-permute-start.5 = (bf16[4,4,16,256]{3,2,1,0:T(8,128)(2,1)S(1)}, bf16[4,4,16,256]{3,2,1,0:T(8,128)(2,1)S(1)}, u32[]{:S(2)}, u32[]{:S(2)}) collective-permute-start(bf16[4,4,16,256]{3,2,1,0:T(8,128)(2,1)S(1)} %get-tuple-element.25.refs_1_), channel_id=1, source_target_pairs={{0,10},{4,14},{8,2},{12,6},{2,8},{6,12},{10,0},{14,4},{1,11},{5,15... | collective-permute-start | bytes 393224 | tf_op jit(solution)/shard_map/ppermute | solution.py:425
  23.3 14.3 %collective-permute-start.4 = (bf16[4,4,16,256]{3,2,1,0:T(8,128)(2,1)S(1)}, bf16[4,4,16,256]{3,2,1,0:T(8,128)(2,1)S(1)}, u32[]{:S(2)}, u32[]{:S(2)}) collective-permute-start(bf16[4,4,16,256]{3,2,1,0:T(8,128)(2,1)S(1)} %get-tuple-element.25.refs_1_), channel_id=1, source_target_pairs={{0,6},{4,2},{8,14},{12,10},{2,4},{6,0},{10,12},{14,8},{1,7},{5,3},... | collective-permute-start | bytes 393224 | tf_op jit(solution)/shard_map/ppermute | solution.py:425
  37.6 2.0 %collective-permute-start.8 = (bf16[4,16,16,256]{3,2,1,0:T(8,128)(2,1)S(1)}, bf16[4,16,16,256]{3,2,1,0:T(8,128)(2,1)S(1)}, u32[]{:S(2)}, u32[]{:S(2)}) collective-permute-start(bf16[4,16,16,256]{3,2,1,0:T(8,128)(2,1)S(1)} %shard_map.73.g_ref), channel_id=1, source_target_pairs={{0,1},{1,0},{2,3},{3,2},{4,5},{5,4},{6,7},{7,6},{8,9},{9,8},{10,11... | collective-permute-start | bytes 1572872 | tf_op jit(solution)/shard_map/ppermute | solution.py:375

commit v11 on v7

--- a/solution.py
+++ b/solution.py
@@ -50,11 +50,14 @@
     w_ref[...] = w_in[...]
     tw_ref[...] = tw_in[...]
     first = pl.multiple_of(lax.axis_index("chan") * share, share)
+    copies = pick_ref.shape[0] // (4 * share)
     for lag in range(3):
-        pick_ref[lag * share : (lag + 1) * share, :] = tw_in[lag, pl.ds(first, share), :]
+        for j in range(lag * copies, (lag + 1) * copies):
+            pick_ref[j * share : (j + 1) * share, :] = tw_in[lag, pl.ds(first, share), :]
     at = lax.broadcasted_iota(jnp.int32, (share, channels), 1) - first
     chosen = at == lax.broadcasted_iota(jnp.int32, (share, channels), 0)
-    pick_ref[3 * share :, :] = jnp.where(chosen, 1.0, 0.0).astype(BF16)
+    for j in range(3 * copies, 4 * copies):
+        pick_ref[j * share : (j + 1) * share, :] = jnp.where(chosen, 1.0, 0.0).astype(BF16)
 
 
 def side_kernel(x_ref, l_ref, r_ref, cot_ref, after_ref, side_ref):
@@ -200,9 +203,8 @@
                 padded[far, pl.ds(place, cols)] = side[at : at + cols]
 
 
-def own_window(gp_ref, slope_ref, w_ref, tw_ref, hg_ref, frames, rows, cols):
+def own_window(gp_ref, r0, slope_ref, w_ref, tw_ref, hg_ref, frames, rows, cols):
     channels = w_ref.shape[-1]
-    r0 = lax.axis_index("space") * rows
     c0 = lax.axis_index("chan") * cols
     window = gp_ref[pl.ds(r0, rows + 2), pl.ds(c0, cols + 2)].reshape(-1, channels)
     window_grad(window, slope_ref, tw_ref, hg_ref, frames)
@@ -215,7 +217,8 @@
 ):
     rows, cols = cot_ref.shape[:2]
     fill_padded(gp_ref, g_ref, other_ref)
-    own, conv = own_window(gp_ref, slope_ref, w_ref, tw_ref, hg_ref, frames, rows, cols)
+    r0 = lax.axis_index("space") * rows
+    own, conv = own_window(gp_ref, r0, slope_ref, w_ref, tw_ref, hg_ref, frames, rows, cols)
     send_on(out_ref, own, conv, cot_ref)
 
 
@@ -237,45 +240,99 @@
                 hidden = term if hidden is None else hidden + term
         active = (hidden * jax.nn.sigmoid(hidden)).astype(BF16)
         act_ref[:, i * span : (i + 1) * span] = active.T
-        slope_ref[i * span : (i + 1) * span, :] = slope_of(pltpu.roll(hidden, turn, 1)[:, :share])
+        slope = slope_of(pltpu.roll(hidden, turn, 1)[:, :share])
+        copies = slope_ref.shape[1] // share
+        slope_ref[i * span : (i + 1) * span, :] = jnp.concatenate([slope] * copies, axis=1)
         xt_ref[:, i * span : (i + 1) * span] = xp_ref[i + 1, 1 : 1 + width].reshape(-1, channels).T
 
 
+def lane_choice(values, share):
+    part = lax.broadcasted_iota(jnp.int32, values[0].shape, 1) // share
+    chosen = values[0]
+    for j in range(1, len(values)):
+        chosen = jnp.where(part == j, values[j], chosen)
+    return chosen
+
+
+def digest(block, slope, pick_ref, frames, share):
+    lanes = slope.shape[1]
+    copies = lanes // share
+    mixed = dot_back(block, pick_ref[...])
+    act = mixed[:, :lanes]
+    for lag in (1, 2):
+        act = act + frame_shift(mixed[:, lag * lanes : (lag + 1) * lanes], lag, frames)
+    own = mixed[:, 3 * lanes :]
+    lagged = [own, frame_shift(own, 1, frames), frame_shift(own, 2, frames)]
+    groups = [lane_choice(lagged[t : t + copies], share) for t in range(0, 3, copies)]
+    return (act * slope).astype(BF16), [group.astype(BF16) for group in groups]
+
+
+def digest_half(half_ref, bottom, slope_ref, act_ref, pick_ref, put, gcols_ref, frames, share):
+    rows, width, steps, channels = half_ref.shape
+    span = width * steps
+    lanes = slope_ref.shape[1]
+    start = bottom * rows * span
+    for r in range(rows):
+        slope = slope_ref[pl.ds(pl.multiple_of(start + r * span, span), span), :]
+        grad, groups = digest(
+            half_ref[r].reshape(span, channels), slope, pick_ref, frames, share
+        )
+        put(r, grad.reshape(width, steps, lanes))
+        for t, group in enumerate(groups):
+            gcols_ref[r * span : (r + 1) * span, t * lanes : (t + 1) * lanes] = group
+    here = pl.ds(pl.multiple_of(start, span), rows * span)
+    return dot(act_ref[:, here], gcols_ref[...])
+
+
+def near_kernel(
+    frames, share, g_ref, slope_ref, act_ref, pick_ref, grad_ref, time_ref, gcols_ref
+):
+    def put(r, grad):
+        grad_ref[r] = grad
+
+    bottom = lax.axis_index("space")
+    time_ref[...] = digest_half(
+        g_ref, bottom, slope_ref, act_ref, pick_ref, put, gcols_ref, frames, share
+    )
+
+
 def final_kernel(
-    frames, g_ref, other_ref, slope_w_ref, slope_s_ref, act_ref, xt_ref, w_ref, tw_ref, pick_ref,
-    out_ref, space_ref, time_ref, gp_ref, hg_ref, hs_ref, hcols_ref, gcols_ref,
+    frames, share, g_ref, other_ref, near_ref, time_near_ref, slope_w_ref, slope_s_ref, act_ref,
+    xt_ref, w_ref, tw_ref, pick_ref,
+    out_ref, space_ref, time_ref, gw_ref, hg_ref, hs_ref, hcols_ref, gcols_ref,
 ):
     rows, width, steps, channels = g_ref.shape
     clips, _, _, cols, _ = out_ref.shape
-    share = slope_s_ref.shape[1]
     height = 2 * rows
     span = width * steps
-    fill_padded(gp_ref, g_ref, other_ref)
-    hs_ref[...] = jnp.zeros(hs_ref.shape, BF16)
-    for i in range(height):
-        block = gp_ref[i + 1, 1 : 1 + width].reshape(-1, channels)
-        mixed = dot_back(block, pick_ref[...])
-        act = mixed[:, :share]
-        for lag in (1, 2):
-            act = act + frame_shift(mixed[:, lag * share : (lag + 1) * share], lag, frames)
-        grad = (act * slope_s_ref[i * span : (i + 1) * span, :]).astype(BF16)
-        hs_ref[i + 1, 1 : 1 + width] = grad.reshape(width, steps, share)
-        own = mixed[:, 3 * share :]
-        for lag in range(3):
-            shifted = own if lag == 0 else frame_shift(own, lag, frames)
-            gcols_ref[i * span : (i + 1) * span, lag * share : (lag + 1) * share] = shifted.astype(
-                BF16
+    lanes = slope_s_ref.shape[1]
+    copies = lanes // share
+    bottom = lax.axis_index("space")
+    clear_rim(hs_ref)
+    hs_ref[pl.ds(1 + bottom * rows, rows), 1 : 1 + width] = near_ref[...]
+
+    def put(r, grad):
+        hs_ref[1 + (1 - bottom) * rows + r, 1 : 1 + width] = grad
+
+    time_sum = time_near_ref[...] + digest_half(
+        other_ref, 1 - bottom, slope_s_ref, act_ref, pick_ref, put, gcols_ref, frames, share
+    )
+    time_ref[...] = time_sum.T[: 3 * share].reshape(time_ref.shape)
+    for n, first in enumerate(range(0, 9, copies)):
+        for i in range(height):
+            taps = [
+                hs_ref[i + 2 - tap // 3, 2 - tap % 3 : 2 - tap % 3 + width].reshape(span, lanes)
+                for tap in range(first, min(first + copies, 9))
+            ]
+            hcols_ref[i * span : (i + 1) * span, n * lanes : (n + 1) * lanes] = lane_choice(
+                taps, share
             )
-    for u in range(3):
-        for v in range(3):
-            tap = 3 * u + v
-            for i in range(height):
-                hcols_ref[i * span : (i + 1) * span, tap * share : (tap + 1) * share] = hs_ref[
-                    i + 2 - u, 2 - v : 2 - v + width
-                ].reshape(-1, share)
-    time_ref[...] = dot(act_ref[...], gcols_ref[...]).T.reshape(time_ref.shape)
-    space_ref[...] = dot(xt_ref[...], hcols_ref[...]).T.reshape(space_ref.shape)
-    own, conv = own_window(gp_ref, slope_w_ref, w_ref, tw_ref, hg_ref, frames, rows, cols)
+    space_sum = dot(xt_ref[...], hcols_ref[...])
+    space_ref[...] = space_sum.T[: 9 * share].reshape(space_ref.shape)
+    clear_rim(gw_ref)
+    gw_ref[1 : 1 + rows, 1 : 1 + width] = g_ref[...]
+    gw_ref[(1 - bottom) * (rows + 1), 1 : 1 + width] = other_ref[bottom * (rows - 1)]
+    own, conv = own_window(gw_ref, 0, slope_w_ref, w_ref, tw_ref, hg_ref, frames, rows, cols)
     grads = (own.astype(F32) + conv).astype(BF16).reshape(rows, cols, steps, channels)
     for r in range(rows):
         out_ref[:, :, r] = jnp.swapaxes(grads[r], 0, 1).reshape(clips, frames, cols, channels)
@@ -301,6 +358,9 @@
     steps = clips * frames
     chan, depth = lax.axis_size("chan"), lax.axis_size("pipe")
     share = channels // chan
+    copies = max(1, 128 // share)
+    lanes = copies * share
+    lag_groups, tap_groups = -(-3 // copies), -(-9 // copies)
     height, width = 2 * rows, chan * cols
     count = height * width * steps
     win = (rows + 2) * (cols + 2) * steps
@@ -325,7 +385,7 @@
         (
             jax.ShapeDtypeStruct((9, channels, channels), BF16),
             jax.ShapeDtypeStruct((3, channels, channels), BF16),
-            jax.ShapeDtypeStruct((4 * share, channels), BF16),
+            jax.ShapeDtypeStruct((4 * copies * share, channels), BF16),
         ),
         [],
         16,
@@ -430,7 +490,7 @@
                 (
                     jax.ShapeDtypeStruct((channels, count), BF16),
                     jax.ShapeDtypeStruct((channels, count), BF16),
-                    jax.ShapeDtypeStruct((count, share), F32),
+                    jax.ShapeDtypeStruct((count, lanes), F32),
                 ),
                 [padded],
                 large,
@@ -441,24 +501,39 @@
                 places=[VM] * len(operands) + [pl.ANY],
             )
         g_all = gathered(arrived, () if tick else (slope_s,))
+    grad_near, time_near = call(
+        functools.partial(near_kernel, frames, share),
+        (
+            jax.ShapeDtypeStruct((rows, width, steps, lanes), BF16),
+            jax.ShapeDtypeStruct((channels, lag_groups * lanes), F32),
+        ),
+        [pltpu.VMEM((count // 2, lag_groups * lanes), BF16)],
+        large,
+        count * channels * channels * 4,
+        4_000_000,
+        g_all[0],
+        slope_s,
+        act_t,
+        pick,
+    )
     grads, space_grad, time_grad = call(
-        functools.partial(final_kernel, frames),
+        functools.partial(final_kernel, frames, share),
         (
             jax.ShapeDtypeStruct((clips, frames, rows, cols, channels), BF16),
             jax.ShapeDtypeStruct((9, share, channels), F32),
             jax.ShapeDtypeStruct((3, share, channels), F32),
         ),
         [
-            padded,
+            pltpu.VMEM((rows + 2, width + 2) + cell, BF16),
             hg_win,
-            pltpu.VMEM((height + 2, width + 2, steps, share), BF16),
-            pltpu.VMEM((count, 9 * share), BF16),
-            pltpu.VMEM((count, 3 * share), BF16),
+            pltpu.VMEM((height + 2, width + 2, steps, lanes), BF16),
+            pltpu.VMEM((count, tap_groups * lanes), BF16),
+            pltpu.VMEM((count // 2, lag_groups * lanes), BF16),
         ],
         large,
         4 * win * 9 * channels * channels,
         8_000_000,
-        *g_all, slope_w, slope_s, act_t, x_t, w, tw, pick,
+        *g_all, grad_near, time_near, slope_w, slope_s, act_t, x_t, w, tw, pick,
     )
     return (
         grads[None],

time: 43.7 us -> 42.2 us (0.966)
  waiting for transfers between devices: 14.2 us -> 13.1 us
  Pallas kernels: 10.8 us -> 10.3 us
    ppermute x1, waiting for transfers between devices: 1.9 us -> 0.98 us  [gathered(): return (half, lax.ppermute(half, 'space', swap))]
    pallas_call x8 -> x9, Pallas kernels: 10.8 us -> 10.3 us  [call(): pl.pallas_call(kernel, out_shape=outs, in_specs=[pl.BlockSpec(memory_spac...]
  transfers between devices with their start and end apart: 9 -> 9, of which waited for: 6 -> 6; matrix products, arithmetic and copies ran while one was open for 0% -> 0% of each run, Pallas kernels for 12% -> 15%
where the time goes in v11:
time: 42.2 us; the launch traced here: 42 us
  waiting for transfers between devices  13.1 us (31%)
  starting transfers between devices  12.4 us (29%)
  Pallas kernels  10.3 us (24%)
  local copies, waits for them, and re-layouts  2.27 us (5%)
  blocking collectives  1.99 us (5%)
  other arithmetic  1.16 us (3%)
  between operations  0.71 us (2%)
    pallas_call x9, Pallas kernels, call(): pl.pallas_call(kernel, out_shape=outs, in_specs=[pl.BlockSpec(memory_spac...  10.3 us
    ppermute x4, waiting for transfers between devices, per_device(): arrived.append(lax.ppermute(payload, ('chan', 'pipe'), pairs))  6.64 us
    ppermute x3, starting transfers between devices, turned(): lax.ppermute(message, 'chan', [(i, (i + by) % chan) for i in range(chan)])  6.53 us
    ppermute x4, starting transfers between devices, per_device(): arrived.append(lax.ppermute(payload, ('chan', 'pipe'), pairs))  5.74 us
    ppermute x3, waiting for transfers between devices, turned(): lax.ppermute(message, 'chan', [(i, (i + by) % chan) for i in range(chan)])  5.08 us
    unnamed x4, local copies, waits for them, and re-layouts  2.27 us
    all_gather x1, blocking collectives, per_device(): from_late = lax.all_gather(to_late, 'space', axis=0, tiled=False)  1.99 us
    another operation x1, other arithmetic, per_device(): jnp.stack([activations[0], cotangent])  1.16 us
  transfers between devices with their start and end apart: 9, of which 6 were waited for; matrix products, arithmetic and copies ran while one was open for 0% of the time, Pallas kernels for 15%

profile of v11, /device:TPU:0, one launch (start us, length us, event | category | flops | bytes accessed | tf_op | source)
XLA Modules:
  0.0 42.0 jit_solution(12632447648389975141)
XLA Ops:
  0.6 1.2 %pad_maximum_fusion.both_ref = bf16[2,2,8,4,4,256]{5,4,3,2,1,0:T(4,128)(2,1)S(1)} fusion(bf16[1,2,8,4,4,256]{5,4,3,2,1,0:T(4,128)(2,1)} %bitcast.16, bf16[1,2,8,4,4,256]{5,4,3,2,1,0:T(4,128)(2,1)} %param.4), kind=kLoop, calls=%fused_computation | loop fusion | flops 131072 | bytes 524288 | tf_op jit(solution)/shard_map/stack | solution.py:381
  1.8 0.1 shard_map.67
  1.9 3.1 %collective-permute-start = (bf16[20,16,256]{2,1,0:T(8,128)(2,1)S(1)}, bf16[20,16,256]{2,1,0:T(8,128)(2,1)S(1)}, u32[]{:S(2)}, u32[]{:S(2)}) collective-permute-start(bf16[20,16,256]{2,1,0:T(8,128)(2,1)S(1)} %get-tuple-element.22), channel_id=1, source_target_pairs={{0,4},{4,8},{8,12},{12,0},{1,5},{5,9},{9,13},{13,1},{2,6},{6,10},{... | collective-permute-start | bytes 491528 | tf_op jit(solution)/shard_map/ppermute | solution.py:401
  5.0 2.1 %collective-permute-start.1 = (bf16[20,16,256]{2,1,0:T(8,128)(2,1)S(1)}, bf16[20,16,256]{2,1,0:T(8,128)(2,1)S(1)}, u32[]{:S(2)}, u32[]{:S(2)}) collective-permute-start(bf16[20,16,256]{2,1,0:T(8,128)(2,1)S(1)} %get-tuple-element.23), channel_id=1, source_target_pairs={{0,12},{4,0},{8,4},{12,8},{1,13},{5,1},{9,5},{13,9},{2,14},{6,2},{... | collective-permute-start | bytes 491528 | tf_op jit(solution)/shard_map/ppermute | solution.py:401
  7.1 0.0 copy-start
  7.1 1.3 %copy-done = bf16[1,3,3,256,256]{4,3,2,1,0:T(8,128)(2,1)S(1)} copy-done((bf16[1,3,3,256,256]{4,3,2,1,0:T(8,128)(2,1)S(1)}, bf16[1,3,3,256,256]{4,3,2,1,0:T(8,128)(2,1)}, u32[]{:S(2)}) %copy-start) | copy-done | bytes 1179672
  8.3 0.0 copy-start.1
  8.3 1.0 %copy-done.1 = bf16[1,3,256,256]{3,2,1,0:T(8,128)(2,1)S(1)} copy-done((bf16[1,3,256,256]{3,2,1,0:T(8,128)(2,1)S(1)}, bf16[1,3,256,256]{3,2,1,0:T(8,128)(2,1)}, u32[]{:S(2)}) %copy-start.1) | copy-done | bytes 393240
  9.3 0.1 shard_map.68
  9.5 2.6 %collective-permute-done.l_ref.refs_1_ = bf16[20,16,256]{2,1,0:T(8,128)(2,1)S(1)} collective-permute-done((bf16[20,16,256]{2,1,0:T(8,128)(2,1)S(1)}, bf16[20,16,256]{2,1,0:T(8,128)(2,1)S(1)}, u32[]{:S(2)}, u32[]{:S(2)}) %collective-permute-start) | collective-permute-done | bytes 163872 | tf_op jit(solution)/shard_map/ppermute | solution.py:401
  12.1 2.1 %collective-permute-done.1.r_ref.refs_3_ = bf16[20,16,256]{2,1,0:T(8,128)(2,1)S(1)} collective-permute-done((bf16[20,16,256]{2,1,0:T(8,128)(2,1)S(1)}, bf16[20,16,256]{2,1,0:T(8,128)(2,1)S(1)}, u32[]{:S(2)}, u32[]{:S(2)}) %collective-permute-start.1) | collective-permute-done | bytes 163872 | tf_op jit(solution)/shard_map/ppermute | solution.py:401
  14.2 0.1 collective-permute-start.2
  14.3 1.4 %collective-permute-start.7 = (bf16[16,16,256]{2,1,0:T(8,128)(2,1)S(1)}, bf16[16,16,256]{2,1,0:T(8,128)(2,1)S(1)}, u32[]{:S(2)}, u32[]{:S(2)}) collective-permute-start(bf16[16,16,256]{2,1,0:T(8,128)(2,1)S(1)} %bitcast.12), channel_id=1, source_target_pairs={{0,8},{4,12},{8,0},{12,4},{1,9},{5,13},{9,1},{13,5},{2,10},{6,14},... | collective-permute-start | bytes 393224 | tf_op jit(solution)/shard_map/ppermute | solution.py:401
  15.6 0.4 collective-permute-done.2.side_ref.refs_4_
  16.0 2.1 %shard_map.70 = (f32[576,256]{1,0:T(8,128)S(1)}, bf16[4,4,16,256]{3,2,1,0:T(8,128)(2,1)S(1)}) custom-call(bf16[4,4,16,256]{3,2,1,0:T(8,128)(2,1)S(1)} %get-tuple-element.20.after_ref.x_ref.refs_0_, bf16[4,4,16,256]{3,2,1,0:T(8,128)(2,1)S(1)} %get-tuple-element.21.cot_ref, bf16[20,16,256]{2,1,0:T(8,128)(2,1)S(1)} %collective-permute-done.l_ref.refs_1_, ...), custom_call_target="tpu_custom_call" | custom-call | flops 1 | bytes 1 | tf_op jit(solution)/shard_map/pallas_call | solution.py:346
  18.2 1.6 %collective-permute-start.3 = (bf16[4,4,16,256]{3,2,1,0:T(8,128)(2,1)S(1)}, bf16[4,4,16,256]{3,2,1,0:T(8,128)(2,1)S(1)}, u32[]{:S(2)}, u32[]{:S(2)}) collective-permute-start(bf16[4,4,16,256]{3,2,1,0:T(8,128)(2,1)S(1)} %get-tuple-element.27.refs_1_), channel_id=1, source_target_pairs={{0,2},{4,6},{8,10},{12,14},{2,0},{6,4},{10,8},{14,12},{1,3},{5,7},... | collective-permute-start | bytes 393224 | tf_op jit(solution)/shard_map/ppermute | solution.py:485
  19.8 2.3 %collective-permute-start.6 = (bf16[4,4,16,256]{3,2,1,0:T(8,128)(2,1)S(1)}, bf16[4,4,16,256]{3,2,1,0:T(8,128)(2,1)S(1)}, u32[]{:S(2)}, u32[]{:S(2)}) collective-permute-start(bf16[4,4,16,256]{3,2,1,0:T(8,128)(2,1)S(1)} %get-tuple-element.27.refs_1_), channel_id=1, source_target_pairs={{0,14},{4,2},{8,6},{12,10},{2,12},{6,0},{10,4},{14,8},{1,15},{5,3}... | collective-permute-start | bytes 393224 | tf_op jit(solution)/shard_map/ppermute | solution.py:485
  22.0 1.2 %collective-permute-start.5 = (bf16[4,4,16,256]{3,2,1,0:T(8,128)(2,1)S(1)}, bf16[4,4,16,256]{3,2,1,0:T(8,128)(2,1)S(1)}, u32[]{:S(2)}, u32[]{:S(2)}) collective-permute-start(bf16[4,4,16,256]{3,2,1,0:T(8,128)(2,1)S(1)} %get-tuple-element.27.refs_1_), channel_id=1, source_target_pairs={{0,10},{4,14},{8,2},{12,6},{2,8},{6,12},{10,0},{14,4},{1,11},{5,15... | collective-permute-start | bytes 393224 | tf_op jit(solution)/shard_map/ppermute | solution.py:485
  23.3 0.7 %collective-permute-start.4 = (bf16[4,4,16,256]{3,2,1,0:T(8,128)(2,1)S(1)}, bf16[4,4,16,256]{3,2,1,0:T(8,128)(2,1)S(1)}, u32[]{:S(2)}, u32[]{:S(2)}) collective-permute-start(bf16[4,4,16,256]{3,2,1,0:T(8,128)(2,1)S(1)} %get-tuple-element.27.refs_1_), channel_id=1, source_target_pairs={{0,6},{4,10},{8,14},{12,2},{2,4},{6,8},{10,12},{14,0},{1,7},{5,11}... | collective-permute-start | bytes 393224 | tf_op jit(solution)/shard_map/ppermute | solution.py:485
  23.9 0.4 collective-permute-done.7.refs_0_.refs_2_
  24.3 2.0 %all-gather = bf16[32,16,256]{2,1,0:T(8,128)(2,1)S(1)} all-gather(bf16[16,16,256]{2,1,0:T(8,128)(2,1)S(1)} %shard_map.71), channel_id=2, replica_groups=mesh['groups'=2,'chan'=4,'pipe'=2,'space'=2] {'space'}, dimensions={0}, use_global_device_ids=true | all-gather | bytes 393216 | tf_op jit(solution)/shard_map/all_gather | solution.py:477
  26.3 0.0 collective-permute-done.3.refs_7_.refs_0_
  26.3 3.1 %shard_map.72 = (bf16[256,2048]{1,0:T(8,128)(2,1)S(1)}, bf16[256,2048]{1,0:T(8,128)(2,1)S(1)}, f32[2048,128]{1,0:T(8,128)S(1)}) custom-call(bf16[4,4,16,256]{3,2,1,0:T(8,128)(2,1)S(1)} %get-tuple-element.20.after_ref.x_ref.refs_0_, bf16[20,16,256]{2,1,0:T(8,128)(2,1)S(1)} %collective-permute-done.l_ref.refs_1_, ...), custom_call_target="tpu_custom_call" | custom-call | flops 1 | bytes 1 | tf_op jit(solution)/shard_map/pallas_call | solution.py:346
  29.4 0.0 collective-permute-done.6.refs_3_
  29.4 6.6 %collective-permute-done.5.refs_2_ = bf16[4,4,16,256]{3,2,1,0:T(8,128)(2,1)S(1)} collective-permute-done((bf16[4,4,16,256]{3,2,1,0:T(8,128)(2,1)S(1)}, bf16[4,4,16,256]{3,2,1,0:T(8,128)(2,1)S(1)}, u32[]{:S(2)}, u32[]{:S(2)}) %collective-permute-start.5) | collective-permute-done | bytes 131104 | tf_op jit(solution)/shard_map/ppermute | solution.py:485
  36.0 0.0 collective-permute-done.4.refs_1_
  36.1 0.1 collective-permute-start.8
  36.2 0.9 %shard_map.74 = (bf16[4,16,16,128]{3,2,1,0:T(8,128)(2,1)S(1)}, f32[256,256]{1,0:T(8,128)S(1)}) custom-call(bf16[4,16,16,256]{3,2,1,0:T(8,128)(2,1)S(1)} %shard_map.73.g_ref, f32[2048,128]{1,0:T(8,128)S(1)} %get-tuple-element.28.refs_4_.slope_ref.slope_s_ref, bf16[256,2048]{1,0:T(8,128)(2,1)S(1)} %get-tuple-element.29.act_ref, ...), custom_call_target="tpu_custom_call" | custom-call | flops 536870912 | bytes 4000000 | tf_op jit(solution)/shard_map/pallas_call | solution.py:346
  37.1 1.0 %collective-permute-done.8.other_ref = bf16[4,16,16,256]{3,2,1,0:T(8,128)(2,1)S(1)} collective-permute-done((bf16[4,16,16,256]{3,2,1,0:T(8,128)(2,1)S(1)}, bf16[4,16,16,256]{3,2,1,0:T(8,128)(2,1)S(1)}, u32[]{:S(2)}, u32[]{:S(2)}) %collective-permute-start.8) | collective-permute-done | bytes 524320 | tf_op jit(solution)/shard_map/ppermute | solution.py:435
  38.1 3.9 %shard_map.75 = (bf16[2,8,4,4,256]{4,3,2,1,0:T(4,128)(2,1)}, f32[9,64,256]{2,1,0:T(8,128)}, f32[3,64,256]{2,1,0:T(8,128)}) custom-call(bf16[4,16,16,256]{3,2,1,0:T(8,128)(2,1)S(1)} %shard_map.73.g_ref, bf16[4,16,16,256]{3,2,1,0:T(8,128)(2,1)S(1)} %collective-permute-done.8.other_ref, bf16[4,16,16,128]{3,2,1,0:T(8,128)(2,1)S(1)} %get-tuple-element.30.near_ref, ...), custom_call_target="tpu_custom_call" | custom-call | flops 1358954496 | bytes 8000000 | tf_op jit(solution)/shard_map/pallas_call | solution.py:346
  (3 shorter events, 0.1 us)
Async XLA Ops:
  1.9 10.2 %collective-permute-start = (bf16[20,16,256]{2,1,0:T(8,128)(2,1)S(1)}, bf16[20,16,256]{2,1,0:T(8,128)(2,1)S(1)}, u32[]{:S(2)}, u32[]{:S(2)}) collective-permute-start(bf16[20,16,256]{2,1,0:T(8,128)(2,1)S(1)} %get-tuple-element.22), channel_id=1, source_target_pairs={{0,4},{4,8},{8,12},{12,0},{1,5},{5,9},{9,13},{13,1},{2,6},{6,10},{... | collective-permute-start | bytes 491528 | tf_op jit(solution)/shard_map/ppermute | solution.py:401
  5.0 9.2 %collective-permute-start.1 = (bf16[20,16,256]{2,1,0:T(8,128)(2,1)S(1)}, bf16[20,16,256]{2,1,0:T(8,128)(2,1)S(1)}, u32[]{:S(2)}, u32[]{:S(2)}) collective-permute-start(bf16[20,16,256]{2,1,0:T(8,128)(2,1)S(1)} %get-tuple-element.23), channel_id=1, source_target_pairs={{0,12},{4,0},{8,4},{12,8},{1,13},{5,1},{9,5},{13,9},{2,14},{6,2},{... | collective-permute-start | bytes 491528 | tf_op jit(solution)/shard_map/ppermute | solution.py:401
  7.1 1.3 %copy-start = (bf16[1,3,3,256,256]{4,3,2,1,0:T(8,128)(2,1)S(1)}, bf16[1,3,3,256,256]{4,3,2,1,0:T(8,128)(2,1)}, u32[]{:S(2)}) copy-start(bf16[1,3,3,256,256]{4,3,2,1,0:T(8,128)(2,1)} %param.6) | copy-start | bytes 3538948
  8.3 1.0 %copy-start.1 = (bf16[1,3,256,256]{3,2,1,0:T(8,128)(2,1)S(1)}, bf16[1,3,256,256]{3,2,1,0:T(8,128)(2,1)}, u32[]{:S(2)}) copy-start(bf16[1,3,256,256]{3,2,1,0:T(8,128)(2,1)} %param.7) | copy-start | bytes 1179652
  14.2 1.9 %collective-permute-start.2 = (bf16[54,16,256]{2,1,0:T(8,128)(2,1)S(1)}, bf16[54,16,256]{2,1,0:T(8,128)(2,1)S(1)}, u32[]{:S(2)}, u32[]{:S(2)}) collective-permute-start(bf16[54,16,256]{2,1,0:T(8,128)(2,1)S(1)} %shard_map.69), channel_id=1, source_target_pairs={{0,1},{1,0},{2,3},{3,2},{4,5},{5,4},{6,7},{7,6},{8,9},{9,8},{10,11... | collective-permute-start | bytes 1327112 | tf_op jit(solution)/shard_map/ppermute | solution.py:421
  14.3 10.1 %collective-permute-start.7 = (bf16[16,16,256]{2,1,0:T(8,128)(2,1)S(1)}, bf16[16,16,256]{2,1,0:T(8,128)(2,1)S(1)}, u32[]{:S(2)}, u32[]{:S(2)}) collective-permute-start(bf16[16,16,256]{2,1,0:T(8,128)(2,1)S(1)} %bitcast.12), channel_id=1, source_target_pairs={{0,8},{4,12},{8,0},{12,4},{1,9},{5,13},{9,1},{13,5},{2,10},{6,14},... | collective-permute-start | bytes 393224 | tf_op jit(solution)/shard_map/ppermute | solution.py:401
  18.2 8.1 %collective-permute-start.3 = (bf16[4,4,16,256]{3,2,1,0:T(8,128)(2,1)S(1)}, bf16[4,4,16,256]{3,2,1,0:T(8,128)(2,1)S(1)}, u32[]{:S(2)}, u32[]{:S(2)}) collective-permute-start(bf16[4,4,16,256]{3,2,1,0:T(8,128)(2,1)S(1)} %get-tuple-element.27.refs_1_), channel_id=1, source_target_pairs={{0,2},{4,6},{8,10},{12,14},{2,0},{6,4},{10,8},{14,12},{1,3},{5,7},... | collective-permute-start | bytes 393224 | tf_op jit(solution)/shard_map/ppermute | solution.py:485
  19.8 9.6 %collective-permute-start.6 = (bf16[4,4,16,256]{3,2,1,0:T(8,128)(2,1)S(1)}, bf16[4,4,16,256]{3,2,1,0:T(8,128)(2,1)S(1)}, u32[]{:S(2)}, u32[]{:S(2)}) collective-permute-start(bf16[4,4,16,256]{3,2,1,0:T(8,128)(2,1)S(1)} %get-tuple-element.27.refs_1_), channel_id=1, source_target_pairs={{0,14},{4,2},{8,6},{12,10},{2,12},{6,0},{10,4},{14,8},{1,15},{5,3}... | collective-permute-start | bytes 393224 | tf_op jit(solution)/shard_map/ppermute | solution.py:485
  22.0 14.0 %collective-permute-start.5 = (bf16[4,4,16,256]{3,2,1,0:T(8,128)(2,1)S(1)}, bf16[4,4,16,256]{3,2,1,0:T(8,128)(2,1)S(1)}, u32[]{:S(2)}, u32[]{:S(2)}) collective-permute-start(bf16[4,4,16,256]{3,2,1,0:T(8,128)(2,1)S(1)} %get-tuple-element.27.refs_1_), channel_id=1, source_target_pairs={{0,10},{4,14},{8,2},{12,6},{2,8},{6,12},{10,0},{14,4},{1,11},{5,15... | collective-permute-start | bytes 393224 | tf_op jit(solution)/shard_map/ppermute | solution.py:485
  23.3 12.8 %collective-permute-start.4 = (bf16[4,4,16,256]{3,2,1,0:T(8,128)(2,1)S(1)}, bf16[4,4,16,256]{3,2,1,0:T(8,128)(2,1)S(1)}, u32[]{:S(2)}, u32[]{:S(2)}) collective-permute-start(bf16[4,4,16,256]{3,2,1,0:T(8,128)(2,1)S(1)} %get-tuple-element.27.refs_1_), channel_id=1, source_target_pairs={{0,6},{4,10},{8,14},{12,2},{2,4},{6,8},{10,12},{14,0},{1,7},{5,11}... | collective-permute-start | bytes 393224 | tf_op jit(solution)/shard_map/ppermute | solution.py:485
  36.1 2.0 %collective-permute-start.8 = (bf16[4,16,16,256]{3,2,1,0:T(8,128)(2,1)S(1)}, bf16[4,16,16,256]{3,2,1,0:T(8,128)(2,1)S(1)}, u32[]{:S(2)}, u32[]{:S(2)}) collective-permute-start(bf16[4,16,16,256]{3,2,1,0:T(8,128)(2,1)S(1)} %shard_map.73.g_ref), channel_id=1, source_target_pairs={{0,1},{1,0},{2,3},{3,2},{4,5},{5,4},{6,7},{7,6},{8,9},{9,8},{10,11... | collective-permute-start | bytes 1572872 | tf_op jit(solution)/shard_map/ppermute | solution.py:435

commit v12 on v11

--- a/solution.py
+++ b/solution.py
@@ -284,50 +284,65 @@
     return dot(act_ref[:, here], gcols_ref[...])
 
 
-def near_kernel(
-    frames, share, g_ref, slope_ref, act_ref, pick_ref, grad_ref, time_ref, gcols_ref
-):
-    def put(r, grad):
-        grad_ref[r] = grad
-
-    bottom = lax.axis_index("space")
-    time_ref[...] = digest_half(
-        g_ref, bottom, slope_ref, act_ref, pick_ref, put, gcols_ref, frames, share
-    )
-
-
-def final_kernel(
-    frames, share, g_ref, other_ref, near_ref, time_near_ref, slope_w_ref, slope_s_ref, act_ref,
-    xt_ref, w_ref, tw_ref, pick_ref,
-    out_ref, space_ref, time_ref, gw_ref, hg_ref, hs_ref, hcols_ref, gcols_ref,
-):
-    rows, width, steps, channels = g_ref.shape
-    clips, _, _, cols, _ = out_ref.shape
-    height = 2 * rows
+def tap_products(hs_ref, top, x_top, count, xt_ref, hcols_ref, share):
+    width, steps, lanes = hs_ref.shape[1] - 2, *hs_ref.shape[2:]
+    copies = lanes // share
     span = width * steps
-    lanes = slope_s_ref.shape[1]
-    copies = lanes // share
-    bottom = lax.axis_index("space")
-    clear_rim(hs_ref)
-    hs_ref[pl.ds(1 + bottom * rows, rows), 1 : 1 + width] = near_ref[...]
-
-    def put(r, grad):
-        hs_ref[1 + (1 - bottom) * rows + r, 1 : 1 + width] = grad
-
-    time_sum = time_near_ref[...] + digest_half(
-        other_ref, 1 - bottom, slope_s_ref, act_ref, pick_ref, put, gcols_ref, frames, share
-    )
-    time_ref[...] = time_sum.T[: 3 * share].reshape(time_ref.shape)
     for n, first in enumerate(range(0, 9, copies)):
-        for i in range(height):
+        for i in range(count):
             taps = [
-                hs_ref[i + 2 - tap // 3, 2 - tap % 3 : 2 - tap % 3 + width].reshape(span, lanes)
+                hs_ref[top + i + 2 - tap // 3, 2 - tap % 3 : 2 - tap % 3 + width].reshape(span, lanes)
                 for tap in range(first, min(first + copies, 9))
             ]
             hcols_ref[i * span : (i + 1) * span, n * lanes : (n + 1) * lanes] = lane_choice(
                 taps, share
             )
-    space_sum = dot(xt_ref[...], hcols_ref[...])
+    here = pl.ds(pl.multiple_of(x_top * span, span), count * span)
+    return dot(xt_ref[:, here], hcols_ref[...])
+
+
+def near_kernel(
+    frames, share, g_ref, slope_ref, act_ref, xt_ref, pick_ref,
+    grad_ref, time_ref, space_ref, gcols_ref, hs_ref, hcols_ref,
+):
+    rows, width = g_ref.shape[:2]
+    clear_rim(hs_ref)
+
+    def put(r, grad):
+        grad_ref[r] = grad
+        hs_ref[1 + r, 1 : 1 + width] = grad
+
+    bottom = lax.axis_index("space")
+    time_ref[...] = digest_half(
+        g_ref, bottom, slope_ref, act_ref, pick_ref, put, gcols_ref, frames, share
+    )
+    space_ref[...] = tap_products(
+        hs_ref, bottom, bottom * (rows + 1), rows - 1, xt_ref, hcols_ref, share
+    )
+
+
+def final_kernel(
+    frames, share, g_ref, other_ref, near_ref, time_near_ref, space_near_ref, slope_w_ref,
+    slope_s_ref, act_ref, xt_ref, w_ref, tw_ref, pick_ref,
+    out_ref, space_ref, time_ref, gw_ref, hg_ref, hs_ref, hcols_ref, gcols_ref,
+):
+    rows, width, steps, channels = g_ref.shape
+    clips, _, _, cols, _ = out_ref.shape
+    bottom = lax.axis_index("space")
+    clear_rim(hs_ref)
+    hs_ref[pl.ds(1 + bottom * rows, rows), 1 : 1 + width] = near_ref[...]
+
+    def put(r, grad):
+        hs_ref[1 + (1 - bottom) * rows + r, 1 : 1 + width] = grad
+
+    time_sum = time_near_ref[...] + digest_half(
+        other_ref, 1 - bottom, slope_s_ref, act_ref, pick_ref, put, gcols_ref, frames, share
+    )
+    time_ref[...] = time_sum.T[: 3 * share].reshape(time_ref.shape)
+    top = (1 - bottom) * (rows - 1)
+    space_sum = space_near_ref[...] + tap_products(
+        hs_ref, top, top, rows + 1, xt_ref, hcols_ref, share
+    )
     space_ref[...] = space_sum.T[: 9 * share].reshape(space_ref.shape)
     clear_rim(gw_ref)
     gw_ref[1 : 1 + rows, 1 : 1 + width] = g_ref[...]
@@ -501,19 +516,25 @@
                 places=[VM] * len(operands) + [pl.ANY],
             )
         g_all = gathered(arrived, () if tick else (slope_s,))
-    grad_near, time_near = call(
+    grad_near, time_near, space_near = call(
         functools.partial(near_kernel, frames, share),
         (
             jax.ShapeDtypeStruct((rows, width, steps, lanes), BF16),
             jax.ShapeDtypeStruct((channels, lag_groups * lanes), F32),
+            jax.ShapeDtypeStruct((channels, tap_groups * lanes), F32),
         ),
-        [pltpu.VMEM((count // 2, lag_groups * lanes), BF16)],
+        [
+            pltpu.VMEM((count // 2, lag_groups * lanes), BF16),
+            pltpu.VMEM((rows + 2, width + 2, steps, lanes), BF16),
+            pltpu.VMEM(((rows - 1) * width * steps, tap_groups * lanes), BF16),
+        ],
         large,
         count * channels * channels * 4,
         4_000_000,
         g_all[0],
         slope_s,
         act_t,
+        x_t,
         pick,
     )
     grads, space_grad, time_grad = call(
@@ -527,13 +548,13 @@
             pltpu.VMEM((rows + 2, width + 2) + cell, BF16),
             hg_win,
             pltpu.VMEM((height + 2, width + 2, steps, lanes), BF16),
-            pltpu.VMEM((count, tap_groups * lanes), BF16),
+            pltpu.VMEM(((rows + 1) * width * steps, tap_groups * lanes), BF16),
             pltpu.VMEM((count // 2, lag_groups * lanes), BF16),
         ],
         large,
         4 * win * 9 * channels * channels,
         8_000_000,
-        *g_all, grad_near, time_near, slope_w, slope_s, act_t, x_t, w, tw, pick,
+        *g_all, grad_near, time_near, space_near, slope_w, slope_s, act_t, x_t, w, tw, pick,
     )
     return (
         grads[None],

time: 42.2 us -> 42 us (level)
  transfers between devices with their start and end apart: 9 -> 9, of which waited for: 6 -> 6; matrix products, arithmetic and copies ran while one was open for 0% -> 0% of each run, Pallas kernels for 15% -> 16%
where the time goes in v12:
time: 42 us; the launch traced here: 41.8 us
  waiting for transfers between devices  12.9 us (31%)
  starting transfers between devices  12.4 us (30%)
  Pallas kernels  10.4 us (25%)
  local copies, waits for them, and re-layouts  2.27 us (5%)
  blocking collectives  1.99 us (5%)
  other arithmetic  1.16 us (3%)
  between operations  0.7 us (2%)
    pallas_call x9, Pallas kernels, call(): pl.pallas_call(kernel, out_shape=outs, in_specs=[pl.BlockSpec(memory_spac...  10.4 us
    ppermute x4, waiting for transfers between devices, per_device(): arrived.append(lax.ppermute(payload, ('chan', 'pipe'), pairs))  6.64 us
    ppermute x3, starting transfers between devices, turned(): lax.ppermute(message, 'chan', [(i, (i + by) % chan) for i in range(chan)])  6.53 us
    ppermute x4, starting transfers between devices, per_device(): arrived.append(lax.ppermute(payload, ('chan', 'pipe'), pairs))  5.74 us
    ppermute x3, waiting for transfers between devices, turned(): lax.ppermute(message, 'chan', [(i, (i + by) % chan) for i in range(chan)])  5.08 us
    unnamed x4, local copies, waits for them, and re-layouts  2.27 us
    all_gather x1, blocking collectives, per_device(): from_late = lax.all_gather(to_late, 'space', axis=0, tiled=False)  1.99 us
    another operation x1, other arithmetic, per_device(): jnp.stack([activations[0], cotangent])  1.16 us
  transfers between devices with their start and end apart: 9, of which 6 were waited for; matrix products, arithmetic and copies ran while one was open for 0% of the time, Pallas kernels for 16%

profile of v12, /device:TPU:0, one launch (start us, length us, event | category | flops | bytes accessed | tf_op | source)
XLA Modules:
  0.0 41.8 jit_solution(662685361228170709)
XLA Ops:
  0.6 1.2 %pad_maximum_fusion.both_ref = bf16[2,2,8,4,4,256]{5,4,3,2,1,0:T(4,128)(2,1)S(1)} fusion(bf16[1,2,8,4,4,256]{5,4,3,2,1,0:T(4,128)(2,1)} %bitcast.16, bf16[1,2,8,4,4,256]{5,4,3,2,1,0:T(4,128)(2,1)} %param.4), kind=kLoop, calls=%fused_computation | loop fusion | flops 131072 | bytes 524288 | tf_op jit(solution)/shard_map/stack | solution.py:396
  1.8 0.1 shard_map.67
  1.9 3.1 %collective-permute-start = (bf16[20,16,256]{2,1,0:T(8,128)(2,1)S(1)}, bf16[20,16,256]{2,1,0:T(8,128)(2,1)S(1)}, u32[]{:S(2)}, u32[]{:S(2)}) collective-permute-start(bf16[20,16,256]{2,1,0:T(8,128)(2,1)S(1)} %get-tuple-element.23), channel_id=1, source_target_pairs={{0,4},{4,8},{8,12},{12,0},{1,5},{5,9},{9,13},{13,1},{2,6},{6,10},{... | collective-permute-start | bytes 491528 | tf_op jit(solution)/shard_map/ppermute | solution.py:416
  5.0 2.1 %collective-permute-start.1 = (bf16[20,16,256]{2,1,0:T(8,128)(2,1)S(1)}, bf16[20,16,256]{2,1,0:T(8,128)(2,1)S(1)}, u32[]{:S(2)}, u32[]{:S(2)}) collective-permute-start(bf16[20,16,256]{2,1,0:T(8,128)(2,1)S(1)} %get-tuple-element.24), channel_id=1, source_target_pairs={{0,12},{4,0},{8,4},{12,8},{1,13},{5,1},{9,5},{13,9},{2,14},{6,2},{... | collective-permute-start | bytes 491528 | tf_op jit(solution)/shard_map/ppermute | solution.py:416
  7.1 0.0 copy-start
  7.1 1.3 %copy-done = bf16[1,3,3,256,256]{4,3,2,1,0:T(8,128)(2,1)S(1)} copy-done((bf16[1,3,3,256,256]{4,3,2,1,0:T(8,128)(2,1)S(1)}, bf16[1,3,3,256,256]{4,3,2,1,0:T(8,128)(2,1)}, u32[]{:S(2)}) %copy-start) | copy-done | bytes 1179672
  8.3 0.0 copy-start.1
  8.3 1.0 %copy-done.1 = bf16[1,3,256,256]{3,2,1,0:T(8,128)(2,1)S(1)} copy-done((bf16[1,3,256,256]{3,2,1,0:T(8,128)(2,1)S(1)}, bf16[1,3,256,256]{3,2,1,0:T(8,128)(2,1)}, u32[]{:S(2)}) %copy-start.1) | copy-done | bytes 393240
  9.3 0.1 shard_map.68
  9.5 2.6 %collective-permute-done.l_ref.refs_1_ = bf16[20,16,256]{2,1,0:T(8,128)(2,1)S(1)} collective-permute-done((bf16[20,16,256]{2,1,0:T(8,128)(2,1)S(1)}, bf16[20,16,256]{2,1,0:T(8,128)(2,1)S(1)}, u32[]{:S(2)}, u32[]{:S(2)}) %collective-permute-start) | collective-permute-done | bytes 163872 | tf_op jit(solution)/shard_map/ppermute | solution.py:416
  12.1 2.1 %collective-permute-done.1.r_ref.refs_3_ = bf16[20,16,256]{2,1,0:T(8,128)(2,1)S(1)} collective-permute-done((bf16[20,16,256]{2,1,0:T(8,128)(2,1)S(1)}, bf16[20,16,256]{2,1,0:T(8,128)(2,1)S(1)}, u32[]{:S(2)}, u32[]{:S(2)}) %collective-permute-start.1) | collective-permute-done | bytes 163872 | tf_op jit(solution)/shard_map/ppermute | solution.py:416
  14.2 0.1 collective-permute-start.2
  14.3 1.4 %collective-permute-start.7 = (bf16[16,16,256]{2,1,0:T(8,128)(2,1)S(1)}, bf16[16,16,256]{2,1,0:T(8,128)(2,1)S(1)}, u32[]{:S(2)}, u32[]{:S(2)}) collective-permute-start(bf16[16,16,256]{2,1,0:T(8,128)(2,1)S(1)} %bitcast.12), channel_id=1, source_target_pairs={{0,8},{4,12},{8,0},{12,4},{1,9},{5,13},{9,1},{13,5},{2,10},{6,14},... | collective-permute-start | bytes 393224 | tf_op jit(solution)/shard_map/ppermute | solution.py:416
  15.6 0.4 %collective-permute-done.2.side_ref.refs_4_ = bf16[54,16,256]{2,1,0:T(8,128)(2,1)S(1)} collective-permute-done((bf16[54,16,256]{2,1,0:T(8,128)(2,1)S(1)}, bf16[54,16,256]{2,1,0:T(8,128)(2,1)S(1)}, u32[]{:S(2)}, u32[]{:S(2)}) %collective-permute-start.2) | collective-permute-done | bytes 442400 | tf_op jit(solution)/shard_map/ppermute | solution.py:436
  16.0 2.1 %shard_map.70 = (f32[576,256]{1,0:T(8,128)S(1)}, bf16[4,4,16,256]{3,2,1,0:T(8,128)(2,1)S(1)}) custom-call(bf16[4,4,16,256]{3,2,1,0:T(8,128)(2,1)S(1)} %get-tuple-element.21.after_ref.x_ref.refs_0_, bf16[4,4,16,256]{3,2,1,0:T(8,128)(2,1)S(1)} %get-tuple-element.22.cot_ref, bf16[20,16,256]{2,1,0:T(8,128)(2,1)S(1)} %collective-permute-done.l_ref.refs_1_, ...), custom_call_target="tpu_custom_call" | custom-call | flops 1 | bytes 1 | tf_op jit(solution)/shard_map/pallas_call | solution.py:361
  18.2 1.6 %collective-permute-start.3 = (bf16[4,4,16,256]{3,2,1,0:T(8,128)(2,1)S(1)}, bf16[4,4,16,256]{3,2,1,0:T(8,128)(2,1)S(1)}, u32[]{:S(2)}, u32[]{:S(2)}) collective-permute-start(bf16[4,4,16,256]{3,2,1,0:T(8,128)(2,1)S(1)} %get-tuple-element.28.refs_1_), channel_id=1, source_target_pairs={{0,2},{4,6},{8,10},{12,14},{2,0},{6,4},{10,8},{14,12},{1,3},{5,7},... | collective-permute-start | bytes 393224 | tf_op jit(solution)/shard_map/ppermute | solution.py:500
  19.8 2.3 %collective-permute-start.6 = (bf16[4,4,16,256]{3,2,1,0:T(8,128)(2,1)S(1)}, bf16[4,4,16,256]{3,2,1,0:T(8,128)(2,1)S(1)}, u32[]{:S(2)}, u32[]{:S(2)}) collective-permute-start(bf16[4,4,16,256]{3,2,1,0:T(8,128)(2,1)S(1)} %get-tuple-element.28.refs_1_), channel_id=1, source_target_pairs={{0,14},{4,2},{8,6},{12,10},{2,12},{6,0},{10,4},{14,8},{1,15},{5,3}... | collective-permute-start | bytes 393224 | tf_op jit(solution)/shard_map/ppermute | solution.py:500
  22.0 1.2 %collective-permute-start.5 = (bf16[4,4,16,256]{3,2,1,0:T(8,128)(2,1)S(1)}, bf16[4,4,16,256]{3,2,1,0:T(8,128)(2,1)S(1)}, u32[]{:S(2)}, u32[]{:S(2)}) collective-permute-start(bf16[4,4,16,256]{3,2,1,0:T(8,128)(2,1)S(1)} %get-tuple-element.28.refs_1_), channel_id=1, source_target_pairs={{0,10},{4,14},{8,2},{12,6},{2,8},{6,12},{10,0},{14,4},{1,11},{5,15... | collective-permute-start | bytes 393224 | tf_op jit(solution)/shard_map/ppermute | solution.py:500
  23.3 0.7 %collective-permute-start.4 = (bf16[4,4,16,256]{3,2,1,0:T(8,128)(2,1)S(1)}, bf16[4,4,16,256]{3,2,1,0:T(8,128)(2,1)S(1)}, u32[]{:S(2)}, u32[]{:S(2)}) collective-permute-start(bf16[4,4,16,256]{3,2,1,0:T(8,128)(2,1)S(1)} %get-tuple-element.28.refs_1_), channel_id=1, source_target_pairs={{0,6},{4,10},{8,14},{12,2},{2,4},{6,8},{10,12},{14,0},{1,7},{5,11}... | collective-permute-start | bytes 393224 | tf_op jit(solution)/shard_map/ppermute | solution.py:500
  23.9 0.4 collective-permute-done.7.refs_0_.refs_2_
  24.3 2.0 %all-gather = bf16[32,16,256]{2,1,0:T(8,128)(2,1)S(1)} all-gather(bf16[16,16,256]{2,1,0:T(8,128)(2,1)S(1)} %shard_map.71), channel_id=2, replica_groups=mesh['groups'=2,'chan'=4,'pipe'=2,'space'=2] {'space'}, dimensions={0}, use_global_device_ids=true | all-gather | bytes 393216 | tf_op jit(solution)/shard_map/all_gather | solution.py:492
  26.3 0.0 collective-permute-done.3.refs_7_.refs_0_
  26.3 3.1 %shard_map.72 = (bf16[256,2048]{1,0:T(8,128)(2,1)S(1)}, bf16[256,2048]{1,0:T(8,128)(2,1)S(1)}, f32[2048,128]{1,0:T(8,128)S(1)}) custom-call(bf16[4,4,16,256]{3,2,1,0:T(8,128)(2,1)S(1)} %get-tuple-element.21.after_ref.x_ref.refs_0_, bf16[20,16,256]{2,1,0:T(8,128)(2,1)S(1)} %collective-permute-done.l_ref.refs_1_, ...), custom_call_target="tpu_custom_call" | custom-call | flops 1 | bytes 1 | tf_op jit(solution)/shard_map/pallas_call | solution.py:361
  29.4 0.0 collective-permute-done.6.refs_3_
  29.4 6.6 %collective-permute-done.5.refs_2_ = bf16[4,4,16,256]{3,2,1,0:T(8,128)(2,1)S(1)} collective-permute-done((bf16[4,4,16,256]{3,2,1,0:T(8,128)(2,1)S(1)}, bf16[4,4,16,256]{3,2,1,0:T(8,128)(2,1)S(1)}, u32[]{:S(2)}, u32[]{:S(2)}) %collective-permute-start.5) | collective-permute-done | bytes 131104 | tf_op jit(solution)/shard_map/ppermute | solution.py:500
  36.0 0.0 collective-permute-done.4.refs_1_
  36.1 0.1 collective-permute-start.8
  36.2 1.2 %shard_map.74 = (bf16[4,16,16,128]{3,2,1,0:T(8,128)(2,1)S(1)}, f32[256,256]{1,0:T(8,128)S(1)}, f32[256,640]{1,0:T(8,128)S(1)}) custom-call(bf16[4,16,16,256]{3,2,1,0:T(8,128)(2,1)S(1)} %shard_map.73.g_ref, f32[2048,128]{1,0:T(8,128)S(1)} %get-tuple-element.29.refs_4_.slope_ref.slope_s_ref, bf16[256,2048]{1,0:T(8,128)(2,1)S(1)} %get-tuple-element.30.act_ref, ...), custom_call_target="tpu_custom_call" | custom-call | flops 536870912 | bytes 4000000 | tf_op jit(solution)/shard_map/pallas_call | solution.py:361
  37.3 0.7 %collective-permute-done.8.other_ref = bf16[4,16,16,256]{3,2,1,0:T(8,128)(2,1)S(1)} collective-permute-done((bf16[4,16,16,256]{3,2,1,0:T(8,128)(2,1)S(1)}, bf16[4,16,16,256]{3,2,1,0:T(8,128)(2,1)S(1)}, u32[]{:S(2)}, u32[]{:S(2)}) %collective-permute-start.8) | collective-permute-done | bytes 524320 | tf_op jit(solution)/shard_map/ppermute | solution.py:450
  38.1 3.7 %shard_map.75 = (bf16[2,8,4,4,256]{4,3,2,1,0:T(4,128)(2,1)}, f32[9,64,256]{2,1,0:T(8,128)}, f32[3,64,256]{2,1,0:T(8,128)}) custom-call(bf16[4,16,16,256]{3,2,1,0:T(8,128)(2,1)S(1)} %shard_map.73.g_ref, bf16[4,16,16,256]{3,2,1,0:T(8,128)(2,1)S(1)} %collective-permute-done.8.other_ref, bf16[4,16,16,128]{3,2,1,0:T(8,128)(2,1)S(1)} %get-tuple-element.32.near_ref, ...), custom_call_target="tpu_custom_call" | custom-call | flops 1358954496 | bytes 8000000 | tf_op jit(solution)/shard_map/pallas_call | solution.py:361
  (3 shorter events, 0.1 us)
Async XLA Ops:
  1.9 10.2 %collective-permute-start = (bf16[20,16,256]{2,1,0:T(8,128)(2,1)S(1)}, bf16[20,16,256]{2,1,0:T(8,128)(2,1)S(1)}, u32[]{:S(2)}, u32[]{:S(2)}) collective-permute-start(bf16[20,16,256]{2,1,0:T(8,128)(2,1)S(1)} %get-tuple-element.23), channel_id=1, source_target_pairs={{0,4},{4,8},{8,12},{12,0},{1,5},{5,9},{9,13},{13,1},{2,6},{6,10},{... | collective-permute-start | bytes 491528 | tf_op jit(solution)/shard_map/ppermute | solution.py:416
  5.0 9.2 %collective-permute-start.1 = (bf16[20,16,256]{2,1,0:T(8,128)(2,1)S(1)}, bf16[20,16,256]{2,1,0:T(8,128)(2,1)S(1)}, u32[]{:S(2)}, u32[]{:S(2)}) collective-permute-start(bf16[20,16,256]{2,1,0:T(8,128)(2,1)S(1)} %get-tuple-element.24), channel_id=1, source_target_pairs={{0,12},{4,0},{8,4},{12,8},{1,13},{5,1},{9,5},{13,9},{2,14},{6,2},{... | collective-permute-start | bytes 491528 | tf_op jit(solution)/shard_map/ppermute | solution.py:416
  7.1 1.3 %copy-start = (bf16[1,3,3,256,256]{4,3,2,1,0:T(8,128)(2,1)S(1)}, bf16[1,3,3,256,256]{4,3,2,1,0:T(8,128)(2,1)}, u32[]{:S(2)}) copy-start(bf16[1,3,3,256,256]{4,3,2,1,0:T(8,128)(2,1)} %param.6) | copy-start | bytes 3538948
  8.3 1.0 %copy-start.1 = (bf16[1,3,256,256]{3,2,1,0:T(8,128)(2,1)S(1)}, bf16[1,3,256,256]{3,2,1,0:T(8,128)(2,1)}, u32[]{:S(2)}) copy-start(bf16[1,3,256,256]{3,2,1,0:T(8,128)(2,1)} %param.7) | copy-start | bytes 1179652
  14.2 1.9 %collective-permute-start.2 = (bf16[54,16,256]{2,1,0:T(8,128)(2,1)S(1)}, bf16[54,16,256]{2,1,0:T(8,128)(2,1)S(1)}, u32[]{:S(2)}, u32[]{:S(2)}) collective-permute-start(bf16[54,16,256]{2,1,0:T(8,128)(2,1)S(1)} %shard_map.69), channel_id=1, source_target_pairs={{0,1},{1,0},{2,3},{3,2},{4,5},{5,4},{6,7},{7,6},{8,9},{9,8},{10,11... | collective-permute-start | bytes 1327112 | tf_op jit(solution)/shard_map/ppermute | solution.py:436
  14.3 10.1 %collective-permute-start.7 = (bf16[16,16,256]{2,1,0:T(8,128)(2,1)S(1)}, bf16[16,16,256]{2,1,0:T(8,128)(2,1)S(1)}, u32[]{:S(2)}, u32[]{:S(2)}) collective-permute-start(bf16[16,16,256]{2,1,0:T(8,128)(2,1)S(1)} %bitcast.12), channel_id=1, source_target_pairs={{0,8},{4,12},{8,0},{12,4},{1,9},{5,13},{9,1},{13,5},{2,10},{6,14},... | collective-permute-start | bytes 393224 | tf_op jit(solution)/shard_map/ppermute | solution.py:416
  18.2 8.1 %collective-permute-start.3 = (bf16[4,4,16,256]{3,2,1,0:T(8,128)(2,1)S(1)}, bf16[4,4,16,256]{3,2,1,0:T(8,128)(2,1)S(1)}, u32[]{:S(2)}, u32[]{:S(2)}) collective-permute-start(bf16[4,4,16,256]{3,2,1,0:T(8,128)(2,1)S(1)} %get-tuple-element.28.refs_1_), channel_id=1, source_target_pairs={{0,2},{4,6},{8,10},{12,14},{2,0},{6,4},{10,8},{14,12},{1,3},{5,7},... | collective-permute-start | bytes 393224 | tf_op jit(solution)/shard_map/ppermute | solution.py:500
  19.8 9.6 %collective-permute-start.6 = (bf16[4,4,16,256]{3,2,1,0:T(8,128)(2,1)S(1)}, bf16[4,4,16,256]{3,2,1,0:T(8,128)(2,1)S(1)}, u32[]{:S(2)}, u32[]{:S(2)}) collective-permute-start(bf16[4,4,16,256]{3,2,1,0:T(8,128)(2,1)S(1)} %get-tuple-element.28.refs_1_), channel_id=1, source_target_pairs={{0,14},{4,2},{8,6},{12,10},{2,12},{6,0},{10,4},{14,8},{1,15},{5,3}... | collective-permute-start | bytes 393224 | tf_op jit(solution)/shard_map/ppermute | solution.py:500
  22.0 14.0 %collective-permute-start.5 = (bf16[4,4,16,256]{3,2,1,0:T(8,128)(2,1)S(1)}, bf16[4,4,16,256]{3,2,1,0:T(8,128)(2,1)S(1)}, u32[]{:S(2)}, u32[]{:S(2)}) collective-permute-start(bf16[4,4,16,256]{3,2,1,0:T(8,128)(2,1)S(1)} %get-tuple-element.28.refs_1_), channel_id=1, source_target_pairs={{0,10},{4,14},{8,2},{12,6},{2,8},{6,12},{10,0},{14,4},{1,11},{5,15... | collective-permute-start | bytes 393224 | tf_op jit(solution)/shard_map/ppermute | solution.py:500
  23.3 12.8 %collective-permute-start.4 = (bf16[4,4,16,256]{3,2,1,0:T(8,128)(2,1)S(1)}, bf16[4,4,16,256]{3,2,1,0:T(8,128)(2,1)S(1)}, u32[]{:S(2)}, u32[]{:S(2)}) collective-permute-start(bf16[4,4,16,256]{3,2,1,0:T(8,128)(2,1)S(1)} %get-tuple-element.28.refs_1_), channel_id=1, source_target_pairs={{0,6},{4,10},{8,14},{12,2},{2,4},{6,8},{10,12},{14,0},{1,7},{5,11}... | collective-permute-start | bytes 393224 | tf_op jit(solution)/shard_map/ppermute | solution.py:500
  36.1 2.0 %collective-permute-start.8 = (bf16[4,16,16,256]{3,2,1,0:T(8,128)(2,1)S(1)}, bf16[4,16,16,256]{3,2,1,0:T(8,128)(2,1)S(1)}, u32[]{:S(2)}, u32[]{:S(2)}) collective-permute-start(bf16[4,16,16,256]{3,2,1,0:T(8,128)(2,1)S(1)} %shard_map.73.g_ref), channel_id=1, source_target_pairs={{0,1},{1,0},{2,3},{3,2},{4,5},{5,4},{6,7},{7,6},{8,9},{9,8},{10,11... | collective-permute-start | bytes 1572872 | tf_op jit(solution)/shard_map/ppermute | solution.py:450

commit v13 on v12

--- a/solution.py
+++ b/solution.py
@@ -324,7 +324,8 @@
 def final_kernel(
     frames, share, g_ref, other_ref, near_ref, time_near_ref, space_near_ref, slope_w_ref,
     slope_s_ref, act_ref, xt_ref, w_ref, tw_ref, pick_ref,
-    out_ref, space_ref, time_ref, gw_ref, hg_ref, hs_ref, hcols_ref, gcols_ref,
+    out_ref, space_out, time_out, gw_ref, hg_ref, hs_ref, hcols_ref, gcols_ref,
+    space_ref, time_ref, sems,
 ):
     rows, width, steps, channels = g_ref.shape
     clips, _, _, cols, _ = out_ref.shape
@@ -339,11 +340,15 @@
         other_ref, 1 - bottom, slope_s_ref, act_ref, pick_ref, put, gcols_ref, frames, share
     )
     time_ref[...] = time_sum.T[: 3 * share].reshape(time_ref.shape)
+    time_copy = pltpu.make_async_copy(time_ref, time_out, sems.at[0])
+    time_copy.start()
     top = (1 - bottom) * (rows - 1)
     space_sum = space_near_ref[...] + tap_products(
         hs_ref, top, top, rows + 1, xt_ref, hcols_ref, share
     )
     space_ref[...] = space_sum.T[: 9 * share].reshape(space_ref.shape)
+    space_copy = pltpu.make_async_copy(space_ref, space_out, sems.at[1])
+    space_copy.start()
     clear_rim(gw_ref)
     gw_ref[1 : 1 + rows, 1 : 1 + width] = g_ref[...]
     gw_ref[(1 - bottom) * (rows + 1), 1 : 1 + width] = other_ref[bottom * (rows - 1)]
@@ -351,17 +356,24 @@
     grads = (own.astype(F32) + conv).astype(BF16).reshape(rows, cols, steps, channels)
     for r in range(rows):
         out_ref[:, :, r] = jnp.swapaxes(grads[r], 0, 1).reshape(clips, frames, cols, channels)
+    time_copy.wait()
+    space_copy.wait()
 
 
 VM = pltpu.VMEM
 
 
-def call(kernel, outs, scratch, limit, flops, moved, *operands, places=None):
+def call(kernel, outs, scratch, limit, flops, moved, *operands, places=None, out_places=None):
     places = places or [VM] * len(operands)
     return pl.pallas_call(
         kernel,
         out_shape=outs,
         in_specs=[pl.BlockSpec(memory_space=place) for place in places],
+        **(
+            {"out_specs": tuple(pl.BlockSpec(memory_space=place) for place in out_places)}
+            if out_places
+            else {}
+        ),
         scratch_shapes=scratch,
         compiler_params=pltpu.CompilerParams(vmem_limit_bytes=limit * MIB),
         cost_estimate=pl.CostEstimate(flops=flops, bytes_accessed=moved, transcendentals=0),
@@ -550,11 +562,15 @@
             pltpu.VMEM((height + 2, width + 2, steps, lanes), BF16),
             pltpu.VMEM(((rows + 1) * width * steps, tap_groups * lanes), BF16),
             pltpu.VMEM((count // 2, lag_groups * lanes), BF16),
+            pltpu.VMEM((9, share, channels), F32),
+            pltpu.VMEM((3, share, channels), F32),
+            pltpu.SemaphoreType.DMA((2,)),
         ],
         large,
         4 * win * 9 * channels * channels,
         8_000_000,
         *g_all, grad_near, time_near, space_near, slope_w, slope_s, act_t, x_t, w, tw, pick,
+        out_places=[VM, pl.ANY, pl.ANY],
     )
     return (
         grads[None],

time: 42 us -> 42.6 us (1.014)
  Pallas kernels: 10.4 us -> 10.9 us
    pallas_call x9, Pallas kernels: 10.4 us -> 10.9 us  [call(): pl.pallas_call(kernel, out_shape=outs, in_specs=[pl.BlockSpec(memory_spac...]
  transfers between devices with their start and end apart: 9 -> 9, of which waited for: 6 -> 6; matrix products, arithmetic and copies ran while one was open for 0% -> 0% of each run, Pallas kernels for 16% -> 15%
where the time goes in v13:
time: 42.6 us; the launch traced here: 42.3 us
  waiting for transfers between devices  12.9 us (30%)
  starting transfers between devices  12.4 us (29%)
  Pallas kernels  10.9 us (26%)
  local copies, waits for them, and re-layouts  2.27 us (5%)
  blocking collectives  1.99 us (5%)
  other arithmetic  1.16 us (3%)
  between operations  0.7 us (2%)
    pallas_call x9, Pallas kernels, call(): pl.pallas_call(kernel, out_shape=outs, in_specs=[pl.BlockSpec(memory_spac...  10.9 us
    ppermute x4, waiting for transfers between devices, per_device(): arrived.append(lax.ppermute(payload, ('chan', 'pipe'), pairs))  6.64 us
    ppermute x3, starting transfers between devices, turned(): lax.ppermute(message, 'chan', [(i, (i + by) % chan) for i in range(chan)])  6.53 us
    ppermute x4, starting transfers between devices, per_device(): arrived.append(lax.ppermute(payload, ('chan', 'pipe'), pairs))  5.74 us
    ppermute x3, waiting for transfers between devices, turned(): lax.ppermute(message, 'chan', [(i, (i + by) % chan) for i in range(chan)])  5.08 us
    unnamed x4, local copies, waits for them, and re-layouts  2.27 us
    all_gather x1, blocking collectives, per_device(): from_late = lax.all_gather(to_late, 'space', axis=0, tiled=False)  1.99 us
    another operation x1, other arithmetic, per_device(): jnp.stack([activations[0], cotangent])  1.16 us
  transfers between devices with their start and end apart: 9, of which 6 were waited for; matrix products, arithmetic and copies ran while one was open for 0% of the time, Pallas kernels for 15%

profile of v13, /device:TPU:0, one launch (start us, length us, event | category | flops | bytes accessed | tf_op | source)
XLA Modules:
  0.0 42.3 jit_solution(18089050556718354374)
XLA Ops:
  0.6 1.2 %pad_maximum_fusion.both_ref = bf16[2,2,8,4,4,256]{5,4,3,2,1,0:T(4,128)(2,1)S(1)} fusion(bf16[1,2,8,4,4,256]{5,4,3,2,1,0:T(4,128)(2,1)} %bitcast.16, bf16[1,2,8,4,4,256]{5,4,3,2,1,0:T(4,128)(2,1)} %param.4), kind=kLoop, calls=%fused_computation | loop fusion | flops 131072 | bytes 524288 | tf_op jit(solution)/shard_map/stack | solution.py:408
  1.8 0.1 shard_map.67
  1.9 3.1 %collective-permute-start = (bf16[20,16,256]{2,1,0:T(8,128)(2,1)S(1)}, bf16[20,16,256]{2,1,0:T(8,128)(2,1)S(1)}, u32[]{:S(2)}, u32[]{:S(2)}) collective-permute-start(bf16[20,16,256]{2,1,0:T(8,128)(2,1)S(1)} %get-tuple-element.23), channel_id=1, source_target_pairs={{0,4},{4,8},{8,12},{12,0},{1,5},{5,9},{9,13},{13,1},{2,6},{6,10},{... | collective-permute-start | bytes 491528 | tf_op jit(solution)/shard_map/ppermute | solution.py:428
  5.0 2.1 %collective-permute-start.1 = (bf16[20,16,256]{2,1,0:T(8,128)(2,1)S(1)}, bf16[20,16,256]{2,1,0:T(8,128)(2,1)S(1)}, u32[]{:S(2)}, u32[]{:S(2)}) collective-permute-start(bf16[20,16,256]{2,1,0:T(8,128)(2,1)S(1)} %get-tuple-element.24), channel_id=1, source_target_pairs={{0,12},{4,0},{8,4},{12,8},{1,13},{5,1},{9,5},{13,9},{2,14},{6,2},{... | collective-permute-start | bytes 491528 | tf_op jit(solution)/shard_map/ppermute | solution.py:428
  7.1 0.0 copy-start
  7.1 1.3 %copy-done = bf16[1,3,3,256,256]{4,3,2,1,0:T(8,128)(2,1)S(1)} copy-done((bf16[1,3,3,256,256]{4,3,2,1,0:T(8,128)(2,1)S(1)}, bf16[1,3,3,256,256]{4,3,2,1,0:T(8,128)(2,1)}, u32[]{:S(2)}) %copy-start) | copy-done | bytes 1179672
  8.3 0.0 copy-start.1
  8.3 1.0 %copy-done.1 = bf16[1,3,256,256]{3,2,1,0:T(8,128)(2,1)S(1)} copy-done((bf16[1,3,256,256]{3,2,1,0:T(8,128)(2,1)S(1)}, bf16[1,3,256,256]{3,2,1,0:T(8,128)(2,1)}, u32[]{:S(2)}) %copy-start.1) | copy-done | bytes 393240
  9.3 0.1 shard_map.68
  9.5 2.6 %collective-permute-done.l_ref.refs_1_ = bf16[20,16,256]{2,1,0:T(8,128)(2,1)S(1)} collective-permute-done((bf16[20,16,256]{2,1,0:T(8,128)(2,1)S(1)}, bf16[20,16,256]{2,1,0:T(8,128)(2,1)S(1)}, u32[]{:S(2)}, u32[]{:S(2)}) %collective-permute-start) | collective-permute-done | bytes 163872 | tf_op jit(solution)/shard_map/ppermute | solution.py:428
  12.1 2.1 %collective-permute-done.1.r_ref.refs_3_ = bf16[20,16,256]{2,1,0:T(8,128)(2,1)S(1)} collective-permute-done((bf16[20,16,256]{2,1,0:T(8,128)(2,1)S(1)}, bf16[20,16,256]{2,1,0:T(8,128)(2,1)S(1)}, u32[]{:S(2)}, u32[]{:S(2)}) %collective-permute-start.1) | collective-permute-done | bytes 163872 | tf_op jit(solution)/shard_map/ppermute | solution.py:428
  14.2 0.1 collective-permute-start.2
  14.3 1.4 %collective-permute-start.7 = (bf16[16,16,256]{2,1,0:T(8,128)(2,1)S(1)}, bf16[16,16,256]{2,1,0:T(8,128)(2,1)S(1)}, u32[]{:S(2)}, u32[]{:S(2)}) collective-permute-start(bf16[16,16,256]{2,1,0:T(8,128)(2,1)S(1)} %bitcast.12), channel_id=1, source_target_pairs={{0,8},{4,12},{8,0},{12,4},{1,9},{5,13},{9,1},{13,5},{2,10},{6,14},... | collective-permute-start | bytes 393224 | tf_op jit(solution)/shard_map/ppermute | solution.py:428
  15.6 0.4 collective-permute-done.2.side_ref.refs_4_
  16.0 2.1 %shard_map.70 = (f32[576,256]{1,0:T(8,128)S(1)}, bf16[4,4,16,256]{3,2,1,0:T(8,128)(2,1)S(1)}) custom-call(bf16[4,4,16,256]{3,2,1,0:T(8,128)(2,1)S(1)} %get-tuple-element.21.after_ref.x_ref.refs_0_, bf16[4,4,16,256]{3,2,1,0:T(8,128)(2,1)S(1)} %get-tuple-element.22.cot_ref, bf16[20,16,256]{2,1,0:T(8,128)(2,1)S(1)} %collective-permute-done.l_ref.refs_1_, ...), custom_call_target="tpu_custom_call" | custom-call | flops 1 | bytes 1 | tf_op jit(solution)/shard_map/pallas_call | solution.py:368
  18.2 1.6 %collective-permute-start.3 = (bf16[4,4,16,256]{3,2,1,0:T(8,128)(2,1)S(1)}, bf16[4,4,16,256]{3,2,1,0:T(8,128)(2,1)S(1)}, u32[]{:S(2)}, u32[]{:S(2)}) collective-permute-start(bf16[4,4,16,256]{3,2,1,0:T(8,128)(2,1)S(1)} %get-tuple-element.28.refs_1_), channel_id=1, source_target_pairs={{0,2},{4,6},{8,10},{12,14},{2,0},{6,4},{10,8},{14,12},{1,3},{5,7},... | collective-permute-start | bytes 393224 | tf_op jit(solution)/shard_map/ppermute | solution.py:512
  19.8 2.3 %collective-permute-start.6 = (bf16[4,4,16,256]{3,2,1,0:T(8,128)(2,1)S(1)}, bf16[4,4,16,256]{3,2,1,0:T(8,128)(2,1)S(1)}, u32[]{:S(2)}, u32[]{:S(2)}) collective-permute-start(bf16[4,4,16,256]{3,2,1,0:T(8,128)(2,1)S(1)} %get-tuple-element.28.refs_1_), channel_id=1, source_target_pairs={{0,14},{4,2},{8,6},{12,10},{2,12},{6,0},{10,4},{14,8},{1,15},{5,3}... | collective-permute-start | bytes 393224 | tf_op jit(solution)/shard_map/ppermute | solution.py:512
  22.0 1.2 %collective-permute-start.5 = (bf16[4,4,16,256]{3,2,1,0:T(8,128)(2,1)S(1)}, bf16[4,4,16,256]{3,2,1,0:T(8,128)(2,1)S(1)}, u32[]{:S(2)}, u32[]{:S(2)}) collective-permute-start(bf16[4,4,16,256]{3,2,1,0:T(8,128)(2,1)S(1)} %get-tuple-element.28.refs_1_), channel_id=1, source_target_pairs={{0,10},{4,14},{8,2},{12,6},{2,8},{6,12},{10,0},{14,4},{1,11},{5,15... | collective-permute-start | bytes 393224 | tf_op jit(solution)/shard_map/ppermute | solution.py:512
  23.3 0.7 %collective-permute-start.4 = (bf16[4,4,16,256]{3,2,1,0:T(8,128)(2,1)S(1)}, bf16[4,4,16,256]{3,2,1,0:T(8,128)(2,1)S(1)}, u32[]{:S(2)}, u32[]{:S(2)}) collective-permute-start(bf16[4,4,16,256]{3,2,1,0:T(8,128)(2,1)S(1)} %get-tuple-element.28.refs_1_), channel_id=1, source_target_pairs={{0,6},{4,10},{8,14},{12,2},{2,4},{6,8},{10,12},{14,0},{1,7},{5,11}... | collective-permute-start | bytes 393224 | tf_op jit(solution)/shard_map/ppermute | solution.py:512
  23.9 0.4 collective-permute-done.7.refs_0_.refs_2_
  24.3 2.0 %all-gather = bf16[32,16,256]{2,1,0:T(8,128)(2,1)S(1)} all-gather(bf16[16,16,256]{2,1,0:T(8,128)(2,1)S(1)} %shard_map.71), channel_id=2, replica_groups=mesh['groups'=2,'chan'=4,'pipe'=2,'space'=2] {'space'}, dimensions={0}, use_global_device_ids=true | all-gather | bytes 393216 | tf_op jit(solution)/shard_map/all_gather | solution.py:504
  26.3 0.0 collective-permute-done.3.refs_7_.refs_0_
  26.3 3.1 %shard_map.72 = (bf16[256,2048]{1,0:T(8,128)(2,1)S(1)}, bf16[256,2048]{1,0:T(8,128)(2,1)S(1)}, f32[2048,128]{1,0:T(8,128)S(1)}) custom-call(bf16[4,4,16,256]{3,2,1,0:T(8,128)(2,1)S(1)} %get-tuple-element.21.after_ref.x_ref.refs_0_, bf16[20,16,256]{2,1,0:T(8,128)(2,1)S(1)} %collective-permute-done.l_ref.refs_1_, ...), custom_call_target="tpu_custom_call" | custom-call | flops 1 | bytes 1 | tf_op jit(solution)/shard_map/pallas_call | solution.py:368
  29.4 0.0 collective-permute-done.6.refs_3_
  29.4 6.6 %collective-permute-done.5.refs_2_ = bf16[4,4,16,256]{3,2,1,0:T(8,128)(2,1)S(1)} collective-permute-done((bf16[4,4,16,256]{3,2,1,0:T(8,128)(2,1)S(1)}, bf16[4,4,16,256]{3,2,1,0:T(8,128)(2,1)S(1)}, u32[]{:S(2)}, u32[]{:S(2)}) %collective-permute-start.5) | collective-permute-done | bytes 131104 | tf_op jit(solution)/shard_map/ppermute | solution.py:512
  36.0 0.0 collective-permute-done.4.refs_1_
  36.1 0.1 collective-permute-start.8
  36.2 1.2 %shard_map.74 = (bf16[4,16,16,128]{3,2,1,0:T(8,128)(2,1)S(1)}, f32[256,256]{1,0:T(8,128)S(1)}, f32[256,640]{1,0:T(8,128)S(1)}) custom-call(bf16[4,16,16,256]{3,2,1,0:T(8,128)(2,1)S(1)} %shard_map.73.g_ref, f32[2048,128]{1,0:T(8,128)S(1)} %get-tuple-element.29.refs_4_.slope_ref.slope_s_ref, bf16[256,2048]{1,0:T(8,128)(2,1)S(1)} %get-tuple-element.30.act_ref, ...), custom_call_target="tpu_custom_call" | custom-call | flops 536870912 | bytes 4000000 | tf_op jit(solution)/shard_map/pallas_call | solution.py:368
  37.3 0.7 %collective-permute-done.8.other_ref = bf16[4,16,16,256]{3,2,1,0:T(8,128)(2,1)S(1)} collective-permute-done((bf16[4,16,16,256]{3,2,1,0:T(8,128)(2,1)S(1)}, bf16[4,16,16,256]{3,2,1,0:T(8,128)(2,1)S(1)}, u32[]{:S(2)}, u32[]{:S(2)}) %collective-permute-start.8) | collective-permute-done | bytes 524320 | tf_op jit(solution)/shard_map/ppermute | solution.py:462
  38.1 4.3 %shard_map.75 = (bf16[2,8,4,4,256]{4,3,2,1,0:T(4,128)(2,1)}, f32[9,64,256]{2,1,0:T(8,128)}, f32[3,64,256]{2,1,0:T(8,128)}) custom-call(bf16[4,16,16,256]{3,2,1,0:T(8,128)(2,1)S(1)} %shard_map.73.g_ref, bf16[4,16,16,256]{3,2,1,0:T(8,128)(2,1)S(1)} %collective-permute-done.8.other_ref, bf16[4,16,16,128]{3,2,1,0:T(8,128)(2,1)S(1)} %get-tuple-element.32.near_ref, ...), custom_call_target="tpu_custom_call" | custom-call | flops 1358954496 | bytes 8000000 | tf_op jit(solution)/shard_map/pallas_call | solution.py:368
  (3 shorter events, 0.1 us)
Async XLA Ops:
  1.9 10.2 %collective-permute-start = (bf16[20,16,256]{2,1,0:T(8,128)(2,1)S(1)}, bf16[20,16,256]{2,1,0:T(8,128)(2,1)S(1)}, u32[]{:S(2)}, u32[]{:S(2)}) collective-permute-start(bf16[20,16,256]{2,1,0:T(8,128)(2,1)S(1)} %get-tuple-element.23), channel_id=1, source_target_pairs={{0,4},{4,8},{8,12},{12,0},{1,5},{5,9},{9,13},{13,1},{2,6},{6,10},{... | collective-permute-start | bytes 491528 | tf_op jit(solution)/shard_map/ppermute | solution.py:428
  5.0 9.2 %collective-permute-start.1 = (bf16[20,16,256]{2,1,0:T(8,128)(2,1)S(1)}, bf16[20,16,256]{2,1,0:T(8,128)(2,1)S(1)}, u32[]{:S(2)}, u32[]{:S(2)}) collective-permute-start(bf16[20,16,256]{2,1,0:T(8,128)(2,1)S(1)} %get-tuple-element.24), channel_id=1, source_target_pairs={{0,12},{4,0},{8,4},{12,8},{1,13},{5,1},{9,5},{13,9},{2,14},{6,2},{... | collective-permute-start | bytes 491528 | tf_op jit(solution)/shard_map/ppermute | solution.py:428
  7.1 1.3 %copy-start = (bf16[1,3,3,256,256]{4,3,2,1,0:T(8,128)(2,1)S(1)}, bf16[1,3,3,256,256]{4,3,2,1,0:T(8,128)(2,1)}, u32[]{:S(2)}) copy-start(bf16[1,3,3,256,256]{4,3,2,1,0:T(8,128)(2,1)} %param.6) | copy-start | bytes 3538948
  8.3 1.0 %copy-start.1 = (bf16[1,3,256,256]{3,2,1,0:T(8,128)(2,1)S(1)}, bf16[1,3,256,256]{3,2,1,0:T(8,128)(2,1)}, u32[]{:S(2)}) copy-start(bf16[1,3,256,256]{3,2,1,0:T(8,128)(2,1)} %param.7) | copy-start | bytes 1179652
  14.2 1.9 %collective-permute-start.2 = (bf16[54,16,256]{2,1,0:T(8,128)(2,1)S(1)}, bf16[54,16,256]{2,1,0:T(8,128)(2,1)S(1)}, u32[]{:S(2)}, u32[]{:S(2)}) collective-permute-start(bf16[54,16,256]{2,1,0:T(8,128)(2,1)S(1)} %shard_map.69), channel_id=1, source_target_pairs={{0,1},{1,0},{2,3},{3,2},{4,5},{5,4},{6,7},{7,6},{8,9},{9,8},{10,11... | collective-permute-start | bytes 1327112 | tf_op jit(solution)/shard_map/ppermute | solution.py:448
  14.3 10.1 %collective-permute-start.7 = (bf16[16,16,256]{2,1,0:T(8,128)(2,1)S(1)}, bf16[16,16,256]{2,1,0:T(8,128)(2,1)S(1)}, u32[]{:S(2)}, u32[]{:S(2)}) collective-permute-start(bf16[16,16,256]{2,1,0:T(8,128)(2,1)S(1)} %bitcast.12), channel_id=1, source_target_pairs={{0,8},{4,12},{8,0},{12,4},{1,9},{5,13},{9,1},{13,5},{2,10},{6,14},... | collective-permute-start | bytes 393224 | tf_op jit(solution)/shard_map/ppermute | solution.py:428
  18.2 8.1 %collective-permute-start.3 = (bf16[4,4,16,256]{3,2,1,0:T(8,128)(2,1)S(1)}, bf16[4,4,16,256]{3,2,1,0:T(8,128)(2,1)S(1)}, u32[]{:S(2)}, u32[]{:S(2)}) collective-permute-start(bf16[4,4,16,256]{3,2,1,0:T(8,128)(2,1)S(1)} %get-tuple-element.28.refs_1_), channel_id=1, source_target_pairs={{0,2},{4,6},{8,10},{12,14},{2,0},{6,4},{10,8},{14,12},{1,3},{5,7},... | collective-permute-start | bytes 393224 | tf_op jit(solution)/shard_map/ppermute | solution.py:512
  19.8 9.6 %collective-permute-start.6 = (bf16[4,4,16,256]{3,2,1,0:T(8,128)(2,1)S(1)}, bf16[4,4,16,256]{3,2,1,0:T(8,128)(2,1)S(1)}, u32[]{:S(2)}, u32[]{:S(2)}) collective-permute-start(bf16[4,4,16,256]{3,2,1,0:T(8,128)(2,1)S(1)} %get-tuple-element.28.refs_1_), channel_id=1, source_target_pairs={{0,14},{4,2},{8,6},{12,10},{2,12},{6,0},{10,4},{14,8},{1,15},{5,3}... | collective-permute-start | bytes 393224 | tf_op jit(solution)/shard_map/ppermute | solution.py:512
  22.0 14.0 %collective-permute-start.5 = (bf16[4,4,16,256]{3,2,1,0:T(8,128)(2,1)S(1)}, bf16[4,4,16,256]{3,2,1,0:T(8,128)(2,1)S(1)}, u32[]{:S(2)}, u32[]{:S(2)}) collective-permute-start(bf16[4,4,16,256]{3,2,1,0:T(8,128)(2,1)S(1)} %get-tuple-element.28.refs_1_), channel_id=1, source_target_pairs={{0,10},{4,14},{8,2},{12,6},{2,8},{6,12},{10,0},{14,4},{1,11},{5,15... | collective-permute-start | bytes 393224 | tf_op jit(solution)/shard_map/ppermute | solution.py:512
  23.3 12.8 %collective-permute-start.4 = (bf16[4,4,16,256]{3,2,1,0:T(8,128)(2,1)S(1)}, bf16[4,4,16,256]{3,2,1,0:T(8,128)(2,1)S(1)}, u32[]{:S(2)}, u32[]{:S(2)}) collective-permute-start(bf16[4,4,16,256]{3,2,1,0:T(8,128)(2,1)S(1)} %get-tuple-element.28.refs_1_), channel_id=1, source_target_pairs={{0,6},{4,10},{8,14},{12,2},{2,4},{6,8},{10,12},{14,0},{1,7},{5,11}... | collective-permute-start | bytes 393224 | tf_op jit(solution)/shard_map/ppermute | solution.py:512
  36.1 2.0 %collective-permute-start.8 = (bf16[4,16,16,256]{3,2,1,0:T(8,128)(2,1)S(1)}, bf16[4,16,16,256]{3,2,1,0:T(8,128)(2,1)S(1)}, u32[]{:S(2)}, u32[]{:S(2)}) collective-permute-start(bf16[4,16,16,256]{3,2,1,0:T(8,128)(2,1)S(1)} %shard_map.73.g_ref), channel_id=1, source_target_pairs={{0,1},{1,0},{2,3},{3,2},{4,5},{5,4},{6,7},{7,6},{8,9},{9,8},{10,11... | collective-permute-start | bytes 1572872 | tf_op jit(solution)/shard_map/ppermute | solution.py:462
